TPU v7x, 32 devices: a whole 2x2x4 slice. The times are simulated.
32 devices in a mesh: gy: 8 (over z, core), gx: 4 (over y, x).
Axes of the slice: x: 2, y: 2, z: 4, core: 2. Of those that a mesh axis runs over, the one named last changes fastest.
Arguments:
- level_in: bfloat16 [64, 256, 128], P('gy', 'gx'), may hold values from -6 to 6
- w_level: bfloat16 [3, 3, 128, 128], replicated, may hold values from -0.1875 to 0.1875
- w_down: bfloat16 [2, 2, 128, 256], replicated, may hold values from -0.25 to 0.25
- w_neck: bfloat16 [3, 3, 256, 256], replicated, may hold values from -0.125 to 0.125
- cotangent: bfloat16 [32, 128, 256], P('gy', None, 'gx'), may hold values from -6 to 6
Outputs:
- neck_out: bfloat16 [32, 128, 256], P('gy', None, 'gx')
- grad_input: bfloat16 [64, 256, 128], P('gy', 'gx')
- grad_level: bfloat16 [3, 3, 128, 128], replicated
- grad_down: bfloat16 [2, 2, 128, 256], replicated
- grad_neck: bfloat16 [3, 3, 256, 256], replicated
All inputs are finite; a program needn't handle non-finite values.
Results may differ from a plain program's by a relative error of at most 0.012.
Values may be sent and summed in bfloat16 or wider, within the bound.
No kernel may reach another device: no remote copies, remote signals or barrier semaphores. Data moves between devices by JAX's collectives and lax.ppermute only.
A program may use at most 64 MiB of HBM per device.

v0:
```python
import math

import jax
import jax.numpy as jnp
from jax import lax
from jax.sharding import PartitionSpec as P


def extended(cells, sides, width):
    for axis, dim in sides:
        count = lax.axis_size(axis)
        ends = count - 1
        head = lax.slice_in_dim(cells, 0, width, axis=dim)
        tail = lax.slice_in_dim(cells, cells.shape[dim] - width, cells.shape[dim], axis=dim)
        cells = jnp.concatenate(
            [
                lax.ppermute(tail, axis, [(i, (i + 1) % count) for i in range(ends)]),
                cells,
                lax.ppermute(head, axis, [((i + 1) % count, i) for i in range(ends)]),
            ],
            axis=dim,
        )
    return cells


def slope_of(value):
    gate = jax.nn.sigmoid(value)
    return gate + value * gate * (1.0 - gate)


def tile_rims(field_in):
    return extended(field_in, (("gy", 0), ("gx", 1)), 1)


def conv_padded(padded, weights):
    row_count = padded.shape[0] - 2
    col_count = padded.shape[1] - 2
    result = jnp.zeros((row_count * col_count, weights.shape[3]), jnp.float32)
    for offset_y in range(3):
        for offset_x in range(3):
            window = padded[offset_y : offset_y + row_count, offset_x : offset_x + col_count]
            window = window.reshape(row_count * col_count, padded.shape[2])
            result = result + jnp.dot(
                window, weights[offset_y, offset_x], preferred_element_type=jnp.float32
            )
    return result


def weight_terms(padded, grads):
    row_count = grads.shape[0]
    col_count = grads.shape[1]
    flat_grads = grads.reshape(row_count * col_count, grads.shape[2])
    kernel_rows = []
    for offset_y in range(3):
        kernel_row = []
        for offset_x in range(3):
            window = padded[offset_y : offset_y + row_count, offset_x : offset_x + col_count]
            window = window.reshape(row_count * col_count, padded.shape[2])
            kernel_row.append(
                lax.dot_general(
                    window, flat_grads, (((0,), (0,)), ((), ())), preferred_element_type=jnp.float32
                )
            )
        kernel_rows.append(jnp.stack(kernel_row))
    return jnp.stack(kernel_rows)


def local(level_in, w_level, w_down, w_neck, cotangent):
    tile_rows = level_in.shape[0]
    tile_cols = level_in.shape[1]
    level_width = level_in.shape[2]
    neck_width = w_neck.shape[3]
    half_rows = tile_rows // 2
    half_cols = tile_cols // 2
    level_pad = tile_rims(level_in)
    level_pre = conv_padded(level_pad, w_level)
    level_flat = level_in.reshape(tile_rows * tile_cols, level_width).astype(jnp.float32)
    level_act = (level_flat + jax.nn.silu(level_pre)).astype(jnp.bfloat16)
    level_grid = level_act.reshape(half_rows, 2, half_cols, 2, level_width)
    neck_in = jnp.einsum(
        "hpwqc,pqcd->hwd", level_grid, w_down, preferred_element_type=jnp.float32
    ).astype(jnp.bfloat16)
    neck_pad = tile_rims(neck_in)
    neck_pre = conv_padded(neck_pad, w_neck)
    neck_flat = neck_in.reshape(half_rows * half_cols, neck_width).astype(jnp.float32)
    neck_tile = (
        (neck_flat + jax.nn.silu(neck_pre))
        .astype(jnp.bfloat16)
        .reshape(half_rows, half_cols, neck_width)
    )
    neck_out = lax.all_to_all(neck_tile, "gx", split_axis=2, concat_axis=1, tiled=True)
    neck_cot = lax.all_to_all(cotangent, "gx", split_axis=1, concat_axis=2, tiled=True)
    cot_flat = neck_cot.reshape(half_rows * half_cols, neck_width).astype(jnp.float32)
    neck_gate = (
        (cot_flat * slope_of(neck_pre))
        .astype(jnp.bfloat16)
        .reshape(half_rows, half_cols, neck_width)
    )
    flip_neck = jnp.transpose(w_neck[::-1, ::-1], (0, 1, 3, 2))
    gate_pad = tile_rims(neck_gate)
    neck_back = conv_padded(gate_pad, flip_neck)
    cot_tile = neck_cot.reshape(half_rows * half_cols, neck_width).astype(jnp.float32)
    neck_grad = (
        (cot_tile + neck_back).astype(jnp.bfloat16).reshape(half_rows, half_cols, neck_width)
    )
    neck_wgrad = weight_terms(neck_pad, neck_gate)
    level_back = jnp.einsum(
        "hwd,pqcd->hpwqc", neck_grad, w_down, preferred_element_type=jnp.float32
    )
    level_back = level_back.reshape(tile_rows * tile_cols, level_width)
    down_wgrad = jnp.einsum(
        "hpwqc,hwd->pqcd", level_grid, neck_grad, preferred_element_type=jnp.float32
    )
    level_gate = (
        (level_back * slope_of(level_pre))
        .astype(jnp.bfloat16)
        .reshape(tile_rows, tile_cols, level_width)
    )
    flip_level = jnp.transpose(w_level[::-1, ::-1], (0, 1, 3, 2))
    level_gpad = tile_rims(level_gate)
    grad_input = (level_back + conv_padded(level_gpad, flip_level)).astype(jnp.bfloat16)
    grad_input = grad_input.reshape(tile_rows, tile_cols, level_width)
    level_wgrad = weight_terms(level_pad, level_gate)
    device_count = lax.axis_size("gy") * lax.axis_size("gx")
    level_count = tile_rows * tile_cols * device_count
    level_scale = 1.0 / math.sqrt(level_count)
    neck_scale = 1.0 / math.sqrt(level_count // 4)
    reduced = lax.psum((level_wgrad, down_wgrad, neck_wgrad), ("gy", "gx"))
    grad_level = (reduced[0] * level_scale).astype(jnp.bfloat16)
    grad_down = (reduced[1] * neck_scale).astype(jnp.bfloat16)
    grad_neck = (reduced[2] * neck_scale).astype(jnp.bfloat16)
    return (neck_out, grad_input, grad_level, grad_down, grad_neck)


def solution(mesh):
    return jax.shard_map(
        local,
        mesh=mesh,
        in_specs=(P("gy", "gx", None), P(), P(), P(), P("gy", None, "gx")),
        out_specs=(P("gy", None, "gx"), P("gy", "gx", None), P(), P(), P()),
        check_vma=False,
    )
```

profile of v0, /device:TPU:0, one launch (start us, length us, event | category | flops | bytes accessed | tf_op | source)
XLA Modules:
  0.0 256.1 jit_solution(9546807290923951225)
XLA Ops:
  9.0 5.2 %all-to-all-start.1 = ((bf16[4,2,4096]{2,1,0:T(2,128)(2,1)}), bf16[4,2,4096]{2,1,0:T(2,128)(2,1)}, u32[]{:S(2)}, u32[]{:S(2)}) async-start(bf16[4,2,4096]{2,1,0:T(2,128)(2,1)} %reshape.213), calls=%async_computation.1 | async-start | bytes 131072 | tf_op jit(solution)/shard_map/all_to_all | solution.py:92
  14.9 1.4 collective-permute-start
  16.4 1.4 collective-permute-start.1
  17.8 1.3 reverse_bitcast_fusion
  19.2 2.2 collective-permute-done.1
  21.6 3.9 %collective-permute-start.2 = (bf16[10,1,128]{2,1,0:T(2,128)(2,1)S(1)}, bf16[10,1,128]{2,1,0:T(2,128)(2,1)S(1)}, u32[]{:S(2)}, u32[]{:S(2)}) collective-permute-start(bf16[10,1,128]{2,1,0:T(2,128)(2,1)S(1)} %get-tuple-element.42), channel_id=1, source_target_pairs={{0,1},{1,2},{2,3},{4,5},{5,6},{6,7},{8,9},{9,10},{10,11},{12,13},{... | collective-permute-start | bytes 7688 | tf_op jit(solution)/shard_map/ppermute | solution.py:17
  25.4 1.3 collective-permute-start.3
  27.1 3.8 %collective-permute-done.3 = bf16[10,1,128]{2,1,0:T(2,128)(2,1)S(1)} collective-permute-done((bf16[10,1,128]{2,1,0:T(2,128)(2,1)S(1)}, bf16[10,1,128]{2,1,0:T(2,128)(2,1)S(1)}, u32[]{:S(2)}, u32[]{:S(2)}) %collective-permute-start.3) | collective-permute-done | bytes 2592 | tf_op jit(solution)/shard_map/ppermute | solution.py:19
  34.1 1.3 collective-permute-start.5
  35.4 3.6 %collective-permute-start.4 = (bf16[1,32,256]{2,1,0:T(8,128)(2,1)S(1)}, bf16[1,32,256]{2,1,0:T(8,128)(2,1)S(1)}, u32[]{:S(2)}, u32[]{:S(2)}) collective-permute-start(bf16[1,32,256]{2,1,0:T(8,128)(2,1)S(1)} %get-tuple-element.81), channel_id=1, source_target_pairs={{0,4},{4,8},{8,12},{12,16},{16,20},{20,24},{24,28},{1,5},{5,9},{9,... | collective-permute-start | bytes 49160 | tf_op jit(solution)/shard_map/ppermute | solution.py:17
  39.8 4.3 %collective-permute-start.6 = (bf16[6,1,256]{2,1,0:T(2,128)(2,1)S(1)}, bf16[6,1,256]{2,1,0:T(2,128)(2,1)S(1)}, u32[]{:S(2)}, u32[]{:S(2)}) collective-permute-start(bf16[6,1,256]{2,1,0:T(2,128)(2,1)S(1)} %get-tuple-element.73), channel_id=1, source_target_pairs={{0,1},{1,2},{2,3},{4,5},{5,6},{6,7},{8,9},{9,10},{10,11},{12,13},{... | collective-permute-start | bytes 9224 | tf_op jit(solution)/shard_map/ppermute | solution.py:17
  44.1 1.3 collective-permute-start.7
  46.2 3.4 %collective-permute-done.7 = bf16[6,1,256]{2,1,0:T(2,128)(2,1)S(1)} collective-permute-done((bf16[6,1,256]{2,1,0:T(2,128)(2,1)S(1)}, bf16[6,1,256]{2,1,0:T(2,128)(2,1)S(1)}, u32[]{:S(2)}, u32[]{:S(2)}) %collective-permute-start.7) | collective-permute-done | bytes 3104 | tf_op jit(solution)/shard_map/ppermute | solution.py:19
  52.3 1.6 reshape.214
  55.8 1.8 reshape.205
  57.6 2.0 multiply_convert_fusion.4
  59.5 1.1 convolution_bitcast_fusion.1
  68.6 3.4 %all-to-all-start = ((bf16[4,2,4096]{2,1,0:T(2,128)(2,1)}), bf16[4,2,4096]{2,1,0:T(2,128)(2,1)S(1)}, u32[]{:S(2)}, u32[]{:S(2)}) async-start(bf16[4,2,4096]{2,1,0:T(2,128)(2,1)} %reshape.211), calls=%async_computation | async-start | bytes 131072 | tf_op jit(solution)/shard_map/all_to_all | solution.py:91
  72.1 1.4 collective-permute-start.9
  73.6 3.0 %collective-permute-start.8 = (bf16[1,32,256]{2,1,0:T(8,128)(2,1)S(1)}, bf16[1,32,256]{2,1,0:T(8,128)(2,1)S(1)}, u32[]{:S(2)}, u32[]{:S(2)}) collective-permute-start(bf16[1,32,256]{2,1,0:T(8,128)(2,1)S(1)} %get-tuple-element.77), channel_id=1, source_target_pairs={{0,4},{4,8},{8,12},{12,16},{16,20},{20,24},{24,28},{1,5},{5,9},{9,... | collective-permute-start | bytes 49160 | tf_op jit(solution)/shard_map/ppermute | solution.py:17
  77.9 1.6 pad_maximum_fusion
  79.4 3.8 %collective-permute-start.10 = (bf16[6,1,256]{2,1,0:T(2,128)(2,1)S(1)}, bf16[6,1,256]{2,1,0:T(2,128)(2,1)S(1)}, u32[]{:S(2)}, u32[]{:S(2)}) collective-permute-start(bf16[6,1,256]{2,1,0:T(2,128)(2,1)S(1)} %get-tuple-element.69), channel_id=1, source_target_pairs={{0,1},{1,2},{2,3},{4,5},{5,6},{6,7},{8,9},{9,10},{10,11},{12,13},{... | collective-permute-start | bytes 9224 | tf_op jit(solution)/shard_map/ppermute | solution.py:17
  83.3 1.3 collective-permute-start.11
  84.8 4.0 %collective-permute-done.11 = bf16[6,1,256]{2,1,0:T(2,128)(2,1)S(1)} collective-permute-done((bf16[6,1,256]{2,1,0:T(2,128)(2,1)S(1)}, bf16[6,1,256]{2,1,0:T(2,128)(2,1)S(1)}, u32[]{:S(2)}, u32[]{:S(2)}) %collective-permute-start.11) | collective-permute-done | bytes 3104 | tf_op jit(solution)/shard_map/ppermute | solution.py:19
  93.3 1.3 collective-permute-start.13
  94.6 4.8 %collective-permute-start.12 = (bf16[1,64,128]{2,1,0:T(8,128)(2,1)S(1)}, bf16[1,64,128]{2,1,0:T(8,128)(2,1)S(1)}, u32[]{:S(2)}, u32[]{:S(2)}) collective-permute-start(bf16[1,64,128]{2,1,0:T(8,128)(2,1)S(1)} %get-tuple-element.46), channel_id=1, source_target_pairs={{0,4},{4,8},{8,12},{12,16},{16,20},{20,24},{24,28},{1,5},{5,9},{9,... | collective-permute-start | bytes 49160 | tf_op jit(solution)/shard_map/ppermute | solution.py:17
  101.5 4.4 %collective-permute-start.14 = (bf16[10,1,128]{2,1,0:T(2,128)(2,1)S(1)}, bf16[10,1,128]{2,1,0:T(2,128)(2,1)S(1)}, u32[]{:S(2)}, u32[]{:S(2)}) collective-permute-start(bf16[10,1,128]{2,1,0:T(2,128)(2,1)S(1)} %get-tuple-element.37), channel_id=1, source_target_pairs={{0,1},{1,2},{2,3},{4,5},{5,6},{6,7},{8,9},{9,10},{10,11},{12,13},{... | collective-permute-start | bytes 7688 | tf_op jit(solution)/shard_map/ppermute | solution.py:17
  105.9 1.3 collective-permute-start.15
  107.5 4.0 %collective-permute-done.15 = bf16[10,1,128]{2,1,0:T(2,128)(2,1)S(1)} collective-permute-done((bf16[10,1,128]{2,1,0:T(2,128)(2,1)S(1)}, bf16[10,1,128]{2,1,0:T(2,128)(2,1)S(1)}, u32[]{:S(2)}, u32[]{:S(2)}) %collective-permute-start.15) | collective-permute-done | bytes 2592 | tf_op jit(solution)/shard_map/ppermute | solution.py:19
  115.0 128.7 %all-reduce.3.cloned.1.call-done = (f32[3,3,128,128]{3,2,1,0:T(8,128)}, f32[2,2,128,256]{3,2,1,0:T(8,128)}, f32[3,3,256,256]{3,2,1,0:T(8,128)}) async-done(((f32[3,3,128,128]{3,2,1,0:T(8,128)}, f32[2,2,128,256]{3,2,1,0:T(8,128)}, f32[3,3,256,256]{3,2,1,0:T(8,128)}), (f32[3,3,128,128]{3,2,1,0:T(8,128)}, f32[2,2,128,256]{3,2,1,0:T(8,128)}, f32[3,3,256,256]{3,2,1,0:T(8,128)})) %all-reduce.3.cloned.1.call-update) | async-done | bytes 3473424 | tf_op jit(solution)/shard_map/psum | solution.py:128
  243.7 1.9 multiply_convert_fusion.1
  246.3 2.9 %multiply_convert_fusion = bf16[3,3,256,256]{3,2,1,0:T(8,128)(2,1)} fusion(f32[3,3,256,256]{3,2,1,0:T(8,128)} %get-tuple-element.22), kind=kLoop, calls=%fused_computation.1 | loop fusion | flops 1179648 | bytes 3538944 | tf_op jit(solution)/shard_map/convert_element_type | solution.py:131
  (186 shorter events, 32.2 us)
Async XLA Ops:
  7.2 26.7 %copy-start = (bf16[2,2,128,256]{3,2,1,0:T(8,128)(2,1)S(1)}, bf16[2,2,128,256]{3,2,1,0:T(8,128)(2,1)}, u32[]{:S(2)}) copy-start(bf16[2,2,128,256]{3,2,1,0:T(8,128)(2,1)} %param.7) | copy-start | bytes 786436
  9.0 43.3 %all-to-all-start.1 = ((bf16[4,2,4096]{2,1,0:T(2,128)(2,1)}), bf16[4,2,4096]{2,1,0:T(2,128)(2,1)}, u32[]{:S(2)}, u32[]{:S(2)}) async-start(bf16[4,2,4096]{2,1,0:T(2,128)(2,1)} %reshape.213), calls=%async_computation.1 | async-start | bytes 131072 | tf_op jit(solution)/shard_map/all_to_all | solution.py:92
  14.9 4.3 %collective-permute-start = (bf16[1,64,128]{2,1,0:T(8,128)(2,1)S(1)}, bf16[1,64,128]{2,1,0:T(8,128)(2,1)S(1)}, u32[]{:S(2)}, u32[]{:S(2)}) collective-permute-start(bf16[1,64,128]{2,1,0:T(8,128)(2,1)S(1)} %get-tuple-element.54), channel_id=1, source_target_pairs={{0,4},{4,8},{8,12},{12,16},{16,20},{20,24},{24,28},{1,5},{5,9},{9,... | collective-permute-start | bytes 49160 | tf_op jit(solution)/shard_map/ppermute | solution.py:17
  16.4 5.1 %copy-start.2 = (bf16[8,64,128]{2,1,0:T(8,128)(2,1)S(1)}, bf16[8,64,128]{2,1,0:T(8,128)(2,1)}, u32[]{:S(2)}) copy-start(bf16[8,64,128]{2,1,0:T(8,128)(2,1)} %param.5) | copy-start | bytes 393220
  16.4 10.4 %copy-start.8 = (bf16[3,3,128,128]{3,2,1,0:T(8,128)(2,1)S(1)}, bf16[3,3,128,128]{3,2,1,0:T(8,128)(2,1)}, u32[]{:S(2)}) copy-start(bf16[3,3,128,128]{3,2,1,0:T(8,128)(2,1)} %param.6) | copy-start | bytes 884740
  16.4 5.0 %collective-permute-start.1 = (bf16[1,64,128]{2,1,0:T(8,128)(2,1)S(1)}, bf16[1,64,128]{2,1,0:T(8,128)(2,1)S(1)}, u32[]{:S(2)}, u32[]{:S(2)}) collective-permute-start(bf16[1,64,128]{2,1,0:T(8,128)(2,1)S(1)} %get-tuple-element.53), channel_id=1, source_target_pairs={{4,0},{8,4},{12,8},{16,12},{20,16},{24,20},{28,24},{5,1},{9,5},{13... | collective-permute-start | bytes 49160 | tf_op jit(solution)/shard_map/ppermute | solution.py:19
  21.6 5.5 %collective-permute-start.2 = (bf16[10,1,128]{2,1,0:T(2,128)(2,1)S(1)}, bf16[10,1,128]{2,1,0:T(2,128)(2,1)S(1)}, u32[]{:S(2)}, u32[]{:S(2)}) collective-permute-start(bf16[10,1,128]{2,1,0:T(2,128)(2,1)S(1)} %get-tuple-element.42), channel_id=1, source_target_pairs={{0,1},{1,2},{2,3},{4,5},{5,6},{6,7},{8,9},{9,10},{10,11},{12,13},{... | collective-permute-start | bytes 7688 | tf_op jit(solution)/shard_map/ppermute | solution.py:17
  25.4 5.5 %collective-permute-start.3 = (bf16[10,1,128]{2,1,0:T(2,128)(2,1)S(1)}, bf16[10,1,128]{2,1,0:T(2,128)(2,1)S(1)}, u32[]{:S(2)}, u32[]{:S(2)}) collective-permute-start(bf16[10,1,128]{2,1,0:T(2,128)(2,1)S(1)} %get-tuple-element.43), channel_id=1, source_target_pairs={{1,0},{2,1},{3,2},{5,4},{6,5},{7,6},{9,8},{10,9},{11,10},{13,12},{... | collective-permute-start | bytes 7688 | tf_op jit(solution)/shard_map/ppermute | solution.py:19
  32.3 13.8 %copy-start.1 = (bf16[3,3,256,256]{3,2,1,0:T(8,128)(2,1)S(1)}, bf16[3,3,256,256]{3,2,1,0:T(8,128)(2,1)}, u32[]{:S(2)}) copy-start(bf16[3,3,256,256]{3,2,1,0:T(8,128)(2,1)} %param.8) | copy-start | bytes 3538948
  34.1 5.6 %collective-permute-start.5 = (bf16[1,32,256]{2,1,0:T(8,128)(2,1)S(1)}, bf16[1,32,256]{2,1,0:T(8,128)(2,1)S(1)}, u32[]{:S(2)}, u32[]{:S(2)}) collective-permute-start(bf16[1,32,256]{2,1,0:T(8,128)(2,1)S(1)} %get-tuple-element.82), channel_id=1, source_target_pairs={{4,0},{8,4},{12,8},{16,12},{20,16},{24,20},{28,24},{5,1},{9,5},{13... | collective-permute-start | bytes 49160 | tf_op jit(solution)/shard_map/ppermute | solution.py:19
  35.4 4.4 %collective-permute-start.4 = (bf16[1,32,256]{2,1,0:T(8,128)(2,1)S(1)}, bf16[1,32,256]{2,1,0:T(8,128)(2,1)S(1)}, u32[]{:S(2)}, u32[]{:S(2)}) collective-permute-start(bf16[1,32,256]{2,1,0:T(8,128)(2,1)S(1)} %get-tuple-element.81), channel_id=1, source_target_pairs={{0,4},{4,8},{8,12},{12,16},{16,20},{20,24},{24,28},{1,5},{5,9},{9,... | collective-permute-start | bytes 49160 | tf_op jit(solution)/shard_map/ppermute | solution.py:17
  39.8 6.4 %collective-permute-start.6 = (bf16[6,1,256]{2,1,0:T(2,128)(2,1)S(1)}, bf16[6,1,256]{2,1,0:T(2,128)(2,1)S(1)}, u32[]{:S(2)}, u32[]{:S(2)}) collective-permute-start(bf16[6,1,256]{2,1,0:T(2,128)(2,1)S(1)} %get-tuple-element.73), channel_id=1, source_target_pairs={{0,1},{1,2},{2,3},{4,5},{5,6},{6,7},{8,9},{9,10},{10,11},{12,13},{... | collective-permute-start | bytes 9224 | tf_op jit(solution)/shard_map/ppermute | solution.py:17
  44.1 5.5 %collective-permute-start.7 = (bf16[6,1,256]{2,1,0:T(2,128)(2,1)S(1)}, bf16[6,1,256]{2,1,0:T(2,128)(2,1)S(1)}, u32[]{:S(2)}, u32[]{:S(2)}) collective-permute-start(bf16[6,1,256]{2,1,0:T(2,128)(2,1)S(1)} %get-tuple-element.74), channel_id=1, source_target_pairs={{1,0},{2,1},{3,2},{5,4},{6,5},{7,6},{9,8},{10,9},{11,10},{13,12},{... | collective-permute-start | bytes 9224 | tf_op jit(solution)/shard_map/ppermute | solution.py:19
  59.5 5.2 %copy-start.20 = (bf16[4,32,256]{2,1,0:T(8,128)(2,1)S(1)}, bf16[4,32,256]{2,1,0:T(8,128)(2,1)}, u32[]{:S(2)}) copy-start(bf16[4,32,256]{2,1,0:T(8,128)(2,1)} %copy-done.19) | copy-start | bytes 196612
  60.6 5.0 %copy-start.16 = (bf16[4,32,256]{2,1,0:T(8,128)(2,1)S(1)}, bf16[4,32,256]{2,1,0:T(8,128)(2,1)}, u32[]{:S(2)}) copy-start(bf16[4,32,256]{2,1,0:T(8,128)(2,1)} %copy-done.15) | copy-start | bytes 196612
  61.7 4.9 %copy-start.18 = (bf16[4,32,256]{2,1,0:T(8,128)(2,1)S(1)}, bf16[4,32,256]{2,1,0:T(8,128)(2,1)}, u32[]{:S(2)}) copy-start(bf16[4,32,256]{2,1,0:T(8,128)(2,1)} %copy-done.17) | copy-start | bytes 196612
  62.0 5.6 %copy-start.35 = (bf16[128,256]{1,0:T(8,128)(2,1)S(1)}, bf16[128,256]{1,0:T(8,128)(2,1)}, u32[]{:S(2)}) copy-start(bf16[128,256]{1,0:T(8,128)(2,1)} %get-tuple-element.49) | copy-start | bytes 196612
  68.6 8.0 %copy-start.9 = (f32[1,256,256]{2,1,0:T(8,128)S(1)}, f32[1,256,256]{2,1,0:T(8,128)}, u32[]{:S(2)}) copy-start(f32[1,256,256]{2,1,0:T(8,128)} %convolution_bitcast_fusion.4) | copy-start | bytes 786436
  68.6 45.3 %all-to-all-start = ((bf16[4,2,4096]{2,1,0:T(2,128)(2,1)}), bf16[4,2,4096]{2,1,0:T(2,128)(2,1)S(1)}, u32[]{:S(2)}, u32[]{:S(2)}) async-start(bf16[4,2,4096]{2,1,0:T(2,128)(2,1)} %reshape.211), calls=%async_computation | async-start | bytes 131072 | tf_op jit(solution)/shard_map/all_to_all | solution.py:91
  72.1 171.7 %all-reduce.3.cloned.1.call-start = ((), (), s32[]{:S(2)}) async-start(), calls=%async_computation.2 | async-start | bytes 6946816 | tf_op jit(solution)/shard_map/psum | solution.py:128
  72.1 4.6 %copy-start.10 = (f32[1,256,256]{2,1,0:T(8,128)S(1)}, f32[1,256,256]{2,1,0:T(8,128)}, u32[]{:S(2)}) copy-start(f32[1,256,256]{2,1,0:T(8,128)} %convolution_bitcast_fusion.5) | copy-start | bytes 786436
  72.1 4.6 %copy-start.11 = (f32[1,256,256]{2,1,0:T(8,128)S(1)}, f32[1,256,256]{2,1,0:T(8,128)}, u32[]{:S(2)}) copy-start(f32[1,256,256]{2,1,0:T(8,128)} %convolution_bitcast_fusion.6) | copy-start | bytes 786436
  72.1 7.3 %collective-permute-start.9 = (bf16[1,32,256]{2,1,0:T(8,128)(2,1)S(1)}, bf16[1,32,256]{2,1,0:T(8,128)(2,1)S(1)}, u32[]{:S(2)}, u32[]{:S(2)}) collective-permute-start(bf16[1,32,256]{2,1,0:T(8,128)(2,1)S(1)} %get-tuple-element.78), channel_id=1, source_target_pairs={{4,0},{8,4},{12,8},{16,12},{20,16},{24,20},{28,24},{5,1},{9,5},{13... | collective-permute-start | bytes 49160 | tf_op jit(solution)/shard_map/ppermute | solution.py:19
  73.6 5.9 %collective-permute-start.8 = (bf16[1,32,256]{2,1,0:T(8,128)(2,1)S(1)}, bf16[1,32,256]{2,1,0:T(8,128)(2,1)S(1)}, u32[]{:S(2)}, u32[]{:S(2)}) collective-permute-start(bf16[1,32,256]{2,1,0:T(8,128)(2,1)S(1)} %get-tuple-element.77), channel_id=1, source_target_pairs={{0,4},{4,8},{8,12},{12,16},{16,20},{20,24},{24,28},{1,5},{5,9},{9,... | collective-permute-start | bytes 49160 | tf_op jit(solution)/shard_map/ppermute | solution.py:17
  79.4 5.4 %collective-permute-start.10 = (bf16[6,1,256]{2,1,0:T(2,128)(2,1)S(1)}, bf16[6,1,256]{2,1,0:T(2,128)(2,1)S(1)}, u32[]{:S(2)}, u32[]{:S(2)}) collective-permute-start(bf16[6,1,256]{2,1,0:T(2,128)(2,1)S(1)} %get-tuple-element.69), channel_id=1, source_target_pairs={{0,1},{1,2},{2,3},{4,5},{5,6},{6,7},{8,9},{9,10},{10,11},{12,13},{... | collective-permute-start | bytes 9224 | tf_op jit(solution)/shard_map/ppermute | solution.py:17
  83.3 5.5 %collective-permute-start.11 = (bf16[6,1,256]{2,1,0:T(2,128)(2,1)S(1)}, bf16[6,1,256]{2,1,0:T(2,128)(2,1)S(1)}, u32[]{:S(2)}, u32[]{:S(2)}) collective-permute-start(bf16[6,1,256]{2,1,0:T(2,128)(2,1)S(1)} %get-tuple-element.70), channel_id=1, source_target_pairs={{1,0},{2,1},{3,2},{5,4},{6,5},{7,6},{9,8},{10,9},{11,10},{13,12},{... | collective-permute-start | bytes 9224 | tf_op jit(solution)/shard_map/ppermute | solution.py:19
  93.3 8.1 %collective-permute-start.13 = (bf16[1,64,128]{2,1,0:T(8,128)(2,1)S(1)}, bf16[1,64,128]{2,1,0:T(8,128)(2,1)S(1)}, u32[]{:S(2)}, u32[]{:S(2)}) collective-permute-start(bf16[1,64,128]{2,1,0:T(8,128)(2,1)S(1)} %get-tuple-element.47), channel_id=1, source_target_pairs={{4,0},{8,4},{12,8},{16,12},{20,16},{24,20},{28,24},{5,1},{9,5},{13... | collective-permute-start | bytes 49160 | tf_op jit(solution)/shard_map/ppermute | solution.py:19
  94.6 5.7 %copy-start.31 = (bf16[512,128]{1,0:T(8,128)(2,1)S(1)}, bf16[512,128]{1,0:T(8,128)(2,1)}, u32[]{:S(2)}) copy-start(bf16[512,128]{1,0:T(8,128)(2,1)} %copy-done.30) | copy-start | bytes 393220
  94.6 6.8 %collective-permute-start.12 = (bf16[1,64,128]{2,1,0:T(8,128)(2,1)S(1)}, bf16[1,64,128]{2,1,0:T(8,128)(2,1)S(1)}, u32[]{:S(2)}, u32[]{:S(2)}) collective-permute-start(bf16[1,64,128]{2,1,0:T(8,128)(2,1)S(1)} %get-tuple-element.46), channel_id=1, source_target_pairs={{0,4},{4,8},{8,12},{12,16},{16,20},{20,24},{24,28},{1,5},{5,9},{9,... | collective-permute-start | bytes 49160 | tf_op jit(solution)/shard_map/ppermute | solution.py:17
  101.4 5.8 %copy-start.7 = (bf16[3,3,128,128]{2,3,1,0:T(8,128)(2,1)S(1)}, bf16[3,3,128,128]{2,3,1,0:T(8,128)(2,1)}, u32[]{:S(2)}) copy-start(bf16[3,3,128,128]{2,3,1,0:T(8,128)(2,1)} %reverse_bitcast_fusion.1) | copy-start | bytes 884740
  101.5 5.9 %collective-permute-start.14 = (bf16[10,1,128]{2,1,0:T(2,128)(2,1)S(1)}, bf16[10,1,128]{2,1,0:T(2,128)(2,1)S(1)}, u32[]{:S(2)}, u32[]{:S(2)}) collective-permute-start(bf16[10,1,128]{2,1,0:T(2,128)(2,1)S(1)} %get-tuple-element.37), channel_id=1, source_target_pairs={{0,1},{1,2},{2,3},{4,5},{5,6},{6,7},{8,9},{9,10},{10,11},{12,13},{... | collective-permute-start | bytes 7688 | tf_op jit(solution)/shard_map/ppermute | solution.py:17
  105.9 5.5 %collective-permute-start.15 = (bf16[10,1,128]{2,1,0:T(2,128)(2,1)S(1)}, bf16[10,1,128]{2,1,0:T(2,128)(2,1)S(1)}, u32[]{:S(2)}, u32[]{:S(2)}) collective-permute-start(bf16[10,1,128]{2,1,0:T(2,128)(2,1)S(1)} %get-tuple-element.38), channel_id=1, source_target_pairs={{1,0},{2,1},{3,2},{5,4},{6,5},{7,6},{9,8},{10,9},{11,10},{13,12},{... | collective-permute-start | bytes 7688 | tf_op jit(solution)/shard_map/ppermute | solution.py:19
  (23 other events, 41.1 us)
Sparse Core Ops, SparseCore 0:
  101.6 142.0 all-reduce.2
where the time goes:
time: 257 us; the launch traced here: 256 us
  waiting for transfers between devices  146 us (57%)
  starting transfers between devices  48.5 us (19%)
  matrix products  22.3 us (9%)
  between operations  15.1 us (6%)
  local copies, waits for them, and re-layouts  14.5 us (6%)
  other arithmetic  9.45 us (4%)
    psum x1, waiting for transfers between devices, local(): reduced = lax.psum((level_wgrad, down_wgrad, neck_wgrad), ('gy', 'gx'))  129 us
    ppermute x8, starting transfers between devices, extended(): lax.ppermute(tail, axis, [(i, (i + 1) % count) for i in range(ends)])  29.2 us
    ppermute x8, waiting for transfers between devices, extended(): lax.ppermute(head, axis, [((i + 1) % count, i) for i in range(ends)])  17.5 us
    dot_general x36, matrix products, conv_padded(): jnp.dot(window, weights[offset_y, offset_x], preferred_element_type=jnp.f...  11 us
    ppermute x8, starting transfers between devices, extended(): lax.ppermute(head, axis, [((i + 1) % count, i) for i in range(ends)])  10.6 us
    dot_general x18, matrix products, weight_terms(): lax.dot_general(window, flat_grads, (((0,), (0,)), ((), ())), preferred_e...  9.89 us
    unnamed x79, local copies, waits for them, and re-layouts  7.19 us
    all_to_all x1, starting transfers between devices, local(): lax.all_to_all(cotangent, 'gx', split_axis=1, concat_axis=2, tiled=True)  5.16 us
  transfers between devices with their start and end apart: 19, of which 7 were waited for; matrix products, arithmetic and copies ran while one was open for 8% of the time, Pallas kernels for 0%

commit v1 on v0

v1 whole, which is shorter than its diff:
```python
import functools
import math

import jax
import jax.numpy as jnp
from jax import lax
from jax.experimental import pallas as pl
from jax.experimental.pallas import tpu as pltpu
from jax.sharding import PartitionSpec as P

BF, F32 = jnp.bfloat16, jnp.float32
HALO = 7
SIDE = 8
VMEM = pl.BlockSpec(memory_space=pltpu.VMEM)


def call(body, out_shapes, args, scratch=(), limit=32):
    return pl.pallas_call(
        body,
        out_shape=out_shapes,
        in_specs=[VMEM] * len(args),
        out_specs=jax.tree.map(lambda _: VMEM, out_shapes),
        scratch_shapes=list(scratch),
        compiler_params=pltpu.CompilerParams(vmem_limit_bytes=limit * 1024 * 1024),
    )(*args)


def shape(dims, dtype=BF):
    return jax.ShapeDtypeStruct(dims, dtype)


def placing(owner, width, total):
    lane = lax.broadcasted_iota(jnp.int32, (128, total), 0)
    channel = lax.broadcasted_iota(jnp.int32, (128, total), 1)
    return jnp.where((lane < width) & (channel == lane + owner * width), 1.0, 0.0).astype(BF)


def dot(a, b, dims=((1,), (0,))):
    return lax.dot_general(a, b, (dims, ((), ())), preferred_element_type=F32)


def strip_piece(padded, tile, half_cols):
    start = pl.multiple_of(tile * half_cols, 8)
    piece = padded[:, pl.ds(start, half_cols + 2 * SIDE), :]
    return jnp.concatenate([piece[:, SIDE:], piece[:, :SIDE]], axis=1).astype(BF)


def pad_strip(cot_ref, padded):
    width = cot_ref.shape[2]
    padded[...] = jnp.zeros(padded.shape, F32)
    padded[:, SIDE : SIDE + cot_ref.shape[1], 0:width] = cot_ref[...].astype(F32)


def pack_cols(count, half_cols, level_ref, cot_ref, *refs):
    outs, padded = refs[:-1], refs[-1]
    me = lax.axis_index("gx")
    pad_strip(cot_ref, padded)
    level = level_ref[...].astype(F32)
    first, last = level[:, :SIDE], level[:, level.shape[1] - SIDE :]
    for turn in range(1, count):
        other = me ^ turn
        piece = strip_piece(padded, other, half_cols)
        cut = piece.shape[0] * piece.shape[1]
        outs[turn - 1][0:cut] = piece.reshape(cut, 128)
        edge = jnp.where(other == me + 1, last, first)
        outs[turn - 1][cut:] = edge.reshape(-1, 128).astype(BF)


def pack_rows(count, half_cols, level_ref, cot_ref, *refs):
    got = refs[: count - 1]
    wide_ref, cot_out, up_ref, down_ref, padded = refs[count - 1 :]
    me = lax.axis_index("gx")
    rows, cols = level_ref.shape[0], level_ref.shape[1]
    half_rows, width = cot_ref.shape[0], cot_ref.shape[2]
    total = cot_out.shape[2]
    pad_strip(cot_ref, padded)
    piece = strip_piece(padded, me, half_cols)
    pitch = piece.shape[1]
    cut = half_rows * pitch
    cot = dot(piece.reshape(cut, 128), placing(me, width, total))
    right = jnp.zeros((rows * SIDE, 128), F32)
    left = jnp.zeros((rows * SIDE, 128), F32)
    for turn in range(1, count):
        other = me ^ turn
        ref = got[turn - 1]
        cot = cot + dot(ref[0:cut], placing(other, width, total))
        edge = ref[cut:].astype(F32)
        right = jnp.where(other == me + 1, edge, right)
        left = jnp.where(other == me - 1, edge, left)
    right, left = right.reshape(rows, SIDE, 128), left.reshape(rows, SIDE, 128)
    cot = cot.astype(BF).reshape(half_rows, pitch, total)
    cot_out[...] = cot
    level = level_ref[...]
    gap = jnp.zeros((rows, 2 * pitch - cols - 2 * SIDE, 128), F32)
    wide_ref[:, :cols] = level
    wide_ref[:, cols:] = jnp.concatenate([right, gap, left], axis=1).astype(BF)
    edges = jnp.concatenate([right, left], axis=1).astype(BF)
    band = jnp.concatenate([level, edges], axis=1)
    cells = HALO * (cols + 2 * SIDE)
    for ref, low, neck in ((up_ref, 0, 0), (down_ref, rows - HALO, half_rows - 2)):
        ref[0:cells] = band[low : low + HALO].reshape(cells, 128)
        side = cot[neck : neck + 2].reshape(2 * pitch, total)
        ref[cells : cells + 2 * pitch] = side[:, :128]
        ref[cells + 2 * pitch :] = side[:, 128:]


def sigmoid_slope(value):
    gate = jax.nn.sigmoid(value)
    return gate, gate + value * gate * (1.0 - gate)


def shifted(value):
    size = value.shape[1]
    return pltpu.roll(value, 1, 1), pltpu.roll(value, size - 1, 1)


def paired(value):
    return jnp.concatenate(
        [pltpu.roll(value[:, :, 128:], 1, 1), pltpu.roll(value[:, :, :128], value.shape[1] - 1, 1)],
        axis=2,
    ).astype(BF)


def flat(value):
    return value.reshape(-1, value.shape[-1])


def main(
    sizes,
    wide_ref, cot_ref, above_ref, below_ref, wl_ref, wlt_ref, wd_ref, wdt_ref, wn_ref, wnt_ref,
    keep_ref, send_ref, pieces_ref, grad_ref,
    field, pair, side, wfwd, wbwd, act, slope, neck, gate, cot_all, ngrad, lback, lgate, lside, spread, store,
):
    rows, half_rows, half_cols, width, count, level_scale, neck_scale = sizes
    cols = 2 * half_cols
    pitch = wide_ref.shape[1] // 2
    total = cot_ref.shape[2]
    me, row = lax.axis_index("gx"), lax.axis_index("gy")
    row_end, col_end = lax.axis_size("gy") * half_rows, lax.axis_size("gx") * half_cols

    cells = HALO * (cols + 2 * SIDE)
    for ref, low in ((above_ref, 0), (below_ref, HALO + rows)):
        band = ref[0:cells].reshape(HALO, cols + 2 * SIDE, 128).astype(F32)
        field[low : low + HALO, 0 : cols + SIDE] = band[:, : cols + SIDE]
        field[low : low + HALO, cols + SIDE : 2 * pitch - SIDE] = jnp.zeros(
            (HALO, 2 * pitch - cols - 2 * SIDE, 128), F32
        )
        field[low : low + HALO, 2 * pitch - SIDE :] = band[:, cols + SIDE :]
        low_neck = 0 if low == 0 else 2 + half_rows
        cot_all[low_neck : low_neck + 2, :, :128] = ref[cells : cells + 2 * pitch].reshape(2, pitch, 128)
        cot_all[low_neck : low_neck + 2, :, 128:] = ref[cells + 2 * pitch :].reshape(2, pitch, 128)
    field[HALO : HALO + rows] = wide_ref[...].astype(F32)
    cot_all[2 : 2 + half_rows] = cot_ref[...]
    even = field[:, pl.ds(0, pitch, stride=2), :]
    odd = field[:, pl.ds(1, pitch, stride=2), :]
    both = jnp.concatenate([even, odd], axis=2)
    pair[...] = both.astype(BF)
    side[...] = paired(both)

    zero = jnp.zeros((128, 128), BF)
    for ky in range(3):
        w = [wl_ref[3 * ky + kx] for kx in range(3)]
        t = [wlt_ref[3 * ky + kx] for kx in range(3)]
        base = 512 * ky
        for ref, blocks in (
            (wfwd, (w[1], w[0], w[2], w[1], w[0], zero, zero, w[2])),
            (wbwd, (t[1], t[2], t[0], t[1], t[2], zero, zero, t[0])),
        ):
            for spot, block in enumerate(blocks):
                low = base + 128 * (spot // 2)
                ref[low : low + 128, 128 * (spot % 2) : 128 * (spot % 2) + 128] = block

    act_rows = act.shape[0]
    step = act_rows // 2
    for low in range(0, act_rows, step):
        taken = [
            flat(ref[low + ky : low + ky + step]) for ky in range(3) for ref in (pair, side)
        ]
        pre = dot(jnp.concatenate(taken, axis=1), wfwd[...])
        sig, slp = sigmoid_slope(pre)
        own = flat(pair[low + 1 : low + 1 + step]).astype(F32)
        act[low : low + step] = (own + pre * sig).astype(BF).reshape(step, pitch, 256)
        slope[low : low + step] = slp.reshape(step, pitch, 256)

    def inside(value, first_row):
        r = lax.broadcasted_iota(jnp.int32, value.shape, 0) + (row * half_rows + first_row)
        c = lax.broadcasted_iota(jnp.int32, value.shape, 1)
        c = jnp.where(c < half_cols + SIDE, c, c - pitch) + me * half_cols
        ok = (r >= 0) & (r < row_end) & (c >= 0) & (c < col_end)
        return jnp.where(ok, value, 0.0)

    neck_rows = act_rows // 2
    grid = act[...].reshape(neck_rows, 2, pitch, 256)
    both = jnp.concatenate([flat(grid[:, 0]), flat(grid[:, 1])], axis=1)
    value = dot(both, wd_ref[...]).reshape(neck_rows, pitch, total)
    value = inside(value, -3).astype(BF)
    before, behind = shifted(value.astype(F32))
    neck[0], neck[1], neck[2] = before.astype(BF), value, behind.astype(BF)

    gate_rows = neck_rows - 2
    taken = [flat(neck[kx, ky : ky + gate_rows]) for ky in range(3) for kx in range(3)]
    pre = dot(jnp.concatenate(taken, axis=1), wn_ref[...])
    sig, slp = sigmoid_slope(pre)
    own = flat(neck[1, 1 : 1 + gate_rows]).astype(F32)
    out = (own + pre * sig).astype(BF).reshape(gate_rows, pitch, total)
    out = out[2 : 2 + half_rows, :half_cols].reshape(half_rows * half_cols, total)
    for turn in range(count):
        pieces_ref[turn] = dot(out, placing(me ^ turn, width, total), ((1,), (1,))).astype(BF)
    value = (flat(cot_all[...]).astype(F32) * slp).astype(BF).reshape(gate_rows, pitch, total)
    before, behind = shifted(value.astype(F32))
    gate[0], gate[1], gate[2] = before.astype(BF), value, behind.astype(BF)

    grad_rows = gate_rows - 2
    taken = [
        flat(gate[2 - kx, 2 - ky : 2 - ky + grad_rows]) for ky in range(3) for kx in range(3)
    ]
    back = dot(jnp.concatenate(taken, axis=1), wnt_ref[...])
    value = flat(cot_all[1 : 1 + grad_rows]).astype(F32) + back
    value = inside(value.reshape(grad_rows, pitch, total), -1)
    ngrad[...] = value.astype(BF)

    value = dot(flat(ngrad[...]), wdt_ref[...]).reshape(grad_rows, pitch, 512)
    for p in range(2):
        for i in range(grad_rows):
            lback[2 * i + p] = value[i, :, 256 * p : 256 * p + 256]
    value = lback[...] * slope[4 : 4 + 2 * grad_rows]
    value = value.astype(BF)
    lgate[...] = value
    lside[...] = paired(value.astype(F32))

    taken = [
        flat(ref[3 - ky : 3 - ky + rows, :half_cols]) for ky in range(3) for ref in (lgate, lside)
    ]
    value = dot(jnp.concatenate(taken, axis=1), wbwd[...]).reshape(rows, half_cols, 256)
    value = value + lback[2 : 2 + rows, :half_cols]
    spread[:, pl.ds(0, half_cols, stride=2), :] = value[:, :, :128]
    spread[:, pl.ds(1, half_cols, stride=2), :] = value[:, :, 128:]
    grad_ref[...] = spread[...].astype(BF)

    half = keep_ref.shape[0]
    taken = [
        flat(neck[kx, 2 + ky : 2 + ky + half_rows, :half_cols]) for ky in range(3) for kx in range(3)
    ]
    own = flat(gate[1, 2 : 2 + half_rows, :half_cols])
    place = 0
    for lhs in taken:
        value = (dot(lhs, own, ((0,), (0,))) * neck_scale).astype(BF)
        store[place : place + 256] = value[:, :128]
        store[place + 256 : place + 512] = value[:, 128:]
        place += 512
    own = flat(ngrad[1 : 1 + half_rows, :half_cols])
    grid = act[6 : 6 + rows].reshape(half_rows, 2, pitch, 256)
    for p in range(2):
        lhs = flat(grid[:, p, :half_cols])
        value = (dot(lhs, own, ((0,), (0,))) * neck_scale).astype(BF)
        for q in range(2):
            for h in range(2):
                store[place : place + 128] = value[128 * q : 128 * q + 128, 128 * h : 128 * h + 128]
                place += 128
    own = flat(lgate[2 : 2 + rows, :half_cols])
    for ky in range(3):
        m = dot(flat(pair[6 + ky : 6 + ky + rows, :half_cols]), own, ((0,), (0,)))
        s = dot(flat(side[6 + ky : 6 + ky + rows, :half_cols]), own, ((0,), (0,)))
        for value in (
            m[:128, 128:] + s[:128, :128],
            m[:128, :128] + m[128:, 128:],
            m[128:, :128] + s[128:, 128:],
        ):
            store[place : place + 128] = (value * level_scale).astype(BF)
            place += 128
    store[place:] = jnp.zeros((2 * half - place, 128), BF)
    core = row & 1
    keep_ref[...] = store[pl.ds(pl.multiple_of(core * half, 16), half), :]
    send_ref[...] = store[pl.ds(pl.multiple_of((1 - core) * half, 16), half), :]


def add_cores(count, keep_ref, got_ref, pieces_ref, own_ref, *outs):
    me = lax.axis_index("gx")
    part = own_ref.shape[0]
    for turn in range(count):
        here = pl.ds(pl.multiple_of((me ^ turn) * part, 16), part)
        value = keep_ref[here, :].astype(F32) + got_ref[here, :].astype(F32)
        if turn == 0:
            own_ref[...] = value
        else:
            outs[turn - 1][0:part] = value.astype(BF)
            outs[turn - 1][part:] = pieces_ref[turn]


def add_cols(count, z_count, own_ref, pieces_ref, *refs):
    got = refs[: count - 1]
    neck_ref, first_ref = refs[count - 1 : count + 1]
    outs = refs[count + 1 : -1]
    total = refs[-1]
    me, z = lax.axis_index("gx"), lax.axis_index("gy") // 2
    part = own_ref.shape[0]
    rows, width = neck_ref.shape[0], neck_ref.shape[2]
    cols = neck_ref.shape[1] // count
    value = own_ref[...]
    for ref in got:
        value = value + ref[0:part].astype(F32)
    total[...] = value
    unit = part // z_count
    for turn in range(z_count):
        value = total[pl.ds(pl.multiple_of((z ^ turn) * unit, 16), unit), :]
        if turn == 0:
            first_ref[...] = value
        else:
            outs[turn - 1][...] = value.astype(BF)
    for turn in range(count):
        piece = pieces_ref[0] if turn == 0 else got[turn - 1][part:]
        here = pl.ds(pl.multiple_of((me ^ turn) * cols, 16), cols)
        neck_ref[:, here, :] = piece.reshape(rows, cols, 128)[:, :, :width]


def add_rows(first_ref, *refs):
    value = first_ref[...]
    for ref in refs[:-1]:
        value = value + ref[...].astype(F32)
    refs[-1][...] = value.astype(BF)


def finish(count, z_count, *refs):
    ours, theirs = refs[:count], refs[count : 2 * count]
    level_ref, down_ref, neck_ref, store = refs[2 * count :]
    me, row = lax.axis_index("gx"), lax.axis_index("gy")
    z, core = row // 2, row & 1
    unit = ours[0].shape[0] // z_count
    for flip, group in ((0, ours), (1, theirs)):
        for turn in range(count):
            for lap in range(z_count):
                place = (((core ^ flip) * count + (me ^ turn)) * z_count + (z ^ lap)) * unit
                store[pl.ds(pl.multiple_of(place, 16), unit), :] = group[turn][
                    unit * lap : unit * lap + unit
                ]
    place = 0
    for ref in (neck_ref, down_ref):
        deep = ref.shape[1]
        for i in range(ref.shape[0]):
            for h in range(2):
                ref[i, :, 128 * h : 128 * h + 128] = store[place : place + deep]
                place += deep
    for i in range(level_ref.shape[0]):
        level_ref[i] = store[place : place + 128]
        place += 128


def local(level_in, w_level, w_down, w_neck, cotangent):
    rows, cols, _ = level_in.shape
    half_rows, half_cols = rows // 2, cols // 2
    total = w_neck.shape[3]
    width = cotangent.shape[2]
    count, gy_count = lax.axis_size("gx"), lax.axis_size("gy")
    z_count = gy_count // 2
    pitch = half_cols + 2 * SIDE
    axes = ("gy", "gx")
    spots = [(y, x) for y in range(gy_count) for x in range(count)]

    def permute(value, target):
        pairs = [(y * count + x, target(y, x)) for y, x in spots]
        return lax.ppermute(value, axes, [(a, b) for a, b in pairs if b is not None])

    def by_col(value, turn):
        return permute(value, lambda y, x: y * count + (x ^ turn))

    def by_z(value, turn):
        return permute(value, lambda y, x: (y ^ (2 * turn)) * count + x)

    def by_core(value):
        return permute(value, lambda y, x: (y ^ 1) * count + x)

    def to_above(value):
        return permute(value, lambda y, x: (y - 1) * count + x if y > 0 else None)

    def to_below(value):
        return permute(value, lambda y, x: (y + 1) * count + x if y + 1 < gy_count else None)

    strip = pltpu.VMEM((half_rows, cotangent.shape[1] + 2 * SIDE, 128), F32)
    packed = shape((half_rows * pitch + rows * SIDE, 128))
    sent = call(
        functools.partial(pack_cols, count, half_cols),
        [packed] * (count - 1), (level_in, cotangent), [strip],
    )
    got = [by_col(value, turn + 1) for turn, value in enumerate(sent)]
    band = shape((HALO * (cols + 2 * SIDE) + 4 * pitch, 128))
    wide, cot, up, down = call(
        functools.partial(pack_rows, count, half_cols),
        [shape((rows, 2 * pitch, 128)), shape((half_rows, pitch, total)), band, band],
        (level_in, cotangent, *got), [strip],
    )
    below, above = to_above(up), to_below(down)

    wl = w_level.reshape(9, 128, 128)
    wlt = jnp.transpose(wl, (0, 2, 1))
    wd = w_down.reshape(512, total)
    wdt = wd.T
    wn = w_neck.reshape(9 * total, total)
    wnt = jnp.transpose(w_neck, (0, 1, 3, 2)).reshape(9 * total, total)
    pixels = rows * cols * count * gy_count
    grain = 2 * count * z_count
    used = 2 * 9 * total + 4 * 2 * 128 + 9 * 128
    unit = -(-used // (grain * 16)) * 16
    half = unit * grain // 2
    sizes = (
        rows, half_rows, half_cols, width, count,
        1.0 / math.sqrt(pixels), 1.0 / math.sqrt(pixels // 4),
    )
    far = rows + 2 * HALO
    keep, send, pieces, grad_input = call(
        functools.partial(main, sizes),
        [shape((half, 128)), shape((half, 128)), shape((count, half_rows * half_cols, 128)), shape(level_in.shape)],
        (wide, cot, above, below, wl, wlt, wd, wdt, wn, wnt),
        [
            pltpu.VMEM((far, 2 * pitch, 128), F32),
            pltpu.VMEM((far, pitch, 256), BF),
            pltpu.VMEM((far, pitch, 256), BF),
            pltpu.VMEM((1536, 256), BF),
            pltpu.VMEM((1536, 256), BF),
            pltpu.VMEM((far - 2, pitch, 256), BF),
            pltpu.VMEM((far - 2, pitch, 256), F32),
            pltpu.VMEM((3, half_rows + 6, pitch, total), BF),
            pltpu.VMEM((3, half_rows + 4, pitch, total), BF),
            pltpu.VMEM((half_rows + 4, pitch, total), BF),
            pltpu.VMEM((half_rows + 2, pitch, total), BF),
            pltpu.VMEM((rows + 4, pitch, 256), F32),
            pltpu.VMEM((rows + 4, pitch, 256), BF),
            pltpu.VMEM((rows + 4, pitch, 256), BF),
            pltpu.VMEM((rows, cols, 128), F32),
            pltpu.VMEM((2 * half, 128), BF),
        ],
        limit=48,
    )

    part = half // count
    tiles = half_rows * half_cols
    own, *sent = call(
        functools.partial(add_cores, count),
        [shape((part, 128), F32)] + [shape((part + tiles, 128))] * (count - 1),
        (keep, by_core(send), pieces),
    )
    got = [by_col(value, turn + 1) for turn, value in enumerate(sent)]
    neck_out, own, *sent = call(
        functools.partial(add_cols, count, z_count),
        [shape(cotangent.shape), shape((unit, 128), F32)] + [shape((unit, 128))] * (z_count - 1),
        (own, pieces, *got),
        [pltpu.VMEM((part, 128), F32)],
    )
    got = [by_z(value, turn + 1) for turn, value in enumerate(sent)]
    own = call(add_rows, shape((unit, 128)), (own, *got))
    own = jnp.concatenate([own] + [by_z(own, turn) for turn in range(1, z_count)])
    ours = [own] + [by_col(own, turn) for turn in range(1, count)]
    theirs = [by_core(value) for value in ours]
    grad_level, grad_down, grad_neck = call(
        functools.partial(finish, count, z_count),
        [shape((9, 128, 128)), shape((4, 128, total)), shape((9, total, total))],
        (*ours, *theirs),
        [pltpu.VMEM((2 * half, 128), BF)],
    )
    return (
        neck_out,
        grad_input,
        grad_level.reshape(w_level.shape),
        grad_down.reshape(w_down.shape),
        grad_neck.reshape(w_neck.shape),
    )


def solution(mesh):
    return jax.shard_map(
        local,
        mesh=mesh,
        in_specs=(P("gy", "gx", None), P(), P(), P(), P("gy", None, "gx")),
        out_specs=(P("gy", None, "gx"), P("gy", "gx", None), P(), P(), P()),
        check_vma=False,
    )
```

time: 257 us -> 80.6 us (0.31)
  waiting for transfers between devices: 146 us -> 34.6 us
  matrix products: 22.3 us -> 0 us
  starting transfers between devices: 48.5 us -> 28.3 us
  between operations: 15.1 us -> 0.76 us
  other arithmetic: 9.45 us -> 0.02 us
  Pallas kernels: 0 us -> 8.75 us
  local copies, waits for them, and re-layouts: 14.5 us -> 7.88 us
    psum x1 -> x0, waiting for transfers between devices: 129 us -> none  [local(): reduced = lax.psum((level_wgrad, down_wgrad, neck_wgrad), ('gy', 'gx'))]
    dot_general x57 -> x0, matrix products: 22.3 us -> none  [the longest x36 11 us: conv_padded(): jnp.dot(window, weights[offset_y, offset_x], preferred_element_type=jnp.f...]
    ppermute x16 -> x22, waiting for transfers between devices: 17.6 us -> 34.6 us  [permute(): lax.ppermute(value, axes, [(a, b) for a, b in pairs if b is not None])]
    ppermute x16 -> x22, starting transfers between devices: 39.8 us -> 28.3 us  [permute(): lax.ppermute(value, axes, [(a, b) for a, b in pairs if b is not None])]
    pallas_call x0 -> x7, Pallas kernels: none -> 8.75 us  [call(): pl.pallas_call(body, out_shape=out_shapes, in_specs=[VMEM] * len(args), o...]
    all_to_all x2 -> x0, starting transfers between devices: 8.58 us -> none  [the longest x1 5.16 us: local(): lax.all_to_all(cotangent, 'gx', split_axis=1, concat_axis=2, tiled=True)]
    convert_element_type x5 -> x0, other arithmetic: 5.67 us -> none  [the longest x1 2.89 us: local(): grad_neck = (reduced[2] * neck_scale).astype(jnp.bfloat16)]
    convert_element_type x2 -> x0, local copies, waits for them, and re-layouts: 2.68 us -> none  [local(): neck_cot.reshape(half_rows * half_cols, neck_width).astype(jnp.float32)]
  transfers between devices with their start and end apart: 19 -> 22, of which waited for: 7 -> 17; matrix products, arithmetic and copies ran while one was open for 8% -> 3% of each run, Pallas kernels for 0% -> 0%
where the time goes in v1:
time: 80.6 us; the launch traced here: 80.3 us
  waiting for transfers between devices  34.6 us (43%)
  starting transfers between devices  28.3 us (35%)
  Pallas kernels  8.75 us (11%)
  local copies, waits for them, and re-layouts  7.88 us (10%)
    ppermute x22, waiting for transfers between devices, permute(): lax.ppermute(value, axes, [(a, b) for a, b in pairs if b is not None])  34.6 us
    ppermute x22, starting transfers between devices, permute(): lax.ppermute(value, axes, [(a, b) for a, b in pairs if b is not None])  28.3 us
    pallas_call x7, Pallas kernels, call(): pl.pallas_call(body, out_shape=out_shapes, in_specs=[VMEM] * len(args), o...  8.75 us
    unnamed x19, local copies, waits for them, and re-layouts  6.06 us
  transfers between devices with their start and end apart: 22, of which 17 were waited for; matrix products, arithmetic and copies ran while one was open for 3% of the time, Pallas kernels for 0%

profile of v1, /device:TPU:0, one launch (start us, length us, event | category | flops | bytes accessed | tf_op | source)
XLA Modules:
  0.0 80.3 jit_solution(713759535444087793)
XLA Ops:
  0.7 1.1 %copy.11.cot_ref = bf16[4,128,64]{2,1,0:T(8,128)(2,1)S(1)} copy(bf16[4,128,64]{1,2,0:T(8,128)(2,1)} %param.9) | data formatting | bytes 131072 | tf_op args[4]
  1.7 0.9 %copy-done.3 = bf16[8,64,128]{2,1,0:T(8,128)(2,1)S(1)} copy-done((bf16[8,64,128]{2,1,0:T(8,128)(2,1)S(1)}, bf16[8,64,128]{2,1,0:T(8,128)(2,1)}, u32[]{:S(2)}) %copy-start.3) | copy-done | bytes 131096
  2.7 3.0 %collective-permute-start = (bf16[256,128]{1,0:T(8,128)(2,1)S(1)}, bf16[256,128]{1,0:T(8,128)(2,1)S(1)}, u32[]{:S(2)}, u32[]{:S(2)}) collective-permute-start(bf16[256,128]{1,0:T(8,128)(2,1)S(1)} %get-tuple-element.28), channel_id=1, source_target_pairs={{0,1},{1,0},{2,3},{3,2},{4,5},{5,4},{6,7},{7,6},{8,9},{9,8},{10,11... | collective-permute-start | bytes 196616 | tf_op jit(solution)/shard_map/ppermute | solution.py:361
  5.7 1.5 %collective-permute-start.1 = (bf16[256,128]{1,0:T(8,128)(2,1)S(1)}, bf16[256,128]{1,0:T(8,128)(2,1)S(1)}, u32[]{:S(2)}, u32[]{:S(2)}) collective-permute-start(bf16[256,128]{1,0:T(8,128)(2,1)S(1)} %get-tuple-element.29), channel_id=1, source_target_pairs={{0,2},{1,3},{2,0},{3,1},{4,6},{5,7},{6,4},{7,5},{8,10},{9,11},{10,... | collective-permute-start | bytes 196616 | tf_op jit(solution)/shard_map/ppermute | solution.py:361
  8.1 1.9 %collective-permute-done.1.refs_1_ = bf16[256,128]{1,0:T(8,128)(2,1)S(1)} collective-permute-done((bf16[256,128]{1,0:T(8,128)(2,1)S(1)}, bf16[256,128]{1,0:T(8,128)(2,1)S(1)}, u32[]{:S(2)}, u32[]{:S(2)}) %collective-permute-start.1) | collective-permute-done | bytes 65568 | tf_op jit(solution)/shard_map/ppermute | solution.py:361
  10.0 2.4 %collective-permute-done.2.refs_2_ = bf16[256,128]{1,0:T(8,128)(2,1)S(1)} collective-permute-done((bf16[256,128]{1,0:T(8,128)(2,1)S(1)}, bf16[256,128]{1,0:T(8,128)(2,1)S(1)}, u32[]{:S(2)}, u32[]{:S(2)}) %collective-permute-start.2) | collective-permute-done | bytes 65568 | tf_op jit(solution)/shard_map/ppermute | solution.py:361
  12.4 1.0 %shard_map.93 = (bf16[8,96,128]{2,1,0:T(8,128)(2,1)S(1)}, bf16[4,48,256]{2,1,0:T(8,128)(2,1)S(1)}, bf16[752,128]{1,0:T(8,128)(2,1)}, bf16[752,128]{1,0:T(8,128)(2,1)}) custom-call(bf16[8,64,128]{2,1,0:T(8,128)(2,1)S(1)} %copy-done.3, bf16[4,128,64]{2,1,0:T(8,128)(2,1)S(1)} %copy.11.cot_ref, bf16[256,128]{1,0:T(8,128)(2,1)S(1)} %collective-permute-done.refs_0_, ...), custom_call_target="tpu_custom_call" | custom-call | tf_op jit(solution)/shard_map/pallas_call | solution.py:18
  14.7 2.0 %collective-permute-start.3 = (bf16[752,128]{1,0:T(8,128)(2,1)}, bf16[752,128]{1,0:T(8,128)(2,1)}, u32[]{:S(2)}, u32[]{:S(2)}) collective-permute-start(bf16[752,128]{1,0:T(8,128)(2,1)} %get-tuple-element.33), channel_id=1, source_target_pairs={{0,4},{1,5},{2,6},{3,7},{4,8},{5,9},{6,10},{7,11},{8,12},{9,13},{1... | collective-permute-start | bytes 577544 | tf_op jit(solution)/shard_map/ppermute | solution.py:361
  16.7 1.3 %collective-permute-start.4 = (bf16[752,128]{1,0:T(8,128)(2,1)}, bf16[752,128]{1,0:T(8,128)(2,1)}, u32[]{:S(2)}, u32[]{:S(2)}) collective-permute-start(bf16[752,128]{1,0:T(8,128)(2,1)} %get-tuple-element.34), channel_id=1, source_target_pairs={{4,0},{5,1},{6,2},{7,3},{8,4},{9,5},{10,6},{11,7},{12,8},{13,9},{1... | collective-permute-start | bytes 577544 | tf_op jit(solution)/shard_map/ppermute | solution.py:361
  18.0 1.1 %copy.19 = bf16[512,256]{0,1:T(8,128)(2,1)S(1)} copy(bf16[512,256]{1,0:T(8,128)(2,1)} %bitcast.17) | data formatting | bytes 524288 | tf_op jit(solution)/shard_map/reshape | solution.py:395
  20.0 1.4 %collective-permute-done.4.below_ref = bf16[752,128]{1,0:T(8,128)(2,1)} collective-permute-done((bf16[752,128]{1,0:T(8,128)(2,1)}, bf16[752,128]{1,0:T(8,128)(2,1)}, u32[]{:S(2)}, u32[]{:S(2)}) %collective-permute-start.4) | collective-permute-done | bytes 192544 | tf_op jit(solution)/shard_map/ppermute | solution.py:361
  21.5 0.9 %copy-done.5 = bf16[8,96,128]{2,1,0:T(8,128)(2,1)S(1)} copy-done((bf16[8,96,128]{2,1,0:T(8,128)(2,1)S(1)}, bf16[8,96,128]{2,1,0:T(8,128)(2,1)}, u32[]{:S(2)}) %copy-start.5) | copy-done | bytes 196632
  22.4 0.9 %copy-done.7 = bf16[4,48,256]{2,1,0:T(8,128)(2,1)S(1)} copy-done((bf16[4,48,256]{2,1,0:T(8,128)(2,1)S(1)}, bf16[4,48,256]{2,1,0:T(8,128)(2,1)}, u32[]{:S(2)}) %copy-start.7) | copy-done | bytes 98328
  23.3 5.8 %shard_map.94 = (bf16[3584,128]{1,0:T(8,128)(2,1)S(1)}, bf16[3584,128]{1,0:T(8,128)(2,1)S(1)}, bf16[4,128,128]{2,1,0:T(8,128)(2,1)S(1)}, bf16[8,64,128]{2,1,0:T(8,128)(2,1)}) custom-call(bf16[8,96,128]{2,1,0:T(8,128)(2,1)S(1)} %copy-done.5, bf16[4,48,256]{2,1,0:T(8,128)(2,1)S(1)} %copy-done.7, bf16[752,128]{1,0:T(8,128)(2,1)} %collective-permute-done.3.above_ref, ...), custom_call_target="tpu_custom_call" | custom-call | tf_op jit(solution)/shard_map/pallas_call | solution.py:18
  29.1 4.2 %collective-permute-start.5 = (bf16[3584,128]{1,0:T(8,128)(2,1)S(1)}, bf16[3584,128]{1,0:T(8,128)(2,1)S(1)}, u32[]{:S(2)}, u32[]{:S(2)}) collective-permute-start(bf16[3584,128]{1,0:T(8,128)(2,1)S(1)} %get-tuple-element.36), channel_id=1, source_target_pairs={{0,4},{1,5},{2,6},{3,7},{4,0},{5,1},{6,2},{7,3},{8,12},{9,13},{10,... | collective-permute-start | bytes 2752520 | tf_op jit(solution)/shard_map/ppermute | solution.py:361
  33.3 2.1 %collective-permute-done.5.got_ref = bf16[3584,128]{1,0:T(8,128)(2,1)S(1)} collective-permute-done((bf16[3584,128]{1,0:T(8,128)(2,1)S(1)}, bf16[3584,128]{1,0:T(8,128)(2,1)S(1)}, u32[]{:S(2)}, u32[]{:S(2)}) %collective-permute-start.5) | collective-permute-done | bytes 917536 | tf_op jit(solution)/shard_map/ppermute | solution.py:361
  36.7 2.5 %collective-permute-start.8 = (bf16[1024,128]{1,0:T(8,128)(2,1)S(1)}, bf16[1024,128]{1,0:T(8,128)(2,1)S(1)}, u32[]{:S(2)}, u32[]{:S(2)}) collective-permute-start(bf16[1024,128]{1,0:T(8,128)(2,1)S(1)} %get-tuple-element.41), channel_id=1, source_target_pairs={{0,3},{1,2},{2,1},{3,0},{4,7},{5,6},{6,5},{7,4},{8,11},{9,10},{10,... | collective-permute-start | bytes 786440 | tf_op jit(solution)/shard_map/ppermute | solution.py:361
  39.1 5.6 %collective-permute-done.6.refs_0_ = bf16[1024,128]{1,0:T(8,128)(2,1)S(1)} collective-permute-done((bf16[1024,128]{1,0:T(8,128)(2,1)S(1)}, bf16[1024,128]{1,0:T(8,128)(2,1)S(1)}, u32[]{:S(2)}, u32[]{:S(2)}) %collective-permute-start.6) | collective-permute-done | bytes 262176 | tf_op jit(solution)/shard_map/ppermute | solution.py:361
  44.8 5.3 %collective-permute-done.7.refs_1_ = bf16[1024,128]{1,0:T(8,128)(2,1)S(1)} collective-permute-done((bf16[1024,128]{1,0:T(8,128)(2,1)S(1)}, bf16[1024,128]{1,0:T(8,128)(2,1)S(1)}, u32[]{:S(2)}, u32[]{:S(2)}) %collective-permute-start.7) | collective-permute-done | bytes 262176 | tf_op jit(solution)/shard_map/ppermute | solution.py:361
  50.3 1.6 %collective-permute-start.9 = (bf16[224,128]{1,0:T(8,128)(2,1)S(1)}, bf16[224,128]{1,0:T(8,128)(2,1)S(1)}, u32[]{:S(2)}, u32[]{:S(2)}) collective-permute-start(bf16[224,128]{1,0:T(8,128)(2,1)S(1)} %get-tuple-element.45), channel_id=1, source_target_pairs={{0,8},{1,9},{2,10},{3,11},{4,12},{5,13},{6,14},{7,15},{8,0},{9,1},... | collective-permute-start | bytes 172040 | tf_op jit(solution)/shard_map/ppermute | solution.py:361
  51.9 1.1 %collective-permute-start.10 = (bf16[224,128]{1,0:T(8,128)(2,1)S(1)}, bf16[224,128]{1,0:T(8,128)(2,1)S(1)}, u32[]{:S(2)}, u32[]{:S(2)}) collective-permute-start(bf16[224,128]{1,0:T(8,128)(2,1)S(1)} %get-tuple-element.46), channel_id=1, source_target_pairs={{0,16},{1,17},{2,18},{3,19},{4,20},{5,21},{6,22},{7,23},{8,24},{9,... | collective-permute-start | bytes 172040 | tf_op jit(solution)/shard_map/ppermute | solution.py:361
  53.0 1.7 %collective-permute-start.11 = (bf16[224,128]{1,0:T(8,128)(2,1)S(1)}, bf16[224,128]{1,0:T(8,128)(2,1)S(1)}, u32[]{:S(2)}, u32[]{:S(2)}) collective-permute-start(bf16[224,128]{1,0:T(8,128)(2,1)S(1)} %get-tuple-element.47), channel_id=1, source_target_pairs={{0,24},{1,25},{2,26},{3,27},{4,28},{5,29},{6,30},{7,31},{8,16},{9,... | collective-permute-start | bytes 172040 | tf_op jit(solution)/shard_map/ppermute | solution.py:361
  55.1 3.2 %collective-permute-done.10.refs_1_ = bf16[224,128]{1,0:T(8,128)(2,1)S(1)} collective-permute-done((bf16[224,128]{1,0:T(8,128)(2,1)S(1)}, bf16[224,128]{1,0:T(8,128)(2,1)S(1)}, u32[]{:S(2)}, u32[]{:S(2)}) %collective-permute-start.10) | collective-permute-done | bytes 57376 | tf_op jit(solution)/shard_map/ppermute | solution.py:361
  59.1 2.0 %collective-permute-start.14 = (bf16[224,128]{1,0:T(8,128)(2,1)S(1)}, bf16[224,128]{1,0:T(8,128)(2,1)S(1)}, u32[]{:S(2)}, u32[]{:S(2)}) collective-permute-start(bf16[224,128]{1,0:T(8,128)(2,1)S(1)} %shard_map.97), channel_id=1, source_target_pairs={{0,24},{1,25},{2,26},{3,27},{4,28},{5,29},{6,30},{7,31},{8,16},{9,... | collective-permute-start | bytes 172040 | tf_op jit(solution)/shard_map/ppermute | solution.py:361
  61.6 2.0 %collective-permute-start.12 = (bf16[224,128]{1,0:T(8,128)(2,1)S(1)}, bf16[224,128]{1,0:T(8,128)(2,1)S(1)}, u32[]{:S(2)}, u32[]{:S(2)}) collective-permute-start(bf16[224,128]{1,0:T(8,128)(2,1)S(1)} %shard_map.97), channel_id=1, source_target_pairs={{0,8},{1,9},{2,10},{3,11},{4,12},{5,13},{6,14},{7,15},{8,0},{9,1},... | collective-permute-start | bytes 172040 | tf_op jit(solution)/shard_map/ppermute | solution.py:361
  63.6 1.6 %collective-permute-done.14 = bf16[224,128]{1,0:T(8,128)(2,1)S(1)} collective-permute-done((bf16[224,128]{1,0:T(8,128)(2,1)S(1)}, bf16[224,128]{1,0:T(8,128)(2,1)S(1)}, u32[]{:S(2)}, u32[]{:S(2)}) %collective-permute-start.14) | collective-permute-done | bytes 57376 | tf_op jit(solution)/shard_map/ppermute | solution.py:361
  65.2 1.3 %collective-permute-done.13 = bf16[224,128]{1,0:T(8,128)(2,1)S(1)} collective-permute-done((bf16[224,128]{1,0:T(8,128)(2,1)S(1)}, bf16[224,128]{1,0:T(8,128)(2,1)S(1)}, u32[]{:S(2)}, u32[]{:S(2)}) %collective-permute-start.13) | collective-permute-done | bytes 57376 | tf_op jit(solution)/shard_map/ppermute | solution.py:361
  66.5 1.6 %collective-permute-start.17 = (bf16[896,128]{1,0:T(8,128)(2,1)S(1)}, bf16[896,128]{1,0:T(8,128)(2,1)S(1)}, u32[]{:S(2)}, u32[]{:S(2)}) collective-permute-start(bf16[896,128]{1,0:T(8,128)(2,1)S(1)} %pad_maximum_fusion.refs_0_), channel_id=1, source_target_pairs={{0,3},{1,2},{2,1},{3,0},{4,7},{5,6},{6,5},{7,4},{8,11},{9,10},{10,... | collective-permute-start | bytes 688136 | tf_op jit(solution)/shard_map/ppermute | solution.py:361
  68.1 1.4 %collective-permute-start.16 = (bf16[896,128]{1,0:T(8,128)(2,1)S(1)}, bf16[896,128]{1,0:T(8,128)(2,1)S(1)}, u32[]{:S(2)}, u32[]{:S(2)}) collective-permute-start(bf16[896,128]{1,0:T(8,128)(2,1)S(1)} %pad_maximum_fusion.refs_0_), channel_id=1, source_target_pairs={{0,2},{1,3},{2,0},{3,1},{4,6},{5,7},{6,4},{7,5},{8,10},{9,11},{10,... | collective-permute-start | bytes 688136 | tf_op jit(solution)/shard_map/ppermute | solution.py:361
  70.1 4.6 %collective-permute-done.17.refs_3_ = bf16[896,128]{1,0:T(8,128)(2,1)S(1)} collective-permute-done((bf16[896,128]{1,0:T(8,128)(2,1)S(1)}, bf16[896,128]{1,0:T(8,128)(2,1)S(1)}, u32[]{:S(2)}, u32[]{:S(2)}) %collective-permute-start.17) | collective-permute-done | bytes 229408 | tf_op jit(solution)/shard_map/ppermute | solution.py:361
  74.7 2.3 %collective-permute-done.16.refs_2_ = bf16[896,128]{1,0:T(8,128)(2,1)S(1)} collective-permute-done((bf16[896,128]{1,0:T(8,128)(2,1)S(1)}, bf16[896,128]{1,0:T(8,128)(2,1)S(1)}, u32[]{:S(2)}, u32[]{:S(2)}) %collective-permute-start.16) | collective-permute-done | bytes 229408 | tf_op jit(solution)/shard_map/ppermute | solution.py:361
  78.8 1.5 %shard_map.98 = (bf16[9,128,128]{2,1,0:T(8,128)(2,1)}, bf16[4,128,256]{2,1,0:T(8,128)(2,1)}, bf16[9,256,256]{2,1,0:T(8,128)(2,1)}) custom-call(bf16[896,128]{1,0:T(8,128)(2,1)S(1)} %pad_maximum_fusion.refs_0_, bf16[896,128]{1,0:T(8,128)(2,1)S(1)} %collective-permute-done.15.refs_1_, bf16[896,128]{1,0:T(8,128)(2,1)S(1)} %collective-permute-done.16.refs_2_, ...), custom_call_target="tpu_custom_call" | custom-call | tf_op jit(solution)/shard_map/pallas_call | solution.py:18
  (41 shorter events, 8.8 us)
Async XLA Ops:
  0.6 18.4 %copy-start.1 = (bf16[3,3,128,128]{3,2,1,0:T(8,128)(2,1)S(1)}, bf16[3,3,128,128]{3,2,1,0:T(8,128)(2,1)}, u32[]{:S(2)}) copy-start(bf16[3,3,128,128]{3,2,1,0:T(8,128)(2,1)} %param.6) | copy-start | bytes 884740
  0.6 18.6 %copy-start = (bf16[3,3,256,256]{3,2,1,0:T(8,128)(2,1)S(1)}, bf16[3,3,256,256]{3,2,1,0:T(8,128)(2,1)}, u32[]{:S(2)}) copy-start(bf16[3,3,256,256]{3,2,1,0:T(8,128)(2,1)} %param.8) | copy-start | bytes 3538948
  1.7 0.9 %copy-start.3 = (bf16[8,64,128]{2,1,0:T(8,128)(2,1)S(1)}, bf16[8,64,128]{2,1,0:T(8,128)(2,1)}, u32[]{:S(2)}) copy-start(bf16[8,64,128]{2,1,0:T(8,128)(2,1)} %level_ref.3) | copy-start | bytes 393220
  2.7 5.4 %collective-permute-start = (bf16[256,128]{1,0:T(8,128)(2,1)S(1)}, bf16[256,128]{1,0:T(8,128)(2,1)S(1)}, u32[]{:S(2)}, u32[]{:S(2)}) collective-permute-start(bf16[256,128]{1,0:T(8,128)(2,1)S(1)} %get-tuple-element.28), channel_id=1, source_target_pairs={{0,1},{1,0},{2,3},{3,2},{4,5},{5,4},{6,7},{7,6},{8,9},{9,8},{10,11... | collective-permute-start | bytes 196616 | tf_op jit(solution)/shard_map/ppermute | solution.py:361
  5.7 4.3 %collective-permute-start.1 = (bf16[256,128]{1,0:T(8,128)(2,1)S(1)}, bf16[256,128]{1,0:T(8,128)(2,1)S(1)}, u32[]{:S(2)}, u32[]{:S(2)}) collective-permute-start(bf16[256,128]{1,0:T(8,128)(2,1)S(1)} %get-tuple-element.29), channel_id=1, source_target_pairs={{0,2},{1,3},{2,0},{3,1},{4,6},{5,7},{6,4},{7,5},{8,10},{9,11},{10,... | collective-permute-start | bytes 196616 | tf_op jit(solution)/shard_map/ppermute | solution.py:361
  7.2 5.2 %collective-permute-start.2 = (bf16[256,128]{1,0:T(8,128)(2,1)S(1)}, bf16[256,128]{1,0:T(8,128)(2,1)S(1)}, u32[]{:S(2)}, u32[]{:S(2)}) collective-permute-start(bf16[256,128]{1,0:T(8,128)(2,1)S(1)} %get-tuple-element.30), channel_id=1, source_target_pairs={{0,3},{1,2},{2,1},{3,0},{4,7},{5,6},{6,5},{7,4},{8,11},{9,10},{10,... | collective-permute-start | bytes 196616 | tf_op jit(solution)/shard_map/ppermute | solution.py:361
  13.4 0.7 copy-start.4
  14.1 0.6 copy-start.6
  14.7 5.3 %collective-permute-start.3 = (bf16[752,128]{1,0:T(8,128)(2,1)}, bf16[752,128]{1,0:T(8,128)(2,1)}, u32[]{:S(2)}, u32[]{:S(2)}) collective-permute-start(bf16[752,128]{1,0:T(8,128)(2,1)} %get-tuple-element.33), channel_id=1, source_target_pairs={{0,4},{1,5},{2,6},{3,7},{4,8},{5,9},{6,10},{7,11},{8,12},{9,13},{1... | collective-permute-start | bytes 577544 | tf_op jit(solution)/shard_map/ppermute | solution.py:361
  16.7 4.8 %collective-permute-start.4 = (bf16[752,128]{1,0:T(8,128)(2,1)}, bf16[752,128]{1,0:T(8,128)(2,1)}, u32[]{:S(2)}, u32[]{:S(2)}) collective-permute-start(bf16[752,128]{1,0:T(8,128)(2,1)} %get-tuple-element.34), channel_id=1, source_target_pairs={{4,0},{5,1},{6,2},{7,3},{8,4},{9,5},{10,6},{11,7},{12,8},{13,9},{1... | collective-permute-start | bytes 577544 | tf_op jit(solution)/shard_map/ppermute | solution.py:361
  19.3 2.2 %copy-start.2 = (bf16[2,2,128,256]{3,2,1,0:T(8,128)(2,1)S(1)}, bf16[2,2,128,256]{3,2,1,0:T(8,128)(2,1)}, u32[]{:S(2)}) copy-start(bf16[2,2,128,256]{3,2,1,0:T(8,128)(2,1)} %param.7) | copy-start | bytes 786436
  21.5 0.9 %copy-start.5 = (bf16[8,96,128]{2,1,0:T(8,128)(2,1)S(1)}, bf16[8,96,128]{2,1,0:T(8,128)(2,1)}, u32[]{:S(2)}) copy-start(bf16[8,96,128]{2,1,0:T(8,128)(2,1)} %copy-done.4) | copy-start | bytes 589828
  22.4 0.9 %copy-start.7 = (bf16[4,48,256]{2,1,0:T(8,128)(2,1)S(1)}, bf16[4,48,256]{2,1,0:T(8,128)(2,1)}, u32[]{:S(2)}) copy-start(bf16[4,48,256]{2,1,0:T(8,128)(2,1)} %copy-done.6) | copy-start | bytes 294916
  29.1 6.3 %collective-permute-start.5 = (bf16[3584,128]{1,0:T(8,128)(2,1)S(1)}, bf16[3584,128]{1,0:T(8,128)(2,1)S(1)}, u32[]{:S(2)}, u32[]{:S(2)}) collective-permute-start(bf16[3584,128]{1,0:T(8,128)(2,1)S(1)} %get-tuple-element.36), channel_id=1, source_target_pairs={{0,4},{1,5},{2,6},{3,7},{4,0},{5,1},{6,2},{7,3},{8,12},{9,13},{10,... | collective-permute-start | bytes 2752520 | tf_op jit(solution)/shard_map/ppermute | solution.py:361
  35.6 9.2 %collective-permute-start.6 = (bf16[1024,128]{1,0:T(8,128)(2,1)S(1)}, bf16[1024,128]{1,0:T(8,128)(2,1)S(1)}, u32[]{:S(2)}, u32[]{:S(2)}) collective-permute-start(bf16[1024,128]{1,0:T(8,128)(2,1)S(1)} %get-tuple-element.39), channel_id=1, source_target_pairs={{0,1},{1,0},{2,3},{3,2},{4,5},{5,4},{6,7},{7,6},{8,9},{9,8},{10,11... | collective-permute-start | bytes 786440 | tf_op jit(solution)/shard_map/ppermute | solution.py:361
  36.2 13.9 %collective-permute-start.7 = (bf16[1024,128]{1,0:T(8,128)(2,1)S(1)}, bf16[1024,128]{1,0:T(8,128)(2,1)S(1)}, u32[]{:S(2)}, u32[]{:S(2)}) collective-permute-start(bf16[1024,128]{1,0:T(8,128)(2,1)S(1)} %get-tuple-element.40), channel_id=1, source_target_pairs={{0,2},{1,3},{2,0},{3,1},{4,6},{5,7},{6,4},{7,5},{8,10},{9,11},{10,... | collective-permute-start | bytes 786440 | tf_op jit(solution)/shard_map/ppermute | solution.py:361
  36.7 13.4 %collective-permute-start.8 = (bf16[1024,128]{1,0:T(8,128)(2,1)S(1)}, bf16[1024,128]{1,0:T(8,128)(2,1)S(1)}, u32[]{:S(2)}, u32[]{:S(2)}) collective-permute-start(bf16[1024,128]{1,0:T(8,128)(2,1)S(1)} %get-tuple-element.41), channel_id=1, source_target_pairs={{0,3},{1,2},{2,1},{3,0},{4,7},{5,6},{6,5},{7,4},{8,11},{9,10},{10,... | collective-permute-start | bytes 786440 | tf_op jit(solution)/shard_map/ppermute | solution.py:361
  50.3 4.8 %collective-permute-start.9 = (bf16[224,128]{1,0:T(8,128)(2,1)S(1)}, bf16[224,128]{1,0:T(8,128)(2,1)S(1)}, u32[]{:S(2)}, u32[]{:S(2)}) collective-permute-start(bf16[224,128]{1,0:T(8,128)(2,1)S(1)} %get-tuple-element.45), channel_id=1, source_target_pairs={{0,8},{1,9},{2,10},{3,11},{4,12},{5,13},{6,14},{7,15},{8,0},{9,1},... | collective-permute-start | bytes 172040 | tf_op jit(solution)/shard_map/ppermute | solution.py:361
  51.9 6.3 %collective-permute-start.10 = (bf16[224,128]{1,0:T(8,128)(2,1)S(1)}, bf16[224,128]{1,0:T(8,128)(2,1)S(1)}, u32[]{:S(2)}, u32[]{:S(2)}) collective-permute-start(bf16[224,128]{1,0:T(8,128)(2,1)S(1)} %get-tuple-element.46), channel_id=1, source_target_pairs={{0,16},{1,17},{2,18},{3,19},{4,20},{5,21},{6,22},{7,23},{8,24},{9,... | collective-permute-start | bytes 172040 | tf_op jit(solution)/shard_map/ppermute | solution.py:361
  53.0 6.1 %collective-permute-start.11 = (bf16[224,128]{1,0:T(8,128)(2,1)S(1)}, bf16[224,128]{1,0:T(8,128)(2,1)S(1)}, u32[]{:S(2)}, u32[]{:S(2)}) collective-permute-start(bf16[224,128]{1,0:T(8,128)(2,1)S(1)} %get-tuple-element.47), channel_id=1, source_target_pairs={{0,24},{1,25},{2,26},{3,27},{4,28},{5,29},{6,30},{7,31},{8,16},{9,... | collective-permute-start | bytes 172040 | tf_op jit(solution)/shard_map/ppermute | solution.py:361
  59.1 6.0 %collective-permute-start.14 = (bf16[224,128]{1,0:T(8,128)(2,1)S(1)}, bf16[224,128]{1,0:T(8,128)(2,1)S(1)}, u32[]{:S(2)}, u32[]{:S(2)}) collective-permute-start(bf16[224,128]{1,0:T(8,128)(2,1)S(1)} %shard_map.97), channel_id=1, source_target_pairs={{0,24},{1,25},{2,26},{3,27},{4,28},{5,29},{6,30},{7,31},{8,16},{9,... | collective-permute-start | bytes 172040 | tf_op jit(solution)/shard_map/ppermute | solution.py:361
  61.1 5.4 %collective-permute-start.13 = (bf16[224,128]{1,0:T(8,128)(2,1)S(1)}, bf16[224,128]{1,0:T(8,128)(2,1)S(1)}, u32[]{:S(2)}, u32[]{:S(2)}) collective-permute-start(bf16[224,128]{1,0:T(8,128)(2,1)S(1)} %shard_map.97), channel_id=1, source_target_pairs={{0,16},{1,17},{2,18},{3,19},{4,20},{5,21},{6,22},{7,23},{8,24},{9,... | collective-permute-start | bytes 172040 | tf_op jit(solution)/shard_map/ppermute | solution.py:361
  61.6 4.9 %collective-permute-start.12 = (bf16[224,128]{1,0:T(8,128)(2,1)S(1)}, bf16[224,128]{1,0:T(8,128)(2,1)S(1)}, u32[]{:S(2)}, u32[]{:S(2)}) collective-permute-start(bf16[224,128]{1,0:T(8,128)(2,1)S(1)} %shard_map.97), channel_id=1, source_target_pairs={{0,8},{1,9},{2,10},{3,11},{4,12},{5,13},{6,14},{7,15},{8,0},{9,1},... | collective-permute-start | bytes 172040 | tf_op jit(solution)/shard_map/ppermute | solution.py:361
  66.5 8.1 %collective-permute-start.17 = (bf16[896,128]{1,0:T(8,128)(2,1)S(1)}, bf16[896,128]{1,0:T(8,128)(2,1)S(1)}, u32[]{:S(2)}, u32[]{:S(2)}) collective-permute-start(bf16[896,128]{1,0:T(8,128)(2,1)S(1)} %pad_maximum_fusion.refs_0_), channel_id=1, source_target_pairs={{0,3},{1,2},{2,1},{3,0},{4,7},{5,6},{6,5},{7,4},{8,11},{9,10},{10,... | collective-permute-start | bytes 688136 | tf_op jit(solution)/shard_map/ppermute | solution.py:361
  68.1 8.9 %collective-permute-start.16 = (bf16[896,128]{1,0:T(8,128)(2,1)S(1)}, bf16[896,128]{1,0:T(8,128)(2,1)S(1)}, u32[]{:S(2)}, u32[]{:S(2)}) collective-permute-start(bf16[896,128]{1,0:T(8,128)(2,1)S(1)} %pad_maximum_fusion.refs_0_), channel_id=1, source_target_pairs={{0,2},{1,3},{2,0},{3,1},{4,6},{5,7},{6,4},{7,5},{8,10},{9,11},{10,... | collective-permute-start | bytes 688136 | tf_op jit(solution)/shard_map/ppermute | solution.py:361
  69.5 7.7 %collective-permute-start.15 = (bf16[896,128]{1,0:T(8,128)(2,1)S(1)}, bf16[896,128]{1,0:T(8,128)(2,1)S(1)}, u32[]{:S(2)}, u32[]{:S(2)}) collective-permute-start(bf16[896,128]{1,0:T(8,128)(2,1)S(1)} %pad_maximum_fusion.refs_0_), channel_id=1, source_target_pairs={{0,1},{1,0},{2,3},{3,2},{4,5},{5,4},{6,7},{7,6},{8,9},{9,8},{10,11... | collective-permute-start | bytes 688136 | tf_op jit(solution)/shard_map/ppermute | solution.py:361
  70.1 8.1 %collective-permute-start.18 = (bf16[896,128]{1,0:T(8,128)(2,1)S(1)}, bf16[896,128]{1,0:T(8,128)(2,1)S(1)}, u32[]{:S(2)}, u32[]{:S(2)}) collective-permute-start(bf16[896,128]{1,0:T(8,128)(2,1)S(1)} %pad_maximum_fusion.refs_0_), channel_id=1, source_target_pairs={{0,4},{1,5},{2,6},{3,7},{4,0},{5,1},{6,2},{7,3},{8,12},{9,13},{10,... | collective-permute-start | bytes 688136 | tf_op jit(solution)/shard_map/ppermute | solution.py:361
  74.7 3.6 %collective-permute-start.21 = (bf16[896,128]{1,0:T(8,128)(2,1)S(1)}, bf16[896,128]{1,0:T(8,128)(2,1)S(1)}, u32[]{:S(2)}, u32[]{:S(2)}) collective-permute-start(bf16[896,128]{1,0:T(8,128)(2,1)S(1)} %collective-permute-done.17.refs_3_), channel_id=1, source_target_pairs={{0,4},{1,5},{2,6},{3,7},{4,0},{5,1},{6,2},{7,3},{8,12},{9,13},{10,... | collective-permute-start | bytes 688136 | tf_op jit(solution)/shard_map/ppermute | solution.py:361
  77.0 1.5 %collective-permute-start.20 = (bf16[896,128]{1,0:T(8,128)(2,1)S(1)}, bf16[896,128]{1,0:T(8,128)(2,1)S(1)}, u32[]{:S(2)}, u32[]{:S(2)}) collective-permute-start(bf16[896,128]{1,0:T(8,128)(2,1)S(1)} %collective-permute-done.16.refs_2_), channel_id=1, source_target_pairs={{0,4},{1,5},{2,6},{3,7},{4,0},{5,1},{6,2},{7,3},{8,12},{9,13},{10,... | collective-permute-start | bytes 688136 | tf_op jit(solution)/shard_map/ppermute | solution.py:361
  77.2 1.6 %collective-permute-start.19 = (bf16[896,128]{1,0:T(8,128)(2,1)S(1)}, bf16[896,128]{1,0:T(8,128)(2,1)S(1)}, u32[]{:S(2)}, u32[]{:S(2)}) collective-permute-start(bf16[896,128]{1,0:T(8,128)(2,1)S(1)} %collective-permute-done.15.refs_1_), channel_id=1, source_target_pairs={{0,4},{1,5},{2,6},{3,7},{4,0},{5,1},{6,2},{7,3},{8,12},{9,13},{10,... | collective-permute-start | bytes 688136 | tf_op jit(solution)/shard_map/ppermute | solution.py:361

commit v2 on v1

v2 whole, which is shorter than its diff:
```python
import functools
import math

import jax
import jax.numpy as jnp
from jax import lax
from jax.experimental import pallas as pl
from jax.experimental.pallas import tpu as pltpu
from jax.sharding import PartitionSpec as P

BF, F32 = jnp.bfloat16, jnp.float32
HALO = 7
SIDE = 8
VMEM = pl.BlockSpec(memory_space=pltpu.VMEM)


def call(body, out_shapes, args, scratch=(), limit=8, flops=10**9):
    return pl.pallas_call(
        body,
        out_shape=out_shapes,
        in_specs=[VMEM] * len(args),
        out_specs=jax.tree.map(lambda _: VMEM, out_shapes),
        scratch_shapes=list(scratch),
        cost_estimate=pl.CostEstimate(flops=flops, bytes_accessed=0, transcendentals=0),
        compiler_params=pltpu.CompilerParams(vmem_limit_bytes=limit * 1024 * 1024),
    )(*args)


def shape(dims, dtype=BF):
    return jax.ShapeDtypeStruct(dims, dtype)


def dot(a, b, dims=((1,), (0,))):
    return lax.dot_general(a, b, (dims, ((), ())), preferred_element_type=F32)


def picking(dims, rule):
    i, j = (lax.broadcasted_iota(jnp.int32, dims, axis) for axis in (0, 1))
    return jnp.where(rule(i, j), 1.0, 0.0).astype(BF)


def groups_of(rows, width):
    return -(-rows * width // 128)


def lanes_to_channels(row, owner, width, total):
    base = row * width % 128
    return picking(
        (128, total),
        lambda lane, channel: (lane >= base)
        & (lane < base + width)
        & (lane - base == channel - owner * width),
    )


def strip_rows(cot_ref):
    half_rows, width, cols = cot_ref.shape
    value = cot_ref[...].reshape(half_rows * width, cols)
    short = 128 * groups_of(half_rows, width) - half_rows * width
    if short:
        value = jnp.concatenate([value, jnp.zeros((short, cols), BF)], axis=0)
    return value


def strip_piece(value, tile, half_cols):
    pitch = half_cols + 2 * SIDE
    pick = picking(
        (pitch, value.shape[1]),
        lambda i, j: j == jnp.where(i < half_cols + SIDE, i, i - pitch) + tile * half_cols,
    )
    parts = [
        dot(pick, value[low : low + 128], ((1,), (1,))) for low in range(0, value.shape[0], 128)
    ]
    return jnp.concatenate(parts, axis=0).astype(BF)


def pack_cols(count, half_cols, level_ref, cot_ref, *outs):
    me = lax.axis_index("gx")
    strip = strip_rows(cot_ref)
    level = level_ref[...].astype(F32)
    first, last = level[:, :SIDE], level[:, level.shape[1] - SIDE :]
    for turn in range(1, count):
        other = me ^ turn
        piece = strip_piece(strip, other, half_cols)
        cut = piece.shape[0]
        outs[turn - 1][0:cut] = piece
        edge = jnp.where(other == me + 1, last, first)
        outs[turn - 1][cut:] = edge.reshape(-1, 128).astype(BF)


def pack_rows(count, half_cols, level_ref, cot_ref, *refs):
    got = refs[: count - 1]
    kept_ref, cross_ref, inner_ref = refs[count - 1 :]
    me, core = lax.axis_index("gx"), lax.axis_index("gy") & 1
    rows, cols = level_ref.shape[0], level_ref.shape[1]
    half_rows, width = cot_ref.shape[0], cot_ref.shape[1]
    total = count * width
    pitch = half_cols + 2 * SIDE
    cut = groups_of(half_rows, width) * pitch
    mine = strip_piece(strip_rows(cot_ref), me, half_cols)
    right = jnp.zeros((rows * SIDE, 128), F32)
    left = jnp.zeros((rows * SIDE, 128), F32)
    for turn in range(1, count):
        edge = got[turn - 1][cut:].astype(F32)
        right = jnp.where(me ^ turn == me + 1, edge, right)
        left = jnp.where(me ^ turn == me - 1, edge, left)
    right, left = right.reshape(rows, SIDE, 128), left.reshape(rows, SIDE, 128)
    level = level_ref[...]
    gap = jnp.zeros((rows, 2 * pitch - cols - 2 * SIDE, 128), F32)
    edges = jnp.concatenate([right, gap, left], axis=1).astype(BF)
    wide = jnp.concatenate([level, edges], axis=1).reshape(2 * rows * pitch, 128)
    kept_ref[0 : 2 * rows * pitch] = wide
    cot = []
    for row in range(half_rows):
        low = row * width // 128 * pitch
        value = jnp.zeros((pitch, total), F32)
        for turn in range(count):
            part = mine[low : low + pitch] if turn == 0 else got[turn - 1][low : low + pitch]
            value = value + dot(part, lanes_to_channels(row, me ^ turn, width, total))
        value = value.astype(BF)
        cot.append(value)
        low = 2 * (rows + row) * pitch
        kept_ref[low : low + pitch] = value[:, :128]
        kept_ref[low + pitch : low + 2 * pitch] = value[:, 128:]
    edges = jnp.concatenate([right, left], axis=1).astype(BF)
    band = jnp.concatenate([level, edges], axis=1)
    cells = HALO * (cols + 2 * SIDE)
    for low, neck, is_cross in ((0, 0, core == 0), (rows - HALO, half_rows - 2, core == 1)):
        for ref, here in ((cross_ref, is_cross), (inner_ref, jnp.logical_not(is_cross))):

            @pl.when(here)
            def _(ref=ref, low=low, neck=neck):
                ref[0:cells] = band[low : low + HALO].reshape(cells, 128)
                for i in range(2):
                    spot = cells + 2 * pitch * i
                    ref[spot : spot + pitch] = cot[neck + i][:, :128]
                    ref[spot + pitch : spot + 2 * pitch] = cot[neck + i][:, 128:]


def turn_weights(wl_ref, wd_ref, wn_ref, wfwd_ref, wbwd_ref, wdt_ref, wnt_ref):
    zero = jnp.zeros((128, 128), BF)
    for ky in range(3):
        w = [wl_ref[3 * ky + kx] for kx in range(3)]
        t = [value.T for value in w]
        for ref, blocks in (
            (wfwd_ref, (w[1], w[0], w[2], w[1], w[0], zero, zero, w[2])),
            (wbwd_ref, (t[1], t[2], t[0], t[1], t[2], zero, zero, t[0])),
        ):
            for spot, block in enumerate(blocks):
                low = 512 * ky + 128 * (spot // 2)
                ref[low : low + 128, 128 * (spot % 2) : 128 * (spot % 2) + 128] = block
    for p in range(2):
        wdt_ref[:, 256 * p : 256 * p + 256] = wd_ref[256 * p : 256 * p + 256].T
    for k in range(9):
        total = wn_ref.shape[1]
        wnt_ref[total * k : total * k + total] = wn_ref[total * k : total * k + total].T


def sigmoid_slope(value):
    gate = jax.nn.sigmoid(value)
    return gate, gate + value * gate * (1.0 - gate)


def shifted(value):
    size = value.shape[1]
    return pltpu.roll(value, 1, 1), pltpu.roll(value, size - 1, 1)


def paired(value):
    return jnp.concatenate(
        [pltpu.roll(value[:, :, 128:], 1, 1), pltpu.roll(value[:, :, :128], value.shape[1] - 1, 1)],
        axis=2,
    ).astype(BF)


def flat(value):
    return value.reshape(-1, value.shape[-1])


def main(
    sizes,
    kept_ref, cross_ref, inner_ref, wfwd, wbwd, wd_ref, wdt_ref, wn_ref, wnt_ref,
    keep_ref, send_ref, pieces_ref, grad_ref,
    field, pair, side, act, slope, neck, gate, cot_all, ngrad, lback, lgate, lside, spread, store,
):
    rows, half_rows, half_cols, width, count, level_scale, neck_scale = sizes
    cols = 2 * half_cols
    pitch = half_cols + 2 * SIDE
    total = wd_ref.shape[1]
    me, row = lax.axis_index("gx"), lax.axis_index("gy")
    row_end, col_end = lax.axis_size("gy") * half_rows, lax.axis_size("gx") * half_cols
    core = row & 1

    cells = HALO * (cols + 2 * SIDE)

    def take(ref, low, low_neck):
        band = ref[0:cells].reshape(HALO, cols + 2 * SIDE, 128).astype(F32)
        field[low : low + HALO, 0 : cols + SIDE] = band[:, : cols + SIDE]
        field[low : low + HALO, cols + SIDE : 2 * pitch - SIDE] = jnp.zeros(
            (HALO, 2 * pitch - cols - 2 * SIDE, 128), F32
        )
        field[low : low + HALO, 2 * pitch - SIDE :] = band[:, cols + SIDE :]
        for i in range(2):
            spot = cells + 2 * pitch * i
            cot_all[low_neck + i, :, :128] = ref[spot : spot + pitch]
            cot_all[low_neck + i, :, 128:] = ref[spot + pitch : spot + 2 * pitch]

    @pl.when(core == 0)
    def _():
        take(cross_ref, 0, 0)
        take(inner_ref, HALO + rows, 2 + half_rows)

    @pl.when(core == 1)
    def _():
        take(inner_ref, 0, 0)
        take(cross_ref, HALO + rows, 2 + half_rows)

    own = kept_ref[0 : 2 * rows * pitch].reshape(rows, 2 * pitch, 128)
    field[HALO : HALO + rows] = own.astype(F32)
    for row_in in range(half_rows):
        low = 2 * (rows + row_in) * pitch
        cot_all[2 + row_in, :, :128] = kept_ref[low : low + pitch]
        cot_all[2 + row_in, :, 128:] = kept_ref[low + pitch : low + 2 * pitch]
    even = field[:, pl.ds(0, pitch, stride=2), :]
    odd = field[:, pl.ds(1, pitch, stride=2), :]
    both = jnp.concatenate([even, odd], axis=2)
    pair[...] = both.astype(BF)
    side[...] = paired(both)

    act_rows = act.shape[0]
    step = act_rows // 2
    for low in range(0, act_rows, step):
        taken = [
            flat(ref[low + ky : low + ky + step]) for ky in range(3) for ref in (pair, side)
        ]
        pre = dot(jnp.concatenate(taken, axis=1), wfwd[...])
        sig, slp = sigmoid_slope(pre)
        own = flat(pair[low + 1 : low + 1 + step]).astype(F32)
        act[low : low + step] = (own + pre * sig).astype(BF).reshape(step, pitch, 256)
        slope[low : low + step] = slp.reshape(step, pitch, 256)

    def inside(value, first_row):
        r = lax.broadcasted_iota(jnp.int32, value.shape, 0) + (row * half_rows + first_row)
        c = lax.broadcasted_iota(jnp.int32, value.shape, 1)
        c = jnp.where(c < half_cols + SIDE, c, c - pitch) + me * half_cols
        ok = (r >= 0) & (r < row_end) & (c >= 0) & (c < col_end)
        return jnp.where(ok, value, 0.0)

    neck_rows = act_rows // 2
    grid = act[...].reshape(neck_rows, 2, pitch, 256)
    both = jnp.concatenate([flat(grid[:, 0]), flat(grid[:, 1])], axis=1)
    value = dot(both, wd_ref[...]).reshape(neck_rows, pitch, total)
    value = inside(value, -3).astype(BF)
    before, behind = shifted(value.astype(F32))
    neck[0], neck[1], neck[2] = before.astype(BF), value, behind.astype(BF)

    gate_rows = neck_rows - 2
    taken = [flat(neck[kx, ky : ky + gate_rows]) for ky in range(3) for kx in range(3)]
    pre = dot(jnp.concatenate(taken, axis=1), wn_ref[...])
    sig, slp = sigmoid_slope(pre)
    own = flat(neck[1, 1 : 1 + gate_rows]).astype(F32)
    out = (own + pre * sig).astype(BF).reshape(gate_rows, pitch, total)
    out = out[2 : 2 + half_rows, :half_cols].reshape(half_rows * half_cols, total)
    for turn in range(count):
        for low in range(0, half_rows, max(1, 128 // width)):
            piece = jnp.zeros((half_cols, 128), F32)
            for r in range(low, min(half_rows, low + 128 // width)):
                pick = lanes_to_channels(r, me ^ turn, width, total)
                piece = piece + dot(out[half_cols * r : half_cols * r + half_cols], pick, ((1,), (1,)))
            group = low * width // 128
            pieces_ref[turn, half_cols * group : half_cols * group + half_cols] = piece.astype(BF)
    value = (flat(cot_all[...]).astype(F32) * slp).astype(BF).reshape(gate_rows, pitch, total)
    before, behind = shifted(value.astype(F32))
    gate[0], gate[1], gate[2] = before.astype(BF), value, behind.astype(BF)

    grad_rows = gate_rows - 2
    taken = [
        flat(gate[2 - kx, 2 - ky : 2 - ky + grad_rows]) for ky in range(3) for kx in range(3)
    ]
    back = dot(jnp.concatenate(taken, axis=1), wnt_ref[...])
    value = flat(cot_all[1 : 1 + grad_rows]).astype(F32) + back
    value = inside(value.reshape(grad_rows, pitch, total), -1)
    ngrad[...] = value.astype(BF)

    value = dot(flat(ngrad[...]), wdt_ref[...]).reshape(grad_rows, pitch, 512)
    for p in range(2):
        for i in range(grad_rows):
            lback[2 * i + p] = value[i, :, 256 * p : 256 * p + 256]
    value = lback[...] * slope[4 : 4 + 2 * grad_rows]
    value = value.astype(BF)
    lgate[...] = value
    lside[...] = paired(value.astype(F32))

    taken = [
        flat(ref[3 - ky : 3 - ky + rows, :half_cols]) for ky in range(3) for ref in (lgate, lside)
    ]
    value = dot(jnp.concatenate(taken, axis=1), wbwd[...]).reshape(rows, half_cols, 256)
    value = value + lback[2 : 2 + rows, :half_cols]
    spread[:, pl.ds(0, half_cols, stride=2), :] = value[:, :, :128]
    spread[:, pl.ds(1, half_cols, stride=2), :] = value[:, :, 128:]
    grad_ref[...] = spread[...].astype(BF)

    half = keep_ref.shape[0]
    taken = [
        flat(neck[kx, 2 + ky : 2 + ky + half_rows, :half_cols]) for ky in range(3) for kx in range(3)
    ]
    own = flat(gate[1, 2 : 2 + half_rows, :half_cols])
    place = 0
    for lhs in taken:
        value = (dot(lhs, own, ((0,), (0,))) * neck_scale).astype(BF)
        store[place : place + 256] = value[:, :128]
        store[place + 256 : place + 512] = value[:, 128:]
        place += 512
    own = flat(ngrad[1 : 1 + half_rows, :half_cols])
    grid = act[6 : 6 + rows].reshape(half_rows, 2, pitch, 256)
    for p in range(2):
        lhs = flat(grid[:, p, :half_cols])
        value = (dot(lhs, own, ((0,), (0,))) * neck_scale).astype(BF)
        for q in range(2):
            for h in range(2):
                store[place : place + 128] = value[128 * q : 128 * q + 128, 128 * h : 128 * h + 128]
                place += 128
    own = flat(lgate[2 : 2 + rows, :half_cols])
    for ky in range(3):
        m = dot(flat(pair[6 + ky : 6 + ky + rows, :half_cols]), own, ((0,), (0,)))
        s = dot(flat(side[6 + ky : 6 + ky + rows, :half_cols]), own, ((0,), (0,)))
        for value in (
            m[:128, 128:] + s[:128, :128],
            m[:128, :128] + m[128:, 128:],
            m[128:, :128] + s[128:, 128:],
        ):
            store[place : place + 128] = (value * level_scale).astype(BF)
            place += 128
    if place < 2 * half:
        store[place:] = jnp.zeros((2 * half - place, 128), BF)
    keep_ref[...] = store[pl.ds(pl.multiple_of(core * half, 16), half), :]
    send_ref[...] = store[pl.ds(pl.multiple_of((1 - core) * half, 16), half), :]


def add_cores(count, keep_ref, got_ref, pieces_ref, own_ref, *outs):
    me = lax.axis_index("gx")
    part = own_ref.shape[0]
    for turn in range(count):
        here = pl.ds(pl.multiple_of((me ^ turn) * part, 16), part)
        value = keep_ref[here, :].astype(F32) + got_ref[here, :].astype(F32)
        if turn == 0:
            own_ref[...] = value
        else:
            outs[turn - 1][0:part] = value.astype(BF)
            outs[turn - 1][part:] = pieces_ref[turn]


def add_cols(count, z_count, own_ref, *refs):
    got = refs[: count - 1]
    first_ref, outs, total = refs[count - 1], refs[count:-1], refs[-1]
    z = lax.axis_index("gy") // 2
    part, unit = own_ref.shape[0], first_ref.shape[0]
    value = own_ref[...]
    for ref in got:
        value = value + ref[0:part].astype(F32)
    total[0:part] = value
    if part < total.shape[0]:
        total[part:] = jnp.zeros((total.shape[0] - part, 128), F32)
    for turn in range(z_count):
        value = total[pl.ds(pl.multiple_of((z ^ turn) * unit, 16), unit), :]
        if turn == 0:
            first_ref[...] = value
        else:
            outs[turn - 1][...] = value.astype(BF)


def place_neck(count, part, pieces_ref, *refs):
    got, neck_ref = refs[:-1], refs[-1]
    me = lax.axis_index("gx")
    half_rows, width, cols = neck_ref.shape
    half_cols = cols // count
    for group in range(groups_of(half_rows, width)):
        value = jnp.zeros((128, cols), F32)
        here = slice(half_cols * group, half_cols * group + half_cols)
        for turn in range(count):
            piece = pieces_ref[0, here] if turn == 0 else got[turn - 1][part:][here]
            pick = picking((half_cols, cols), lambda i, j, t=turn: j == i + (me ^ t) * half_cols)
            value = value + dot(piece, pick, ((0,), (0,)))
        per = min(half_rows, 128 // width)
        value = value[: per * width].astype(BF).reshape(per, width, cols)
        neck_ref[group * per : group * per + per] = value


def add_rows(first_ref, *refs):
    value = first_ref[...]
    for ref in refs[:-1]:
        value = value + ref[...].astype(F32)
    refs[-1][...] = value.astype(BF)


def join(z_count, *refs):
    pieces, (out_ref, store) = refs[:z_count], refs[z_count:]
    z = lax.axis_index("gy") // 2
    unit = pieces[0].shape[0]
    for turn in range(z_count):
        store[pl.ds(pl.multiple_of((z ^ turn) * unit, 16), unit), :] = pieces[turn][...]
    out_ref[...] = store[0 : out_ref.shape[0]]


def finish(count, *refs):
    ours, theirs = refs[:count], refs[count : 2 * count]
    level_ref, down_ref, neck_ref, store = refs[2 * count :]
    me, row = lax.axis_index("gx"), lax.axis_index("gy")
    part = ours[0].shape[0]
    for flip, group in ((0, ours), (1, theirs)):
        for turn in range(count):
            place = (((row & 1) ^ flip) * count + (me ^ turn)) * part
            store[pl.ds(pl.multiple_of(place, 16), part), :] = group[turn][...]
    place = 0
    for ref in (neck_ref, down_ref):
        deep = ref.shape[1]
        for i in range(ref.shape[0]):
            for h in range(2):
                ref[i, :, 128 * h : 128 * h + 128] = store[place : place + deep]
                place += deep
    for i in range(level_ref.shape[0]):
        level_ref[i] = store[place : place + 128]
        place += 128


def local(level_in, w_level, w_down, w_neck, cotangent):
    rows, cols, _ = level_in.shape
    half_rows, half_cols = rows // 2, cols // 2
    total = w_neck.shape[3]
    count, gy_count = lax.axis_size("gx"), lax.axis_size("gy")
    z_count = gy_count // 2
    pitch = half_cols + 2 * SIDE
    axes = ("gy", "gx")
    spots = [(y, x) for y in range(gy_count) for x in range(count)]

    def permute(value, target):
        pairs = [(y * count + x, target(y, x)) for y, x in spots]
        return lax.ppermute(value, axes, [(a, b) for a, b in pairs if b is not None])

    def by_col(value, turn):
        return permute(value, lambda y, x: y * count + (x ^ turn))

    def by_z(value, turn):
        return permute(value, lambda y, x: (y ^ (2 * turn)) * count + x)

    def by_core(value):
        return permute(value, lambda y, x: (y ^ 1) * count + x)

    def by_seam(value):
        def target(y, x):
            other = y + 1 if y % 2 else y - 1
            return other * count + x if 0 <= other < gy_count else None

        return permute(value, target)

    strip = jnp.swapaxes(cotangent, 1, 2)
    width = strip.shape[1]
    packed = shape((groups_of(half_rows, width) * pitch + rows * SIDE, 128))
    sent = call(
        functools.partial(pack_cols, count, half_cols), [packed] * (count - 1), (level_in, strip)
    )
    got = [by_col(value, turn + 1) for turn, value in enumerate(sent)]
    band = shape((HALO * (cols + 2 * SIDE) + 4 * pitch, 128))
    kept, cross, inner = call(
        functools.partial(pack_rows, count, half_cols),
        [shape((3 * rows * pitch, 128)), band, band],
        (level_in, strip, *got),
    )
    cross, inner = by_seam(cross), by_core(inner)

    wl = w_level.reshape(9, 128, 128)
    wd = w_down.reshape(512, total)
    wn = w_neck.reshape(9 * total, total)
    wfwd, wbwd, wdt, wnt = call(
        turn_weights,
        [shape((1536, 256)), shape((1536, 256)), shape((total, 512)), shape(wn.shape)],
        (wl, wd, wn),
    )
    pixels = rows * cols * count * gy_count
    used = 2 * 9 * total + 4 * 2 * 128 + 9 * 128
    part = -(-used // (2 * count * 16)) * 16
    half = part * count
    unit = -(-part // (z_count * 16)) * 16
    tiles = groups_of(half_rows, width) * half_cols
    sizes = (
        rows, half_rows, half_cols, width, count,
        1.0 / math.sqrt(pixels), 1.0 / math.sqrt(pixels // 4),
    )
    far = rows + 2 * HALO
    keep, send, pieces, grad_input = call(
        functools.partial(main, sizes),
        [shape((half, 128)), shape((half, 128)), shape((count, tiles, 128)), shape(level_in.shape)],
        (kept, cross, inner, wfwd, wbwd, wd, wdt, wn, wnt),
        [
            pltpu.VMEM((far, 2 * pitch, 128), F32),
            pltpu.VMEM((far, pitch, 256), BF),
            pltpu.VMEM((far, pitch, 256), BF),
            pltpu.VMEM((far - 2, pitch, 256), BF),
            pltpu.VMEM((far - 2, pitch, 256), F32),
            pltpu.VMEM((3, half_rows + 6, pitch, total), BF),
            pltpu.VMEM((3, half_rows + 4, pitch, total), BF),
            pltpu.VMEM((half_rows + 4, pitch, total), BF),
            pltpu.VMEM((half_rows + 2, pitch, total), BF),
            pltpu.VMEM((rows + 4, pitch, 256), F32),
            pltpu.VMEM((rows + 4, pitch, 256), BF),
            pltpu.VMEM((rows + 4, pitch, 256), BF),
            pltpu.VMEM((rows, cols, 128), F32),
            pltpu.VMEM((2 * half, 128), BF),
        ],
        limit=20,
        flops=6 * 10**9,
    )

    own, *sent = call(
        functools.partial(add_cores, count),
        [shape((part, 128), F32)] + [shape((part + tiles, 128))] * (count - 1),
        (keep, by_core(send), pieces),
    )
    got = [by_col(value, turn + 1) for turn, value in enumerate(sent)]
    own, *sent = call(
        functools.partial(add_cols, count, z_count),
        [shape((unit, 128), F32)] + [shape((unit, 128))] * (z_count - 1),
        (own, *got),
        [pltpu.VMEM((unit * z_count, 128), F32)],
    )
    neck_out = call(functools.partial(place_neck, count, part), shape(strip.shape), (pieces, *got))
    got = [by_z(value, turn + 1) for turn, value in enumerate(sent)]
    own = call(add_rows, shape((unit, 128)), (own, *got))
    own = call(
        functools.partial(join, z_count),
        shape((part, 128)),
        [own] + [by_z(own, turn) for turn in range(1, z_count)],
        [pltpu.VMEM((unit * z_count, 128), BF)],
    )
    ours = [own] + [by_col(own, turn) for turn in range(1, count)]
    theirs = [by_core(value) for value in ours]
    grad_level, grad_down, grad_neck = call(
        functools.partial(finish, count),
        [shape((9, 128, 128)), shape((4, 128, total)), shape((9, total, total))],
        (*ours, *theirs),
        [pltpu.VMEM((2 * half, 128), BF)],
    )
    return (
        jnp.swapaxes(neck_out, 1, 2),
        grad_input,
        grad_level.reshape(w_level.shape),
        grad_down.reshape(w_down.shape),
        grad_neck.reshape(w_neck.shape),
    )


def solution(mesh):
    return jax.shard_map(
        local,
        mesh=mesh,
        in_specs=(P("gy", "gx", None), P(), P(), P(), P("gy", None, "gx")),
        out_specs=(P("gy", None, "gx"), P("gy", "gx", None), P(), P(), P()),
        check_vma=False,
    )
```

time: 80.6 us -> 70.9 us (0.88)
  local copies, waits for them, and re-layouts: 7.88 us -> 1.75 us
  waiting for transfers between devices: 34.6 us -> 32.1 us
  starting transfers between devices: 28.3 us -> 27 us
    unnamed x19 -> x10, local copies, waits for them, and re-layouts: 6.06 us -> 1.75 us
    ppermute x22, waiting for transfers between devices: 34.6 us -> 32.1 us  [permute(): lax.ppermute(value, axes, [(a, b) for a, b in pairs if b is not None])]
    ppermute x22, starting transfers between devices: 28.3 us -> 27 us  [permute(): lax.ppermute(value, axes, [(a, b) for a, b in pairs if b is not None])]
    reshape x1 -> x0, local copies, waits for them, and re-layouts: 1.09 us -> none  [local(): wd = w_down.reshape(512, total)]
    pallas_call x7 -> x10, Pallas kernels: 8.75 us -> 9.11 us  [call(): pl.pallas_call(body, out_shape=out_shapes, in_specs=[VMEM] * len(args), o...]
  transfers between devices with their start and end apart: 22 -> 22, of which waited for: 17 -> 16; matrix products, arithmetic and copies ran while one was open for 3% -> 0% of each run, Pallas kernels for 0% -> 2%
where the time goes in v2:
time: 70.9 us; the launch traced here: 70.7 us
  waiting for transfers between devices  32.1 us (45%)
  starting transfers between devices  27 us (38%)
  Pallas kernels  9.11 us (13%)
  local copies, waits for them, and re-layouts  1.75 us (2%)
  between operations  0.72 us (1%)
    ppermute x22, waiting for transfers between devices, permute(): lax.ppermute(value, axes, [(a, b) for a, b in pairs if b is not None])  32.1 us
    ppermute x22, starting transfers between devices, permute(): lax.ppermute(value, axes, [(a, b) for a, b in pairs if b is not None])  27 us
    pallas_call x10, Pallas kernels, call(): pl.pallas_call(body, out_shape=out_shapes, in_specs=[VMEM] * len(args), o...  9.11 us
    unnamed x10, local copies, waits for them, and re-layouts  1.75 us
  transfers between devices with their start and end apart: 22, of which 16 were waited for; matrix products, arithmetic and copies ran while one was open for 0% of the time, Pallas kernels for 2%

profile of v2, /device:TPU:0, one launch (start us, length us, event | category | flops | bytes accessed | tf_op | source)
XLA Modules:
  0.0 70.7 jit_solution(4206820156658209659)
XLA Ops:
  0.6 0.9 %copy-done.3 = bf16[8,64,128]{2,1,0:T(8,128)(2,1)S(1)} copy-done((bf16[8,64,128]{2,1,0:T(8,128)(2,1)S(1)}, bf16[8,64,128]{2,1,0:T(8,128)(2,1)}, u32[]{:S(2)}) %copy-start.3) | copy-done | bytes 131096
  1.5 0.8 %copy-done.4 = bf16[4,128,64]{1,2,0:T(8,128)(2,1)S(1)} copy-done((bf16[4,128,64]{1,2,0:T(8,128)(2,1)S(1)}, bf16[4,128,64]{1,2,0:T(8,128)(2,1)}, u32[]{:S(2)}) %copy-start.4) | copy-done | bytes 65560
  2.6 3.0 %collective-permute-start = (bf16[160,128]{1,0:T(8,128)(2,1)S(1)}, bf16[160,128]{1,0:T(8,128)(2,1)S(1)}, u32[]{:S(2)}, u32[]{:S(2)}) collective-permute-start(bf16[160,128]{1,0:T(8,128)(2,1)S(1)} %get-tuple-element.30), channel_id=1, source_target_pairs={{0,1},{1,0},{2,3},{3,2},{4,5},{5,4},{6,7},{7,6},{8,9},{9,8},{10,11... | collective-permute-start | bytes 122888 | tf_op jit(solution)/shard_map/ppermute | solution.py:438
  5.6 1.5 %collective-permute-start.1 = (bf16[160,128]{1,0:T(8,128)(2,1)S(1)}, bf16[160,128]{1,0:T(8,128)(2,1)S(1)}, u32[]{:S(2)}, u32[]{:S(2)}) collective-permute-start(bf16[160,128]{1,0:T(8,128)(2,1)S(1)} %get-tuple-element.31), channel_id=1, source_target_pairs={{0,2},{1,3},{2,0},{3,1},{4,6},{5,7},{6,4},{7,5},{8,10},{9,11},{10,... | collective-permute-start | bytes 122888 | tf_op jit(solution)/shard_map/ppermute | solution.py:438
  7.6 2.0 %collective-permute-done.1.refs_1_ = bf16[160,128]{1,0:T(8,128)(2,1)S(1)} collective-permute-done((bf16[160,128]{1,0:T(8,128)(2,1)S(1)}, bf16[160,128]{1,0:T(8,128)(2,1)S(1)}, u32[]{:S(2)}, u32[]{:S(2)}) %collective-permute-start.1) | collective-permute-done | bytes 40992 | tf_op jit(solution)/shard_map/ppermute | solution.py:438
  9.6 2.4 %collective-permute-done.2.refs_2_ = bf16[160,128]{1,0:T(8,128)(2,1)S(1)} collective-permute-done((bf16[160,128]{1,0:T(8,128)(2,1)S(1)}, bf16[160,128]{1,0:T(8,128)(2,1)S(1)}, u32[]{:S(2)}, u32[]{:S(2)}) %collective-permute-start.2) | collective-permute-done | bytes 40992 | tf_op jit(solution)/shard_map/ppermute | solution.py:438
  12.5 0.7 collective-permute-start.3
  13.2 3.0 %collective-permute-start.4 = (bf16[752,128]{1,0:T(8,128)(2,1)S(1)}, bf16[752,128]{1,0:T(8,128)(2,1)S(1)}, u32[]{:S(2)}, u32[]{:S(2)}) collective-permute-start(bf16[752,128]{1,0:T(8,128)(2,1)S(1)} %get-tuple-element.35), channel_id=1, source_target_pairs={{0,4},{1,5},{2,6},{3,7},{4,0},{5,1},{6,2},{7,3},{8,12},{9,13},{10,... | collective-permute-start | bytes 577544 | tf_op jit(solution)/shard_map/ppermute | solution.py:438
  16.2 0.6 shard_map.94
  17.2 5.1 %shard_map.95 = (bf16[3392,128]{1,0:T(8,128)(2,1)S(1)}, bf16[3392,128]{1,0:T(8,128)(2,1)S(1)}, bf16[4,64,128]{2,1,0:T(8,128)(2,1)S(1)}, bf16[8,64,128]{2,1,0:T(8,128)(2,1)}) custom-call(bf16[1152,128]{1,0:T(8,128)(2,1)S(1)} %get-tuple-element.33.kept_ref, bf16[752,128]{1,0:T(8,128)(2,1)S(1)} %collective-permute-done.3.cross_ref, ...), custom_call_target="tpu_custom_call" | custom-call | flops 6000000000 | tf_op jit(solution)/shard_map/pallas_call | solution.py:18
  22.3 2.3 %collective-permute-start.5 = (bf16[3392,128]{1,0:T(8,128)(2,1)S(1)}, bf16[3392,128]{1,0:T(8,128)(2,1)S(1)}, u32[]{:S(2)}, u32[]{:S(2)}) collective-permute-start(bf16[3392,128]{1,0:T(8,128)(2,1)S(1)} %get-tuple-element.42), channel_id=1, source_target_pairs={{0,4},{1,5},{2,6},{3,7},{4,0},{5,1},{6,2},{7,3},{8,12},{9,13},{10,... | collective-permute-start | bytes 2605064 | tf_op jit(solution)/shard_map/ppermute | solution.py:438
  24.5 2.0 %collective-permute-done.5.got_ref = bf16[3392,128]{1,0:T(8,128)(2,1)S(1)} collective-permute-done((bf16[3392,128]{1,0:T(8,128)(2,1)S(1)}, bf16[3392,128]{1,0:T(8,128)(2,1)S(1)}, u32[]{:S(2)}, u32[]{:S(2)}) %collective-permute-start.5) | collective-permute-done | bytes 868384 | tf_op jit(solution)/shard_map/ppermute | solution.py:438
  26.8 0.6 collective-permute-start.6
  27.4 0.5 collective-permute-start.7
  27.9 2.4 %collective-permute-start.8 = (bf16[912,128]{1,0:T(8,128)(2,1)S(1)}, bf16[912,128]{1,0:T(8,128)(2,1)S(1)}, u32[]{:S(2)}, u32[]{:S(2)}) collective-permute-start(bf16[912,128]{1,0:T(8,128)(2,1)S(1)} %get-tuple-element.45), channel_id=1, source_target_pairs={{0,3},{1,2},{2,1},{3,0},{4,7},{5,6},{6,5},{7,4},{8,11},{9,10},{10,... | collective-permute-start | bytes 700424 | tf_op jit(solution)/shard_map/ppermute | solution.py:438
  30.4 5.0 %collective-permute-done.6.refs_0_ = bf16[912,128]{1,0:T(8,128)(2,1)S(1)} collective-permute-done((bf16[912,128]{1,0:T(8,128)(2,1)S(1)}, bf16[912,128]{1,0:T(8,128)(2,1)S(1)}, u32[]{:S(2)}, u32[]{:S(2)}) %collective-permute-start.6) | collective-permute-done | bytes 233504 | tf_op jit(solution)/shard_map/ppermute | solution.py:438
  35.4 4.7 %collective-permute-done.7.refs_1_ = bf16[912,128]{1,0:T(8,128)(2,1)S(1)} collective-permute-done((bf16[912,128]{1,0:T(8,128)(2,1)S(1)}, bf16[912,128]{1,0:T(8,128)(2,1)S(1)}, u32[]{:S(2)}, u32[]{:S(2)}) %collective-permute-start.7) | collective-permute-done | bytes 233504 | tf_op jit(solution)/shard_map/ppermute | solution.py:438
  40.3 1.8 %collective-permute-start.9 = (bf16[224,128]{1,0:T(8,128)(2,1)S(1)}, bf16[224,128]{1,0:T(8,128)(2,1)S(1)}, u32[]{:S(2)}, u32[]{:S(2)}) collective-permute-start(bf16[224,128]{1,0:T(8,128)(2,1)S(1)} %get-tuple-element.49), channel_id=1, source_target_pairs={{0,8},{1,9},{2,10},{3,11},{4,12},{5,13},{6,14},{7,15},{8,0},{9,1},... | collective-permute-start | bytes 172040 | tf_op jit(solution)/shard_map/ppermute | solution.py:438
  42.1 2.6 %collective-permute-start.10 = (bf16[224,128]{1,0:T(8,128)(2,1)S(1)}, bf16[224,128]{1,0:T(8,128)(2,1)S(1)}, u32[]{:S(2)}, u32[]{:S(2)}) collective-permute-start(bf16[224,128]{1,0:T(8,128)(2,1)S(1)} %get-tuple-element.50), channel_id=1, source_target_pairs={{0,16},{1,17},{2,18},{3,19},{4,20},{5,21},{6,22},{7,23},{8,24},{9,... | collective-permute-start | bytes 172040 | tf_op jit(solution)/shard_map/ppermute | solution.py:438
  45.1 3.3 %collective-permute-done.10.refs_1_ = bf16[224,128]{1,0:T(8,128)(2,1)S(1)} collective-permute-done((bf16[224,128]{1,0:T(8,128)(2,1)S(1)}, bf16[224,128]{1,0:T(8,128)(2,1)S(1)}, u32[]{:S(2)}, u32[]{:S(2)}) %collective-permute-start.10) | collective-permute-done | bytes 57376 | tf_op jit(solution)/shard_map/ppermute | solution.py:438
  48.4 2.2 %collective-permute-done.11.refs_2_ = bf16[224,128]{1,0:T(8,128)(2,1)S(1)} collective-permute-done((bf16[224,128]{1,0:T(8,128)(2,1)S(1)}, bf16[224,128]{1,0:T(8,128)(2,1)S(1)}, u32[]{:S(2)}, u32[]{:S(2)}) %collective-permute-start.11) | collective-permute-done | bytes 57376 | tf_op jit(solution)/shard_map/ppermute | solution.py:438
  50.7 0.8 %collective-permute-start.14 = (bf16[224,128]{1,0:T(8,128)(2,1)S(1)}, bf16[224,128]{1,0:T(8,128)(2,1)S(1)}, u32[]{:S(2)}, u32[]{:S(2)}) collective-permute-start(bf16[224,128]{1,0:T(8,128)(2,1)S(1)} %shard_map.99.refs_0_), channel_id=1, source_target_pairs={{0,24},{1,25},{2,26},{3,27},{4,28},{5,29},{6,30},{7,31},{8,16},{9,... | collective-permute-start | bytes 172040 | tf_op jit(solution)/shard_map/ppermute | solution.py:438
  51.4 3.7 %collective-permute-start.12 = (bf16[224,128]{1,0:T(8,128)(2,1)S(1)}, bf16[224,128]{1,0:T(8,128)(2,1)S(1)}, u32[]{:S(2)}, u32[]{:S(2)}) collective-permute-start(bf16[224,128]{1,0:T(8,128)(2,1)S(1)} %shard_map.99.refs_0_), channel_id=1, source_target_pairs={{0,8},{1,9},{2,10},{3,11},{4,12},{5,13},{6,14},{7,15},{8,0},{9,1},... | collective-permute-start | bytes 172040 | tf_op jit(solution)/shard_map/ppermute | solution.py:438
  55.1 1.7 %collective-permute-done.14.refs_3_ = bf16[224,128]{1,0:T(8,128)(2,1)S(1)} collective-permute-done((bf16[224,128]{1,0:T(8,128)(2,1)S(1)}, bf16[224,128]{1,0:T(8,128)(2,1)S(1)}, u32[]{:S(2)}, u32[]{:S(2)}) %collective-permute-start.14) | collective-permute-done | bytes 57376 | tf_op jit(solution)/shard_map/ppermute | solution.py:438
  56.8 0.9 %collective-permute-done.13.refs_2_ = bf16[224,128]{1,0:T(8,128)(2,1)S(1)} collective-permute-done((bf16[224,128]{1,0:T(8,128)(2,1)S(1)}, bf16[224,128]{1,0:T(8,128)(2,1)S(1)}, u32[]{:S(2)}, u32[]{:S(2)}) %collective-permute-start.13) | collective-permute-done | bytes 57376 | tf_op jit(solution)/shard_map/ppermute | solution.py:438
  57.8 1.5 %collective-permute-start.17 = (bf16[848,128]{1,0:T(8,128)(2,1)S(1)}, bf16[848,128]{1,0:T(8,128)(2,1)S(1)}, u32[]{:S(2)}, u32[]{:S(2)}) collective-permute-start(bf16[848,128]{1,0:T(8,128)(2,1)S(1)} %shard_map.100.refs_0_), channel_id=1, source_target_pairs={{0,3},{1,2},{2,1},{3,0},{4,7},{5,6},{6,5},{7,4},{8,11},{9,10},{10,... | collective-permute-start | bytes 651272 | tf_op jit(solution)/shard_map/ppermute | solution.py:438
  59.3 1.5 %collective-permute-start.16 = (bf16[848,128]{1,0:T(8,128)(2,1)S(1)}, bf16[848,128]{1,0:T(8,128)(2,1)S(1)}, u32[]{:S(2)}, u32[]{:S(2)}) collective-permute-start(bf16[848,128]{1,0:T(8,128)(2,1)S(1)} %shard_map.100.refs_0_), channel_id=1, source_target_pairs={{0,2},{1,3},{2,0},{3,1},{4,6},{5,7},{6,4},{7,5},{8,10},{9,11},{10,... | collective-permute-start | bytes 651272 | tf_op jit(solution)/shard_map/ppermute | solution.py:438
  60.8 0.5 collective-permute-start.15
  61.4 3.9 %collective-permute-done.17.refs_3_ = bf16[848,128]{1,0:T(8,128)(2,1)S(1)} collective-permute-done((bf16[848,128]{1,0:T(8,128)(2,1)S(1)}, bf16[848,128]{1,0:T(8,128)(2,1)S(1)}, u32[]{:S(2)}, u32[]{:S(2)}) %collective-permute-start.17) | collective-permute-done | bytes 217120 | tf_op jit(solution)/shard_map/ppermute | solution.py:438
  65.3 2.2 %collective-permute-done.16.refs_2_ = bf16[848,128]{1,0:T(8,128)(2,1)S(1)} collective-permute-done((bf16[848,128]{1,0:T(8,128)(2,1)S(1)}, bf16[848,128]{1,0:T(8,128)(2,1)S(1)}, u32[]{:S(2)}, u32[]{:S(2)}) %collective-permute-start.16) | collective-permute-done | bytes 217120 | tf_op jit(solution)/shard_map/ppermute | solution.py:438
  68.0 0.9 %shard_map.97 = bf16[4,64,128]{2,1,0:T(8,128)(2,1)} custom-call(bf16[4,64,128]{2,1,0:T(8,128)(2,1)S(1)} %get-tuple-element.40.pieces_ref, bf16[912,128]{1,0:T(8,128)(2,1)S(1)} %collective-permute-done.6.refs_0_, bf16[912,128]{1,0:T(8,128)(2,1)S(1)} %collective-permute-done.7.refs_1_, bf16[912,128]{1,0:T(8,128)(2,1)S(1)} %collective-permute-done.8.refs_2_), custom_call_target="tpu_custom_call" | custom-call | flops 1000000000 | tf_op jit(solution)/shard_map/pallas_call | solution.py:18
  69.2 1.5 %shard_map.101 = (bf16[9,128,128]{2,1,0:T(8,128)(2,1)}, bf16[4,128,256]{2,1,0:T(8,128)(2,1)}, bf16[9,256,256]{2,1,0:T(8,128)(2,1)}) custom-call(bf16[848,128]{1,0:T(8,128)(2,1)S(1)} %shard_map.100.refs_0_, bf16[848,128]{1,0:T(8,128)(2,1)S(1)} %collective-permute-done.15.refs_1_, bf16[848,128]{1,0:T(8,128)(2,1)S(1)} %collective-permute-done.16.refs_2_, ...), custom_call_target="tpu_custom_call" | custom-call | flops 1000000000 | tf_op jit(solution)/shard_map/pallas_call | solution.py:18
  (32 shorter events, 3.4 us)
Async XLA Ops:
  0.6 0.9 %copy-start.3 = (bf16[8,64,128]{2,1,0:T(8,128)(2,1)S(1)}, bf16[8,64,128]{2,1,0:T(8,128)(2,1)}, u32[]{:S(2)}) copy-start(bf16[8,64,128]{2,1,0:T(8,128)(2,1)} %level_ref.3) | copy-start | bytes 393220
  1.5 0.8 %copy-start.4 = (bf16[4,128,64]{1,2,0:T(8,128)(2,1)S(1)}, bf16[4,128,64]{1,2,0:T(8,128)(2,1)}, u32[]{:S(2)}) copy-start(bf16[4,128,64]{1,2,0:T(8,128)(2,1)} %param.9) | copy-start | bytes 196612
  2.6 5.0 %collective-permute-start = (bf16[160,128]{1,0:T(8,128)(2,1)S(1)}, bf16[160,128]{1,0:T(8,128)(2,1)S(1)}, u32[]{:S(2)}, u32[]{:S(2)}) collective-permute-start(bf16[160,128]{1,0:T(8,128)(2,1)S(1)} %get-tuple-element.30), channel_id=1, source_target_pairs={{0,1},{1,0},{2,3},{3,2},{4,5},{5,4},{6,7},{7,6},{8,9},{9,8},{10,11... | collective-permute-start | bytes 122888 | tf_op jit(solution)/shard_map/ppermute | solution.py:438
  5.6 4.0 %collective-permute-start.1 = (bf16[160,128]{1,0:T(8,128)(2,1)S(1)}, bf16[160,128]{1,0:T(8,128)(2,1)S(1)}, u32[]{:S(2)}, u32[]{:S(2)}) collective-permute-start(bf16[160,128]{1,0:T(8,128)(2,1)S(1)} %get-tuple-element.31), channel_id=1, source_target_pairs={{0,2},{1,3},{2,0},{3,1},{4,6},{5,7},{6,4},{7,5},{8,10},{9,11},{10,... | collective-permute-start | bytes 122888 | tf_op jit(solution)/shard_map/ppermute | solution.py:438
  7.1 9.0 %copy-start = (bf16[3,3,256,256]{3,2,1,0:T(8,128)(2,1)S(1)}, bf16[3,3,256,256]{3,2,1,0:T(8,128)(2,1)}, u32[]{:S(2)}) copy-start(bf16[3,3,256,256]{3,2,1,0:T(8,128)(2,1)} %param.8) | copy-start | bytes 3538948
  7.1 9.0 %copy-start.1 = (bf16[3,3,128,128]{3,2,1,0:T(8,128)(2,1)S(1)}, bf16[3,3,128,128]{3,2,1,0:T(8,128)(2,1)}, u32[]{:S(2)}) copy-start(bf16[3,3,128,128]{3,2,1,0:T(8,128)(2,1)} %param.6) | copy-start | bytes 884740
  7.2 9.0 %copy-start.2 = (bf16[2,2,128,256]{3,2,1,0:T(8,128)(2,1)S(1)}, bf16[2,2,128,256]{3,2,1,0:T(8,128)(2,1)}, u32[]{:S(2)}) copy-start(bf16[2,2,128,256]{3,2,1,0:T(8,128)(2,1)} %param.7) | copy-start | bytes 786436
  7.2 4.9 %collective-permute-start.2 = (bf16[160,128]{1,0:T(8,128)(2,1)S(1)}, bf16[160,128]{1,0:T(8,128)(2,1)S(1)}, u32[]{:S(2)}, u32[]{:S(2)}) collective-permute-start(bf16[160,128]{1,0:T(8,128)(2,1)S(1)} %get-tuple-element.32), channel_id=1, source_target_pairs={{0,3},{1,2},{2,1},{3,0},{4,7},{5,6},{6,5},{7,4},{8,11},{9,10},{10,... | collective-permute-start | bytes 122888 | tf_op jit(solution)/shard_map/ppermute | solution.py:438
  12.5 4.3 %collective-permute-start.3 = (bf16[752,128]{1,0:T(8,128)(2,1)S(1)}, bf16[752,128]{1,0:T(8,128)(2,1)S(1)}, u32[]{:S(2)}, u32[]{:S(2)}) collective-permute-start(bf16[752,128]{1,0:T(8,128)(2,1)S(1)} %get-tuple-element.34), channel_id=1, source_target_pairs={{4,8},{5,9},{6,10},{7,11},{8,4},{9,5},{10,6},{11,7},{12,16},{13,17... | collective-permute-start | bytes 577544 | tf_op jit(solution)/shard_map/ppermute | solution.py:438
  13.2 4.1 %collective-permute-start.4 = (bf16[752,128]{1,0:T(8,128)(2,1)S(1)}, bf16[752,128]{1,0:T(8,128)(2,1)S(1)}, u32[]{:S(2)}, u32[]{:S(2)}) collective-permute-start(bf16[752,128]{1,0:T(8,128)(2,1)S(1)} %get-tuple-element.35), channel_id=1, source_target_pairs={{0,4},{1,5},{2,6},{3,7},{4,0},{5,1},{6,2},{7,3},{8,12},{9,13},{10,... | collective-permute-start | bytes 577544 | tf_op jit(solution)/shard_map/ppermute | solution.py:438
  22.3 4.3 %collective-permute-start.5 = (bf16[3392,128]{1,0:T(8,128)(2,1)S(1)}, bf16[3392,128]{1,0:T(8,128)(2,1)S(1)}, u32[]{:S(2)}, u32[]{:S(2)}) collective-permute-start(bf16[3392,128]{1,0:T(8,128)(2,1)S(1)} %get-tuple-element.42), channel_id=1, source_target_pairs={{0,4},{1,5},{2,6},{3,7},{4,0},{5,1},{6,2},{7,3},{8,12},{9,13},{10,... | collective-permute-start | bytes 2605064 | tf_op jit(solution)/shard_map/ppermute | solution.py:438
  26.8 8.6 %collective-permute-start.6 = (bf16[912,128]{1,0:T(8,128)(2,1)S(1)}, bf16[912,128]{1,0:T(8,128)(2,1)S(1)}, u32[]{:S(2)}, u32[]{:S(2)}) collective-permute-start(bf16[912,128]{1,0:T(8,128)(2,1)S(1)} %get-tuple-element.43), channel_id=1, source_target_pairs={{0,1},{1,0},{2,3},{3,2},{4,5},{5,4},{6,7},{7,6},{8,9},{9,8},{10,11... | collective-permute-start | bytes 700424 | tf_op jit(solution)/shard_map/ppermute | solution.py:438
  27.4 12.7 %collective-permute-start.7 = (bf16[912,128]{1,0:T(8,128)(2,1)S(1)}, bf16[912,128]{1,0:T(8,128)(2,1)S(1)}, u32[]{:S(2)}, u32[]{:S(2)}) collective-permute-start(bf16[912,128]{1,0:T(8,128)(2,1)S(1)} %get-tuple-element.44), channel_id=1, source_target_pairs={{0,2},{1,3},{2,0},{3,1},{4,6},{5,7},{6,4},{7,5},{8,10},{9,11},{10,... | collective-permute-start | bytes 700424 | tf_op jit(solution)/shard_map/ppermute | solution.py:438
  27.9 12.2 %collective-permute-start.8 = (bf16[912,128]{1,0:T(8,128)(2,1)S(1)}, bf16[912,128]{1,0:T(8,128)(2,1)S(1)}, u32[]{:S(2)}, u32[]{:S(2)}) collective-permute-start(bf16[912,128]{1,0:T(8,128)(2,1)S(1)} %get-tuple-element.45), channel_id=1, source_target_pairs={{0,3},{1,2},{2,1},{3,0},{4,7},{5,6},{6,5},{7,4},{8,11},{9,10},{10,... | collective-permute-start | bytes 700424 | tf_op jit(solution)/shard_map/ppermute | solution.py:438
  40.3 4.8 %collective-permute-start.9 = (bf16[224,128]{1,0:T(8,128)(2,1)S(1)}, bf16[224,128]{1,0:T(8,128)(2,1)S(1)}, u32[]{:S(2)}, u32[]{:S(2)}) collective-permute-start(bf16[224,128]{1,0:T(8,128)(2,1)S(1)} %get-tuple-element.49), channel_id=1, source_target_pairs={{0,8},{1,9},{2,10},{3,11},{4,12},{5,13},{6,14},{7,15},{8,0},{9,1},... | collective-permute-start | bytes 172040 | tf_op jit(solution)/shard_map/ppermute | solution.py:438
  42.1 6.3 %collective-permute-start.10 = (bf16[224,128]{1,0:T(8,128)(2,1)S(1)}, bf16[224,128]{1,0:T(8,128)(2,1)S(1)}, u32[]{:S(2)}, u32[]{:S(2)}) collective-permute-start(bf16[224,128]{1,0:T(8,128)(2,1)S(1)} %get-tuple-element.50), channel_id=1, source_target_pairs={{0,16},{1,17},{2,18},{3,19},{4,20},{5,21},{6,22},{7,23},{8,24},{9,... | collective-permute-start | bytes 172040 | tf_op jit(solution)/shard_map/ppermute | solution.py:438
  44.6 6.0 %collective-permute-start.11 = (bf16[224,128]{1,0:T(8,128)(2,1)S(1)}, bf16[224,128]{1,0:T(8,128)(2,1)S(1)}, u32[]{:S(2)}, u32[]{:S(2)}) collective-permute-start(bf16[224,128]{1,0:T(8,128)(2,1)S(1)} %get-tuple-element.51), channel_id=1, source_target_pairs={{0,24},{1,25},{2,26},{3,27},{4,28},{5,29},{6,30},{7,31},{8,16},{9,... | collective-permute-start | bytes 172040 | tf_op jit(solution)/shard_map/ppermute | solution.py:438
  50.7 6.2 %collective-permute-start.14 = (bf16[224,128]{1,0:T(8,128)(2,1)S(1)}, bf16[224,128]{1,0:T(8,128)(2,1)S(1)}, u32[]{:S(2)}, u32[]{:S(2)}) collective-permute-start(bf16[224,128]{1,0:T(8,128)(2,1)S(1)} %shard_map.99.refs_0_), channel_id=1, source_target_pairs={{0,24},{1,25},{2,26},{3,27},{4,28},{5,29},{6,30},{7,31},{8,16},{9,... | collective-permute-start | bytes 172040 | tf_op jit(solution)/shard_map/ppermute | solution.py:438
  51.4 6.3 %collective-permute-start.13 = (bf16[224,128]{1,0:T(8,128)(2,1)S(1)}, bf16[224,128]{1,0:T(8,128)(2,1)S(1)}, u32[]{:S(2)}, u32[]{:S(2)}) collective-permute-start(bf16[224,128]{1,0:T(8,128)(2,1)S(1)} %shard_map.99.refs_0_), channel_id=1, source_target_pairs={{0,16},{1,17},{2,18},{3,19},{4,20},{5,21},{6,22},{7,23},{8,24},{9,... | collective-permute-start | bytes 172040 | tf_op jit(solution)/shard_map/ppermute | solution.py:438
  51.4 6.3 %collective-permute-start.12 = (bf16[224,128]{1,0:T(8,128)(2,1)S(1)}, bf16[224,128]{1,0:T(8,128)(2,1)S(1)}, u32[]{:S(2)}, u32[]{:S(2)}) collective-permute-start(bf16[224,128]{1,0:T(8,128)(2,1)S(1)} %shard_map.99.refs_0_), channel_id=1, source_target_pairs={{0,8},{1,9},{2,10},{3,11},{4,12},{5,13},{6,14},{7,15},{8,0},{9,1},... | collective-permute-start | bytes 172040 | tf_op jit(solution)/shard_map/ppermute | solution.py:438
  57.8 7.5 %collective-permute-start.17 = (bf16[848,128]{1,0:T(8,128)(2,1)S(1)}, bf16[848,128]{1,0:T(8,128)(2,1)S(1)}, u32[]{:S(2)}, u32[]{:S(2)}) collective-permute-start(bf16[848,128]{1,0:T(8,128)(2,1)S(1)} %shard_map.100.refs_0_), channel_id=1, source_target_pairs={{0,3},{1,2},{2,1},{3,0},{4,7},{5,6},{6,5},{7,4},{8,11},{9,10},{10,... | collective-permute-start | bytes 651272 | tf_op jit(solution)/shard_map/ppermute | solution.py:438
  59.3 8.2 %collective-permute-start.16 = (bf16[848,128]{1,0:T(8,128)(2,1)S(1)}, bf16[848,128]{1,0:T(8,128)(2,1)S(1)}, u32[]{:S(2)}, u32[]{:S(2)}) collective-permute-start(bf16[848,128]{1,0:T(8,128)(2,1)S(1)} %shard_map.100.refs_0_), channel_id=1, source_target_pairs={{0,2},{1,3},{2,0},{3,1},{4,6},{5,7},{6,4},{7,5},{8,10},{9,11},{10,... | collective-permute-start | bytes 651272 | tf_op jit(solution)/shard_map/ppermute | solution.py:438
  60.8 6.7 %collective-permute-start.15 = (bf16[848,128]{1,0:T(8,128)(2,1)S(1)}, bf16[848,128]{1,0:T(8,128)(2,1)S(1)}, u32[]{:S(2)}, u32[]{:S(2)}) collective-permute-start(bf16[848,128]{1,0:T(8,128)(2,1)S(1)} %shard_map.100.refs_0_), channel_id=1, source_target_pairs={{0,1},{1,0},{2,3},{3,2},{4,5},{5,4},{6,7},{7,6},{8,9},{9,8},{10,11... | collective-permute-start | bytes 651272 | tf_op jit(solution)/shard_map/ppermute | solution.py:438
  61.4 7.5 %collective-permute-start.18 = (bf16[848,128]{1,0:T(8,128)(2,1)S(1)}, bf16[848,128]{1,0:T(8,128)(2,1)S(1)}, u32[]{:S(2)}, u32[]{:S(2)}) collective-permute-start(bf16[848,128]{1,0:T(8,128)(2,1)S(1)} %shard_map.100.refs_0_), channel_id=1, source_target_pairs={{0,4},{1,5},{2,6},{3,7},{4,0},{5,1},{6,2},{7,3},{8,12},{9,13},{10,... | collective-permute-start | bytes 651272 | tf_op jit(solution)/shard_map/ppermute | solution.py:438
  65.3 3.6 %collective-permute-start.21 = (bf16[848,128]{1,0:T(8,128)(2,1)S(1)}, bf16[848,128]{1,0:T(8,128)(2,1)S(1)}, u32[]{:S(2)}, u32[]{:S(2)}) collective-permute-start(bf16[848,128]{1,0:T(8,128)(2,1)S(1)} %collective-permute-done.17.refs_3_), channel_id=1, source_target_pairs={{0,4},{1,5},{2,6},{3,7},{4,0},{5,1},{6,2},{7,3},{8,12},{9,13},{10,... | collective-permute-start | bytes 651272 | tf_op jit(solution)/shard_map/ppermute | solution.py:438
  67.5 1.5 %collective-permute-start.20 = (bf16[848,128]{1,0:T(8,128)(2,1)S(1)}, bf16[848,128]{1,0:T(8,128)(2,1)S(1)}, u32[]{:S(2)}, u32[]{:S(2)}) collective-permute-start(bf16[848,128]{1,0:T(8,128)(2,1)S(1)} %collective-permute-done.16.refs_2_), channel_id=1, source_target_pairs={{0,4},{1,5},{2,6},{3,7},{4,0},{5,1},{6,2},{7,3},{8,12},{9,13},{10,... | collective-permute-start | bytes 651272 | tf_op jit(solution)/shard_map/ppermute | solution.py:438
  67.5 1.8 %collective-permute-start.19 = (bf16[848,128]{1,0:T(8,128)(2,1)S(1)}, bf16[848,128]{1,0:T(8,128)(2,1)S(1)}, u32[]{:S(2)}, u32[]{:S(2)}) collective-permute-start(bf16[848,128]{1,0:T(8,128)(2,1)S(1)} %collective-permute-done.15.refs_1_), channel_id=1, source_target_pairs={{0,4},{1,5},{2,6},{3,7},{4,0},{5,1},{6,2},{7,3},{8,12},{9,13},{10,... | collective-permute-start | bytes 651272 | tf_op jit(solution)/shard_map/ppermute | solution.py:438

commit v3 on v2

--- a/solution.py
+++ b/solution.py
@@ -173,6 +173,10 @@
     ).astype(BF)
 
 
+def dot_rows(a, b, step):
+    return jnp.concatenate([dot(a[i : i + step], b) for i in range(0, a.shape[0], step)], axis=0)
+
+
 def flat(value):
     return value.reshape(-1, value.shape[-1])
 
@@ -180,10 +184,10 @@
 def main(
     sizes,
     kept_ref, cross_ref, inner_ref, wfwd, wbwd, wd_ref, wdt_ref, wn_ref, wnt_ref,
-    keep_ref, send_ref, pieces_ref, grad_ref,
-    field, pair, side, act, slope, neck, gate, cot_all, ngrad, lback, lgate, lside, spread, store,
+    sums_ref, send_ref, out_ref, grad_ref,
+    field, pair, side, act, slope, neck, gate, cot_all, ngrad, lback, lgate, lside, spread,
 ):
-    rows, half_rows, half_cols, width, count, level_scale, neck_scale = sizes
+    rows, half_rows, half_cols, _, _ = sizes
     cols = 2 * half_cols
     pitch = half_cols + 2 * SIDE
     total = wd_ref.shape[1]
@@ -249,26 +253,19 @@
     neck_rows = act_rows // 2
     grid = act[...].reshape(neck_rows, 2, pitch, 256)
     both = jnp.concatenate([flat(grid[:, 0]), flat(grid[:, 1])], axis=1)
-    value = dot(both, wd_ref[...]).reshape(neck_rows, pitch, total)
+    value = dot_rows(both, wd_ref[...], 5 * pitch).reshape(neck_rows, pitch, total)
     value = inside(value, -3).astype(BF)
     before, behind = shifted(value.astype(F32))
     neck[0], neck[1], neck[2] = before.astype(BF), value, behind.astype(BF)
 
     gate_rows = neck_rows - 2
     taken = [flat(neck[kx, ky : ky + gate_rows]) for ky in range(3) for kx in range(3)]
-    pre = dot(jnp.concatenate(taken, axis=1), wn_ref[...])
+    pre = dot_rows(jnp.concatenate(taken, axis=1), wn_ref[...], 4 * pitch)
     sig, slp = sigmoid_slope(pre)
     own = flat(neck[1, 1 : 1 + gate_rows]).astype(F32)
     out = (own + pre * sig).astype(BF).reshape(gate_rows, pitch, total)
     out = out[2 : 2 + half_rows, :half_cols].reshape(half_rows * half_cols, total)
-    for turn in range(count):
-        for low in range(0, half_rows, max(1, 128 // width)):
-            piece = jnp.zeros((half_cols, 128), F32)
-            for r in range(low, min(half_rows, low + 128 // width)):
-                pick = lanes_to_channels(r, me ^ turn, width, total)
-                piece = piece + dot(out[half_cols * r : half_cols * r + half_cols], pick, ((1,), (1,)))
-            group = low * width // 128
-            pieces_ref[turn, half_cols * group : half_cols * group + half_cols] = piece.astype(BF)
+    out_ref[...] = out
     value = (flat(cot_all[...]).astype(F32) * slp).astype(BF).reshape(gate_rows, pitch, total)
     before, behind = shifted(value.astype(F32))
     gate[0], gate[1], gate[2] = before.astype(BF), value, behind.astype(BF)
@@ -277,12 +274,12 @@
     taken = [
         flat(gate[2 - kx, 2 - ky : 2 - ky + grad_rows]) for ky in range(3) for kx in range(3)
     ]
-    back = dot(jnp.concatenate(taken, axis=1), wnt_ref[...])
+    back = dot_rows(jnp.concatenate(taken, axis=1), wnt_ref[...], 3 * pitch)
     value = flat(cot_all[1 : 1 + grad_rows]).astype(F32) + back
     value = inside(value.reshape(grad_rows, pitch, total), -1)
     ngrad[...] = value.astype(BF)
 
-    value = dot(flat(ngrad[...]), wdt_ref[...]).reshape(grad_rows, pitch, 512)
+    value = dot_rows(flat(ngrad[...]), wdt_ref[...], 3 * pitch).reshape(grad_rows, pitch, 512)
     for p in range(2):
         for i in range(grad_rows):
             lback[2 * i + p] = value[i, :, 256 * p : 256 * p + 256]
@@ -294,23 +291,34 @@
     taken = [
         flat(ref[3 - ky : 3 - ky + rows, :half_cols]) for ky in range(3) for ref in (lgate, lside)
     ]
-    value = dot(jnp.concatenate(taken, axis=1), wbwd[...]).reshape(rows, half_cols, 256)
+    value = dot_rows(jnp.concatenate(taken, axis=1), wbwd[...], 4 * half_cols).reshape(rows, half_cols, 256)
     value = value + lback[2 : 2 + rows, :half_cols]
     spread[:, pl.ds(0, half_cols, stride=2), :] = value[:, :, :128]
     spread[:, pl.ds(1, half_cols, stride=2), :] = value[:, :, 128:]
     grad_ref[...] = spread[...].astype(BF)
 
-    half = keep_ref.shape[0]
-    taken = [
-        flat(neck[kx, 2 + ky : 2 + ky + half_rows, :half_cols]) for ky in range(3) for kx in range(3)
-    ]
+    weight_sums(sizes, sums_ref, neck, gate, act, ngrad, pair, side, lgate)
+    half = send_ref.shape[0]
+    send_ref[...] = sums_ref[pl.ds(pl.multiple_of((1 - core) * half, 16), half), :]
+
+
+def weight_sums(sizes, sums_ref, neck, gate, act, ngrad, pair, side, lgate):
+    rows, half_rows, half_cols, level_scale, neck_scale = sizes
+    pitch = act.shape[1]
+    place = 0
+
+    def put(value):
+        nonlocal place
+        sums_ref[place : place + value.shape[0]] = value
+        place += value.shape[0]
+
     own = flat(gate[1, 2 : 2 + half_rows, :half_cols])
-    place = 0
-    for lhs in taken:
-        value = (dot(lhs, own, ((0,), (0,))) * neck_scale).astype(BF)
-        store[place : place + 256] = value[:, :128]
-        store[place + 256 : place + 512] = value[:, 128:]
-        place += 512
+    for ky in range(3):
+        for kx in range(3):
+            lhs = flat(neck[kx, 2 + ky : 2 + ky + half_rows, :half_cols])
+            value = (dot(lhs, own, ((0,), (0,))) * neck_scale).astype(BF)
+            put(value[:, :128])
+            put(value[:, 128:])
     own = flat(ngrad[1 : 1 + half_rows, :half_cols])
     grid = act[6 : 6 + rows].reshape(half_rows, 2, pitch, 256)
     for p in range(2):
@@ -318,8 +326,7 @@
         value = (dot(lhs, own, ((0,), (0,))) * neck_scale).astype(BF)
         for q in range(2):
             for h in range(2):
-                store[place : place + 128] = value[128 * q : 128 * q + 128, 128 * h : 128 * h + 128]
-                place += 128
+                put(value[128 * q : 128 * q + 128, 128 * h : 128 * h + 128])
     own = flat(lgate[2 : 2 + rows, :half_cols])
     for ky in range(3):
         m = dot(flat(pair[6 + ky : 6 + ky + rows, :half_cols]), own, ((0,), (0,)))
@@ -329,20 +336,32 @@
             m[:128, :128] + m[128:, 128:],
             m[128:, :128] + s[128:, 128:],
         ):
-            store[place : place + 128] = (value * level_scale).astype(BF)
-            place += 128
-    if place < 2 * half:
-        store[place:] = jnp.zeros((2 * half - place, 128), BF)
-    keep_ref[...] = store[pl.ds(pl.multiple_of(core * half, 16), half), :]
-    send_ref[...] = store[pl.ds(pl.multiple_of((1 - core) * half, 16), half), :]
-
-
-def add_cores(count, keep_ref, got_ref, pieces_ref, own_ref, *outs):
+            put((value * level_scale).astype(BF))
+    if place < sums_ref.shape[0]:
+        put(jnp.zeros((sums_ref.shape[0] - place, 128), BF))
+
+
+def pack_neck(count, half_rows, width, out_ref, pieces_ref):
     me = lax.axis_index("gx")
+    cells, total = out_ref.shape
+    half_cols, per = cells // half_rows, 128 // width
+    for turn in range(count):
+        for low in range(0, half_rows, per):
+            piece = jnp.zeros((half_cols, 128), F32)
+            for r in range(low, min(half_rows, low + per)):
+                pick = lanes_to_channels(r, me ^ turn, width, total)
+                piece = piece + dot(out_ref[half_cols * r : half_cols * r + half_cols], pick, ((1,), (1,)))
+            group = low // per
+            pieces_ref[turn, half_cols * group : half_cols * group + half_cols] = piece.astype(BF)
+
+
+def add_cores(count, sums_ref, got_ref, pieces_ref, own_ref, *outs):
+    me, core = lax.axis_index("gx"), lax.axis_index("gy") & 1
     part = own_ref.shape[0]
     for turn in range(count):
-        here = pl.ds(pl.multiple_of((me ^ turn) * part, 16), part)
-        value = keep_ref[here, :].astype(F32) + got_ref[here, :].astype(F32)
+        mine = pl.ds(pl.multiple_of((core * count + (me ^ turn)) * part, 16), part)
+        theirs = pl.ds(pl.multiple_of((me ^ turn) * part, 16), part)
+        value = sums_ref[mine, :].astype(F32) + got_ref[theirs, :].astype(F32)
         if turn == 0:
             own_ref[...] = value
         else:
@@ -483,13 +502,13 @@
     unit = -(-part // (z_count * 16)) * 16
     tiles = groups_of(half_rows, width) * half_cols
     sizes = (
-        rows, half_rows, half_cols, width, count,
+        rows, half_rows, half_cols,
         1.0 / math.sqrt(pixels), 1.0 / math.sqrt(pixels // 4),
     )
     far = rows + 2 * HALO
-    keep, send, pieces, grad_input = call(
+    sums, send, out, grad_input = call(
         functools.partial(main, sizes),
-        [shape((half, 128)), shape((half, 128)), shape((count, tiles, 128)), shape(level_in.shape)],
+        [shape((2 * half, 128)), shape((half, 128)), shape((half_rows * half_cols, total)), shape(level_in.shape)],
         (kept, cross, inner, wfwd, wbwd, wd, wdt, wn, wnt),
         [
             pltpu.VMEM((far, 2 * pitch, 128), F32),
@@ -505,16 +524,18 @@
             pltpu.VMEM((rows + 4, pitch, 256), BF),
             pltpu.VMEM((rows + 4, pitch, 256), BF),
             pltpu.VMEM((rows, cols, 128), F32),
-            pltpu.VMEM((2 * half, 128), BF),
         ],
         limit=20,
         flops=6 * 10**9,
     )
 
+    pieces = call(
+        functools.partial(pack_neck, count, half_rows, width), shape((count, tiles, 128)), (out,)
+    )
     own, *sent = call(
         functools.partial(add_cores, count),
         [shape((part, 128), F32)] + [shape((part + tiles, 128))] * (count - 1),
-        (keep, by_core(send), pieces),
+        (sums, by_core(send), pieces),
     )
     got = [by_col(value, turn + 1) for turn, value in enumerate(sent)]
     own, *sent = call(

time: 70.9 us -> 69.6 us (0.982)
  Pallas kernels: 9.11 us -> 8.17 us
    pallas_call x10 -> x11, Pallas kernels: 9.11 us -> 8.17 us  [call(): pl.pallas_call(body, out_shape=out_shapes, in_specs=[VMEM] * len(args), o...]
  transfers between devices with their start and end apart: 22 -> 22, of which waited for: 16 -> 15; matrix products, arithmetic and copies ran while one was open for 0% -> 0% of each run, Pallas kernels for 2% -> 3%
where the time goes in v3:
time: 69.6 us; the launch traced here: 69.4 us
  waiting for transfers between devices  31.8 us (46%)
  starting transfers between devices  27 us (39%)
  Pallas kernels  8.17 us (12%)
  local copies, waits for them, and re-layouts  1.75 us (3%)
  between operations  0.72 us (1%)
    ppermute x22, waiting for transfers between devices, permute(): lax.ppermute(value, axes, [(a, b) for a, b in pairs if b is not None])  31.8 us
    ppermute x22, starting transfers between devices, permute(): lax.ppermute(value, axes, [(a, b) for a, b in pairs if b is not None])  27 us
    pallas_call x11, Pallas kernels, call(): pl.pallas_call(body, out_shape=out_shapes, in_specs=[VMEM] * len(args), o...  8.17 us
    unnamed x10, local copies, waits for them, and re-layouts  1.75 us
  transfers between devices with their start and end apart: 22, of which 15 were waited for; matrix products, arithmetic and copies ran while one was open for 0% of the time, Pallas kernels for 3%

profile of v3, /device:TPU:0, one launch (start us, length us, event | category | flops | bytes accessed | tf_op | source)
XLA Modules:
  0.0 69.4 jit_solution(11514332520853201284)
XLA Ops:
  0.6 0.9 %copy-done.3 = bf16[8,64,128]{2,1,0:T(8,128)(2,1)S(1)} copy-done((bf16[8,64,128]{2,1,0:T(8,128)(2,1)S(1)}, bf16[8,64,128]{2,1,0:T(8,128)(2,1)}, u32[]{:S(2)}) %copy-start.3) | copy-done | bytes 131096
  1.5 0.8 %copy-done.4 = bf16[4,128,64]{1,2,0:T(8,128)(2,1)S(1)} copy-done((bf16[4,128,64]{1,2,0:T(8,128)(2,1)S(1)}, bf16[4,128,64]{1,2,0:T(8,128)(2,1)}, u32[]{:S(2)}) %copy-start.4) | copy-done | bytes 65560
  2.6 3.0 %collective-permute-start = (bf16[160,128]{1,0:T(8,128)(2,1)S(1)}, bf16[160,128]{1,0:T(8,128)(2,1)S(1)}, u32[]{:S(2)}, u32[]{:S(2)}) collective-permute-start(bf16[160,128]{1,0:T(8,128)(2,1)S(1)} %get-tuple-element.30), channel_id=1, source_target_pairs={{0,1},{1,0},{2,3},{3,2},{4,5},{5,4},{6,7},{7,6},{8,9},{9,8},{10,11... | collective-permute-start | bytes 122888 | tf_op jit(solution)/shard_map/ppermute | solution.py:457
  5.6 1.5 %collective-permute-start.1 = (bf16[160,128]{1,0:T(8,128)(2,1)S(1)}, bf16[160,128]{1,0:T(8,128)(2,1)S(1)}, u32[]{:S(2)}, u32[]{:S(2)}) collective-permute-start(bf16[160,128]{1,0:T(8,128)(2,1)S(1)} %get-tuple-element.31), channel_id=1, source_target_pairs={{0,2},{1,3},{2,0},{3,1},{4,6},{5,7},{6,4},{7,5},{8,10},{9,11},{10,... | collective-permute-start | bytes 122888 | tf_op jit(solution)/shard_map/ppermute | solution.py:457
  7.6 2.0 %collective-permute-done.1.refs_1_ = bf16[160,128]{1,0:T(8,128)(2,1)S(1)} collective-permute-done((bf16[160,128]{1,0:T(8,128)(2,1)S(1)}, bf16[160,128]{1,0:T(8,128)(2,1)S(1)}, u32[]{:S(2)}, u32[]{:S(2)}) %collective-permute-start.1) | collective-permute-done | bytes 40992 | tf_op jit(solution)/shard_map/ppermute | solution.py:457
  9.6 2.4 %collective-permute-done.2.refs_2_ = bf16[160,128]{1,0:T(8,128)(2,1)S(1)} collective-permute-done((bf16[160,128]{1,0:T(8,128)(2,1)S(1)}, bf16[160,128]{1,0:T(8,128)(2,1)S(1)}, u32[]{:S(2)}, u32[]{:S(2)}) %collective-permute-start.2) | collective-permute-done | bytes 40992 | tf_op jit(solution)/shard_map/ppermute | solution.py:457
  12.5 0.7 collective-permute-start.3
  13.2 3.0 %collective-permute-start.4 = (bf16[752,128]{1,0:T(8,128)(2,1)S(1)}, bf16[752,128]{1,0:T(8,128)(2,1)S(1)}, u32[]{:S(2)}, u32[]{:S(2)}) collective-permute-start(bf16[752,128]{1,0:T(8,128)(2,1)S(1)} %get-tuple-element.35), channel_id=1, source_target_pairs={{0,4},{1,5},{2,6},{3,7},{4,0},{5,1},{6,2},{7,3},{8,12},{9,13},{10,... | collective-permute-start | bytes 577544 | tf_op jit(solution)/shard_map/ppermute | solution.py:457
  16.2 0.6 shard_map.94
  17.2 3.8 %shard_map.95 = (bf16[6784,128]{1,0:T(8,128)(2,1)S(1)}, bf16[3392,128]{1,0:T(8,128)(2,1)S(1)}, bf16[128,256]{1,0:T(8,128)(2,1)S(1)}, bf16[8,64,128]{2,1,0:T(8,128)(2,1)}) custom-call(bf16[1152,128]{1,0:T(8,128)(2,1)S(1)} %get-tuple-element.33.kept_ref, bf16[752,128]{1,0:T(8,128)(2,1)S(1)} %collective-permute-done.3.cross_ref, ...), custom_call_target="tpu_custom_call" | custom-call | flops 6000000000 | tf_op jit(solution)/shard_map/pallas_call | solution.py:18
  21.0 2.1 %collective-permute-start.5 = (bf16[3392,128]{1,0:T(8,128)(2,1)S(1)}, bf16[3392,128]{1,0:T(8,128)(2,1)S(1)}, u32[]{:S(2)}, u32[]{:S(2)}) collective-permute-start(bf16[3392,128]{1,0:T(8,128)(2,1)S(1)} %get-tuple-element.42), channel_id=1, source_target_pairs={{0,4},{1,5},{2,6},{3,7},{4,0},{5,1},{6,2},{7,3},{8,12},{9,13},{10,... | collective-permute-start | bytes 2605064 | tf_op jit(solution)/shard_map/ppermute | solution.py:457
  23.5 1.7 %collective-permute-done.5.got_ref = bf16[3392,128]{1,0:T(8,128)(2,1)S(1)} collective-permute-done((bf16[3392,128]{1,0:T(8,128)(2,1)S(1)}, bf16[3392,128]{1,0:T(8,128)(2,1)S(1)}, u32[]{:S(2)}, u32[]{:S(2)}) %collective-permute-start.5) | collective-permute-done | bytes 868384 | tf_op jit(solution)/shard_map/ppermute | solution.py:457
  25.4 0.6 collective-permute-start.6
  26.0 0.5 collective-permute-start.7
  26.5 2.4 %collective-permute-start.8 = (bf16[912,128]{1,0:T(8,128)(2,1)S(1)}, bf16[912,128]{1,0:T(8,128)(2,1)S(1)}, u32[]{:S(2)}, u32[]{:S(2)}) collective-permute-start(bf16[912,128]{1,0:T(8,128)(2,1)S(1)} %get-tuple-element.45), channel_id=1, source_target_pairs={{0,3},{1,2},{2,1},{3,0},{4,7},{5,6},{6,5},{7,4},{8,11},{9,10},{10,... | collective-permute-start | bytes 700424 | tf_op jit(solution)/shard_map/ppermute | solution.py:457
  29.0 5.0 %collective-permute-done.6.refs_0_ = bf16[912,128]{1,0:T(8,128)(2,1)S(1)} collective-permute-done((bf16[912,128]{1,0:T(8,128)(2,1)S(1)}, bf16[912,128]{1,0:T(8,128)(2,1)S(1)}, u32[]{:S(2)}, u32[]{:S(2)}) %collective-permute-start.6) | collective-permute-done | bytes 233504 | tf_op jit(solution)/shard_map/ppermute | solution.py:457
  34.0 4.7 %collective-permute-done.7.refs_1_ = bf16[912,128]{1,0:T(8,128)(2,1)S(1)} collective-permute-done((bf16[912,128]{1,0:T(8,128)(2,1)S(1)}, bf16[912,128]{1,0:T(8,128)(2,1)S(1)}, u32[]{:S(2)}, u32[]{:S(2)}) %collective-permute-start.7) | collective-permute-done | bytes 233504 | tf_op jit(solution)/shard_map/ppermute | solution.py:457
  38.9 1.9 %collective-permute-start.9 = (bf16[224,128]{1,0:T(8,128)(2,1)S(1)}, bf16[224,128]{1,0:T(8,128)(2,1)S(1)}, u32[]{:S(2)}, u32[]{:S(2)}) collective-permute-start(bf16[224,128]{1,0:T(8,128)(2,1)S(1)} %get-tuple-element.49), channel_id=1, source_target_pairs={{0,8},{1,9},{2,10},{3,11},{4,12},{5,13},{6,14},{7,15},{8,0},{9,1},... | collective-permute-start | bytes 172040 | tf_op jit(solution)/shard_map/ppermute | solution.py:457
  40.8 2.6 %collective-permute-start.10 = (bf16[224,128]{1,0:T(8,128)(2,1)S(1)}, bf16[224,128]{1,0:T(8,128)(2,1)S(1)}, u32[]{:S(2)}, u32[]{:S(2)}) collective-permute-start(bf16[224,128]{1,0:T(8,128)(2,1)S(1)} %get-tuple-element.50), channel_id=1, source_target_pairs={{0,16},{1,17},{2,18},{3,19},{4,20},{5,21},{6,22},{7,23},{8,24},{9,... | collective-permute-start | bytes 172040 | tf_op jit(solution)/shard_map/ppermute | solution.py:457
  43.4 3.7 %collective-permute-done.10.refs_1_ = bf16[224,128]{1,0:T(8,128)(2,1)S(1)} collective-permute-done((bf16[224,128]{1,0:T(8,128)(2,1)S(1)}, bf16[224,128]{1,0:T(8,128)(2,1)S(1)}, u32[]{:S(2)}, u32[]{:S(2)}) %collective-permute-start.10) | collective-permute-done | bytes 57376 | tf_op jit(solution)/shard_map/ppermute | solution.py:457
  47.1 2.3 %collective-permute-done.11.refs_2_ = bf16[224,128]{1,0:T(8,128)(2,1)S(1)} collective-permute-done((bf16[224,128]{1,0:T(8,128)(2,1)S(1)}, bf16[224,128]{1,0:T(8,128)(2,1)S(1)}, u32[]{:S(2)}, u32[]{:S(2)}) %collective-permute-start.11) | collective-permute-done | bytes 57376 | tf_op jit(solution)/shard_map/ppermute | solution.py:457
  49.4 0.8 %collective-permute-start.14 = (bf16[224,128]{1,0:T(8,128)(2,1)S(1)}, bf16[224,128]{1,0:T(8,128)(2,1)S(1)}, u32[]{:S(2)}, u32[]{:S(2)}) collective-permute-start(bf16[224,128]{1,0:T(8,128)(2,1)S(1)} %shard_map.100.refs_0_), channel_id=1, source_target_pairs={{0,24},{1,25},{2,26},{3,27},{4,28},{5,29},{6,30},{7,31},{8,16},{9,... | collective-permute-start | bytes 172040 | tf_op jit(solution)/shard_map/ppermute | solution.py:457
  50.2 3.7 %collective-permute-start.12 = (bf16[224,128]{1,0:T(8,128)(2,1)S(1)}, bf16[224,128]{1,0:T(8,128)(2,1)S(1)}, u32[]{:S(2)}, u32[]{:S(2)}) collective-permute-start(bf16[224,128]{1,0:T(8,128)(2,1)S(1)} %shard_map.100.refs_0_), channel_id=1, source_target_pairs={{0,8},{1,9},{2,10},{3,11},{4,12},{5,13},{6,14},{7,15},{8,0},{9,1},... | collective-permute-start | bytes 172040 | tf_op jit(solution)/shard_map/ppermute | solution.py:457
  53.8 1.7 %collective-permute-done.14.refs_3_ = bf16[224,128]{1,0:T(8,128)(2,1)S(1)} collective-permute-done((bf16[224,128]{1,0:T(8,128)(2,1)S(1)}, bf16[224,128]{1,0:T(8,128)(2,1)S(1)}, u32[]{:S(2)}, u32[]{:S(2)}) %collective-permute-start.14) | collective-permute-done | bytes 57376 | tf_op jit(solution)/shard_map/ppermute | solution.py:457
  55.5 0.9 %collective-permute-done.13.refs_2_ = bf16[224,128]{1,0:T(8,128)(2,1)S(1)} collective-permute-done((bf16[224,128]{1,0:T(8,128)(2,1)S(1)}, bf16[224,128]{1,0:T(8,128)(2,1)S(1)}, u32[]{:S(2)}, u32[]{:S(2)}) %collective-permute-start.13) | collective-permute-done | bytes 57376 | tf_op jit(solution)/shard_map/ppermute | solution.py:457
  56.5 1.5 %collective-permute-start.17 = (bf16[848,128]{1,0:T(8,128)(2,1)S(1)}, bf16[848,128]{1,0:T(8,128)(2,1)S(1)}, u32[]{:S(2)}, u32[]{:S(2)}) collective-permute-start(bf16[848,128]{1,0:T(8,128)(2,1)S(1)} %shard_map.101.refs_0_), channel_id=1, source_target_pairs={{0,3},{1,2},{2,1},{3,0},{4,7},{5,6},{6,5},{7,4},{8,11},{9,10},{10,... | collective-permute-start | bytes 651272 | tf_op jit(solution)/shard_map/ppermute | solution.py:457
  58.0 1.5 %collective-permute-start.16 = (bf16[848,128]{1,0:T(8,128)(2,1)S(1)}, bf16[848,128]{1,0:T(8,128)(2,1)S(1)}, u32[]{:S(2)}, u32[]{:S(2)}) collective-permute-start(bf16[848,128]{1,0:T(8,128)(2,1)S(1)} %shard_map.101.refs_0_), channel_id=1, source_target_pairs={{0,2},{1,3},{2,0},{3,1},{4,6},{5,7},{6,4},{7,5},{8,10},{9,11},{10,... | collective-permute-start | bytes 651272 | tf_op jit(solution)/shard_map/ppermute | solution.py:457
  59.6 0.5 collective-permute-start.15
  60.1 3.9 %collective-permute-done.17.refs_3_ = bf16[848,128]{1,0:T(8,128)(2,1)S(1)} collective-permute-done((bf16[848,128]{1,0:T(8,128)(2,1)S(1)}, bf16[848,128]{1,0:T(8,128)(2,1)S(1)}, u32[]{:S(2)}, u32[]{:S(2)}) %collective-permute-start.17) | collective-permute-done | bytes 217120 | tf_op jit(solution)/shard_map/ppermute | solution.py:457
  64.0 2.2 %collective-permute-done.16.refs_2_ = bf16[848,128]{1,0:T(8,128)(2,1)S(1)} collective-permute-done((bf16[848,128]{1,0:T(8,128)(2,1)S(1)}, bf16[848,128]{1,0:T(8,128)(2,1)S(1)}, u32[]{:S(2)}, u32[]{:S(2)}) %collective-permute-start.16) | collective-permute-done | bytes 217120 | tf_op jit(solution)/shard_map/ppermute | solution.py:457
  66.7 0.9 %shard_map.98 = bf16[4,64,128]{2,1,0:T(8,128)(2,1)} custom-call(bf16[4,64,128]{2,1,0:T(8,128)(2,1)S(1)} %shard_map.96.pieces_ref, bf16[912,128]{1,0:T(8,128)(2,1)S(1)} %collective-permute-done.6.refs_0_, bf16[912,128]{1,0:T(8,128)(2,1)S(1)} %collective-permute-done.7.refs_1_, bf16[912,128]{1,0:T(8,128)(2,1)S(1)} %collective-permute-done.8.refs_2_), custom_call_target="tpu_custom_call" | custom-call | flops 1000000000 | tf_op jit(solution)/shard_map/pallas_call | solution.py:18
  67.9 1.5 %shard_map.102 = (bf16[9,128,128]{2,1,0:T(8,128)(2,1)}, bf16[4,128,256]{2,1,0:T(8,128)(2,1)}, bf16[9,256,256]{2,1,0:T(8,128)(2,1)}) custom-call(bf16[848,128]{1,0:T(8,128)(2,1)S(1)} %shard_map.101.refs_0_, bf16[848,128]{1,0:T(8,128)(2,1)S(1)} %collective-permute-done.15.refs_1_, bf16[848,128]{1,0:T(8,128)(2,1)S(1)} %collective-permute-done.16.refs_2_, ...), custom_call_target="tpu_custom_call" | custom-call | flops 1000000000 | tf_op jit(solution)/shard_map/pallas_call | solution.py:18
  (33 shorter events, 3.3 us)
Async XLA Ops:
  0.6 0.9 %copy-start.3 = (bf16[8,64,128]{2,1,0:T(8,128)(2,1)S(1)}, bf16[8,64,128]{2,1,0:T(8,128)(2,1)}, u32[]{:S(2)}) copy-start(bf16[8,64,128]{2,1,0:T(8,128)(2,1)} %level_ref.3) | copy-start | bytes 393220
  1.5 0.8 %copy-start.4 = (bf16[4,128,64]{1,2,0:T(8,128)(2,1)S(1)}, bf16[4,128,64]{1,2,0:T(8,128)(2,1)}, u32[]{:S(2)}) copy-start(bf16[4,128,64]{1,2,0:T(8,128)(2,1)} %param.9) | copy-start | bytes 196612
  2.6 5.0 %collective-permute-start = (bf16[160,128]{1,0:T(8,128)(2,1)S(1)}, bf16[160,128]{1,0:T(8,128)(2,1)S(1)}, u32[]{:S(2)}, u32[]{:S(2)}) collective-permute-start(bf16[160,128]{1,0:T(8,128)(2,1)S(1)} %get-tuple-element.30), channel_id=1, source_target_pairs={{0,1},{1,0},{2,3},{3,2},{4,5},{5,4},{6,7},{7,6},{8,9},{9,8},{10,11... | collective-permute-start | bytes 122888 | tf_op jit(solution)/shard_map/ppermute | solution.py:457
  5.6 4.0 %collective-permute-start.1 = (bf16[160,128]{1,0:T(8,128)(2,1)S(1)}, bf16[160,128]{1,0:T(8,128)(2,1)S(1)}, u32[]{:S(2)}, u32[]{:S(2)}) collective-permute-start(bf16[160,128]{1,0:T(8,128)(2,1)S(1)} %get-tuple-element.31), channel_id=1, source_target_pairs={{0,2},{1,3},{2,0},{3,1},{4,6},{5,7},{6,4},{7,5},{8,10},{9,11},{10,... | collective-permute-start | bytes 122888 | tf_op jit(solution)/shard_map/ppermute | solution.py:457
  7.1 9.0 %copy-start = (bf16[3,3,256,256]{3,2,1,0:T(8,128)(2,1)S(1)}, bf16[3,3,256,256]{3,2,1,0:T(8,128)(2,1)}, u32[]{:S(2)}) copy-start(bf16[3,3,256,256]{3,2,1,0:T(8,128)(2,1)} %param.8) | copy-start | bytes 3538948
  7.1 9.0 %copy-start.1 = (bf16[3,3,128,128]{3,2,1,0:T(8,128)(2,1)S(1)}, bf16[3,3,128,128]{3,2,1,0:T(8,128)(2,1)}, u32[]{:S(2)}) copy-start(bf16[3,3,128,128]{3,2,1,0:T(8,128)(2,1)} %param.6) | copy-start | bytes 884740
  7.2 9.0 %copy-start.2 = (bf16[2,2,128,256]{3,2,1,0:T(8,128)(2,1)S(1)}, bf16[2,2,128,256]{3,2,1,0:T(8,128)(2,1)}, u32[]{:S(2)}) copy-start(bf16[2,2,128,256]{3,2,1,0:T(8,128)(2,1)} %param.7) | copy-start | bytes 786436
  7.2 4.9 %collective-permute-start.2 = (bf16[160,128]{1,0:T(8,128)(2,1)S(1)}, bf16[160,128]{1,0:T(8,128)(2,1)S(1)}, u32[]{:S(2)}, u32[]{:S(2)}) collective-permute-start(bf16[160,128]{1,0:T(8,128)(2,1)S(1)} %get-tuple-element.32), channel_id=1, source_target_pairs={{0,3},{1,2},{2,1},{3,0},{4,7},{5,6},{6,5},{7,4},{8,11},{9,10},{10,... | collective-permute-start | bytes 122888 | tf_op jit(solution)/shard_map/ppermute | solution.py:457
  12.5 4.3 %collective-permute-start.3 = (bf16[752,128]{1,0:T(8,128)(2,1)S(1)}, bf16[752,128]{1,0:T(8,128)(2,1)S(1)}, u32[]{:S(2)}, u32[]{:S(2)}) collective-permute-start(bf16[752,128]{1,0:T(8,128)(2,1)S(1)} %get-tuple-element.34), channel_id=1, source_target_pairs={{4,8},{5,9},{6,10},{7,11},{8,4},{9,5},{10,6},{11,7},{12,16},{13,17... | collective-permute-start | bytes 577544 | tf_op jit(solution)/shard_map/ppermute | solution.py:457
  13.2 4.1 %collective-permute-start.4 = (bf16[752,128]{1,0:T(8,128)(2,1)S(1)}, bf16[752,128]{1,0:T(8,128)(2,1)S(1)}, u32[]{:S(2)}, u32[]{:S(2)}) collective-permute-start(bf16[752,128]{1,0:T(8,128)(2,1)S(1)} %get-tuple-element.35), channel_id=1, source_target_pairs={{0,4},{1,5},{2,6},{3,7},{4,0},{5,1},{6,2},{7,3},{8,12},{9,13},{10,... | collective-permute-start | bytes 577544 | tf_op jit(solution)/shard_map/ppermute | solution.py:457
  21.0 4.2 %collective-permute-start.5 = (bf16[3392,128]{1,0:T(8,128)(2,1)S(1)}, bf16[3392,128]{1,0:T(8,128)(2,1)S(1)}, u32[]{:S(2)}, u32[]{:S(2)}) collective-permute-start(bf16[3392,128]{1,0:T(8,128)(2,1)S(1)} %get-tuple-element.42), channel_id=1, source_target_pairs={{0,4},{1,5},{2,6},{3,7},{4,0},{5,1},{6,2},{7,3},{8,12},{9,13},{10,... | collective-permute-start | bytes 2605064 | tf_op jit(solution)/shard_map/ppermute | solution.py:457
  25.4 8.6 %collective-permute-start.6 = (bf16[912,128]{1,0:T(8,128)(2,1)S(1)}, bf16[912,128]{1,0:T(8,128)(2,1)S(1)}, u32[]{:S(2)}, u32[]{:S(2)}) collective-permute-start(bf16[912,128]{1,0:T(8,128)(2,1)S(1)} %get-tuple-element.43), channel_id=1, source_target_pairs={{0,1},{1,0},{2,3},{3,2},{4,5},{5,4},{6,7},{7,6},{8,9},{9,8},{10,11... | collective-permute-start | bytes 700424 | tf_op jit(solution)/shard_map/ppermute | solution.py:457
  26.0 12.7 %collective-permute-start.7 = (bf16[912,128]{1,0:T(8,128)(2,1)S(1)}, bf16[912,128]{1,0:T(8,128)(2,1)S(1)}, u32[]{:S(2)}, u32[]{:S(2)}) collective-permute-start(bf16[912,128]{1,0:T(8,128)(2,1)S(1)} %get-tuple-element.44), channel_id=1, source_target_pairs={{0,2},{1,3},{2,0},{3,1},{4,6},{5,7},{6,4},{7,5},{8,10},{9,11},{10,... | collective-permute-start | bytes 700424 | tf_op jit(solution)/shard_map/ppermute | solution.py:457
  26.5 12.2 %collective-permute-start.8 = (bf16[912,128]{1,0:T(8,128)(2,1)S(1)}, bf16[912,128]{1,0:T(8,128)(2,1)S(1)}, u32[]{:S(2)}, u32[]{:S(2)}) collective-permute-start(bf16[912,128]{1,0:T(8,128)(2,1)S(1)} %get-tuple-element.45), channel_id=1, source_target_pairs={{0,3},{1,2},{2,1},{3,0},{4,7},{5,6},{6,5},{7,4},{8,11},{9,10},{10,... | collective-permute-start | bytes 700424 | tf_op jit(solution)/shard_map/ppermute | solution.py:457
  38.9 4.5 %collective-permute-start.9 = (bf16[224,128]{1,0:T(8,128)(2,1)S(1)}, bf16[224,128]{1,0:T(8,128)(2,1)S(1)}, u32[]{:S(2)}, u32[]{:S(2)}) collective-permute-start(bf16[224,128]{1,0:T(8,128)(2,1)S(1)} %get-tuple-element.49), channel_id=1, source_target_pairs={{0,8},{1,9},{2,10},{3,11},{4,12},{5,13},{6,14},{7,15},{8,0},{9,1},... | collective-permute-start | bytes 172040 | tf_op jit(solution)/shard_map/ppermute | solution.py:457
  40.8 6.3 %collective-permute-start.10 = (bf16[224,128]{1,0:T(8,128)(2,1)S(1)}, bf16[224,128]{1,0:T(8,128)(2,1)S(1)}, u32[]{:S(2)}, u32[]{:S(2)}) collective-permute-start(bf16[224,128]{1,0:T(8,128)(2,1)S(1)} %get-tuple-element.50), channel_id=1, source_target_pairs={{0,16},{1,17},{2,18},{3,19},{4,20},{5,21},{6,22},{7,23},{8,24},{9,... | collective-permute-start | bytes 172040 | tf_op jit(solution)/shard_map/ppermute | solution.py:457
  43.4 6.0 %collective-permute-start.11 = (bf16[224,128]{1,0:T(8,128)(2,1)S(1)}, bf16[224,128]{1,0:T(8,128)(2,1)S(1)}, u32[]{:S(2)}, u32[]{:S(2)}) collective-permute-start(bf16[224,128]{1,0:T(8,128)(2,1)S(1)} %get-tuple-element.51), channel_id=1, source_target_pairs={{0,24},{1,25},{2,26},{3,27},{4,28},{5,29},{6,30},{7,31},{8,16},{9,... | collective-permute-start | bytes 172040 | tf_op jit(solution)/shard_map/ppermute | solution.py:457
  49.4 6.2 %collective-permute-start.14 = (bf16[224,128]{1,0:T(8,128)(2,1)S(1)}, bf16[224,128]{1,0:T(8,128)(2,1)S(1)}, u32[]{:S(2)}, u32[]{:S(2)}) collective-permute-start(bf16[224,128]{1,0:T(8,128)(2,1)S(1)} %shard_map.100.refs_0_), channel_id=1, source_target_pairs={{0,24},{1,25},{2,26},{3,27},{4,28},{5,29},{6,30},{7,31},{8,16},{9,... | collective-permute-start | bytes 172040 | tf_op jit(solution)/shard_map/ppermute | solution.py:457
  50.2 6.3 %collective-permute-start.13 = (bf16[224,128]{1,0:T(8,128)(2,1)S(1)}, bf16[224,128]{1,0:T(8,128)(2,1)S(1)}, u32[]{:S(2)}, u32[]{:S(2)}) collective-permute-start(bf16[224,128]{1,0:T(8,128)(2,1)S(1)} %shard_map.100.refs_0_), channel_id=1, source_target_pairs={{0,16},{1,17},{2,18},{3,19},{4,20},{5,21},{6,22},{7,23},{8,24},{9,... | collective-permute-start | bytes 172040 | tf_op jit(solution)/shard_map/ppermute | solution.py:457
  50.2 6.3 %collective-permute-start.12 = (bf16[224,128]{1,0:T(8,128)(2,1)S(1)}, bf16[224,128]{1,0:T(8,128)(2,1)S(1)}, u32[]{:S(2)}, u32[]{:S(2)}) collective-permute-start(bf16[224,128]{1,0:T(8,128)(2,1)S(1)} %shard_map.100.refs_0_), channel_id=1, source_target_pairs={{0,8},{1,9},{2,10},{3,11},{4,12},{5,13},{6,14},{7,15},{8,0},{9,1},... | collective-permute-start | bytes 172040 | tf_op jit(solution)/shard_map/ppermute | solution.py:457
  56.5 7.5 %collective-permute-start.17 = (bf16[848,128]{1,0:T(8,128)(2,1)S(1)}, bf16[848,128]{1,0:T(8,128)(2,1)S(1)}, u32[]{:S(2)}, u32[]{:S(2)}) collective-permute-start(bf16[848,128]{1,0:T(8,128)(2,1)S(1)} %shard_map.101.refs_0_), channel_id=1, source_target_pairs={{0,3},{1,2},{2,1},{3,0},{4,7},{5,6},{6,5},{7,4},{8,11},{9,10},{10,... | collective-permute-start | bytes 651272 | tf_op jit(solution)/shard_map/ppermute | solution.py:457
  58.0 8.1 %collective-permute-start.16 = (bf16[848,128]{1,0:T(8,128)(2,1)S(1)}, bf16[848,128]{1,0:T(8,128)(2,1)S(1)}, u32[]{:S(2)}, u32[]{:S(2)}) collective-permute-start(bf16[848,128]{1,0:T(8,128)(2,1)S(1)} %shard_map.101.refs_0_), channel_id=1, source_target_pairs={{0,2},{1,3},{2,0},{3,1},{4,6},{5,7},{6,4},{7,5},{8,10},{9,11},{10,... | collective-permute-start | bytes 651272 | tf_op jit(solution)/shard_map/ppermute | solution.py:457
  59.6 6.6 %collective-permute-start.15 = (bf16[848,128]{1,0:T(8,128)(2,1)S(1)}, bf16[848,128]{1,0:T(8,128)(2,1)S(1)}, u32[]{:S(2)}, u32[]{:S(2)}) collective-permute-start(bf16[848,128]{1,0:T(8,128)(2,1)S(1)} %shard_map.101.refs_0_), channel_id=1, source_target_pairs={{0,1},{1,0},{2,3},{3,2},{4,5},{5,4},{6,7},{7,6},{8,9},{9,8},{10,11... | collective-permute-start | bytes 651272 | tf_op jit(solution)/shard_map/ppermute | solution.py:457
  60.1 7.5 %collective-permute-start.18 = (bf16[848,128]{1,0:T(8,128)(2,1)S(1)}, bf16[848,128]{1,0:T(8,128)(2,1)S(1)}, u32[]{:S(2)}, u32[]{:S(2)}) collective-permute-start(bf16[848,128]{1,0:T(8,128)(2,1)S(1)} %shard_map.101.refs_0_), channel_id=1, source_target_pairs={{0,4},{1,5},{2,6},{3,7},{4,0},{5,1},{6,2},{7,3},{8,12},{9,13},{10,... | collective-permute-start | bytes 651272 | tf_op jit(solution)/shard_map/ppermute | solution.py:457
  64.0 3.6 %collective-permute-start.21 = (bf16[848,128]{1,0:T(8,128)(2,1)S(1)}, bf16[848,128]{1,0:T(8,128)(2,1)S(1)}, u32[]{:S(2)}, u32[]{:S(2)}) collective-permute-start(bf16[848,128]{1,0:T(8,128)(2,1)S(1)} %collective-permute-done.17.refs_3_), channel_id=1, source_target_pairs={{0,4},{1,5},{2,6},{3,7},{4,0},{5,1},{6,2},{7,3},{8,12},{9,13},{10,... | collective-permute-start | bytes 651272 | tf_op jit(solution)/shard_map/ppermute | solution.py:457
  66.2 1.5 %collective-permute-start.20 = (bf16[848,128]{1,0:T(8,128)(2,1)S(1)}, bf16[848,128]{1,0:T(8,128)(2,1)S(1)}, u32[]{:S(2)}, u32[]{:S(2)}) collective-permute-start(bf16[848,128]{1,0:T(8,128)(2,1)S(1)} %collective-permute-done.16.refs_2_), channel_id=1, source_target_pairs={{0,4},{1,5},{2,6},{3,7},{4,0},{5,1},{6,2},{7,3},{8,12},{9,13},{10,... | collective-permute-start | bytes 651272 | tf_op jit(solution)/shard_map/ppermute | solution.py:457
  66.2 1.8 %collective-permute-start.19 = (bf16[848,128]{1,0:T(8,128)(2,1)S(1)}, bf16[848,128]{1,0:T(8,128)(2,1)S(1)}, u32[]{:S(2)}, u32[]{:S(2)}) collective-permute-start(bf16[848,128]{1,0:T(8,128)(2,1)S(1)} %collective-permute-done.15.refs_1_), channel_id=1, source_target_pairs={{0,4},{1,5},{2,6},{3,7},{4,0},{5,1},{6,2},{7,3},{8,12},{9,13},{10,... | collective-permute-start | bytes 651272 | tf_op jit(solution)/shard_map/ppermute | solution.py:457

commit v4 on v3

--- a/solution.py
+++ b/solution.py
@@ -74,7 +74,11 @@
     return jnp.concatenate(parts, axis=0).astype(BF)
 
 
-def pack_cols(count, half_cols, level_ref, cot_ref, *outs):
+def begin(out_ref):
+    out_ref[...] = jnp.zeros(out_ref.shape, BF)
+
+
+def pack_cols(count, half_cols, level_ref, cot_ref, begin_ref, *outs):
     me = lax.axis_index("gx")
     strip = strip_rows(cot_ref)
     level = level_ref[...].astype(F32)
@@ -111,12 +115,16 @@
     wide = jnp.concatenate([level, edges], axis=1).reshape(2 * rows * pitch, 128)
     kept_ref[0 : 2 * rows * pitch] = wide
     cot = []
+    picks = {}
     for row in range(half_rows):
         low = row * width // 128 * pitch
         value = jnp.zeros((pitch, total), F32)
         for turn in range(count):
             part = mine[low : low + pitch] if turn == 0 else got[turn - 1][low : low + pitch]
-            value = value + dot(part, lanes_to_channels(row, me ^ turn, width, total))
+            key = (row * width % 128, turn)
+            if key not in picks:
+                picks[key] = lanes_to_channels(row, me ^ turn, width, total)
+            value = value + dot(part, picks[key])
         value = value.astype(BF)
         cot.append(value)
         low = 2 * (rows + row) * pitch
@@ -237,7 +245,7 @@
         taken = [
             flat(ref[low + ky : low + ky + step]) for ky in range(3) for ref in (pair, side)
         ]
-        pre = dot(jnp.concatenate(taken, axis=1), wfwd[...])
+        pre = dot_rows(jnp.concatenate(taken, axis=1), wfwd[...], step * pitch // 3)
         sig, slp = sigmoid_slope(pre)
         own = flat(pair[low + 1 : low + 1 + step]).astype(F32)
         act[low : low + step] = (own + pre * sig).astype(BF).reshape(step, pitch, 256)
@@ -475,8 +483,9 @@
     strip = jnp.swapaxes(cotangent, 1, 2)
     width = strip.shape[1]
     packed = shape((groups_of(half_rows, width) * pitch + rows * SIDE, 128))
+    first = call(begin, shape((16, 128)), (), flops=10**10)
     sent = call(
-        functools.partial(pack_cols, count, half_cols), [packed] * (count - 1), (level_in, strip)
+        functools.partial(pack_cols, count, half_cols), [packed] * (count - 1), (level_in, strip, first)
     )
     got = [by_col(value, turn + 1) for turn, value in enumerate(sent)]
     band = shape((HALO * (cols + 2 * SIDE) + 4 * pitch, 128))

time: 69.6 us -> 68.7 us (0.987)
  local copies, waits for them, and re-layouts: 1.75 us -> 0.89 us
    unnamed x10, local copies, waits for them, and re-layouts: 1.75 us -> 0.89 us
    pallas_call x11 -> x12, Pallas kernels: 8.17 us -> 8.12 us  [call(): pl.pallas_call(body, out_shape=out_shapes, in_specs=[VMEM] * len(args), o...]
  transfers between devices with their start and end apart: 22 -> 22, of which waited for: 15 -> 16; matrix products, arithmetic and copies ran while one was open for 0% -> 0% of each run, Pallas kernels for 3% -> 3%
where the time goes in v4:
time: 68.7 us; the launch traced here: 68.5 us
  waiting for transfers between devices  31.8 us (46%)
  starting transfers between devices  27 us (39%)
  Pallas kernels  8.12 us (12%)
  local copies, waits for them, and re-layouts  0.89 us (1%)
  between operations  0.74 us (1%)
    ppermute x22, waiting for transfers between devices, permute(): lax.ppermute(value, axes, [(a, b) for a, b in pairs if b is not None])  31.8 us
    ppermute x22, starting transfers between devices, permute(): lax.ppermute(value, axes, [(a, b) for a, b in pairs if b is not None])  27 us
    pallas_call x12, Pallas kernels, call(): pl.pallas_call(body, out_shape=out_shapes, in_specs=[VMEM] * len(args), o...  8.12 us
  transfers between devices with their start and end apart: 22, of which 16 were waited for; matrix products, arithmetic and copies ran while one was open for 0% of the time, Pallas kernels for 3%

profile of v4, /device:TPU:0, one launch (start us, length us, event | category | flops | bytes accessed | tf_op | source)
XLA Modules:
  0.0 68.5 jit_solution(662322111328410240)
XLA Ops:
  0.7 0.9 %copy-done.3 = bf16[8,64,128]{2,1,0:T(8,128)(2,1)S(1)} copy-done((bf16[8,64,128]{2,1,0:T(8,128)(2,1)S(1)}, bf16[8,64,128]{2,1,0:T(8,128)(2,1)}, u32[]{:S(2)}) %copy-start.3) | copy-done | bytes 131096
  1.8 3.0 %collective-permute-start = (bf16[160,128]{1,0:T(8,128)(2,1)S(1)}, bf16[160,128]{1,0:T(8,128)(2,1)S(1)}, u32[]{:S(2)}, u32[]{:S(2)}) collective-permute-start(bf16[160,128]{1,0:T(8,128)(2,1)S(1)} %get-tuple-element.30), channel_id=1, source_target_pairs={{0,1},{1,0},{2,3},{3,2},{4,5},{5,4},{6,7},{7,6},{8,9},{9,8},{10,11... | collective-permute-start | bytes 122888 | tf_op jit(solution)/shard_map/ppermute | solution.py:465
  4.8 1.5 %collective-permute-start.1 = (bf16[160,128]{1,0:T(8,128)(2,1)S(1)}, bf16[160,128]{1,0:T(8,128)(2,1)S(1)}, u32[]{:S(2)}, u32[]{:S(2)}) collective-permute-start(bf16[160,128]{1,0:T(8,128)(2,1)S(1)} %get-tuple-element.31), channel_id=1, source_target_pairs={{0,2},{1,3},{2,0},{3,1},{4,6},{5,7},{6,4},{7,5},{8,10},{9,11},{10,... | collective-permute-start | bytes 122888 | tf_op jit(solution)/shard_map/ppermute | solution.py:465
  6.8 2.0 %collective-permute-done.1.refs_1_ = bf16[160,128]{1,0:T(8,128)(2,1)S(1)} collective-permute-done((bf16[160,128]{1,0:T(8,128)(2,1)S(1)}, bf16[160,128]{1,0:T(8,128)(2,1)S(1)}, u32[]{:S(2)}, u32[]{:S(2)}) %collective-permute-start.1) | collective-permute-done | bytes 40992 | tf_op jit(solution)/shard_map/ppermute | solution.py:465
  8.8 2.4 %collective-permute-done.2.refs_2_ = bf16[160,128]{1,0:T(8,128)(2,1)S(1)} collective-permute-done((bf16[160,128]{1,0:T(8,128)(2,1)S(1)}, bf16[160,128]{1,0:T(8,128)(2,1)S(1)}, u32[]{:S(2)}, u32[]{:S(2)}) %collective-permute-start.2) | collective-permute-done | bytes 40992 | tf_op jit(solution)/shard_map/ppermute | solution.py:465
  11.7 0.7 collective-permute-start.3
  12.3 3.0 %collective-permute-start.4 = (bf16[752,128]{1,0:T(8,128)(2,1)S(1)}, bf16[752,128]{1,0:T(8,128)(2,1)S(1)}, u32[]{:S(2)}, u32[]{:S(2)}) collective-permute-start(bf16[752,128]{1,0:T(8,128)(2,1)S(1)} %get-tuple-element.35), channel_id=1, source_target_pairs={{0,4},{1,5},{2,6},{3,7},{4,0},{5,1},{6,2},{7,3},{8,12},{9,13},{10,... | collective-permute-start | bytes 577544 | tf_op jit(solution)/shard_map/ppermute | solution.py:465
  15.3 0.6 shard_map.95
  16.4 3.8 %shard_map.96 = (bf16[6784,128]{1,0:T(8,128)(2,1)S(1)}, bf16[3392,128]{1,0:T(8,128)(2,1)S(1)}, bf16[128,256]{1,0:T(8,128)(2,1)S(1)}, bf16[8,64,128]{2,1,0:T(8,128)(2,1)}) custom-call(bf16[1152,128]{1,0:T(8,128)(2,1)S(1)} %get-tuple-element.33.kept_ref, bf16[752,128]{1,0:T(8,128)(2,1)S(1)} %collective-permute-done.3.cross_ref, ...), custom_call_target="tpu_custom_call" | custom-call | flops 6000000000 | tf_op jit(solution)/shard_map/pallas_call | solution.py:18
  20.2 2.2 %collective-permute-start.5 = (bf16[3392,128]{1,0:T(8,128)(2,1)S(1)}, bf16[3392,128]{1,0:T(8,128)(2,1)S(1)}, u32[]{:S(2)}, u32[]{:S(2)}) collective-permute-start(bf16[3392,128]{1,0:T(8,128)(2,1)S(1)} %get-tuple-element.42), channel_id=1, source_target_pairs={{0,4},{1,5},{2,6},{3,7},{4,0},{5,1},{6,2},{7,3},{8,12},{9,13},{10,... | collective-permute-start | bytes 2605064 | tf_op jit(solution)/shard_map/ppermute | solution.py:465
  22.6 1.7 %collective-permute-done.5.got_ref = bf16[3392,128]{1,0:T(8,128)(2,1)S(1)} collective-permute-done((bf16[3392,128]{1,0:T(8,128)(2,1)S(1)}, bf16[3392,128]{1,0:T(8,128)(2,1)S(1)}, u32[]{:S(2)}, u32[]{:S(2)}) %collective-permute-start.5) | collective-permute-done | bytes 868384 | tf_op jit(solution)/shard_map/ppermute | solution.py:465
  24.5 0.6 collective-permute-start.6
  25.2 0.5 collective-permute-start.7
  25.7 2.4 %collective-permute-start.8 = (bf16[912,128]{1,0:T(8,128)(2,1)S(1)}, bf16[912,128]{1,0:T(8,128)(2,1)S(1)}, u32[]{:S(2)}, u32[]{:S(2)}) collective-permute-start(bf16[912,128]{1,0:T(8,128)(2,1)S(1)} %get-tuple-element.45), channel_id=1, source_target_pairs={{0,3},{1,2},{2,1},{3,0},{4,7},{5,6},{6,5},{7,4},{8,11},{9,10},{10,... | collective-permute-start | bytes 700424 | tf_op jit(solution)/shard_map/ppermute | solution.py:465
  28.1 5.0 %collective-permute-done.6.refs_0_ = bf16[912,128]{1,0:T(8,128)(2,1)S(1)} collective-permute-done((bf16[912,128]{1,0:T(8,128)(2,1)S(1)}, bf16[912,128]{1,0:T(8,128)(2,1)S(1)}, u32[]{:S(2)}, u32[]{:S(2)}) %collective-permute-start.6) | collective-permute-done | bytes 233504 | tf_op jit(solution)/shard_map/ppermute | solution.py:465
  33.1 4.7 %collective-permute-done.7.refs_1_ = bf16[912,128]{1,0:T(8,128)(2,1)S(1)} collective-permute-done((bf16[912,128]{1,0:T(8,128)(2,1)S(1)}, bf16[912,128]{1,0:T(8,128)(2,1)S(1)}, u32[]{:S(2)}, u32[]{:S(2)}) %collective-permute-start.7) | collective-permute-done | bytes 233504 | tf_op jit(solution)/shard_map/ppermute | solution.py:465
  38.0 1.9 %collective-permute-start.9 = (bf16[224,128]{1,0:T(8,128)(2,1)S(1)}, bf16[224,128]{1,0:T(8,128)(2,1)S(1)}, u32[]{:S(2)}, u32[]{:S(2)}) collective-permute-start(bf16[224,128]{1,0:T(8,128)(2,1)S(1)} %get-tuple-element.49), channel_id=1, source_target_pairs={{0,8},{1,9},{2,10},{3,11},{4,12},{5,13},{6,14},{7,15},{8,0},{9,1},... | collective-permute-start | bytes 172040 | tf_op jit(solution)/shard_map/ppermute | solution.py:465
  39.9 2.6 %collective-permute-start.10 = (bf16[224,128]{1,0:T(8,128)(2,1)S(1)}, bf16[224,128]{1,0:T(8,128)(2,1)S(1)}, u32[]{:S(2)}, u32[]{:S(2)}) collective-permute-start(bf16[224,128]{1,0:T(8,128)(2,1)S(1)} %get-tuple-element.50), channel_id=1, source_target_pairs={{0,16},{1,17},{2,18},{3,19},{4,20},{5,21},{6,22},{7,23},{8,24},{9,... | collective-permute-start | bytes 172040 | tf_op jit(solution)/shard_map/ppermute | solution.py:465
  42.8 3.4 %collective-permute-done.10.refs_1_ = bf16[224,128]{1,0:T(8,128)(2,1)S(1)} collective-permute-done((bf16[224,128]{1,0:T(8,128)(2,1)S(1)}, bf16[224,128]{1,0:T(8,128)(2,1)S(1)}, u32[]{:S(2)}, u32[]{:S(2)}) %collective-permute-start.10) | collective-permute-done | bytes 57376 | tf_op jit(solution)/shard_map/ppermute | solution.py:465
  46.2 2.3 %collective-permute-done.11.refs_2_ = bf16[224,128]{1,0:T(8,128)(2,1)S(1)} collective-permute-done((bf16[224,128]{1,0:T(8,128)(2,1)S(1)}, bf16[224,128]{1,0:T(8,128)(2,1)S(1)}, u32[]{:S(2)}, u32[]{:S(2)}) %collective-permute-start.11) | collective-permute-done | bytes 57376 | tf_op jit(solution)/shard_map/ppermute | solution.py:465
  48.5 0.8 %collective-permute-start.14 = (bf16[224,128]{1,0:T(8,128)(2,1)S(1)}, bf16[224,128]{1,0:T(8,128)(2,1)S(1)}, u32[]{:S(2)}, u32[]{:S(2)}) collective-permute-start(bf16[224,128]{1,0:T(8,128)(2,1)S(1)} %shard_map.101.refs_0_), channel_id=1, source_target_pairs={{0,24},{1,25},{2,26},{3,27},{4,28},{5,29},{6,30},{7,31},{8,16},{9,... | collective-permute-start | bytes 172040 | tf_op jit(solution)/shard_map/ppermute | solution.py:465
  49.3 3.7 %collective-permute-start.12 = (bf16[224,128]{1,0:T(8,128)(2,1)S(1)}, bf16[224,128]{1,0:T(8,128)(2,1)S(1)}, u32[]{:S(2)}, u32[]{:S(2)}) collective-permute-start(bf16[224,128]{1,0:T(8,128)(2,1)S(1)} %shard_map.101.refs_0_), channel_id=1, source_target_pairs={{0,8},{1,9},{2,10},{3,11},{4,12},{5,13},{6,14},{7,15},{8,0},{9,1},... | collective-permute-start | bytes 172040 | tf_op jit(solution)/shard_map/ppermute | solution.py:465
  53.0 1.7 %collective-permute-done.14.refs_3_ = bf16[224,128]{1,0:T(8,128)(2,1)S(1)} collective-permute-done((bf16[224,128]{1,0:T(8,128)(2,1)S(1)}, bf16[224,128]{1,0:T(8,128)(2,1)S(1)}, u32[]{:S(2)}, u32[]{:S(2)}) %collective-permute-start.14) | collective-permute-done | bytes 57376 | tf_op jit(solution)/shard_map/ppermute | solution.py:465
  54.7 0.9 %collective-permute-done.13.refs_2_ = bf16[224,128]{1,0:T(8,128)(2,1)S(1)} collective-permute-done((bf16[224,128]{1,0:T(8,128)(2,1)S(1)}, bf16[224,128]{1,0:T(8,128)(2,1)S(1)}, u32[]{:S(2)}, u32[]{:S(2)}) %collective-permute-start.13) | collective-permute-done | bytes 57376 | tf_op jit(solution)/shard_map/ppermute | solution.py:465
  55.6 1.5 %collective-permute-start.17 = (bf16[848,128]{1,0:T(8,128)(2,1)S(1)}, bf16[848,128]{1,0:T(8,128)(2,1)S(1)}, u32[]{:S(2)}, u32[]{:S(2)}) collective-permute-start(bf16[848,128]{1,0:T(8,128)(2,1)S(1)} %shard_map.102.refs_0_), channel_id=1, source_target_pairs={{0,3},{1,2},{2,1},{3,0},{4,7},{5,6},{6,5},{7,4},{8,11},{9,10},{10,... | collective-permute-start | bytes 651272 | tf_op jit(solution)/shard_map/ppermute | solution.py:465
  57.1 1.5 %collective-permute-start.16 = (bf16[848,128]{1,0:T(8,128)(2,1)S(1)}, bf16[848,128]{1,0:T(8,128)(2,1)S(1)}, u32[]{:S(2)}, u32[]{:S(2)}) collective-permute-start(bf16[848,128]{1,0:T(8,128)(2,1)S(1)} %shard_map.102.refs_0_), channel_id=1, source_target_pairs={{0,2},{1,3},{2,0},{3,1},{4,6},{5,7},{6,4},{7,5},{8,10},{9,11},{10,... | collective-permute-start | bytes 651272 | tf_op jit(solution)/shard_map/ppermute | solution.py:465
  58.7 0.5 collective-permute-start.15
  59.2 3.9 %collective-permute-done.17.refs_3_ = bf16[848,128]{1,0:T(8,128)(2,1)S(1)} collective-permute-done((bf16[848,128]{1,0:T(8,128)(2,1)S(1)}, bf16[848,128]{1,0:T(8,128)(2,1)S(1)}, u32[]{:S(2)}, u32[]{:S(2)}) %collective-permute-start.17) | collective-permute-done | bytes 217120 | tf_op jit(solution)/shard_map/ppermute | solution.py:465
  63.1 2.2 %collective-permute-done.16.refs_2_ = bf16[848,128]{1,0:T(8,128)(2,1)S(1)} collective-permute-done((bf16[848,128]{1,0:T(8,128)(2,1)S(1)}, bf16[848,128]{1,0:T(8,128)(2,1)S(1)}, u32[]{:S(2)}, u32[]{:S(2)}) %collective-permute-start.16) | collective-permute-done | bytes 217120 | tf_op jit(solution)/shard_map/ppermute | solution.py:465
  65.3 0.5 collective-permute-start.19
  65.8 0.9 %shard_map.99 = bf16[4,64,128]{2,1,0:T(8,128)(2,1)} custom-call(bf16[4,64,128]{2,1,0:T(8,128)(2,1)S(1)} %shard_map.97.pieces_ref, bf16[912,128]{1,0:T(8,128)(2,1)S(1)} %collective-permute-done.6.refs_0_, bf16[912,128]{1,0:T(8,128)(2,1)S(1)} %collective-permute-done.7.refs_1_, bf16[912,128]{1,0:T(8,128)(2,1)S(1)} %collective-permute-done.8.refs_2_), custom_call_target="tpu_custom_call" | custom-call | flops 1000000000 | tf_op jit(solution)/shard_map/pallas_call | solution.py:18
  67.1 1.5 %shard_map.103 = (bf16[9,128,128]{2,1,0:T(8,128)(2,1)}, bf16[4,128,256]{2,1,0:T(8,128)(2,1)}, bf16[9,256,256]{2,1,0:T(8,128)(2,1)}) custom-call(bf16[848,128]{1,0:T(8,128)(2,1)S(1)} %shard_map.102.refs_0_, bf16[848,128]{1,0:T(8,128)(2,1)S(1)} %collective-permute-done.15.refs_1_, bf16[848,128]{1,0:T(8,128)(2,1)S(1)} %collective-permute-done.16.refs_2_, ...), custom_call_target="tpu_custom_call" | custom-call | flops 1000000000 | tf_op jit(solution)/shard_map/pallas_call | solution.py:18
  (34 shorter events, 3.1 us)
Async XLA Ops:
  0.6 0.9 %copy-start.3 = (bf16[8,64,128]{2,1,0:T(8,128)(2,1)S(1)}, bf16[8,64,128]{2,1,0:T(8,128)(2,1)}, u32[]{:S(2)}) copy-start(bf16[8,64,128]{2,1,0:T(8,128)(2,1)} %level_ref.3) | copy-start | bytes 393220
  0.6 0.9 %copy-start.4 = (bf16[4,128,64]{1,2,0:T(8,128)(2,1)S(1)}, bf16[4,128,64]{1,2,0:T(8,128)(2,1)}, u32[]{:S(2)}) copy-start(bf16[4,128,64]{1,2,0:T(8,128)(2,1)} %param.9) | copy-start | bytes 196612
  1.8 5.0 %collective-permute-start = (bf16[160,128]{1,0:T(8,128)(2,1)S(1)}, bf16[160,128]{1,0:T(8,128)(2,1)S(1)}, u32[]{:S(2)}, u32[]{:S(2)}) collective-permute-start(bf16[160,128]{1,0:T(8,128)(2,1)S(1)} %get-tuple-element.30), channel_id=1, source_target_pairs={{0,1},{1,0},{2,3},{3,2},{4,5},{5,4},{6,7},{7,6},{8,9},{9,8},{10,11... | collective-permute-start | bytes 122888 | tf_op jit(solution)/shard_map/ppermute | solution.py:465
  4.8 4.0 %collective-permute-start.1 = (bf16[160,128]{1,0:T(8,128)(2,1)S(1)}, bf16[160,128]{1,0:T(8,128)(2,1)S(1)}, u32[]{:S(2)}, u32[]{:S(2)}) collective-permute-start(bf16[160,128]{1,0:T(8,128)(2,1)S(1)} %get-tuple-element.31), channel_id=1, source_target_pairs={{0,2},{1,3},{2,0},{3,1},{4,6},{5,7},{6,4},{7,5},{8,10},{9,11},{10,... | collective-permute-start | bytes 122888 | tf_op jit(solution)/shard_map/ppermute | solution.py:465
  6.3 9.0 %copy-start = (bf16[3,3,256,256]{3,2,1,0:T(8,128)(2,1)S(1)}, bf16[3,3,256,256]{3,2,1,0:T(8,128)(2,1)}, u32[]{:S(2)}) copy-start(bf16[3,3,256,256]{3,2,1,0:T(8,128)(2,1)} %param.8) | copy-start | bytes 3538948
  6.3 9.0 %copy-start.1 = (bf16[3,3,128,128]{3,2,1,0:T(8,128)(2,1)S(1)}, bf16[3,3,128,128]{3,2,1,0:T(8,128)(2,1)}, u32[]{:S(2)}) copy-start(bf16[3,3,128,128]{3,2,1,0:T(8,128)(2,1)} %param.6) | copy-start | bytes 884740
  6.3 9.0 %copy-start.2 = (bf16[2,2,128,256]{3,2,1,0:T(8,128)(2,1)S(1)}, bf16[2,2,128,256]{3,2,1,0:T(8,128)(2,1)}, u32[]{:S(2)}) copy-start(bf16[2,2,128,256]{3,2,1,0:T(8,128)(2,1)} %param.7) | copy-start | bytes 786436
  6.3 4.9 %collective-permute-start.2 = (bf16[160,128]{1,0:T(8,128)(2,1)S(1)}, bf16[160,128]{1,0:T(8,128)(2,1)S(1)}, u32[]{:S(2)}, u32[]{:S(2)}) collective-permute-start(bf16[160,128]{1,0:T(8,128)(2,1)S(1)} %get-tuple-element.32), channel_id=1, source_target_pairs={{0,3},{1,2},{2,1},{3,0},{4,7},{5,6},{6,5},{7,4},{8,11},{9,10},{10,... | collective-permute-start | bytes 122888 | tf_op jit(solution)/shard_map/ppermute | solution.py:465
  11.7 4.3 %collective-permute-start.3 = (bf16[752,128]{1,0:T(8,128)(2,1)S(1)}, bf16[752,128]{1,0:T(8,128)(2,1)S(1)}, u32[]{:S(2)}, u32[]{:S(2)}) collective-permute-start(bf16[752,128]{1,0:T(8,128)(2,1)S(1)} %get-tuple-element.34), channel_id=1, source_target_pairs={{4,8},{5,9},{6,10},{7,11},{8,4},{9,5},{10,6},{11,7},{12,16},{13,17... | collective-permute-start | bytes 577544 | tf_op jit(solution)/shard_map/ppermute | solution.py:465
  12.3 4.1 %collective-permute-start.4 = (bf16[752,128]{1,0:T(8,128)(2,1)S(1)}, bf16[752,128]{1,0:T(8,128)(2,1)S(1)}, u32[]{:S(2)}, u32[]{:S(2)}) collective-permute-start(bf16[752,128]{1,0:T(8,128)(2,1)S(1)} %get-tuple-element.35), channel_id=1, source_target_pairs={{0,4},{1,5},{2,6},{3,7},{4,0},{5,1},{6,2},{7,3},{8,12},{9,13},{10,... | collective-permute-start | bytes 577544 | tf_op jit(solution)/shard_map/ppermute | solution.py:465
  20.2 4.2 %collective-permute-start.5 = (bf16[3392,128]{1,0:T(8,128)(2,1)S(1)}, bf16[3392,128]{1,0:T(8,128)(2,1)S(1)}, u32[]{:S(2)}, u32[]{:S(2)}) collective-permute-start(bf16[3392,128]{1,0:T(8,128)(2,1)S(1)} %get-tuple-element.42), channel_id=1, source_target_pairs={{0,4},{1,5},{2,6},{3,7},{4,0},{5,1},{6,2},{7,3},{8,12},{9,13},{10,... | collective-permute-start | bytes 2605064 | tf_op jit(solution)/shard_map/ppermute | solution.py:465
  24.5 8.6 %collective-permute-start.6 = (bf16[912,128]{1,0:T(8,128)(2,1)S(1)}, bf16[912,128]{1,0:T(8,128)(2,1)S(1)}, u32[]{:S(2)}, u32[]{:S(2)}) collective-permute-start(bf16[912,128]{1,0:T(8,128)(2,1)S(1)} %get-tuple-element.43), channel_id=1, source_target_pairs={{0,1},{1,0},{2,3},{3,2},{4,5},{5,4},{6,7},{7,6},{8,9},{9,8},{10,11... | collective-permute-start | bytes 700424 | tf_op jit(solution)/shard_map/ppermute | solution.py:465
  25.2 12.7 %collective-permute-start.7 = (bf16[912,128]{1,0:T(8,128)(2,1)S(1)}, bf16[912,128]{1,0:T(8,128)(2,1)S(1)}, u32[]{:S(2)}, u32[]{:S(2)}) collective-permute-start(bf16[912,128]{1,0:T(8,128)(2,1)S(1)} %get-tuple-element.44), channel_id=1, source_target_pairs={{0,2},{1,3},{2,0},{3,1},{4,6},{5,7},{6,4},{7,5},{8,10},{9,11},{10,... | collective-permute-start | bytes 700424 | tf_op jit(solution)/shard_map/ppermute | solution.py:465
  25.7 12.2 %collective-permute-start.8 = (bf16[912,128]{1,0:T(8,128)(2,1)S(1)}, bf16[912,128]{1,0:T(8,128)(2,1)S(1)}, u32[]{:S(2)}, u32[]{:S(2)}) collective-permute-start(bf16[912,128]{1,0:T(8,128)(2,1)S(1)} %get-tuple-element.45), channel_id=1, source_target_pairs={{0,3},{1,2},{2,1},{3,0},{4,7},{5,6},{6,5},{7,4},{8,11},{9,10},{10,... | collective-permute-start | bytes 700424 | tf_op jit(solution)/shard_map/ppermute | solution.py:465
  38.0 4.8 %collective-permute-start.9 = (bf16[224,128]{1,0:T(8,128)(2,1)S(1)}, bf16[224,128]{1,0:T(8,128)(2,1)S(1)}, u32[]{:S(2)}, u32[]{:S(2)}) collective-permute-start(bf16[224,128]{1,0:T(8,128)(2,1)S(1)} %get-tuple-element.49), channel_id=1, source_target_pairs={{0,8},{1,9},{2,10},{3,11},{4,12},{5,13},{6,14},{7,15},{8,0},{9,1},... | collective-permute-start | bytes 172040 | tf_op jit(solution)/shard_map/ppermute | solution.py:465
  39.9 6.3 %collective-permute-start.10 = (bf16[224,128]{1,0:T(8,128)(2,1)S(1)}, bf16[224,128]{1,0:T(8,128)(2,1)S(1)}, u32[]{:S(2)}, u32[]{:S(2)}) collective-permute-start(bf16[224,128]{1,0:T(8,128)(2,1)S(1)} %get-tuple-element.50), channel_id=1, source_target_pairs={{0,16},{1,17},{2,18},{3,19},{4,20},{5,21},{6,22},{7,23},{8,24},{9,... | collective-permute-start | bytes 172040 | tf_op jit(solution)/shard_map/ppermute | solution.py:465
  42.5 6.0 %collective-permute-start.11 = (bf16[224,128]{1,0:T(8,128)(2,1)S(1)}, bf16[224,128]{1,0:T(8,128)(2,1)S(1)}, u32[]{:S(2)}, u32[]{:S(2)}) collective-permute-start(bf16[224,128]{1,0:T(8,128)(2,1)S(1)} %get-tuple-element.51), channel_id=1, source_target_pairs={{0,24},{1,25},{2,26},{3,27},{4,28},{5,29},{6,30},{7,31},{8,16},{9,... | collective-permute-start | bytes 172040 | tf_op jit(solution)/shard_map/ppermute | solution.py:465
  48.5 6.2 %collective-permute-start.14 = (bf16[224,128]{1,0:T(8,128)(2,1)S(1)}, bf16[224,128]{1,0:T(8,128)(2,1)S(1)}, u32[]{:S(2)}, u32[]{:S(2)}) collective-permute-start(bf16[224,128]{1,0:T(8,128)(2,1)S(1)} %shard_map.101.refs_0_), channel_id=1, source_target_pairs={{0,24},{1,25},{2,26},{3,27},{4,28},{5,29},{6,30},{7,31},{8,16},{9,... | collective-permute-start | bytes 172040 | tf_op jit(solution)/shard_map/ppermute | solution.py:465
  49.3 6.3 %collective-permute-start.13 = (bf16[224,128]{1,0:T(8,128)(2,1)S(1)}, bf16[224,128]{1,0:T(8,128)(2,1)S(1)}, u32[]{:S(2)}, u32[]{:S(2)}) collective-permute-start(bf16[224,128]{1,0:T(8,128)(2,1)S(1)} %shard_map.101.refs_0_), channel_id=1, source_target_pairs={{0,16},{1,17},{2,18},{3,19},{4,20},{5,21},{6,22},{7,23},{8,24},{9,... | collective-permute-start | bytes 172040 | tf_op jit(solution)/shard_map/ppermute | solution.py:465
  49.3 6.3 %collective-permute-start.12 = (bf16[224,128]{1,0:T(8,128)(2,1)S(1)}, bf16[224,128]{1,0:T(8,128)(2,1)S(1)}, u32[]{:S(2)}, u32[]{:S(2)}) collective-permute-start(bf16[224,128]{1,0:T(8,128)(2,1)S(1)} %shard_map.101.refs_0_), channel_id=1, source_target_pairs={{0,8},{1,9},{2,10},{3,11},{4,12},{5,13},{6,14},{7,15},{8,0},{9,1},... | collective-permute-start | bytes 172040 | tf_op jit(solution)/shard_map/ppermute | solution.py:465
  55.6 7.5 %collective-permute-start.17 = (bf16[848,128]{1,0:T(8,128)(2,1)S(1)}, bf16[848,128]{1,0:T(8,128)(2,1)S(1)}, u32[]{:S(2)}, u32[]{:S(2)}) collective-permute-start(bf16[848,128]{1,0:T(8,128)(2,1)S(1)} %shard_map.102.refs_0_), channel_id=1, source_target_pairs={{0,3},{1,2},{2,1},{3,0},{4,7},{5,6},{6,5},{7,4},{8,11},{9,10},{10,... | collective-permute-start | bytes 651272 | tf_op jit(solution)/shard_map/ppermute | solution.py:465
  57.1 8.1 %collective-permute-start.16 = (bf16[848,128]{1,0:T(8,128)(2,1)S(1)}, bf16[848,128]{1,0:T(8,128)(2,1)S(1)}, u32[]{:S(2)}, u32[]{:S(2)}) collective-permute-start(bf16[848,128]{1,0:T(8,128)(2,1)S(1)} %shard_map.102.refs_0_), channel_id=1, source_target_pairs={{0,2},{1,3},{2,0},{3,1},{4,6},{5,7},{6,4},{7,5},{8,10},{9,11},{10,... | collective-permute-start | bytes 651272 | tf_op jit(solution)/shard_map/ppermute | solution.py:465
  58.7 6.6 %collective-permute-start.15 = (bf16[848,128]{1,0:T(8,128)(2,1)S(1)}, bf16[848,128]{1,0:T(8,128)(2,1)S(1)}, u32[]{:S(2)}, u32[]{:S(2)}) collective-permute-start(bf16[848,128]{1,0:T(8,128)(2,1)S(1)} %shard_map.102.refs_0_), channel_id=1, source_target_pairs={{0,1},{1,0},{2,3},{3,2},{4,5},{5,4},{6,7},{7,6},{8,9},{9,8},{10,11... | collective-permute-start | bytes 651272 | tf_op jit(solution)/shard_map/ppermute | solution.py:465
  59.2 7.5 %collective-permute-start.18 = (bf16[848,128]{1,0:T(8,128)(2,1)S(1)}, bf16[848,128]{1,0:T(8,128)(2,1)S(1)}, u32[]{:S(2)}, u32[]{:S(2)}) collective-permute-start(bf16[848,128]{1,0:T(8,128)(2,1)S(1)} %shard_map.102.refs_0_), channel_id=1, source_target_pairs={{0,4},{1,5},{2,6},{3,7},{4,0},{5,1},{6,2},{7,3},{8,12},{9,13},{10,... | collective-permute-start | bytes 651272 | tf_op jit(solution)/shard_map/ppermute | solution.py:465
  63.1 3.6 %collective-permute-start.21 = (bf16[848,128]{1,0:T(8,128)(2,1)S(1)}, bf16[848,128]{1,0:T(8,128)(2,1)S(1)}, u32[]{:S(2)}, u32[]{:S(2)}) collective-permute-start(bf16[848,128]{1,0:T(8,128)(2,1)S(1)} %collective-permute-done.17.refs_3_), channel_id=1, source_target_pairs={{0,4},{1,5},{2,6},{3,7},{4,0},{5,1},{6,2},{7,3},{8,12},{9,13},{10,... | collective-permute-start | bytes 651272 | tf_op jit(solution)/shard_map/ppermute | solution.py:465
  65.3 1.5 %collective-permute-start.20 = (bf16[848,128]{1,0:T(8,128)(2,1)S(1)}, bf16[848,128]{1,0:T(8,128)(2,1)S(1)}, u32[]{:S(2)}, u32[]{:S(2)}) collective-permute-start(bf16[848,128]{1,0:T(8,128)(2,1)S(1)} %collective-permute-done.16.refs_2_), channel_id=1, source_target_pairs={{0,4},{1,5},{2,6},{3,7},{4,0},{5,1},{6,2},{7,3},{8,12},{9,13},{10,... | collective-permute-start | bytes 651272 | tf_op jit(solution)/shard_map/ppermute | solution.py:465
  65.3 1.8 %collective-permute-start.19 = (bf16[848,128]{1,0:T(8,128)(2,1)S(1)}, bf16[848,128]{1,0:T(8,128)(2,1)S(1)}, u32[]{:S(2)}, u32[]{:S(2)}) collective-permute-start(bf16[848,128]{1,0:T(8,128)(2,1)S(1)} %collective-permute-done.15.refs_1_), channel_id=1, source_target_pairs={{0,4},{1,5},{2,6},{3,7},{4,0},{5,1},{6,2},{7,3},{8,12},{9,13},{10,... | collective-permute-start | bytes 651272 | tf_op jit(solution)/shard_map/ppermute | solution.py:465

commit v5 on v4

--- a/solution.py
+++ b/solution.py
@@ -363,9 +363,10 @@
             pieces_ref[turn, half_cols * group : half_cols * group + half_cols] = piece.astype(BF)
 
 
-def add_cores(count, sums_ref, got_ref, pieces_ref, own_ref, *outs):
+def add_cores(count, cut, sums_ref, got_ref, pieces_ref, own_ref, *outs):
     me, core = lax.axis_index("gx"), lax.axis_index("gy") & 1
     part = own_ref.shape[0]
+    early, late = outs[: count - 1], outs[count - 1 :]
     for turn in range(count):
         mine = pl.ds(pl.multiple_of((core * count + (me ^ turn)) * part, 16), part)
         theirs = pl.ds(pl.multiple_of((me ^ turn) * part, 16), part)
@@ -373,27 +374,32 @@
         if turn == 0:
             own_ref[...] = value
         else:
-            outs[turn - 1][0:part] = value.astype(BF)
-            outs[turn - 1][part:] = pieces_ref[turn]
-
-
-def add_cols(count, z_count, own_ref, *refs):
+            early[turn - 1][...] = value[:cut].astype(BF)
+            late[turn - 1][0 : part - cut] = value[cut:].astype(BF)
+            late[turn - 1][part - cut :] = pieces_ref[turn]
+
+
+def row_turns(z_count):
+    return [*range(2, z_count), 1] if z_count > 1 else []
+
+
+def add_cols(count, z_count, low, size, own_ref, *refs):
     got = refs[: count - 1]
     first_ref, outs, total = refs[count - 1], refs[count:-1], refs[-1]
     z = lax.axis_index("gy") // 2
-    part, unit = own_ref.shape[0], first_ref.shape[0]
-    value = own_ref[...]
+    unit = first_ref.shape[0]
+    value = own_ref[low : low + size]
     for ref in got:
-        value = value + ref[0:part].astype(F32)
-    total[0:part] = value
-    if part < total.shape[0]:
-        total[part:] = jnp.zeros((total.shape[0] - part, 128), F32)
+        value = value + ref[0:size].astype(F32)
+    total[0:size] = value
+    if size < total.shape[0]:
+        total[size:] = jnp.zeros((total.shape[0] - size, 128), F32)
     for turn in range(z_count):
         value = total[pl.ds(pl.multiple_of((z ^ turn) * unit, 16), unit), :]
         if turn == 0:
             first_ref[...] = value
         else:
-            outs[turn - 1][...] = value.astype(BF)
+            outs[row_turns(z_count).index(turn)][...] = value.astype(BF)
 
 
 def place_neck(count, part, pieces_ref, *refs):
@@ -413,20 +419,27 @@
         neck_ref[group * per : group * per + per] = value
 
 
-def add_rows(first_ref, *refs):
-    value = first_ref[...]
-    for ref in refs[:-1]:
-        value = value + ref[...].astype(F32)
-    refs[-1][...] = value.astype(BF)
-
-
-def join(z_count, *refs):
+def add_rows(z_count, *refs):
+    low = 0
+    for group in (refs[:z_count], refs[z_count:-1]):
+        value = group[0][...]
+        for ref in group[1:]:
+            value = value + ref[...].astype(F32)
+        refs[-1][low : low + value.shape[0]] = value.astype(BF)
+        low += value.shape[0]
+
+
+def join(z_count, cut, unit, *refs):
     pieces, (out_ref, store) = refs[:z_count], refs[z_count:]
     z = lax.axis_index("gy") // 2
-    unit = pieces[0].shape[0]
+    rest = pieces[0].shape[0] - unit
     for turn in range(z_count):
-        store[pl.ds(pl.multiple_of((z ^ turn) * unit, 16), unit), :] = pieces[turn][...]
-    out_ref[...] = store[0 : out_ref.shape[0]]
+        here = z ^ turn
+        store[pl.ds(pl.multiple_of(here * unit, 16), unit), :] = pieces[turn][0:unit]
+        here = unit * z_count + here * rest
+        store[pl.ds(pl.multiple_of(here, 16), rest), :] = pieces[turn][unit:]
+    out_ref[0:cut] = store[0:cut]
+    out_ref[cut:] = store[unit * z_count : unit * z_count + out_ref.shape[0] - cut]
 
 
 def finish(count, *refs):
@@ -508,7 +521,6 @@
     used = 2 * 9 * total + 4 * 2 * 128 + 9 * 128
     part = -(-used // (2 * count * 16)) * 16
     half = part * count
-    unit = -(-part // (z_count * 16)) * 16
     tiles = groups_of(half_rows, width) * half_cols
     sizes = (
         rows, half_rows, half_cols,
@@ -541,26 +553,36 @@
     pieces = call(
         functools.partial(pack_neck, count, half_rows, width), shape((count, tiles, 128)), (out,)
     )
+    cut = -(-part // 32) * 16
+    rest = part - cut
+    units = [-(-size // (z_count * 16)) * 16 for size in (cut, rest)]
     own, *sent = call(
-        functools.partial(add_cores, count),
-        [shape((part, 128), F32)] + [shape((part + tiles, 128))] * (count - 1),
+        functools.partial(add_cores, count, cut),
+        [shape((part, 128), F32)]
+        + [shape((cut, 128))] * (count - 1)
+        + [shape((rest + tiles, 128))] * (count - 1),
         (sums, by_core(send), pieces),
     )
-    got = [by_col(value, turn + 1) for turn, value in enumerate(sent)]
-    own, *sent = call(
-        functools.partial(add_cols, count, z_count),
-        [shape((unit, 128), F32)] + [shape((unit, 128))] * (z_count - 1),
-        (own, *got),
-        [pltpu.VMEM((unit * z_count, 128), F32)],
-    )
-    neck_out = call(functools.partial(place_neck, count, part), shape(strip.shape), (pieces, *got))
-    got = [by_z(value, turn + 1) for turn, value in enumerate(sent)]
-    own = call(add_rows, shape((unit, 128)), (own, *got))
+    early = [by_col(value, turn + 1) for turn, value in enumerate(sent[: count - 1])]
+    late = [by_col(value, turn + 1) for turn, value in enumerate(sent[count - 1 :])]
+    terms = []
+    for low, size, unit, got in ((0, cut, units[0], early), (cut, rest, units[1], late)):
+        first, *sent = call(
+            functools.partial(add_cols, count, z_count, low, size),
+            [shape((unit, 128), F32)] + [shape((unit, 128))] * (z_count - 1),
+            (own, *got),
+            [pltpu.VMEM((unit * z_count, 128), F32)],
+        )
+        terms += [first] + [by_z(value, turn) for turn, value in zip(row_turns(z_count), sent)]
+    neck_out = call(
+        functools.partial(place_neck, count, rest), shape(strip.shape), (pieces, *late)
+    )
+    own = call(functools.partial(add_rows, z_count), shape((sum(units), 128)), terms)
     own = call(
-        functools.partial(join, z_count),
+        functools.partial(join, z_count, cut, units[0]),
         shape((part, 128)),
         [own] + [by_z(own, turn) for turn in range(1, z_count)],
-        [pltpu.VMEM((unit * z_count, 128), BF)],
+        [pltpu.VMEM((sum(units) * z_count, 128), BF)],
     )
     ours = [own] + [by_col(own, turn) for turn in range(1, count)]
     theirs = [by_core(value) for value in ours]

time: 68.7 us -> 67.1 us (0.977)
  waiting for transfers between devices: 31.8 us -> 23 us
  starting transfers between devices: 27 us -> 34.1 us
    ppermute x22 -> x28, waiting for transfers between devices: 31.8 us -> 23 us  [permute(): lax.ppermute(value, axes, [(a, b) for a, b in pairs if b is not None])]
    ppermute x22 -> x28, starting transfers between devices: 27 us -> 34.1 us  [permute(): lax.ppermute(value, axes, [(a, b) for a, b in pairs if b is not None])]
    pallas_call x12 -> x13, Pallas kernels: 8.12 us -> 8.1 us  [call(): pl.pallas_call(body, out_shape=out_shapes, in_specs=[VMEM] * len(args), o...]
  transfers between devices with their start and end apart: 22 -> 28, of which waited for: 16 -> 18; matrix products, arithmetic and copies ran while one was open for 0% -> 0% of each run, Pallas kernels for 3% -> 3%
where the time goes in v5:
time: 67.1 us; the launch traced here: 66.9 us
  starting transfers between devices  34.1 us (51%)
  waiting for transfers between devices  23 us (34%)
  Pallas kernels  8.1 us (12%)
  local copies, waits for them, and re-layouts  0.89 us (1%)
  between operations  0.75 us (1%)
    ppermute x28, starting transfers between devices, permute(): lax.ppermute(value, axes, [(a, b) for a, b in pairs if b is not None])  34.1 us
    ppermute x28, waiting for transfers between devices, permute(): lax.ppermute(value, axes, [(a, b) for a, b in pairs if b is not None])  23 us
    pallas_call x13, Pallas kernels, call(): pl.pallas_call(body, out_shape=out_shapes, in_specs=[VMEM] * len(args), o...  8.1 us
  transfers between devices with their start and end apart: 28, of which 18 were waited for; matrix products, arithmetic and copies ran while one was open for 0% of the time, Pallas kernels for 3%

profile of v5, /device:TPU:0, one launch (start us, length us, event | category | flops | bytes accessed | tf_op | source)
XLA Modules:
  0.0 66.9 jit_solution(7814181129144380898)
XLA Ops:
  0.7 0.9 %copy-done.3 = bf16[8,64,128]{2,1,0:T(8,128)(2,1)S(1)} copy-done((bf16[8,64,128]{2,1,0:T(8,128)(2,1)S(1)}, bf16[8,64,128]{2,1,0:T(8,128)(2,1)}, u32[]{:S(2)}) %copy-start.3) | copy-done | bytes 131096
  1.8 3.0 %collective-permute-start = (bf16[160,128]{1,0:T(8,128)(2,1)S(1)}, bf16[160,128]{1,0:T(8,128)(2,1)S(1)}, u32[]{:S(2)}, u32[]{:S(2)}) collective-permute-start(bf16[160,128]{1,0:T(8,128)(2,1)S(1)} %get-tuple-element.37), channel_id=1, source_target_pairs={{0,1},{1,0},{2,3},{3,2},{4,5},{5,4},{6,7},{7,6},{8,9},{9,8},{10,11... | collective-permute-start | bytes 122888 | tf_op jit(solution)/shard_map/ppermute | solution.py:478
  4.8 1.5 %collective-permute-start.1 = (bf16[160,128]{1,0:T(8,128)(2,1)S(1)}, bf16[160,128]{1,0:T(8,128)(2,1)S(1)}, u32[]{:S(2)}, u32[]{:S(2)}) collective-permute-start(bf16[160,128]{1,0:T(8,128)(2,1)S(1)} %get-tuple-element.38), channel_id=1, source_target_pairs={{0,2},{1,3},{2,0},{3,1},{4,6},{5,7},{6,4},{7,5},{8,10},{9,11},{10,... | collective-permute-start | bytes 122888 | tf_op jit(solution)/shard_map/ppermute | solution.py:478
  6.8 2.0 %collective-permute-done.1.refs_1_ = bf16[160,128]{1,0:T(8,128)(2,1)S(1)} collective-permute-done((bf16[160,128]{1,0:T(8,128)(2,1)S(1)}, bf16[160,128]{1,0:T(8,128)(2,1)S(1)}, u32[]{:S(2)}, u32[]{:S(2)}) %collective-permute-start.1) | collective-permute-done | bytes 40992 | tf_op jit(solution)/shard_map/ppermute | solution.py:478
  8.8 2.4 %collective-permute-done.2.refs_2_ = bf16[160,128]{1,0:T(8,128)(2,1)S(1)} collective-permute-done((bf16[160,128]{1,0:T(8,128)(2,1)S(1)}, bf16[160,128]{1,0:T(8,128)(2,1)S(1)}, u32[]{:S(2)}, u32[]{:S(2)}) %collective-permute-start.2) | collective-permute-done | bytes 40992 | tf_op jit(solution)/shard_map/ppermute | solution.py:478
  11.7 0.7 %collective-permute-start.3 = (bf16[752,128]{1,0:T(8,128)(2,1)S(1)}, bf16[752,128]{1,0:T(8,128)(2,1)S(1)}, u32[]{:S(2)}, u32[]{:S(2)}) collective-permute-start(bf16[752,128]{1,0:T(8,128)(2,1)S(1)} %get-tuple-element.41), channel_id=1, source_target_pairs={{4,8},{5,9},{6,10},{7,11},{8,4},{9,5},{10,6},{11,7},{12,16},{13,17... | collective-permute-start | bytes 577544 | tf_op jit(solution)/shard_map/ppermute | solution.py:478
  12.3 3.0 %collective-permute-start.4 = (bf16[752,128]{1,0:T(8,128)(2,1)S(1)}, bf16[752,128]{1,0:T(8,128)(2,1)S(1)}, u32[]{:S(2)}, u32[]{:S(2)}) collective-permute-start(bf16[752,128]{1,0:T(8,128)(2,1)S(1)} %get-tuple-element.42), channel_id=1, source_target_pairs={{0,4},{1,5},{2,6},{3,7},{4,0},{5,1},{6,2},{7,3},{8,12},{9,13},{10,... | collective-permute-start | bytes 577544 | tf_op jit(solution)/shard_map/ppermute | solution.py:478
  15.3 0.6 shard_map.95
  16.4 3.8 %shard_map.96 = (bf16[6784,128]{1,0:T(8,128)(2,1)S(1)}, bf16[3392,128]{1,0:T(8,128)(2,1)S(1)}, bf16[128,256]{1,0:T(8,128)(2,1)S(1)}, bf16[8,64,128]{2,1,0:T(8,128)(2,1)}) custom-call(bf16[1152,128]{1,0:T(8,128)(2,1)S(1)} %get-tuple-element.40.kept_ref, bf16[752,128]{1,0:T(8,128)(2,1)S(1)} %collective-permute-done.3.cross_ref, ...), custom_call_target="tpu_custom_call" | custom-call | flops 6000000000 | tf_op jit(solution)/shard_map/pallas_call | solution.py:18
  20.2 2.2 %collective-permute-start.5 = (bf16[3392,128]{1,0:T(8,128)(2,1)S(1)}, bf16[3392,128]{1,0:T(8,128)(2,1)S(1)}, u32[]{:S(2)}, u32[]{:S(2)}) collective-permute-start(bf16[3392,128]{1,0:T(8,128)(2,1)S(1)} %get-tuple-element.49), channel_id=1, source_target_pairs={{0,4},{1,5},{2,6},{3,7},{4,0},{5,1},{6,2},{7,3},{8,12},{9,13},{10,... | collective-permute-start | bytes 2605064 | tf_op jit(solution)/shard_map/ppermute | solution.py:478
  22.6 1.7 %collective-permute-done.5.got_ref = bf16[3392,128]{1,0:T(8,128)(2,1)S(1)} collective-permute-done((bf16[3392,128]{1,0:T(8,128)(2,1)S(1)}, bf16[3392,128]{1,0:T(8,128)(2,1)S(1)}, u32[]{:S(2)}, u32[]{:S(2)}) %collective-permute-start.5) | collective-permute-done | bytes 868384 | tf_op jit(solution)/shard_map/ppermute | solution.py:478
  24.5 0.6 collective-permute-start.9
  25.7 2.4 %collective-permute-start.11 = (bf16[432,128]{1,0:T(8,128)(2,1)S(1)}, bf16[432,128]{1,0:T(8,128)(2,1)S(1)}, u32[]{:S(2)}, u32[]{:S(2)}) collective-permute-start(bf16[432,128]{1,0:T(8,128)(2,1)S(1)} %get-tuple-element.57), channel_id=1, source_target_pairs={{0,3},{1,2},{2,1},{3,0},{4,7},{5,6},{6,5},{7,4},{8,11},{9,10},{10,... | collective-permute-start | bytes 331784 | tf_op jit(solution)/shard_map/ppermute | solution.py:478
  28.1 0.5 collective-permute-start.6
  29.2 1.3 %collective-permute-done.9.refs_0_ = bf16[432,128]{1,0:T(8,128)(2,1)S(1)} collective-permute-done((bf16[432,128]{1,0:T(8,128)(2,1)S(1)}, bf16[432,128]{1,0:T(8,128)(2,1)S(1)}, u32[]{:S(2)}, u32[]{:S(2)}) %collective-permute-start.9) | collective-permute-done | bytes 110624 | tf_op jit(solution)/shard_map/ppermute | solution.py:478
  30.5 1.1 %collective-permute-start.8 = (bf16[480,128]{1,0:T(8,128)(2,1)S(1)}, bf16[480,128]{1,0:T(8,128)(2,1)S(1)}, u32[]{:S(2)}, u32[]{:S(2)}) collective-permute-start(bf16[480,128]{1,0:T(8,128)(2,1)S(1)} %get-tuple-element.52), channel_id=1, source_target_pairs={{0,3},{1,2},{2,1},{3,0},{4,7},{5,6},{6,5},{7,4},{8,11},{9,10},{10,... | collective-permute-start | bytes 368648 | tf_op jit(solution)/shard_map/ppermute | solution.py:478
  31.6 1.1 %collective-permute-done.10.refs_1_ = bf16[432,128]{1,0:T(8,128)(2,1)S(1)} collective-permute-done((bf16[432,128]{1,0:T(8,128)(2,1)S(1)}, bf16[432,128]{1,0:T(8,128)(2,1)S(1)}, u32[]{:S(2)}, u32[]{:S(2)}) %collective-permute-start.10) | collective-permute-done | bytes 110624 | tf_op jit(solution)/shard_map/ppermute | solution.py:478
  32.9 3.1 %collective-permute-start.12 = (bf16[112,128]{1,0:T(8,128)(2,1)S(1)}, bf16[112,128]{1,0:T(8,128)(2,1)S(1)}, u32[]{:S(2)}, u32[]{:S(2)}) collective-permute-start(bf16[112,128]{1,0:T(8,128)(2,1)S(1)} %get-tuple-element.59), channel_id=1, source_target_pairs={{0,16},{1,17},{2,18},{3,19},{4,20},{5,21},{6,22},{7,23},{8,24},{9,... | collective-permute-start | bytes 86024 | tf_op jit(solution)/shard_map/ppermute | solution.py:478
  36.0 1.4 %collective-permute-start.13 = (bf16[112,128]{1,0:T(8,128)(2,1)S(1)}, bf16[112,128]{1,0:T(8,128)(2,1)S(1)}, u32[]{:S(2)}, u32[]{:S(2)}) collective-permute-start(bf16[112,128]{1,0:T(8,128)(2,1)S(1)} %get-tuple-element.60), channel_id=1, source_target_pairs={{0,24},{1,25},{2,26},{3,27},{4,28},{5,29},{6,30},{7,31},{8,16},{9,... | collective-permute-start | bytes 86024 | tf_op jit(solution)/shard_map/ppermute | solution.py:478
  37.9 2.9 %collective-permute-start.15 = (bf16[112,128]{1,0:T(8,128)(2,1)S(1)}, bf16[112,128]{1,0:T(8,128)(2,1)S(1)}, u32[]{:S(2)}, u32[]{:S(2)}) collective-permute-start(bf16[112,128]{1,0:T(8,128)(2,1)S(1)} %get-tuple-element.63), channel_id=1, source_target_pairs={{0,16},{1,17},{2,18},{3,19},{4,20},{5,21},{6,22},{7,23},{8,24},{9,... | collective-permute-start | bytes 86024 | tf_op jit(solution)/shard_map/ppermute | solution.py:478
  40.8 1.4 %collective-permute-start.16 = (bf16[112,128]{1,0:T(8,128)(2,1)S(1)}, bf16[112,128]{1,0:T(8,128)(2,1)S(1)}, u32[]{:S(2)}, u32[]{:S(2)}) collective-permute-start(bf16[112,128]{1,0:T(8,128)(2,1)S(1)} %get-tuple-element.64), channel_id=1, source_target_pairs={{0,24},{1,25},{2,26},{3,27},{4,28},{5,29},{6,30},{7,31},{8,16},{9,... | collective-permute-start | bytes 86024 | tf_op jit(solution)/shard_map/ppermute | solution.py:478
  42.8 3.7 %collective-permute-done.16.refs_6_ = bf16[112,128]{1,0:T(8,128)(2,1)S(1)} collective-permute-done((bf16[112,128]{1,0:T(8,128)(2,1)S(1)}, bf16[112,128]{1,0:T(8,128)(2,1)S(1)}, u32[]{:S(2)}, u32[]{:S(2)}) %collective-permute-start.16) | collective-permute-done | bytes 28704 | tf_op jit(solution)/shard_map/ppermute | solution.py:478
  46.5 2.1 %collective-permute-start.20 = (bf16[224,128]{1,0:T(8,128)(2,1)S(1)}, bf16[224,128]{1,0:T(8,128)(2,1)S(1)}, u32[]{:S(2)}, u32[]{:S(2)}) collective-permute-start(bf16[224,128]{1,0:T(8,128)(2,1)S(1)} %shard_map.102.refs_0_), channel_id=1, source_target_pairs={{0,24},{1,25},{2,26},{3,27},{4,28},{5,29},{6,30},{7,31},{8,16},{9,... | collective-permute-start | bytes 172040 | tf_op jit(solution)/shard_map/ppermute | solution.py:478
  48.6 2.4 %collective-permute-start.18 = (bf16[224,128]{1,0:T(8,128)(2,1)S(1)}, bf16[224,128]{1,0:T(8,128)(2,1)S(1)}, u32[]{:S(2)}, u32[]{:S(2)}) collective-permute-start(bf16[224,128]{1,0:T(8,128)(2,1)S(1)} %shard_map.102.refs_0_), channel_id=1, source_target_pairs={{0,8},{1,9},{2,10},{3,11},{4,12},{5,13},{6,14},{7,15},{8,0},{9,1},... | collective-permute-start | bytes 172040 | tf_op jit(solution)/shard_map/ppermute | solution.py:478
  51.0 1.6 %collective-permute-done.20.refs_3_ = bf16[224,128]{1,0:T(8,128)(2,1)S(1)} collective-permute-done((bf16[224,128]{1,0:T(8,128)(2,1)S(1)}, bf16[224,128]{1,0:T(8,128)(2,1)S(1)}, u32[]{:S(2)}, u32[]{:S(2)}) %collective-permute-start.20) | collective-permute-done | bytes 57376 | tf_op jit(solution)/shard_map/ppermute | solution.py:478
  52.6 1.2 %collective-permute-done.19.refs_2_ = bf16[224,128]{1,0:T(8,128)(2,1)S(1)} collective-permute-done((bf16[224,128]{1,0:T(8,128)(2,1)S(1)}, bf16[224,128]{1,0:T(8,128)(2,1)S(1)}, u32[]{:S(2)}, u32[]{:S(2)}) %collective-permute-start.19) | collective-permute-done | bytes 57376 | tf_op jit(solution)/shard_map/ppermute | solution.py:478
  53.9 2.0 %collective-permute-start.23 = (bf16[848,128]{1,0:T(8,128)(2,1)S(1)}, bf16[848,128]{1,0:T(8,128)(2,1)S(1)}, u32[]{:S(2)}, u32[]{:S(2)}) collective-permute-start(bf16[848,128]{1,0:T(8,128)(2,1)S(1)} %shard_map.103.refs_0_), channel_id=1, source_target_pairs={{0,3},{1,2},{2,1},{3,0},{4,7},{5,6},{6,5},{7,4},{8,11},{9,10},{10,... | collective-permute-start | bytes 651272 | tf_op jit(solution)/shard_map/ppermute | solution.py:478
  55.9 2.1 %collective-permute-start.22 = (bf16[848,128]{1,0:T(8,128)(2,1)S(1)}, bf16[848,128]{1,0:T(8,128)(2,1)S(1)}, u32[]{:S(2)}, u32[]{:S(2)}) collective-permute-start(bf16[848,128]{1,0:T(8,128)(2,1)S(1)} %shard_map.103.refs_0_), channel_id=1, source_target_pairs={{0,2},{1,3},{2,0},{3,1},{4,6},{5,7},{6,4},{7,5},{8,10},{9,11},{10,... | collective-permute-start | bytes 651272 | tf_op jit(solution)/shard_map/ppermute | solution.py:478
  58.0 3.6 %collective-permute-done.23.refs_3_ = bf16[848,128]{1,0:T(8,128)(2,1)S(1)} collective-permute-done((bf16[848,128]{1,0:T(8,128)(2,1)S(1)}, bf16[848,128]{1,0:T(8,128)(2,1)S(1)}, u32[]{:S(2)}, u32[]{:S(2)}) %collective-permute-start.23) | collective-permute-done | bytes 217120 | tf_op jit(solution)/shard_map/ppermute | solution.py:478
  61.6 2.0 %collective-permute-done.22.refs_2_ = bf16[848,128]{1,0:T(8,128)(2,1)S(1)} collective-permute-done((bf16[848,128]{1,0:T(8,128)(2,1)S(1)}, bf16[848,128]{1,0:T(8,128)(2,1)S(1)}, u32[]{:S(2)}, u32[]{:S(2)}) %collective-permute-start.22) | collective-permute-done | bytes 217120 | tf_op jit(solution)/shard_map/ppermute | solution.py:478
  64.2 0.9 %shard_map.99 = bf16[4,64,128]{2,1,0:T(8,128)(2,1)} custom-call(bf16[4,64,128]{2,1,0:T(8,128)(2,1)S(1)} %shard_map.97.pieces_ref, bf16[480,128]{1,0:T(8,128)(2,1)S(1)} %collective-permute-done.6.refs_0_, bf16[480,128]{1,0:T(8,128)(2,1)S(1)} %collective-permute-done.7.refs_1_, bf16[480,128]{1,0:T(8,128)(2,1)S(1)} %collective-permute-done.8.refs_2_), custom_call_target="tpu_custom_call" | custom-call | flops 1000000000 | tf_op jit(solution)/shard_map/pallas_call | solution.py:18
  65.4 1.5 %shard_map.104 = (bf16[9,128,128]{2,1,0:T(8,128)(2,1)}, bf16[4,128,256]{2,1,0:T(8,128)(2,1)}, bf16[9,256,256]{2,1,0:T(8,128)(2,1)}) custom-call(bf16[848,128]{1,0:T(8,128)(2,1)S(1)} %shard_map.103.refs_0_, bf16[848,128]{1,0:T(8,128)(2,1)S(1)} %collective-permute-done.21.refs_1_, bf16[848,128]{1,0:T(8,128)(2,1)S(1)} %collective-permute-done.22.refs_2_, ...), custom_call_target="tpu_custom_call" | custom-call | flops 1000000000 | tf_op jit(solution)/shard_map/pallas_call | solution.py:18
  (47 shorter events, 5.5 us)
Async XLA Ops:
  0.6 0.9 %copy-start.3 = (bf16[8,64,128]{2,1,0:T(8,128)(2,1)S(1)}, bf16[8,64,128]{2,1,0:T(8,128)(2,1)}, u32[]{:S(2)}) copy-start(bf16[8,64,128]{2,1,0:T(8,128)(2,1)} %level_ref.3) | copy-start | bytes 393220
  1.8 5.0 %collective-permute-start = (bf16[160,128]{1,0:T(8,128)(2,1)S(1)}, bf16[160,128]{1,0:T(8,128)(2,1)S(1)}, u32[]{:S(2)}, u32[]{:S(2)}) collective-permute-start(bf16[160,128]{1,0:T(8,128)(2,1)S(1)} %get-tuple-element.37), channel_id=1, source_target_pairs={{0,1},{1,0},{2,3},{3,2},{4,5},{5,4},{6,7},{7,6},{8,9},{9,8},{10,11... | collective-permute-start | bytes 122888 | tf_op jit(solution)/shard_map/ppermute | solution.py:478
  4.8 4.0 %collective-permute-start.1 = (bf16[160,128]{1,0:T(8,128)(2,1)S(1)}, bf16[160,128]{1,0:T(8,128)(2,1)S(1)}, u32[]{:S(2)}, u32[]{:S(2)}) collective-permute-start(bf16[160,128]{1,0:T(8,128)(2,1)S(1)} %get-tuple-element.38), channel_id=1, source_target_pairs={{0,2},{1,3},{2,0},{3,1},{4,6},{5,7},{6,4},{7,5},{8,10},{9,11},{10,... | collective-permute-start | bytes 122888 | tf_op jit(solution)/shard_map/ppermute | solution.py:478
  6.3 9.0 %copy-start = (bf16[3,3,256,256]{3,2,1,0:T(8,128)(2,1)S(1)}, bf16[3,3,256,256]{3,2,1,0:T(8,128)(2,1)}, u32[]{:S(2)}) copy-start(bf16[3,3,256,256]{3,2,1,0:T(8,128)(2,1)} %param.8) | copy-start | bytes 3538948
  6.3 9.0 %copy-start.1 = (bf16[3,3,128,128]{3,2,1,0:T(8,128)(2,1)S(1)}, bf16[3,3,128,128]{3,2,1,0:T(8,128)(2,1)}, u32[]{:S(2)}) copy-start(bf16[3,3,128,128]{3,2,1,0:T(8,128)(2,1)} %param.6) | copy-start | bytes 884740
  6.3 9.0 %copy-start.2 = (bf16[2,2,128,256]{3,2,1,0:T(8,128)(2,1)S(1)}, bf16[2,2,128,256]{3,2,1,0:T(8,128)(2,1)}, u32[]{:S(2)}) copy-start(bf16[2,2,128,256]{3,2,1,0:T(8,128)(2,1)} %param.7) | copy-start | bytes 786436
  6.3 4.9 %collective-permute-start.2 = (bf16[160,128]{1,0:T(8,128)(2,1)S(1)}, bf16[160,128]{1,0:T(8,128)(2,1)S(1)}, u32[]{:S(2)}, u32[]{:S(2)}) collective-permute-start(bf16[160,128]{1,0:T(8,128)(2,1)S(1)} %get-tuple-element.39), channel_id=1, source_target_pairs={{0,3},{1,2},{2,1},{3,0},{4,7},{5,6},{6,5},{7,4},{8,11},{9,10},{10,... | collective-permute-start | bytes 122888 | tf_op jit(solution)/shard_map/ppermute | solution.py:478
  11.7 4.3 %collective-permute-start.3 = (bf16[752,128]{1,0:T(8,128)(2,1)S(1)}, bf16[752,128]{1,0:T(8,128)(2,1)S(1)}, u32[]{:S(2)}, u32[]{:S(2)}) collective-permute-start(bf16[752,128]{1,0:T(8,128)(2,1)S(1)} %get-tuple-element.41), channel_id=1, source_target_pairs={{4,8},{5,9},{6,10},{7,11},{8,4},{9,5},{10,6},{11,7},{12,16},{13,17... | collective-permute-start | bytes 577544 | tf_op jit(solution)/shard_map/ppermute | solution.py:478
  12.3 4.1 %collective-permute-start.4 = (bf16[752,128]{1,0:T(8,128)(2,1)S(1)}, bf16[752,128]{1,0:T(8,128)(2,1)S(1)}, u32[]{:S(2)}, u32[]{:S(2)}) collective-permute-start(bf16[752,128]{1,0:T(8,128)(2,1)S(1)} %get-tuple-element.42), channel_id=1, source_target_pairs={{0,4},{1,5},{2,6},{3,7},{4,0},{5,1},{6,2},{7,3},{8,12},{9,13},{10,... | collective-permute-start | bytes 577544 | tf_op jit(solution)/shard_map/ppermute | solution.py:478
  20.2 4.2 %collective-permute-start.5 = (bf16[3392,128]{1,0:T(8,128)(2,1)S(1)}, bf16[3392,128]{1,0:T(8,128)(2,1)S(1)}, u32[]{:S(2)}, u32[]{:S(2)}) collective-permute-start(bf16[3392,128]{1,0:T(8,128)(2,1)S(1)} %get-tuple-element.49), channel_id=1, source_target_pairs={{0,4},{1,5},{2,6},{3,7},{4,0},{5,1},{6,2},{7,3},{8,12},{9,13},{10,... | collective-permute-start | bytes 2605064 | tf_op jit(solution)/shard_map/ppermute | solution.py:478
  24.5 6.0 %collective-permute-start.9 = (bf16[432,128]{1,0:T(8,128)(2,1)S(1)}, bf16[432,128]{1,0:T(8,128)(2,1)S(1)}, u32[]{:S(2)}, u32[]{:S(2)}) collective-permute-start(bf16[432,128]{1,0:T(8,128)(2,1)S(1)} %get-tuple-element.55), channel_id=1, source_target_pairs={{0,1},{1,0},{2,3},{3,2},{4,5},{5,4},{6,7},{7,6},{8,9},{9,8},{10,11... | collective-permute-start | bytes 331784 | tf_op jit(solution)/shard_map/ppermute | solution.py:478
  25.2 7.6 %collective-permute-start.10 = (bf16[432,128]{1,0:T(8,128)(2,1)S(1)}, bf16[432,128]{1,0:T(8,128)(2,1)S(1)}, u32[]{:S(2)}, u32[]{:S(2)}) collective-permute-start(bf16[432,128]{1,0:T(8,128)(2,1)S(1)} %get-tuple-element.56), channel_id=1, source_target_pairs={{0,2},{1,3},{2,0},{3,1},{4,6},{5,7},{6,4},{7,5},{8,10},{9,11},{10,... | collective-permute-start | bytes 331784 | tf_op jit(solution)/shard_map/ppermute | solution.py:478
  25.7 7.2 %collective-permute-start.11 = (bf16[432,128]{1,0:T(8,128)(2,1)S(1)}, bf16[432,128]{1,0:T(8,128)(2,1)S(1)}, u32[]{:S(2)}, u32[]{:S(2)}) collective-permute-start(bf16[432,128]{1,0:T(8,128)(2,1)S(1)} %get-tuple-element.57), channel_id=1, source_target_pairs={{0,3},{1,2},{2,1},{3,0},{4,7},{5,6},{6,5},{7,4},{8,11},{9,10},{10,... | collective-permute-start | bytes 331784 | tf_op jit(solution)/shard_map/ppermute | solution.py:478
  28.1 9.3 %collective-permute-start.6 = (bf16[480,128]{1,0:T(8,128)(2,1)S(1)}, bf16[480,128]{1,0:T(8,128)(2,1)S(1)}, u32[]{:S(2)}, u32[]{:S(2)}) collective-permute-start(bf16[480,128]{1,0:T(8,128)(2,1)S(1)} %get-tuple-element.50), channel_id=1, source_target_pairs={{0,1},{1,0},{2,3},{3,2},{4,5},{5,4},{6,7},{7,6},{8,9},{9,8},{10,11... | collective-permute-start | bytes 368648 | tf_op jit(solution)/shard_map/ppermute | solution.py:478
  28.7 9.2 %collective-permute-start.7 = (bf16[480,128]{1,0:T(8,128)(2,1)S(1)}, bf16[480,128]{1,0:T(8,128)(2,1)S(1)}, u32[]{:S(2)}, u32[]{:S(2)}) collective-permute-start(bf16[480,128]{1,0:T(8,128)(2,1)S(1)} %get-tuple-element.51), channel_id=1, source_target_pairs={{0,2},{1,3},{2,0},{3,1},{4,6},{5,7},{6,4},{7,5},{8,10},{9,11},{10,... | collective-permute-start | bytes 368648 | tf_op jit(solution)/shard_map/ppermute | solution.py:478
  30.5 7.4 %collective-permute-start.8 = (bf16[480,128]{1,0:T(8,128)(2,1)S(1)}, bf16[480,128]{1,0:T(8,128)(2,1)S(1)}, u32[]{:S(2)}, u32[]{:S(2)}) collective-permute-start(bf16[480,128]{1,0:T(8,128)(2,1)S(1)} %get-tuple-element.52), channel_id=1, source_target_pairs={{0,3},{1,2},{2,1},{3,0},{4,7},{5,6},{6,5},{7,4},{8,11},{9,10},{10,... | collective-permute-start | bytes 368648 | tf_op jit(solution)/shard_map/ppermute | solution.py:478
  32.9 9.2 %collective-permute-start.12 = (bf16[112,128]{1,0:T(8,128)(2,1)S(1)}, bf16[112,128]{1,0:T(8,128)(2,1)S(1)}, u32[]{:S(2)}, u32[]{:S(2)}) collective-permute-start(bf16[112,128]{1,0:T(8,128)(2,1)S(1)} %get-tuple-element.59), channel_id=1, source_target_pairs={{0,16},{1,17},{2,18},{3,19},{4,20},{5,21},{6,22},{7,23},{8,24},{9,... | collective-permute-start | bytes 86024 | tf_op jit(solution)/shard_map/ppermute | solution.py:478
  36.0 6.4 %collective-permute-start.13 = (bf16[112,128]{1,0:T(8,128)(2,1)S(1)}, bf16[112,128]{1,0:T(8,128)(2,1)S(1)}, u32[]{:S(2)}, u32[]{:S(2)}) collective-permute-start(bf16[112,128]{1,0:T(8,128)(2,1)S(1)} %get-tuple-element.60), channel_id=1, source_target_pairs={{0,24},{1,25},{2,26},{3,27},{4,28},{5,29},{6,30},{7,31},{8,16},{9,... | collective-permute-start | bytes 86024 | tf_op jit(solution)/shard_map/ppermute | solution.py:478
  37.4 5.0 %collective-permute-start.14 = (bf16[112,128]{1,0:T(8,128)(2,1)S(1)}, bf16[112,128]{1,0:T(8,128)(2,1)S(1)}, u32[]{:S(2)}, u32[]{:S(2)}) collective-permute-start(bf16[112,128]{1,0:T(8,128)(2,1)S(1)} %get-tuple-element.61), channel_id=1, source_target_pairs={{0,8},{1,9},{2,10},{3,11},{4,12},{5,13},{6,14},{7,15},{8,0},{9,1},... | collective-permute-start | bytes 86024 | tf_op jit(solution)/shard_map/ppermute | solution.py:478
  37.9 4.8 %collective-permute-start.15 = (bf16[112,128]{1,0:T(8,128)(2,1)S(1)}, bf16[112,128]{1,0:T(8,128)(2,1)S(1)}, u32[]{:S(2)}, u32[]{:S(2)}) collective-permute-start(bf16[112,128]{1,0:T(8,128)(2,1)S(1)} %get-tuple-element.63), channel_id=1, source_target_pairs={{0,16},{1,17},{2,18},{3,19},{4,20},{5,21},{6,22},{7,23},{8,24},{9,... | collective-permute-start | bytes 86024 | tf_op jit(solution)/shard_map/ppermute | solution.py:478
  40.8 5.7 %collective-permute-start.16 = (bf16[112,128]{1,0:T(8,128)(2,1)S(1)}, bf16[112,128]{1,0:T(8,128)(2,1)S(1)}, u32[]{:S(2)}, u32[]{:S(2)}) collective-permute-start(bf16[112,128]{1,0:T(8,128)(2,1)S(1)} %get-tuple-element.64), channel_id=1, source_target_pairs={{0,24},{1,25},{2,26},{3,27},{4,28},{5,29},{6,30},{7,31},{8,16},{9,... | collective-permute-start | bytes 86024 | tf_op jit(solution)/shard_map/ppermute | solution.py:478
  42.2 4.3 %collective-permute-start.17 = (bf16[112,128]{1,0:T(8,128)(2,1)S(1)}, bf16[112,128]{1,0:T(8,128)(2,1)S(1)}, u32[]{:S(2)}, u32[]{:S(2)}) collective-permute-start(bf16[112,128]{1,0:T(8,128)(2,1)S(1)} %get-tuple-element.65), channel_id=1, source_target_pairs={{0,8},{1,9},{2,10},{3,11},{4,12},{5,13},{6,14},{7,15},{8,0},{9,1},... | collective-permute-start | bytes 86024 | tf_op jit(solution)/shard_map/ppermute | solution.py:478
  46.5 6.0 %collective-permute-start.20 = (bf16[224,128]{1,0:T(8,128)(2,1)S(1)}, bf16[224,128]{1,0:T(8,128)(2,1)S(1)}, u32[]{:S(2)}, u32[]{:S(2)}) collective-permute-start(bf16[224,128]{1,0:T(8,128)(2,1)S(1)} %shard_map.102.refs_0_), channel_id=1, source_target_pairs={{0,24},{1,25},{2,26},{3,27},{4,28},{5,29},{6,30},{7,31},{8,16},{9,... | collective-permute-start | bytes 172040 | tf_op jit(solution)/shard_map/ppermute | solution.py:478
  48.6 5.2 %collective-permute-start.19 = (bf16[224,128]{1,0:T(8,128)(2,1)S(1)}, bf16[224,128]{1,0:T(8,128)(2,1)S(1)}, u32[]{:S(2)}, u32[]{:S(2)}) collective-permute-start(bf16[224,128]{1,0:T(8,128)(2,1)S(1)} %shard_map.102.refs_0_), channel_id=1, source_target_pairs={{0,16},{1,17},{2,18},{3,19},{4,20},{5,21},{6,22},{7,23},{8,24},{9,... | collective-permute-start | bytes 172040 | tf_op jit(solution)/shard_map/ppermute | solution.py:478
  48.6 5.2 %collective-permute-start.18 = (bf16[224,128]{1,0:T(8,128)(2,1)S(1)}, bf16[224,128]{1,0:T(8,128)(2,1)S(1)}, u32[]{:S(2)}, u32[]{:S(2)}) collective-permute-start(bf16[224,128]{1,0:T(8,128)(2,1)S(1)} %shard_map.102.refs_0_), channel_id=1, source_target_pairs={{0,8},{1,9},{2,10},{3,11},{4,12},{5,13},{6,14},{7,15},{8,0},{9,1},... | collective-permute-start | bytes 172040 | tf_op jit(solution)/shard_map/ppermute | solution.py:478
  53.9 7.8 %collective-permute-start.23 = (bf16[848,128]{1,0:T(8,128)(2,1)S(1)}, bf16[848,128]{1,0:T(8,128)(2,1)S(1)}, u32[]{:S(2)}, u32[]{:S(2)}) collective-permute-start(bf16[848,128]{1,0:T(8,128)(2,1)S(1)} %shard_map.103.refs_0_), channel_id=1, source_target_pairs={{0,3},{1,2},{2,1},{3,0},{4,7},{5,6},{6,5},{7,4},{8,11},{9,10},{10,... | collective-permute-start | bytes 651272 | tf_op jit(solution)/shard_map/ppermute | solution.py:478
  55.9 7.8 %collective-permute-start.22 = (bf16[848,128]{1,0:T(8,128)(2,1)S(1)}, bf16[848,128]{1,0:T(8,128)(2,1)S(1)}, u32[]{:S(2)}, u32[]{:S(2)}) collective-permute-start(bf16[848,128]{1,0:T(8,128)(2,1)S(1)} %shard_map.103.refs_0_), channel_id=1, source_target_pairs={{0,2},{1,3},{2,0},{3,1},{4,6},{5,7},{6,4},{7,5},{8,10},{9,11},{10,... | collective-permute-start | bytes 651272 | tf_op jit(solution)/shard_map/ppermute | solution.py:478
  58.0 5.9 %collective-permute-start.21 = (bf16[848,128]{1,0:T(8,128)(2,1)S(1)}, bf16[848,128]{1,0:T(8,128)(2,1)S(1)}, u32[]{:S(2)}, u32[]{:S(2)}) collective-permute-start(bf16[848,128]{1,0:T(8,128)(2,1)S(1)} %shard_map.103.refs_0_), channel_id=1, source_target_pairs={{0,1},{1,0},{2,3},{3,2},{4,5},{5,4},{6,7},{7,6},{8,9},{9,8},{10,11... | collective-permute-start | bytes 651272 | tf_op jit(solution)/shard_map/ppermute | solution.py:478
  58.0 7.0 %collective-permute-start.24 = (bf16[848,128]{1,0:T(8,128)(2,1)S(1)}, bf16[848,128]{1,0:T(8,128)(2,1)S(1)}, u32[]{:S(2)}, u32[]{:S(2)}) collective-permute-start(bf16[848,128]{1,0:T(8,128)(2,1)S(1)} %shard_map.103.refs_0_), channel_id=1, source_target_pairs={{0,4},{1,5},{2,6},{3,7},{4,0},{5,1},{6,2},{7,3},{8,12},{9,13},{10,... | collective-permute-start | bytes 651272 | tf_op jit(solution)/shard_map/ppermute | solution.py:478
  61.6 3.4 %collective-permute-start.27 = (bf16[848,128]{1,0:T(8,128)(2,1)S(1)}, bf16[848,128]{1,0:T(8,128)(2,1)S(1)}, u32[]{:S(2)}, u32[]{:S(2)}) collective-permute-start(bf16[848,128]{1,0:T(8,128)(2,1)S(1)} %collective-permute-done.23.refs_3_), channel_id=1, source_target_pairs={{0,4},{1,5},{2,6},{3,7},{4,0},{5,1},{6,2},{7,3},{8,12},{9,13},{10,... | collective-permute-start | bytes 651272 | tf_op jit(solution)/shard_map/ppermute | solution.py:478
  63.7 1.5 %collective-permute-start.26 = (bf16[848,128]{1,0:T(8,128)(2,1)S(1)}, bf16[848,128]{1,0:T(8,128)(2,1)S(1)}, u32[]{:S(2)}, u32[]{:S(2)}) collective-permute-start(bf16[848,128]{1,0:T(8,128)(2,1)S(1)} %collective-permute-done.22.refs_2_), channel_id=1, source_target_pairs={{0,4},{1,5},{2,6},{3,7},{4,0},{5,1},{6,2},{7,3},{8,12},{9,13},{10,... | collective-permute-start | bytes 651272 | tf_op jit(solution)/shard_map/ppermute | solution.py:478
  63.9 1.5 %collective-permute-start.25 = (bf16[848,128]{1,0:T(8,128)(2,1)S(1)}, bf16[848,128]{1,0:T(8,128)(2,1)S(1)}, u32[]{:S(2)}, u32[]{:S(2)}) collective-permute-start(bf16[848,128]{1,0:T(8,128)(2,1)S(1)} %collective-permute-done.21.refs_1_), channel_id=1, source_target_pairs={{0,4},{1,5},{2,6},{3,7},{4,0},{5,1},{6,2},{7,3},{8,12},{9,13},{10,... | collective-permute-start | bytes 651272 | tf_op jit(solution)/shard_map/ppermute | solution.py:478
  (1 other events, 0.9 us)

commit v6 on v5

--- a/solution.py
+++ b/solution.py
@@ -211,7 +211,7 @@
         field[low : low + HALO, cols + SIDE : 2 * pitch - SIDE] = jnp.zeros(
             (HALO, 2 * pitch - cols - 2 * SIDE, 128), F32
         )
-        field[low : low + HALO, 2 * pitch - SIDE :] = band[:, cols + SIDE :]
+        field[low : low + HALO, 2 * pitch - SIDE : 2 * pitch] = band[:, cols + SIDE :]
         for i in range(2):
             spot = cells + 2 * pitch * i
             cot_all[low_neck + i, :, :128] = ref[spot : spot + pitch]
@@ -228,7 +228,7 @@
         take(cross_ref, HALO + rows, 2 + half_rows)
 
     own = kept_ref[0 : 2 * rows * pitch].reshape(rows, 2 * pitch, 128)
-    field[HALO : HALO + rows] = own.astype(F32)
+    field[HALO : HALO + rows, : 2 * pitch] = own.astype(F32)
     for row_in in range(half_rows):
         low = 2 * (rows + row_in) * pitch
         cot_all[2 + row_in, :, :128] = kept_ref[low : low + pitch]
@@ -303,7 +303,7 @@
     value = value + lback[2 : 2 + rows, :half_cols]
     spread[:, pl.ds(0, half_cols, stride=2), :] = value[:, :, :128]
     spread[:, pl.ds(1, half_cols, stride=2), :] = value[:, :, 128:]
-    grad_ref[...] = spread[...].astype(BF)
+    grad_ref[...] = spread[:, :cols].astype(BF)
 
     weight_sums(sizes, sums_ref, neck, gate, act, ngrad, pair, side, lgate)
     half = send_ref.shape[0]
@@ -532,7 +532,7 @@
         [shape((2 * half, 128)), shape((half, 128)), shape((half_rows * half_cols, total)), shape(level_in.shape)],
         (kept, cross, inner, wfwd, wbwd, wd, wdt, wn, wnt),
         [
-            pltpu.VMEM((far, 2 * pitch, 128), F32),
+            pltpu.VMEM((far, 2 * pitch + 8, 128), F32),
             pltpu.VMEM((far, pitch, 256), BF),
             pltpu.VMEM((far, pitch, 256), BF),
             pltpu.VMEM((far - 2, pitch, 256), BF),
@@ -544,7 +544,7 @@
             pltpu.VMEM((rows + 4, pitch, 256), F32),
             pltpu.VMEM((rows + 4, pitch, 256), BF),
             pltpu.VMEM((rows + 4, pitch, 256), BF),
-            pltpu.VMEM((rows, cols, 128), F32),
+            pltpu.VMEM((rows, cols + 8, 128), F32),
         ],
         limit=20,
         flops=6 * 10**9,

time: 67.1 us -> 67.1 us (level)
  no operation moved by 1% of the time
where the time goes in v6:
time: 67.1 us; the launch traced here: 66.9 us
  starting transfers between devices  34.2 us (51%)
  waiting for transfers between devices  23 us (34%)
  Pallas kernels  8.1 us (12%)
  local copies, waits for them, and re-layouts  0.89 us (1%)
  between operations  0.75 us (1%)
    ppermute x28, starting transfers between devices, permute(): lax.ppermute(value, axes, [(a, b) for a, b in pairs if b is not None])  34.2 us
    ppermute x28, waiting for transfers between devices, permute(): lax.ppermute(value, axes, [(a, b) for a, b in pairs if b is not None])  23 us
    pallas_call x13, Pallas kernels, call(): pl.pallas_call(body, out_shape=out_shapes, in_specs=[VMEM] * len(args), o...  8.1 us
  transfers between devices with their start and end apart: 28, of which 18 were waited for; matrix products, arithmetic and copies ran while one was open for 0% of the time, Pallas kernels for 3%

profile of v6, /device:TPU:0, one launch (start us, length us, event | category | flops | bytes accessed | tf_op | source)
XLA Modules:
  0.0 66.9 jit_solution(18224186943923728151)
XLA Ops:
  0.7 0.9 %copy-done.3 = bf16[8,64,128]{2,1,0:T(8,128)(2,1)S(1)} copy-done((bf16[8,64,128]{2,1,0:T(8,128)(2,1)S(1)}, bf16[8,64,128]{2,1,0:T(8,128)(2,1)}, u32[]{:S(2)}) %copy-start.3) | copy-done | bytes 131096
  1.8 3.0 %collective-permute-start = (bf16[160,128]{1,0:T(8,128)(2,1)S(1)}, bf16[160,128]{1,0:T(8,128)(2,1)S(1)}, u32[]{:S(2)}, u32[]{:S(2)}) collective-permute-start(bf16[160,128]{1,0:T(8,128)(2,1)S(1)} %get-tuple-element.37), channel_id=1, source_target_pairs={{0,1},{1,0},{2,3},{3,2},{4,5},{5,4},{6,7},{7,6},{8,9},{9,8},{10,11... | collective-permute-start | bytes 122888 | tf_op jit(solution)/shard_map/ppermute | solution.py:478
  4.8 1.5 %collective-permute-start.1 = (bf16[160,128]{1,0:T(8,128)(2,1)S(1)}, bf16[160,128]{1,0:T(8,128)(2,1)S(1)}, u32[]{:S(2)}, u32[]{:S(2)}) collective-permute-start(bf16[160,128]{1,0:T(8,128)(2,1)S(1)} %get-tuple-element.38), channel_id=1, source_target_pairs={{0,2},{1,3},{2,0},{3,1},{4,6},{5,7},{6,4},{7,5},{8,10},{9,11},{10,... | collective-permute-start | bytes 122888 | tf_op jit(solution)/shard_map/ppermute | solution.py:478
  6.8 2.0 %collective-permute-done.1.refs_1_ = bf16[160,128]{1,0:T(8,128)(2,1)S(1)} collective-permute-done((bf16[160,128]{1,0:T(8,128)(2,1)S(1)}, bf16[160,128]{1,0:T(8,128)(2,1)S(1)}, u32[]{:S(2)}, u32[]{:S(2)}) %collective-permute-start.1) | collective-permute-done | bytes 40992 | tf_op jit(solution)/shard_map/ppermute | solution.py:478
  8.8 2.4 %collective-permute-done.2.refs_2_ = bf16[160,128]{1,0:T(8,128)(2,1)S(1)} collective-permute-done((bf16[160,128]{1,0:T(8,128)(2,1)S(1)}, bf16[160,128]{1,0:T(8,128)(2,1)S(1)}, u32[]{:S(2)}, u32[]{:S(2)}) %collective-permute-start.2) | collective-permute-done | bytes 40992 | tf_op jit(solution)/shard_map/ppermute | solution.py:478
  11.7 0.7 %collective-permute-start.3 = (bf16[752,128]{1,0:T(8,128)(2,1)S(1)}, bf16[752,128]{1,0:T(8,128)(2,1)S(1)}, u32[]{:S(2)}, u32[]{:S(2)}) collective-permute-start(bf16[752,128]{1,0:T(8,128)(2,1)S(1)} %get-tuple-element.41), channel_id=1, source_target_pairs={{4,8},{5,9},{6,10},{7,11},{8,4},{9,5},{10,6},{11,7},{12,16},{13,17... | collective-permute-start | bytes 577544 | tf_op jit(solution)/shard_map/ppermute | solution.py:478
  12.3 3.0 %collective-permute-start.4 = (bf16[752,128]{1,0:T(8,128)(2,1)S(1)}, bf16[752,128]{1,0:T(8,128)(2,1)S(1)}, u32[]{:S(2)}, u32[]{:S(2)}) collective-permute-start(bf16[752,128]{1,0:T(8,128)(2,1)S(1)} %get-tuple-element.42), channel_id=1, source_target_pairs={{0,4},{1,5},{2,6},{3,7},{4,0},{5,1},{6,2},{7,3},{8,12},{9,13},{10,... | collective-permute-start | bytes 577544 | tf_op jit(solution)/shard_map/ppermute | solution.py:478
  15.3 0.6 shard_map.95
  16.4 3.8 %shard_map.96 = (bf16[6784,128]{1,0:T(8,128)(2,1)S(1)}, bf16[3392,128]{1,0:T(8,128)(2,1)S(1)}, bf16[128,256]{1,0:T(8,128)(2,1)S(1)}, bf16[8,64,128]{2,1,0:T(8,128)(2,1)}) custom-call(bf16[1152,128]{1,0:T(8,128)(2,1)S(1)} %get-tuple-element.40.kept_ref, bf16[752,128]{1,0:T(8,128)(2,1)S(1)} %collective-permute-done.3.cross_ref, ...), custom_call_target="tpu_custom_call" | custom-call | flops 6000000000 | tf_op jit(solution)/shard_map/pallas_call | solution.py:18
  20.2 2.2 %collective-permute-start.5 = (bf16[3392,128]{1,0:T(8,128)(2,1)S(1)}, bf16[3392,128]{1,0:T(8,128)(2,1)S(1)}, u32[]{:S(2)}, u32[]{:S(2)}) collective-permute-start(bf16[3392,128]{1,0:T(8,128)(2,1)S(1)} %get-tuple-element.49), channel_id=1, source_target_pairs={{0,4},{1,5},{2,6},{3,7},{4,0},{5,1},{6,2},{7,3},{8,12},{9,13},{10,... | collective-permute-start | bytes 2605064 | tf_op jit(solution)/shard_map/ppermute | solution.py:478
  22.6 1.7 %collective-permute-done.5.got_ref = bf16[3392,128]{1,0:T(8,128)(2,1)S(1)} collective-permute-done((bf16[3392,128]{1,0:T(8,128)(2,1)S(1)}, bf16[3392,128]{1,0:T(8,128)(2,1)S(1)}, u32[]{:S(2)}, u32[]{:S(2)}) %collective-permute-start.5) | collective-permute-done | bytes 868384 | tf_op jit(solution)/shard_map/ppermute | solution.py:478
  24.5 0.6 collective-permute-start.9
  25.7 2.4 %collective-permute-start.11 = (bf16[432,128]{1,0:T(8,128)(2,1)S(1)}, bf16[432,128]{1,0:T(8,128)(2,1)S(1)}, u32[]{:S(2)}, u32[]{:S(2)}) collective-permute-start(bf16[432,128]{1,0:T(8,128)(2,1)S(1)} %get-tuple-element.57), channel_id=1, source_target_pairs={{0,3},{1,2},{2,1},{3,0},{4,7},{5,6},{6,5},{7,4},{8,11},{9,10},{10,... | collective-permute-start | bytes 331784 | tf_op jit(solution)/shard_map/ppermute | solution.py:478
  28.1 0.5 collective-permute-start.6
  29.2 1.3 %collective-permute-done.9.refs_0_ = bf16[432,128]{1,0:T(8,128)(2,1)S(1)} collective-permute-done((bf16[432,128]{1,0:T(8,128)(2,1)S(1)}, bf16[432,128]{1,0:T(8,128)(2,1)S(1)}, u32[]{:S(2)}, u32[]{:S(2)}) %collective-permute-start.9) | collective-permute-done | bytes 110624 | tf_op jit(solution)/shard_map/ppermute | solution.py:478
  30.5 1.1 %collective-permute-start.8 = (bf16[480,128]{1,0:T(8,128)(2,1)S(1)}, bf16[480,128]{1,0:T(8,128)(2,1)S(1)}, u32[]{:S(2)}, u32[]{:S(2)}) collective-permute-start(bf16[480,128]{1,0:T(8,128)(2,1)S(1)} %get-tuple-element.52), channel_id=1, source_target_pairs={{0,3},{1,2},{2,1},{3,0},{4,7},{5,6},{6,5},{7,4},{8,11},{9,10},{10,... | collective-permute-start | bytes 368648 | tf_op jit(solution)/shard_map/ppermute | solution.py:478
  31.6 1.1 %collective-permute-done.10.refs_1_ = bf16[432,128]{1,0:T(8,128)(2,1)S(1)} collective-permute-done((bf16[432,128]{1,0:T(8,128)(2,1)S(1)}, bf16[432,128]{1,0:T(8,128)(2,1)S(1)}, u32[]{:S(2)}, u32[]{:S(2)}) %collective-permute-start.10) | collective-permute-done | bytes 110624 | tf_op jit(solution)/shard_map/ppermute | solution.py:478
  32.9 3.1 %collective-permute-start.12 = (bf16[112,128]{1,0:T(8,128)(2,1)S(1)}, bf16[112,128]{1,0:T(8,128)(2,1)S(1)}, u32[]{:S(2)}, u32[]{:S(2)}) collective-permute-start(bf16[112,128]{1,0:T(8,128)(2,1)S(1)} %get-tuple-element.59), channel_id=1, source_target_pairs={{0,16},{1,17},{2,18},{3,19},{4,20},{5,21},{6,22},{7,23},{8,24},{9,... | collective-permute-start | bytes 86024 | tf_op jit(solution)/shard_map/ppermute | solution.py:478
  36.0 1.4 %collective-permute-start.13 = (bf16[112,128]{1,0:T(8,128)(2,1)S(1)}, bf16[112,128]{1,0:T(8,128)(2,1)S(1)}, u32[]{:S(2)}, u32[]{:S(2)}) collective-permute-start(bf16[112,128]{1,0:T(8,128)(2,1)S(1)} %get-tuple-element.60), channel_id=1, source_target_pairs={{0,24},{1,25},{2,26},{3,27},{4,28},{5,29},{6,30},{7,31},{8,16},{9,... | collective-permute-start | bytes 86024 | tf_op jit(solution)/shard_map/ppermute | solution.py:478
  37.9 2.9 %collective-permute-start.15 = (bf16[112,128]{1,0:T(8,128)(2,1)S(1)}, bf16[112,128]{1,0:T(8,128)(2,1)S(1)}, u32[]{:S(2)}, u32[]{:S(2)}) collective-permute-start(bf16[112,128]{1,0:T(8,128)(2,1)S(1)} %get-tuple-element.63), channel_id=1, source_target_pairs={{0,16},{1,17},{2,18},{3,19},{4,20},{5,21},{6,22},{7,23},{8,24},{9,... | collective-permute-start | bytes 86024 | tf_op jit(solution)/shard_map/ppermute | solution.py:478
  40.8 1.4 %collective-permute-start.16 = (bf16[112,128]{1,0:T(8,128)(2,1)S(1)}, bf16[112,128]{1,0:T(8,128)(2,1)S(1)}, u32[]{:S(2)}, u32[]{:S(2)}) collective-permute-start(bf16[112,128]{1,0:T(8,128)(2,1)S(1)} %get-tuple-element.64), channel_id=1, source_target_pairs={{0,24},{1,25},{2,26},{3,27},{4,28},{5,29},{6,30},{7,31},{8,16},{9,... | collective-permute-start | bytes 86024 | tf_op jit(solution)/shard_map/ppermute | solution.py:478
  42.8 3.7 %collective-permute-done.16.refs_6_ = bf16[112,128]{1,0:T(8,128)(2,1)S(1)} collective-permute-done((bf16[112,128]{1,0:T(8,128)(2,1)S(1)}, bf16[112,128]{1,0:T(8,128)(2,1)S(1)}, u32[]{:S(2)}, u32[]{:S(2)}) %collective-permute-start.16) | collective-permute-done | bytes 28704 | tf_op jit(solution)/shard_map/ppermute | solution.py:478
  46.5 2.1 %collective-permute-start.20 = (bf16[224,128]{1,0:T(8,128)(2,1)S(1)}, bf16[224,128]{1,0:T(8,128)(2,1)S(1)}, u32[]{:S(2)}, u32[]{:S(2)}) collective-permute-start(bf16[224,128]{1,0:T(8,128)(2,1)S(1)} %shard_map.102.refs_0_), channel_id=1, source_target_pairs={{0,24},{1,25},{2,26},{3,27},{4,28},{5,29},{6,30},{7,31},{8,16},{9,... | collective-permute-start | bytes 172040 | tf_op jit(solution)/shard_map/ppermute | solution.py:478
  48.6 2.4 %collective-permute-start.18 = (bf16[224,128]{1,0:T(8,128)(2,1)S(1)}, bf16[224,128]{1,0:T(8,128)(2,1)S(1)}, u32[]{:S(2)}, u32[]{:S(2)}) collective-permute-start(bf16[224,128]{1,0:T(8,128)(2,1)S(1)} %shard_map.102.refs_0_), channel_id=1, source_target_pairs={{0,8},{1,9},{2,10},{3,11},{4,12},{5,13},{6,14},{7,15},{8,0},{9,1},... | collective-permute-start | bytes 172040 | tf_op jit(solution)/shard_map/ppermute | solution.py:478
  51.0 1.6 %collective-permute-done.20.refs_3_ = bf16[224,128]{1,0:T(8,128)(2,1)S(1)} collective-permute-done((bf16[224,128]{1,0:T(8,128)(2,1)S(1)}, bf16[224,128]{1,0:T(8,128)(2,1)S(1)}, u32[]{:S(2)}, u32[]{:S(2)}) %collective-permute-start.20) | collective-permute-done | bytes 57376 | tf_op jit(solution)/shard_map/ppermute | solution.py:478
  52.6 1.2 %collective-permute-done.19.refs_2_ = bf16[224,128]{1,0:T(8,128)(2,1)S(1)} collective-permute-done((bf16[224,128]{1,0:T(8,128)(2,1)S(1)}, bf16[224,128]{1,0:T(8,128)(2,1)S(1)}, u32[]{:S(2)}, u32[]{:S(2)}) %collective-permute-start.19) | collective-permute-done | bytes 57376 | tf_op jit(solution)/shard_map/ppermute | solution.py:478
  53.9 2.0 %collective-permute-start.23 = (bf16[848,128]{1,0:T(8,128)(2,1)S(1)}, bf16[848,128]{1,0:T(8,128)(2,1)S(1)}, u32[]{:S(2)}, u32[]{:S(2)}) collective-permute-start(bf16[848,128]{1,0:T(8,128)(2,1)S(1)} %shard_map.103.refs_0_), channel_id=1, source_target_pairs={{0,3},{1,2},{2,1},{3,0},{4,7},{5,6},{6,5},{7,4},{8,11},{9,10},{10,... | collective-permute-start | bytes 651272 | tf_op jit(solution)/shard_map/ppermute | solution.py:478
  55.9 2.1 %collective-permute-start.22 = (bf16[848,128]{1,0:T(8,128)(2,1)S(1)}, bf16[848,128]{1,0:T(8,128)(2,1)S(1)}, u32[]{:S(2)}, u32[]{:S(2)}) collective-permute-start(bf16[848,128]{1,0:T(8,128)(2,1)S(1)} %shard_map.103.refs_0_), channel_id=1, source_target_pairs={{0,2},{1,3},{2,0},{3,1},{4,6},{5,7},{6,4},{7,5},{8,10},{9,11},{10,... | collective-permute-start | bytes 651272 | tf_op jit(solution)/shard_map/ppermute | solution.py:478
  58.0 3.6 %collective-permute-done.23.refs_3_ = bf16[848,128]{1,0:T(8,128)(2,1)S(1)} collective-permute-done((bf16[848,128]{1,0:T(8,128)(2,1)S(1)}, bf16[848,128]{1,0:T(8,128)(2,1)S(1)}, u32[]{:S(2)}, u32[]{:S(2)}) %collective-permute-start.23) | collective-permute-done | bytes 217120 | tf_op jit(solution)/shard_map/ppermute | solution.py:478
  61.6 2.0 %collective-permute-done.22.refs_2_ = bf16[848,128]{1,0:T(8,128)(2,1)S(1)} collective-permute-done((bf16[848,128]{1,0:T(8,128)(2,1)S(1)}, bf16[848,128]{1,0:T(8,128)(2,1)S(1)}, u32[]{:S(2)}, u32[]{:S(2)}) %collective-permute-start.22) | collective-permute-done | bytes 217120 | tf_op jit(solution)/shard_map/ppermute | solution.py:478
  64.2 0.9 %shard_map.99 = bf16[4,64,128]{2,1,0:T(8,128)(2,1)} custom-call(bf16[4,64,128]{2,1,0:T(8,128)(2,1)S(1)} %shard_map.97.pieces_ref, bf16[480,128]{1,0:T(8,128)(2,1)S(1)} %collective-permute-done.6.refs_0_, bf16[480,128]{1,0:T(8,128)(2,1)S(1)} %collective-permute-done.7.refs_1_, bf16[480,128]{1,0:T(8,128)(2,1)S(1)} %collective-permute-done.8.refs_2_), custom_call_target="tpu_custom_call" | custom-call | flops 1000000000 | tf_op jit(solution)/shard_map/pallas_call | solution.py:18
  65.4 1.5 %shard_map.104 = (bf16[9,128,128]{2,1,0:T(8,128)(2,1)}, bf16[4,128,256]{2,1,0:T(8,128)(2,1)}, bf16[9,256,256]{2,1,0:T(8,128)(2,1)}) custom-call(bf16[848,128]{1,0:T(8,128)(2,1)S(1)} %shard_map.103.refs_0_, bf16[848,128]{1,0:T(8,128)(2,1)S(1)} %collective-permute-done.21.refs_1_, bf16[848,128]{1,0:T(8,128)(2,1)S(1)} %collective-permute-done.22.refs_2_, ...), custom_call_target="tpu_custom_call" | custom-call | flops 1000000000 | tf_op jit(solution)/shard_map/pallas_call | solution.py:18
  (47 shorter events, 5.5 us)
Async XLA Ops:
  0.6 0.9 %copy-start.3 = (bf16[8,64,128]{2,1,0:T(8,128)(2,1)S(1)}, bf16[8,64,128]{2,1,0:T(8,128)(2,1)}, u32[]{:S(2)}) copy-start(bf16[8,64,128]{2,1,0:T(8,128)(2,1)} %level_ref.3) | copy-start | bytes 393220
  1.8 5.0 %collective-permute-start = (bf16[160,128]{1,0:T(8,128)(2,1)S(1)}, bf16[160,128]{1,0:T(8,128)(2,1)S(1)}, u32[]{:S(2)}, u32[]{:S(2)}) collective-permute-start(bf16[160,128]{1,0:T(8,128)(2,1)S(1)} %get-tuple-element.37), channel_id=1, source_target_pairs={{0,1},{1,0},{2,3},{3,2},{4,5},{5,4},{6,7},{7,6},{8,9},{9,8},{10,11... | collective-permute-start | bytes 122888 | tf_op jit(solution)/shard_map/ppermute | solution.py:478
  4.8 4.0 %collective-permute-start.1 = (bf16[160,128]{1,0:T(8,128)(2,1)S(1)}, bf16[160,128]{1,0:T(8,128)(2,1)S(1)}, u32[]{:S(2)}, u32[]{:S(2)}) collective-permute-start(bf16[160,128]{1,0:T(8,128)(2,1)S(1)} %get-tuple-element.38), channel_id=1, source_target_pairs={{0,2},{1,3},{2,0},{3,1},{4,6},{5,7},{6,4},{7,5},{8,10},{9,11},{10,... | collective-permute-start | bytes 122888 | tf_op jit(solution)/shard_map/ppermute | solution.py:478
  6.3 9.0 %copy-start = (bf16[3,3,256,256]{3,2,1,0:T(8,128)(2,1)S(1)}, bf16[3,3,256,256]{3,2,1,0:T(8,128)(2,1)}, u32[]{:S(2)}) copy-start(bf16[3,3,256,256]{3,2,1,0:T(8,128)(2,1)} %param.8) | copy-start | bytes 3538948
  6.3 9.0 %copy-start.1 = (bf16[3,3,128,128]{3,2,1,0:T(8,128)(2,1)S(1)}, bf16[3,3,128,128]{3,2,1,0:T(8,128)(2,1)}, u32[]{:S(2)}) copy-start(bf16[3,3,128,128]{3,2,1,0:T(8,128)(2,1)} %param.6) | copy-start | bytes 884740
  6.3 9.0 %copy-start.2 = (bf16[2,2,128,256]{3,2,1,0:T(8,128)(2,1)S(1)}, bf16[2,2,128,256]{3,2,1,0:T(8,128)(2,1)}, u32[]{:S(2)}) copy-start(bf16[2,2,128,256]{3,2,1,0:T(8,128)(2,1)} %param.7) | copy-start | bytes 786436
  6.3 4.9 %collective-permute-start.2 = (bf16[160,128]{1,0:T(8,128)(2,1)S(1)}, bf16[160,128]{1,0:T(8,128)(2,1)S(1)}, u32[]{:S(2)}, u32[]{:S(2)}) collective-permute-start(bf16[160,128]{1,0:T(8,128)(2,1)S(1)} %get-tuple-element.39), channel_id=1, source_target_pairs={{0,3},{1,2},{2,1},{3,0},{4,7},{5,6},{6,5},{7,4},{8,11},{9,10},{10,... | collective-permute-start | bytes 122888 | tf_op jit(solution)/shard_map/ppermute | solution.py:478
  11.7 4.3 %collective-permute-start.3 = (bf16[752,128]{1,0:T(8,128)(2,1)S(1)}, bf16[752,128]{1,0:T(8,128)(2,1)S(1)}, u32[]{:S(2)}, u32[]{:S(2)}) collective-permute-start(bf16[752,128]{1,0:T(8,128)(2,1)S(1)} %get-tuple-element.41), channel_id=1, source_target_pairs={{4,8},{5,9},{6,10},{7,11},{8,4},{9,5},{10,6},{11,7},{12,16},{13,17... | collective-permute-start | bytes 577544 | tf_op jit(solution)/shard_map/ppermute | solution.py:478
  12.3 4.1 %collective-permute-start.4 = (bf16[752,128]{1,0:T(8,128)(2,1)S(1)}, bf16[752,128]{1,0:T(8,128)(2,1)S(1)}, u32[]{:S(2)}, u32[]{:S(2)}) collective-permute-start(bf16[752,128]{1,0:T(8,128)(2,1)S(1)} %get-tuple-element.42), channel_id=1, source_target_pairs={{0,4},{1,5},{2,6},{3,7},{4,0},{5,1},{6,2},{7,3},{8,12},{9,13},{10,... | collective-permute-start | bytes 577544 | tf_op jit(solution)/shard_map/ppermute | solution.py:478
  20.2 4.2 %collective-permute-start.5 = (bf16[3392,128]{1,0:T(8,128)(2,1)S(1)}, bf16[3392,128]{1,0:T(8,128)(2,1)S(1)}, u32[]{:S(2)}, u32[]{:S(2)}) collective-permute-start(bf16[3392,128]{1,0:T(8,128)(2,1)S(1)} %get-tuple-element.49), channel_id=1, source_target_pairs={{0,4},{1,5},{2,6},{3,7},{4,0},{5,1},{6,2},{7,3},{8,12},{9,13},{10,... | collective-permute-start | bytes 2605064 | tf_op jit(solution)/shard_map/ppermute | solution.py:478
  24.5 6.0 %collective-permute-start.9 = (bf16[432,128]{1,0:T(8,128)(2,1)S(1)}, bf16[432,128]{1,0:T(8,128)(2,1)S(1)}, u32[]{:S(2)}, u32[]{:S(2)}) collective-permute-start(bf16[432,128]{1,0:T(8,128)(2,1)S(1)} %get-tuple-element.55), channel_id=1, source_target_pairs={{0,1},{1,0},{2,3},{3,2},{4,5},{5,4},{6,7},{7,6},{8,9},{9,8},{10,11... | collective-permute-start | bytes 331784 | tf_op jit(solution)/shard_map/ppermute | solution.py:478
  25.2 7.5 %collective-permute-start.10 = (bf16[432,128]{1,0:T(8,128)(2,1)S(1)}, bf16[432,128]{1,0:T(8,128)(2,1)S(1)}, u32[]{:S(2)}, u32[]{:S(2)}) collective-permute-start(bf16[432,128]{1,0:T(8,128)(2,1)S(1)} %get-tuple-element.56), channel_id=1, source_target_pairs={{0,2},{1,3},{2,0},{3,1},{4,6},{5,7},{6,4},{7,5},{8,10},{9,11},{10,... | collective-permute-start | bytes 331784 | tf_op jit(solution)/shard_map/ppermute | solution.py:478
  25.7 7.2 %collective-permute-start.11 = (bf16[432,128]{1,0:T(8,128)(2,1)S(1)}, bf16[432,128]{1,0:T(8,128)(2,1)S(1)}, u32[]{:S(2)}, u32[]{:S(2)}) collective-permute-start(bf16[432,128]{1,0:T(8,128)(2,1)S(1)} %get-tuple-element.57), channel_id=1, source_target_pairs={{0,3},{1,2},{2,1},{3,0},{4,7},{5,6},{6,5},{7,4},{8,11},{9,10},{10,... | collective-permute-start | bytes 331784 | tf_op jit(solution)/shard_map/ppermute | solution.py:478
  28.1 9.3 %collective-permute-start.6 = (bf16[480,128]{1,0:T(8,128)(2,1)S(1)}, bf16[480,128]{1,0:T(8,128)(2,1)S(1)}, u32[]{:S(2)}, u32[]{:S(2)}) collective-permute-start(bf16[480,128]{1,0:T(8,128)(2,1)S(1)} %get-tuple-element.50), channel_id=1, source_target_pairs={{0,1},{1,0},{2,3},{3,2},{4,5},{5,4},{6,7},{7,6},{8,9},{9,8},{10,11... | collective-permute-start | bytes 368648 | tf_op jit(solution)/shard_map/ppermute | solution.py:478
  28.6 9.2 %collective-permute-start.7 = (bf16[480,128]{1,0:T(8,128)(2,1)S(1)}, bf16[480,128]{1,0:T(8,128)(2,1)S(1)}, u32[]{:S(2)}, u32[]{:S(2)}) collective-permute-start(bf16[480,128]{1,0:T(8,128)(2,1)S(1)} %get-tuple-element.51), channel_id=1, source_target_pairs={{0,2},{1,3},{2,0},{3,1},{4,6},{5,7},{6,4},{7,5},{8,10},{9,11},{10,... | collective-permute-start | bytes 368648 | tf_op jit(solution)/shard_map/ppermute | solution.py:478
  30.5 7.3 %collective-permute-start.8 = (bf16[480,128]{1,0:T(8,128)(2,1)S(1)}, bf16[480,128]{1,0:T(8,128)(2,1)S(1)}, u32[]{:S(2)}, u32[]{:S(2)}) collective-permute-start(bf16[480,128]{1,0:T(8,128)(2,1)S(1)} %get-tuple-element.52), channel_id=1, source_target_pairs={{0,3},{1,2},{2,1},{3,0},{4,7},{5,6},{6,5},{7,4},{8,11},{9,10},{10,... | collective-permute-start | bytes 368648 | tf_op jit(solution)/shard_map/ppermute | solution.py:478
  32.9 9.2 %collective-permute-start.12 = (bf16[112,128]{1,0:T(8,128)(2,1)S(1)}, bf16[112,128]{1,0:T(8,128)(2,1)S(1)}, u32[]{:S(2)}, u32[]{:S(2)}) collective-permute-start(bf16[112,128]{1,0:T(8,128)(2,1)S(1)} %get-tuple-element.59), channel_id=1, source_target_pairs={{0,16},{1,17},{2,18},{3,19},{4,20},{5,21},{6,22},{7,23},{8,24},{9,... | collective-permute-start | bytes 86024 | tf_op jit(solution)/shard_map/ppermute | solution.py:478
  36.0 6.4 %collective-permute-start.13 = (bf16[112,128]{1,0:T(8,128)(2,1)S(1)}, bf16[112,128]{1,0:T(8,128)(2,1)S(1)}, u32[]{:S(2)}, u32[]{:S(2)}) collective-permute-start(bf16[112,128]{1,0:T(8,128)(2,1)S(1)} %get-tuple-element.60), channel_id=1, source_target_pairs={{0,24},{1,25},{2,26},{3,27},{4,28},{5,29},{6,30},{7,31},{8,16},{9,... | collective-permute-start | bytes 86024 | tf_op jit(solution)/shard_map/ppermute | solution.py:478
  37.4 5.0 %collective-permute-start.14 = (bf16[112,128]{1,0:T(8,128)(2,1)S(1)}, bf16[112,128]{1,0:T(8,128)(2,1)S(1)}, u32[]{:S(2)}, u32[]{:S(2)}) collective-permute-start(bf16[112,128]{1,0:T(8,128)(2,1)S(1)} %get-tuple-element.61), channel_id=1, source_target_pairs={{0,8},{1,9},{2,10},{3,11},{4,12},{5,13},{6,14},{7,15},{8,0},{9,1},... | collective-permute-start | bytes 86024 | tf_op jit(solution)/shard_map/ppermute | solution.py:478
  37.9 4.8 %collective-permute-start.15 = (bf16[112,128]{1,0:T(8,128)(2,1)S(1)}, bf16[112,128]{1,0:T(8,128)(2,1)S(1)}, u32[]{:S(2)}, u32[]{:S(2)}) collective-permute-start(bf16[112,128]{1,0:T(8,128)(2,1)S(1)} %get-tuple-element.63), channel_id=1, source_target_pairs={{0,16},{1,17},{2,18},{3,19},{4,20},{5,21},{6,22},{7,23},{8,24},{9,... | collective-permute-start | bytes 86024 | tf_op jit(solution)/shard_map/ppermute | solution.py:478
  40.8 5.7 %collective-permute-start.16 = (bf16[112,128]{1,0:T(8,128)(2,1)S(1)}, bf16[112,128]{1,0:T(8,128)(2,1)S(1)}, u32[]{:S(2)}, u32[]{:S(2)}) collective-permute-start(bf16[112,128]{1,0:T(8,128)(2,1)S(1)} %get-tuple-element.64), channel_id=1, source_target_pairs={{0,24},{1,25},{2,26},{3,27},{4,28},{5,29},{6,30},{7,31},{8,16},{9,... | collective-permute-start | bytes 86024 | tf_op jit(solution)/shard_map/ppermute | solution.py:478
  42.2 4.3 %collective-permute-start.17 = (bf16[112,128]{1,0:T(8,128)(2,1)S(1)}, bf16[112,128]{1,0:T(8,128)(2,1)S(1)}, u32[]{:S(2)}, u32[]{:S(2)}) collective-permute-start(bf16[112,128]{1,0:T(8,128)(2,1)S(1)} %get-tuple-element.65), channel_id=1, source_target_pairs={{0,8},{1,9},{2,10},{3,11},{4,12},{5,13},{6,14},{7,15},{8,0},{9,1},... | collective-permute-start | bytes 86024 | tf_op jit(solution)/shard_map/ppermute | solution.py:478
  46.5 6.0 %collective-permute-start.20 = (bf16[224,128]{1,0:T(8,128)(2,1)S(1)}, bf16[224,128]{1,0:T(8,128)(2,1)S(1)}, u32[]{:S(2)}, u32[]{:S(2)}) collective-permute-start(bf16[224,128]{1,0:T(8,128)(2,1)S(1)} %shard_map.102.refs_0_), channel_id=1, source_target_pairs={{0,24},{1,25},{2,26},{3,27},{4,28},{5,29},{6,30},{7,31},{8,16},{9,... | collective-permute-start | bytes 172040 | tf_op jit(solution)/shard_map/ppermute | solution.py:478
  48.6 5.2 %collective-permute-start.19 = (bf16[224,128]{1,0:T(8,128)(2,1)S(1)}, bf16[224,128]{1,0:T(8,128)(2,1)S(1)}, u32[]{:S(2)}, u32[]{:S(2)}) collective-permute-start(bf16[224,128]{1,0:T(8,128)(2,1)S(1)} %shard_map.102.refs_0_), channel_id=1, source_target_pairs={{0,16},{1,17},{2,18},{3,19},{4,20},{5,21},{6,22},{7,23},{8,24},{9,... | collective-permute-start | bytes 172040 | tf_op jit(solution)/shard_map/ppermute | solution.py:478
  48.6 5.2 %collective-permute-start.18 = (bf16[224,128]{1,0:T(8,128)(2,1)S(1)}, bf16[224,128]{1,0:T(8,128)(2,1)S(1)}, u32[]{:S(2)}, u32[]{:S(2)}) collective-permute-start(bf16[224,128]{1,0:T(8,128)(2,1)S(1)} %shard_map.102.refs_0_), channel_id=1, source_target_pairs={{0,8},{1,9},{2,10},{3,11},{4,12},{5,13},{6,14},{7,15},{8,0},{9,1},... | collective-permute-start | bytes 172040 | tf_op jit(solution)/shard_map/ppermute | solution.py:478
  53.9 7.8 %collective-permute-start.23 = (bf16[848,128]{1,0:T(8,128)(2,1)S(1)}, bf16[848,128]{1,0:T(8,128)(2,1)S(1)}, u32[]{:S(2)}, u32[]{:S(2)}) collective-permute-start(bf16[848,128]{1,0:T(8,128)(2,1)S(1)} %shard_map.103.refs_0_), channel_id=1, source_target_pairs={{0,3},{1,2},{2,1},{3,0},{4,7},{5,6},{6,5},{7,4},{8,11},{9,10},{10,... | collective-permute-start | bytes 651272 | tf_op jit(solution)/shard_map/ppermute | solution.py:478
  55.9 7.8 %collective-permute-start.22 = (bf16[848,128]{1,0:T(8,128)(2,1)S(1)}, bf16[848,128]{1,0:T(8,128)(2,1)S(1)}, u32[]{:S(2)}, u32[]{:S(2)}) collective-permute-start(bf16[848,128]{1,0:T(8,128)(2,1)S(1)} %shard_map.103.refs_0_), channel_id=1, source_target_pairs={{0,2},{1,3},{2,0},{3,1},{4,6},{5,7},{6,4},{7,5},{8,10},{9,11},{10,... | collective-permute-start | bytes 651272 | tf_op jit(solution)/shard_map/ppermute | solution.py:478
  58.0 5.9 %collective-permute-start.21 = (bf16[848,128]{1,0:T(8,128)(2,1)S(1)}, bf16[848,128]{1,0:T(8,128)(2,1)S(1)}, u32[]{:S(2)}, u32[]{:S(2)}) collective-permute-start(bf16[848,128]{1,0:T(8,128)(2,1)S(1)} %shard_map.103.refs_0_), channel_id=1, source_target_pairs={{0,1},{1,0},{2,3},{3,2},{4,5},{5,4},{6,7},{7,6},{8,9},{9,8},{10,11... | collective-permute-start | bytes 651272 | tf_op jit(solution)/shard_map/ppermute | solution.py:478
  58.0 7.0 %collective-permute-start.24 = (bf16[848,128]{1,0:T(8,128)(2,1)S(1)}, bf16[848,128]{1,0:T(8,128)(2,1)S(1)}, u32[]{:S(2)}, u32[]{:S(2)}) collective-permute-start(bf16[848,128]{1,0:T(8,128)(2,1)S(1)} %shard_map.103.refs_0_), channel_id=1, source_target_pairs={{0,4},{1,5},{2,6},{3,7},{4,0},{5,1},{6,2},{7,3},{8,12},{9,13},{10,... | collective-permute-start | bytes 651272 | tf_op jit(solution)/shard_map/ppermute | solution.py:478
  61.6 3.4 %collective-permute-start.27 = (bf16[848,128]{1,0:T(8,128)(2,1)S(1)}, bf16[848,128]{1,0:T(8,128)(2,1)S(1)}, u32[]{:S(2)}, u32[]{:S(2)}) collective-permute-start(bf16[848,128]{1,0:T(8,128)(2,1)S(1)} %collective-permute-done.23.refs_3_), channel_id=1, source_target_pairs={{0,4},{1,5},{2,6},{3,7},{4,0},{5,1},{6,2},{7,3},{8,12},{9,13},{10,... | collective-permute-start | bytes 651272 | tf_op jit(solution)/shard_map/ppermute | solution.py:478
  63.7 1.5 %collective-permute-start.26 = (bf16[848,128]{1,0:T(8,128)(2,1)S(1)}, bf16[848,128]{1,0:T(8,128)(2,1)S(1)}, u32[]{:S(2)}, u32[]{:S(2)}) collective-permute-start(bf16[848,128]{1,0:T(8,128)(2,1)S(1)} %collective-permute-done.22.refs_2_), channel_id=1, source_target_pairs={{0,4},{1,5},{2,6},{3,7},{4,0},{5,1},{6,2},{7,3},{8,12},{9,13},{10,... | collective-permute-start | bytes 651272 | tf_op jit(solution)/shard_map/ppermute | solution.py:478
  63.9 1.5 %collective-permute-start.25 = (bf16[848,128]{1,0:T(8,128)(2,1)S(1)}, bf16[848,128]{1,0:T(8,128)(2,1)S(1)}, u32[]{:S(2)}, u32[]{:S(2)}) collective-permute-start(bf16[848,128]{1,0:T(8,128)(2,1)S(1)} %collective-permute-done.21.refs_1_), channel_id=1, source_target_pairs={{0,4},{1,5},{2,6},{3,7},{4,0},{5,1},{6,2},{7,3},{8,12},{9,13},{10,... | collective-permute-start | bytes 651272 | tf_op jit(solution)/shard_map/ppermute | solution.py:478
  (1 other events, 0.9 us)

commit v7 on v6

--- a/solution.py
+++ b/solution.py
@@ -62,16 +62,35 @@
     return value
 
 
-def strip_piece(value, tile, half_cols):
-    pitch = half_cols + 2 * SIDE
+def span_of(half_cols):
+    return half_cols + SIDE
+
+
+def cut_of(half_rows, width, half_cols):
+    return -(-groups_of(half_rows, width) * span_of(half_cols) // 16) * 16
+
+
+def strip_piece(value, tile, half_cols, cut):
+    span = span_of(half_cols)
     pick = picking(
-        (pitch, value.shape[1]),
-        lambda i, j: j == jnp.where(i < half_cols + SIDE, i, i - pitch) + tile * half_cols,
+        (span, value.shape[1]),
+        lambda i, j: j == jnp.where(i < half_cols + SIDE // 2, i, i - span) + tile * half_cols,
     )
     parts = [
         dot(pick, value[low : low + 128], ((1,), (1,))) for low in range(0, value.shape[0], 128)
     ]
+    short = cut - span * len(parts)
+    if short:
+        parts.append(jnp.zeros((short, 128), F32))
     return jnp.concatenate(parts, axis=0).astype(BF)
+
+
+def spread_out(value):
+    return jnp.concatenate([value, value[value.shape[0] - SIDE :]], axis=0)
+
+
+def has_edge(turn):
+    return turn & (turn + 1) == 0
 
 
 def begin(out_ref):
@@ -85,26 +104,26 @@
     first, last = level[:, :SIDE], level[:, level.shape[1] - SIDE :]
     for turn in range(1, count):
         other = me ^ turn
-        piece = strip_piece(strip, other, half_cols)
-        cut = piece.shape[0]
-        outs[turn - 1][0:cut] = piece
-        edge = jnp.where(other == me + 1, last, first)
-        outs[turn - 1][cut:] = edge.reshape(-1, 128).astype(BF)
+        cut = cut_of(cot_ref.shape[0], cot_ref.shape[1], half_cols)
+        outs[turn - 1][0:cut] = strip_piece(strip, other, half_cols, cut)
+        if has_edge(turn):
+            edge = jnp.where(other == me + 1, last, first)
+            outs[turn - 1][cut:] = edge.reshape(-1, 128).astype(BF)
 
 
 def pack_rows(count, half_cols, level_ref, cot_ref, *refs):
     got = refs[: count - 1]
-    kept_ref, cross_ref, inner_ref = refs[count - 1 :]
+    kept_ref, cross_ref, inner_ref, held = refs[count - 1 :]
     me, core = lax.axis_index("gx"), lax.axis_index("gy") & 1
     rows, cols = level_ref.shape[0], level_ref.shape[1]
     half_rows, width = cot_ref.shape[0], cot_ref.shape[1]
     total = count * width
     pitch = half_cols + 2 * SIDE
-    cut = groups_of(half_rows, width) * pitch
-    mine = strip_piece(strip_rows(cot_ref), me, half_cols)
+    span, cut = span_of(half_cols), cut_of(half_rows, width, half_cols)
+    mine = strip_piece(strip_rows(cot_ref), me, half_cols, cut)
     right = jnp.zeros((rows * SIDE, 128), F32)
     left = jnp.zeros((rows * SIDE, 128), F32)
-    for turn in range(1, count):
+    for turn in filter(has_edge, range(1, count)):
         edge = got[turn - 1][cut:].astype(F32)
         right = jnp.where(me ^ turn == me + 1, edge, right)
         left = jnp.where(me ^ turn == me - 1, edge, left)
@@ -114,19 +133,35 @@
     edges = jnp.concatenate([right, gap, left], axis=1).astype(BF)
     wide = jnp.concatenate([level, edges], axis=1).reshape(2 * rows * pitch, 128)
     kept_ref[0 : 2 * rows * pitch] = wide
-    cot = []
-    picks = {}
+    cot, picks = [], {}
+    halves = 2 * width == 128 and count % 2 == 0
+    if halves:
+        for turn in range(count):
+            held[me ^ turn] = (mine if turn == 0 else got[turn - 1][0:cut]).astype(F32)
+        left_half = lax.broadcasted_iota(jnp.int32, (span, 128), 1) < width
     for row in range(half_rows):
-        low = row * width // 128 * pitch
-        value = jnp.zeros((pitch, total), F32)
-        for turn in range(count):
-            part = mine[low : low + pitch] if turn == 0 else got[turn - 1][low : low + pitch]
-            key = (row * width % 128, turn)
-            if key not in picks:
-                picks[key] = lanes_to_channels(row, me ^ turn, width, total)
-            value = value + dot(part, picks[key])
+        low = row * width // 128 * span
+        if halves:
+            tiles = []
+            for owner in range(0, count, 2):
+                a, b = (held[owner + i, low : low + span] for i in range(2))
+                if row % 2:
+                    a = pltpu.roll(a, width, 1)
+                else:
+                    b = pltpu.roll(b, width, 1)
+                tiles.append(jnp.where(left_half, a, b))
+            value = jnp.concatenate(tiles, axis=1)
+        else:
+            value = jnp.zeros((span, total), F32)
+            for turn in range(count):
+                part = mine[low : low + span] if turn == 0 else got[turn - 1][low : low + span]
+                key = (row * width % 128, turn)
+                if key not in picks:
+                    picks[key] = lanes_to_channels(row, me ^ turn, width, total)
+                value = value + dot(part, picks[key])
+        cot.append(value)
+        value = spread_out(value)
         value = value.astype(BF)
-        cot.append(value)
         low = 2 * (rows + row) * pitch
         kept_ref[low : low + pitch] = value[:, :128]
         kept_ref[low + pitch : low + 2 * pitch] = value[:, 128:]
@@ -140,9 +175,9 @@
             def _(ref=ref, low=low, neck=neck):
                 ref[0:cells] = band[low : low + HALO].reshape(cells, 128)
                 for i in range(2):
-                    spot = cells + 2 * pitch * i
-                    ref[spot : spot + pitch] = cot[neck + i][:, :128]
-                    ref[spot + pitch : spot + 2 * pitch] = cot[neck + i][:, 128:]
+                    spot = cells + 2 * span * i
+                    both = jnp.concatenate([cot[neck + i][:, :128], cot[neck + i][:, 128:]], axis=0)
+                    ref[spot : spot + 2 * span] = both.astype(BF)
 
 
 def turn_weights(wl_ref, wd_ref, wn_ref, wfwd_ref, wbwd_ref, wdt_ref, wnt_ref):
@@ -213,9 +248,11 @@
         )
         field[low : low + HALO, 2 * pitch - SIDE : 2 * pitch] = band[:, cols + SIDE :]
         for i in range(2):
-            spot = cells + 2 * pitch * i
-            cot_all[low_neck + i, :, :128] = ref[spot : spot + pitch]
-            cot_all[low_neck + i, :, 128:] = ref[spot + pitch : spot + 2 * pitch]
+            span = span_of(half_cols)
+            spot = cells + 2 * span * i
+            both = ref[spot : spot + 2 * span].astype(F32)
+            both = jnp.concatenate([spread_out(both[:span]), spread_out(both[span:])], axis=1)
+            cot_all[low_neck + i] = both.astype(BF)
 
     @pl.when(core == 0)
     def _():
@@ -495,17 +532,19 @@
 
     strip = jnp.swapaxes(cotangent, 1, 2)
     width = strip.shape[1]
-    packed = shape((groups_of(half_rows, width) * pitch + rows * SIDE, 128))
+    cut = cut_of(half_rows, width, half_cols)
+    packed = [shape((cut + rows * SIDE * has_edge(turn), 128)) for turn in range(1, count)]
     first = call(begin, shape((16, 128)), (), flops=10**10)
     sent = call(
-        functools.partial(pack_cols, count, half_cols), [packed] * (count - 1), (level_in, strip, first)
+        functools.partial(pack_cols, count, half_cols), packed, (level_in, strip, first)
     )
     got = [by_col(value, turn + 1) for turn, value in enumerate(sent)]
-    band = shape((HALO * (cols + 2 * SIDE) + 4 * pitch, 128))
+    band = shape((HALO * (cols + 2 * SIDE) + 4 * span_of(half_cols), 128))
     kept, cross, inner = call(
         functools.partial(pack_rows, count, half_cols),
         [shape((3 * rows * pitch, 128)), band, band],
         (level_in, strip, *got),
+        [pltpu.VMEM((count, cut, 128), F32)],
     )
     cross, inner = by_seam(cross), by_core(inner)
 

time: 67.1 us -> 66.3 us (0.988)
  waiting for transfers between devices: 23 us -> 21.5 us
  starting transfers between devices: 34.2 us -> 35.1 us
    ppermute x28, waiting for transfers between devices: 23 us -> 21.5 us  [permute(): lax.ppermute(value, axes, [(a, b) for a, b in pairs if b is not None])]
    ppermute x28, starting transfers between devices: 34.2 us -> 35.1 us  [permute(): lax.ppermute(value, axes, [(a, b) for a, b in pairs if b is not None])]
  transfers between devices with their start and end apart: 28 -> 28, of which waited for: 18 -> 13; matrix products, arithmetic and copies ran while one was open for 0% -> 0% of each run, Pallas kernels for 3% -> 3%
where the time goes in v7:
time: 66.3 us; the launch traced here: 66.1 us
  starting transfers between devices  35.1 us (53%)
  waiting for transfers between devices  21.5 us (32%)
  Pallas kernels  7.97 us (12%)
  local copies, waits for them, and re-layouts  0.89 us (1%)
  between operations  0.74 us (1%)
    ppermute x28, starting transfers between devices, permute(): lax.ppermute(value, axes, [(a, b) for a, b in pairs if b is not None])  35.1 us
    ppermute x28, waiting for transfers between devices, permute(): lax.ppermute(value, axes, [(a, b) for a, b in pairs if b is not None])  21.5 us
    pallas_call x13, Pallas kernels, call(): pl.pallas_call(body, out_shape=out_shapes, in_specs=[VMEM] * len(args), o...  7.97 us
  transfers between devices with their start and end apart: 28, of which 13 were waited for; matrix products, arithmetic and copies ran while one was open for 0% of the time, Pallas kernels for 3%

profile of v7, /device:TPU:0, one launch (start us, length us, event | category | flops | bytes accessed | tf_op | source)
XLA Modules:
  0.0 66.1 jit_solution(14086163316762744449)
XLA Ops:
  0.7 0.9 %copy-done.3 = bf16[8,64,128]{2,1,0:T(8,128)(2,1)S(1)} copy-done((bf16[8,64,128]{2,1,0:T(8,128)(2,1)S(1)}, bf16[8,64,128]{2,1,0:T(8,128)(2,1)}, u32[]{:S(2)}) %copy-start.3) | copy-done | bytes 131096
  1.8 3.0 %collective-permute-start = (bf16[144,128]{1,0:T(8,128)(2,1)S(1)}, bf16[144,128]{1,0:T(8,128)(2,1)S(1)}, u32[]{:S(2)}, u32[]{:S(2)}) collective-permute-start(bf16[144,128]{1,0:T(8,128)(2,1)S(1)} %get-tuple-element.37), channel_id=1, source_target_pairs={{0,1},{1,0},{2,3},{3,2},{4,5},{5,4},{6,7},{7,6},{8,9},{9,8},{10,11... | collective-permute-start | bytes 110600 | tf_op jit(solution)/shard_map/ppermute | solution.py:515
  4.8 1.5 %collective-permute-start.2 = (bf16[144,128]{1,0:T(8,128)(2,1)S(1)}, bf16[144,128]{1,0:T(8,128)(2,1)S(1)}, u32[]{:S(2)}, u32[]{:S(2)}) collective-permute-start(bf16[144,128]{1,0:T(8,128)(2,1)S(1)} %get-tuple-element.39), channel_id=1, source_target_pairs={{0,3},{1,2},{2,1},{3,0},{4,7},{5,6},{6,5},{7,4},{8,11},{9,10},{10,... | collective-permute-start | bytes 110600 | tf_op jit(solution)/shard_map/ppermute | solution.py:515
  6.4 3.7 %collective-permute-done.1.refs_1_ = bf16[80,128]{1,0:T(8,128)(2,1)S(1)} collective-permute-done((bf16[80,128]{1,0:T(8,128)(2,1)S(1)}, bf16[80,128]{1,0:T(8,128)(2,1)S(1)}, u32[]{:S(2)}, u32[]{:S(2)}) %collective-permute-start.1) | collective-permute-done | bytes 20512 | tf_op jit(solution)/shard_map/ppermute | solution.py:515
  10.4 0.7 %collective-permute-start.3 = (bf16[720,128]{1,0:T(8,128)(2,1)S(1)}, bf16[720,128]{1,0:T(8,128)(2,1)S(1)}, u32[]{:S(2)}, u32[]{:S(2)}) collective-permute-start(bf16[720,128]{1,0:T(8,128)(2,1)S(1)} %get-tuple-element.41), channel_id=1, source_target_pairs={{4,8},{5,9},{6,10},{7,11},{8,4},{9,5},{10,6},{11,7},{12,16},{13,17... | collective-permute-start | bytes 552968 | tf_op jit(solution)/shard_map/ppermute | solution.py:515
  11.1 3.0 %collective-permute-start.4 = (bf16[720,128]{1,0:T(8,128)(2,1)S(1)}, bf16[720,128]{1,0:T(8,128)(2,1)S(1)}, u32[]{:S(2)}, u32[]{:S(2)}) collective-permute-start(bf16[720,128]{1,0:T(8,128)(2,1)S(1)} %get-tuple-element.42), channel_id=1, source_target_pairs={{0,4},{1,5},{2,6},{3,7},{4,0},{5,1},{6,2},{7,3},{8,12},{9,13},{10,... | collective-permute-start | bytes 552968 | tf_op jit(solution)/shard_map/ppermute | solution.py:515
  14.1 0.6 shard_map.95
  15.1 3.8 %shard_map.96 = (bf16[6784,128]{1,0:T(8,128)(2,1)S(1)}, bf16[3392,128]{1,0:T(8,128)(2,1)S(1)}, bf16[128,256]{1,0:T(8,128)(2,1)S(1)}, bf16[8,64,128]{2,1,0:T(8,128)(2,1)}) custom-call(bf16[1152,128]{1,0:T(8,128)(2,1)S(1)} %get-tuple-element.40.kept_ref, bf16[720,128]{1,0:T(8,128)(2,1)S(1)} %collective-permute-done.3.cross_ref, ...), custom_call_target="tpu_custom_call" | custom-call | flops 6000000000 | tf_op jit(solution)/shard_map/pallas_call | solution.py:18
  18.9 2.0 %collective-permute-start.5 = (bf16[3392,128]{1,0:T(8,128)(2,1)S(1)}, bf16[3392,128]{1,0:T(8,128)(2,1)S(1)}, u32[]{:S(2)}, u32[]{:S(2)}) collective-permute-start(bf16[3392,128]{1,0:T(8,128)(2,1)S(1)} %get-tuple-element.49), channel_id=1, source_target_pairs={{0,4},{1,5},{2,6},{3,7},{4,0},{5,1},{6,2},{7,3},{8,12},{9,13},{10,... | collective-permute-start | bytes 2605064 | tf_op jit(solution)/shard_map/ppermute | solution.py:515
  21.3 1.7 %collective-permute-done.5.got_ref = bf16[3392,128]{1,0:T(8,128)(2,1)S(1)} collective-permute-done((bf16[3392,128]{1,0:T(8,128)(2,1)S(1)}, bf16[3392,128]{1,0:T(8,128)(2,1)S(1)}, u32[]{:S(2)}, u32[]{:S(2)}) %collective-permute-start.5) | collective-permute-done | bytes 868384 | tf_op jit(solution)/shard_map/ppermute | solution.py:515
  23.2 1.6 %collective-permute-start.9 = (bf16[432,128]{1,0:T(8,128)(2,1)S(1)}, bf16[432,128]{1,0:T(8,128)(2,1)S(1)}, u32[]{:S(2)}, u32[]{:S(2)}) collective-permute-start(bf16[432,128]{1,0:T(8,128)(2,1)S(1)} %get-tuple-element.55), channel_id=1, source_target_pairs={{0,1},{1,0},{2,3},{3,2},{4,5},{5,4},{6,7},{7,6},{8,9},{9,8},{10,11... | collective-permute-start | bytes 331784 | tf_op jit(solution)/shard_map/ppermute | solution.py:515
  24.7 0.5 collective-permute-start.10
  25.2 1.5 %collective-permute-start.11 = (bf16[432,128]{1,0:T(8,128)(2,1)S(1)}, bf16[432,128]{1,0:T(8,128)(2,1)S(1)}, u32[]{:S(2)}, u32[]{:S(2)}) collective-permute-start(bf16[432,128]{1,0:T(8,128)(2,1)S(1)} %get-tuple-element.57), channel_id=1, source_target_pairs={{0,3},{1,2},{2,1},{3,0},{4,7},{5,6},{6,5},{7,4},{8,11},{9,10},{10,... | collective-permute-start | bytes 331784 | tf_op jit(solution)/shard_map/ppermute | solution.py:515
  26.7 1.5 %collective-permute-start.6 = (bf16[480,128]{1,0:T(8,128)(2,1)S(1)}, bf16[480,128]{1,0:T(8,128)(2,1)S(1)}, u32[]{:S(2)}, u32[]{:S(2)}) collective-permute-start(bf16[480,128]{1,0:T(8,128)(2,1)S(1)} %get-tuple-element.50), channel_id=1, source_target_pairs={{0,1},{1,0},{2,3},{3,2},{4,5},{5,4},{6,7},{7,6},{8,9},{9,8},{10,11... | collective-permute-start | bytes 368648 | tf_op jit(solution)/shard_map/ppermute | solution.py:515
  28.7 1.6 %collective-permute-start.8 = (bf16[480,128]{1,0:T(8,128)(2,1)S(1)}, bf16[480,128]{1,0:T(8,128)(2,1)S(1)}, u32[]{:S(2)}, u32[]{:S(2)}) collective-permute-start(bf16[480,128]{1,0:T(8,128)(2,1)S(1)} %get-tuple-element.52), channel_id=1, source_target_pairs={{0,3},{1,2},{2,1},{3,0},{4,7},{5,6},{6,5},{7,4},{8,11},{9,10},{10,... | collective-permute-start | bytes 368648 | tf_op jit(solution)/shard_map/ppermute | solution.py:515
  30.3 2.4 %collective-permute-done.10.refs_1_ = bf16[432,128]{1,0:T(8,128)(2,1)S(1)} collective-permute-done((bf16[432,128]{1,0:T(8,128)(2,1)S(1)}, bf16[432,128]{1,0:T(8,128)(2,1)S(1)}, u32[]{:S(2)}, u32[]{:S(2)}) %collective-permute-start.10) | collective-permute-done | bytes 110624 | tf_op jit(solution)/shard_map/ppermute | solution.py:515
  32.7 3.0 %collective-permute-start.12 = (bf16[112,128]{1,0:T(8,128)(2,1)S(1)}, bf16[112,128]{1,0:T(8,128)(2,1)S(1)}, u32[]{:S(2)}, u32[]{:S(2)}) collective-permute-start(bf16[112,128]{1,0:T(8,128)(2,1)S(1)} %get-tuple-element.59), channel_id=1, source_target_pairs={{0,16},{1,17},{2,18},{3,19},{4,20},{5,21},{6,22},{7,23},{8,24},{9,... | collective-permute-start | bytes 86024 | tf_op jit(solution)/shard_map/ppermute | solution.py:515
  35.7 1.3 %collective-permute-start.13 = (bf16[112,128]{1,0:T(8,128)(2,1)S(1)}, bf16[112,128]{1,0:T(8,128)(2,1)S(1)}, u32[]{:S(2)}, u32[]{:S(2)}) collective-permute-start(bf16[112,128]{1,0:T(8,128)(2,1)S(1)} %get-tuple-element.60), channel_id=1, source_target_pairs={{0,24},{1,25},{2,26},{3,27},{4,28},{5,29},{6,30},{7,31},{8,16},{9,... | collective-permute-start | bytes 86024 | tf_op jit(solution)/shard_map/ppermute | solution.py:515
  37.5 2.9 %collective-permute-start.15 = (bf16[112,128]{1,0:T(8,128)(2,1)S(1)}, bf16[112,128]{1,0:T(8,128)(2,1)S(1)}, u32[]{:S(2)}, u32[]{:S(2)}) collective-permute-start(bf16[112,128]{1,0:T(8,128)(2,1)S(1)} %get-tuple-element.63), channel_id=1, source_target_pairs={{0,16},{1,17},{2,18},{3,19},{4,20},{5,21},{6,22},{7,23},{8,24},{9,... | collective-permute-start | bytes 86024 | tf_op jit(solution)/shard_map/ppermute | solution.py:515
  40.4 1.3 %collective-permute-start.16 = (bf16[112,128]{1,0:T(8,128)(2,1)S(1)}, bf16[112,128]{1,0:T(8,128)(2,1)S(1)}, u32[]{:S(2)}, u32[]{:S(2)}) collective-permute-start(bf16[112,128]{1,0:T(8,128)(2,1)S(1)} %get-tuple-element.64), channel_id=1, source_target_pairs={{0,24},{1,25},{2,26},{3,27},{4,28},{5,29},{6,30},{7,31},{8,16},{9,... | collective-permute-start | bytes 86024 | tf_op jit(solution)/shard_map/ppermute | solution.py:515
  42.3 3.9 %collective-permute-done.16.refs_6_ = bf16[112,128]{1,0:T(8,128)(2,1)S(1)} collective-permute-done((bf16[112,128]{1,0:T(8,128)(2,1)S(1)}, bf16[112,128]{1,0:T(8,128)(2,1)S(1)}, u32[]{:S(2)}, u32[]{:S(2)}) %collective-permute-start.16) | collective-permute-done | bytes 28704 | tf_op jit(solution)/shard_map/ppermute | solution.py:515
  46.2 2.0 %collective-permute-start.20 = (bf16[224,128]{1,0:T(8,128)(2,1)S(1)}, bf16[224,128]{1,0:T(8,128)(2,1)S(1)}, u32[]{:S(2)}, u32[]{:S(2)}) collective-permute-start(bf16[224,128]{1,0:T(8,128)(2,1)S(1)} %shard_map.102.refs_0_), channel_id=1, source_target_pairs={{0,24},{1,25},{2,26},{3,27},{4,28},{5,29},{6,30},{7,31},{8,16},{9,... | collective-permute-start | bytes 172040 | tf_op jit(solution)/shard_map/ppermute | solution.py:515
  48.2 2.5 %collective-permute-start.18 = (bf16[224,128]{1,0:T(8,128)(2,1)S(1)}, bf16[224,128]{1,0:T(8,128)(2,1)S(1)}, u32[]{:S(2)}, u32[]{:S(2)}) collective-permute-start(bf16[224,128]{1,0:T(8,128)(2,1)S(1)} %shard_map.102.refs_0_), channel_id=1, source_target_pairs={{0,8},{1,9},{2,10},{3,11},{4,12},{5,13},{6,14},{7,15},{8,0},{9,1},... | collective-permute-start | bytes 172040 | tf_op jit(solution)/shard_map/ppermute | solution.py:515
  50.7 1.6 %collective-permute-done.20.refs_3_ = bf16[224,128]{1,0:T(8,128)(2,1)S(1)} collective-permute-done((bf16[224,128]{1,0:T(8,128)(2,1)S(1)}, bf16[224,128]{1,0:T(8,128)(2,1)S(1)}, u32[]{:S(2)}, u32[]{:S(2)}) %collective-permute-start.20) | collective-permute-done | bytes 57376 | tf_op jit(solution)/shard_map/ppermute | solution.py:515
  52.3 1.2 %collective-permute-done.19.refs_2_ = bf16[224,128]{1,0:T(8,128)(2,1)S(1)} collective-permute-done((bf16[224,128]{1,0:T(8,128)(2,1)S(1)}, bf16[224,128]{1,0:T(8,128)(2,1)S(1)}, u32[]{:S(2)}, u32[]{:S(2)}) %collective-permute-start.19) | collective-permute-done | bytes 57376 | tf_op jit(solution)/shard_map/ppermute | solution.py:515
  53.6 1.2 %collective-permute-start.23 = (bf16[848,128]{1,0:T(8,128)(2,1)S(1)}, bf16[848,128]{1,0:T(8,128)(2,1)S(1)}, u32[]{:S(2)}, u32[]{:S(2)}) collective-permute-start(bf16[848,128]{1,0:T(8,128)(2,1)S(1)} %shard_map.103.refs_0_), channel_id=1, source_target_pairs={{0,3},{1,2},{2,1},{3,0},{4,7},{5,6},{6,5},{7,4},{8,11},{9,10},{10,... | collective-permute-start | bytes 651272 | tf_op jit(solution)/shard_map/ppermute | solution.py:515
  54.8 0.9 %collective-permute-start.22 = (bf16[848,128]{1,0:T(8,128)(2,1)S(1)}, bf16[848,128]{1,0:T(8,128)(2,1)S(1)}, u32[]{:S(2)}, u32[]{:S(2)}) collective-permute-start(bf16[848,128]{1,0:T(8,128)(2,1)S(1)} %shard_map.103.refs_0_), channel_id=1, source_target_pairs={{0,2},{1,3},{2,0},{3,1},{4,6},{5,7},{6,4},{7,5},{8,10},{9,11},{10,... | collective-permute-start | bytes 651272 | tf_op jit(solution)/shard_map/ppermute | solution.py:515
  55.7 1.4 %collective-permute-start.21 = (bf16[848,128]{1,0:T(8,128)(2,1)S(1)}, bf16[848,128]{1,0:T(8,128)(2,1)S(1)}, u32[]{:S(2)}, u32[]{:S(2)}) collective-permute-start(bf16[848,128]{1,0:T(8,128)(2,1)S(1)} %shard_map.103.refs_0_), channel_id=1, source_target_pairs={{0,1},{1,0},{2,3},{3,2},{4,5},{5,4},{6,7},{7,6},{8,9},{9,8},{10,11... | collective-permute-start | bytes 651272 | tf_op jit(solution)/shard_map/ppermute | solution.py:515
  57.1 3.5 %collective-permute-done.23.refs_3_ = bf16[848,128]{1,0:T(8,128)(2,1)S(1)} collective-permute-done((bf16[848,128]{1,0:T(8,128)(2,1)S(1)}, bf16[848,128]{1,0:T(8,128)(2,1)S(1)}, u32[]{:S(2)}, u32[]{:S(2)}) %collective-permute-start.23) | collective-permute-done | bytes 217120 | tf_op jit(solution)/shard_map/ppermute | solution.py:515
  60.7 2.2 %collective-permute-done.22.refs_2_ = bf16[848,128]{1,0:T(8,128)(2,1)S(1)} collective-permute-done((bf16[848,128]{1,0:T(8,128)(2,1)S(1)}, bf16[848,128]{1,0:T(8,128)(2,1)S(1)}, u32[]{:S(2)}, u32[]{:S(2)}) %collective-permute-start.22) | collective-permute-done | bytes 217120 | tf_op jit(solution)/shard_map/ppermute | solution.py:515
  63.4 0.9 %shard_map.99 = bf16[4,64,128]{2,1,0:T(8,128)(2,1)} custom-call(bf16[4,64,128]{2,1,0:T(8,128)(2,1)S(1)} %shard_map.97.pieces_ref, bf16[480,128]{1,0:T(8,128)(2,1)S(1)} %collective-permute-done.6.refs_0_, bf16[480,128]{1,0:T(8,128)(2,1)S(1)} %collective-permute-done.7.refs_1_, bf16[480,128]{1,0:T(8,128)(2,1)S(1)} %collective-permute-done.8.refs_2_), custom_call_target="tpu_custom_call" | custom-call | flops 1000000000 | tf_op jit(solution)/shard_map/pallas_call | solution.py:18
  64.7 1.5 %shard_map.104 = (bf16[9,128,128]{2,1,0:T(8,128)(2,1)}, bf16[4,128,256]{2,1,0:T(8,128)(2,1)}, bf16[9,256,256]{2,1,0:T(8,128)(2,1)}) custom-call(bf16[848,128]{1,0:T(8,128)(2,1)S(1)} %shard_map.103.refs_0_, bf16[848,128]{1,0:T(8,128)(2,1)S(1)} %collective-permute-done.21.refs_1_, bf16[848,128]{1,0:T(8,128)(2,1)S(1)} %collective-permute-done.22.refs_2_, ...), custom_call_target="tpu_custom_call" | custom-call | flops 1000000000 | tf_op jit(solution)/shard_map/pallas_call | solution.py:18
  (47 shorter events, 4.2 us)
Async XLA Ops:
  0.6 0.9 %copy-start.3 = (bf16[8,64,128]{2,1,0:T(8,128)(2,1)S(1)}, bf16[8,64,128]{2,1,0:T(8,128)(2,1)}, u32[]{:S(2)}) copy-start(bf16[8,64,128]{2,1,0:T(8,128)(2,1)} %level_ref.3) | copy-start | bytes 393220
  1.8 8.3 %collective-permute-start = (bf16[144,128]{1,0:T(8,128)(2,1)S(1)}, bf16[144,128]{1,0:T(8,128)(2,1)S(1)}, u32[]{:S(2)}, u32[]{:S(2)}) collective-permute-start(bf16[144,128]{1,0:T(8,128)(2,1)S(1)} %get-tuple-element.37), channel_id=1, source_target_pairs={{0,1},{1,0},{2,3},{3,2},{4,5},{5,4},{6,7},{7,6},{8,9},{9,8},{10,11... | collective-permute-start | bytes 110600 | tf_op jit(solution)/shard_map/ppermute | solution.py:515
  4.8 5.3 %collective-permute-start.2 = (bf16[144,128]{1,0:T(8,128)(2,1)S(1)}, bf16[144,128]{1,0:T(8,128)(2,1)S(1)}, u32[]{:S(2)}, u32[]{:S(2)}) collective-permute-start(bf16[144,128]{1,0:T(8,128)(2,1)S(1)} %get-tuple-element.39), channel_id=1, source_target_pairs={{0,3},{1,2},{2,1},{3,0},{4,7},{5,6},{6,5},{7,4},{8,11},{9,10},{10,... | collective-permute-start | bytes 110600 | tf_op jit(solution)/shard_map/ppermute | solution.py:515
  6.3 7.8 %copy-start = (bf16[3,3,256,256]{3,2,1,0:T(8,128)(2,1)S(1)}, bf16[3,3,256,256]{3,2,1,0:T(8,128)(2,1)}, u32[]{:S(2)}) copy-start(bf16[3,3,256,256]{3,2,1,0:T(8,128)(2,1)} %param.8) | copy-start | bytes 3538948
  6.3 7.8 %copy-start.1 = (bf16[3,3,128,128]{3,2,1,0:T(8,128)(2,1)S(1)}, bf16[3,3,128,128]{3,2,1,0:T(8,128)(2,1)}, u32[]{:S(2)}) copy-start(bf16[3,3,128,128]{3,2,1,0:T(8,128)(2,1)} %param.6) | copy-start | bytes 884740
  6.3 7.8 %copy-start.2 = (bf16[2,2,128,256]{3,2,1,0:T(8,128)(2,1)S(1)}, bf16[2,2,128,256]{3,2,1,0:T(8,128)(2,1)}, u32[]{:S(2)}) copy-start(bf16[2,2,128,256]{3,2,1,0:T(8,128)(2,1)} %param.7) | copy-start | bytes 786436
  6.3 3.8 %collective-permute-start.1 = (bf16[80,128]{1,0:T(8,128)(2,1)S(1)}, bf16[80,128]{1,0:T(8,128)(2,1)S(1)}, u32[]{:S(2)}, u32[]{:S(2)}) collective-permute-start(bf16[80,128]{1,0:T(8,128)(2,1)S(1)} %get-tuple-element.38), channel_id=1, source_target_pairs={{0,2},{1,3},{2,0},{3,1},{4,6},{5,7},{6,4},{7,5},{8,10},{9,11},{10,... | collective-permute-start | bytes 61448 | tf_op jit(solution)/shard_map/ppermute | solution.py:515
  10.4 4.2 %collective-permute-start.3 = (bf16[720,128]{1,0:T(8,128)(2,1)S(1)}, bf16[720,128]{1,0:T(8,128)(2,1)S(1)}, u32[]{:S(2)}, u32[]{:S(2)}) collective-permute-start(bf16[720,128]{1,0:T(8,128)(2,1)S(1)} %get-tuple-element.41), channel_id=1, source_target_pairs={{4,8},{5,9},{6,10},{7,11},{8,4},{9,5},{10,6},{11,7},{12,16},{13,17... | collective-permute-start | bytes 552968 | tf_op jit(solution)/shard_map/ppermute | solution.py:515
  11.1 4.0 %collective-permute-start.4 = (bf16[720,128]{1,0:T(8,128)(2,1)S(1)}, bf16[720,128]{1,0:T(8,128)(2,1)S(1)}, u32[]{:S(2)}, u32[]{:S(2)}) collective-permute-start(bf16[720,128]{1,0:T(8,128)(2,1)S(1)} %get-tuple-element.42), channel_id=1, source_target_pairs={{0,4},{1,5},{2,6},{3,7},{4,0},{5,1},{6,2},{7,3},{8,12},{9,13},{10,... | collective-permute-start | bytes 552968 | tf_op jit(solution)/shard_map/ppermute | solution.py:515
  18.9 4.1 %collective-permute-start.5 = (bf16[3392,128]{1,0:T(8,128)(2,1)S(1)}, bf16[3392,128]{1,0:T(8,128)(2,1)S(1)}, u32[]{:S(2)}, u32[]{:S(2)}) collective-permute-start(bf16[3392,128]{1,0:T(8,128)(2,1)S(1)} %get-tuple-element.49), channel_id=1, source_target_pairs={{0,4},{1,5},{2,6},{3,7},{4,0},{5,1},{6,2},{7,3},{8,12},{9,13},{10,... | collective-permute-start | bytes 2605064 | tf_op jit(solution)/shard_map/ppermute | solution.py:515
  23.2 5.6 %collective-permute-start.9 = (bf16[432,128]{1,0:T(8,128)(2,1)S(1)}, bf16[432,128]{1,0:T(8,128)(2,1)S(1)}, u32[]{:S(2)}, u32[]{:S(2)}) collective-permute-start(bf16[432,128]{1,0:T(8,128)(2,1)S(1)} %get-tuple-element.55), channel_id=1, source_target_pairs={{0,1},{1,0},{2,3},{3,2},{4,5},{5,4},{6,7},{7,6},{8,9},{9,8},{10,11... | collective-permute-start | bytes 331784 | tf_op jit(solution)/shard_map/ppermute | solution.py:515
  24.7 7.9 %collective-permute-start.10 = (bf16[432,128]{1,0:T(8,128)(2,1)S(1)}, bf16[432,128]{1,0:T(8,128)(2,1)S(1)}, u32[]{:S(2)}, u32[]{:S(2)}) collective-permute-start(bf16[432,128]{1,0:T(8,128)(2,1)S(1)} %get-tuple-element.56), channel_id=1, source_target_pairs={{0,2},{1,3},{2,0},{3,1},{4,6},{5,7},{6,4},{7,5},{8,10},{9,11},{10,... | collective-permute-start | bytes 331784 | tf_op jit(solution)/shard_map/ppermute | solution.py:515
  25.2 7.4 %collective-permute-start.11 = (bf16[432,128]{1,0:T(8,128)(2,1)S(1)}, bf16[432,128]{1,0:T(8,128)(2,1)S(1)}, u32[]{:S(2)}, u32[]{:S(2)}) collective-permute-start(bf16[432,128]{1,0:T(8,128)(2,1)S(1)} %get-tuple-element.57), channel_id=1, source_target_pairs={{0,3},{1,2},{2,1},{3,0},{4,7},{5,6},{6,5},{7,4},{8,11},{9,10},{10,... | collective-permute-start | bytes 331784 | tf_op jit(solution)/shard_map/ppermute | solution.py:515
  26.7 10.4 %collective-permute-start.6 = (bf16[480,128]{1,0:T(8,128)(2,1)S(1)}, bf16[480,128]{1,0:T(8,128)(2,1)S(1)}, u32[]{:S(2)}, u32[]{:S(2)}) collective-permute-start(bf16[480,128]{1,0:T(8,128)(2,1)S(1)} %get-tuple-element.50), channel_id=1, source_target_pairs={{0,1},{1,0},{2,3},{3,2},{4,5},{5,4},{6,7},{7,6},{8,9},{9,8},{10,11... | collective-permute-start | bytes 368648 | tf_op jit(solution)/shard_map/ppermute | solution.py:515
  28.2 9.2 %collective-permute-start.7 = (bf16[480,128]{1,0:T(8,128)(2,1)S(1)}, bf16[480,128]{1,0:T(8,128)(2,1)S(1)}, u32[]{:S(2)}, u32[]{:S(2)}) collective-permute-start(bf16[480,128]{1,0:T(8,128)(2,1)S(1)} %get-tuple-element.51), channel_id=1, source_target_pairs={{0,2},{1,3},{2,0},{3,1},{4,6},{5,7},{6,4},{7,5},{8,10},{9,11},{10,... | collective-permute-start | bytes 368648 | tf_op jit(solution)/shard_map/ppermute | solution.py:515
  28.7 8.7 %collective-permute-start.8 = (bf16[480,128]{1,0:T(8,128)(2,1)S(1)}, bf16[480,128]{1,0:T(8,128)(2,1)S(1)}, u32[]{:S(2)}, u32[]{:S(2)}) collective-permute-start(bf16[480,128]{1,0:T(8,128)(2,1)S(1)} %get-tuple-element.52), channel_id=1, source_target_pairs={{0,3},{1,2},{2,1},{3,0},{4,7},{5,6},{6,5},{7,4},{8,11},{9,10},{10,... | collective-permute-start | bytes 368648 | tf_op jit(solution)/shard_map/ppermute | solution.py:515
  32.7 9.0 %collective-permute-start.12 = (bf16[112,128]{1,0:T(8,128)(2,1)S(1)}, bf16[112,128]{1,0:T(8,128)(2,1)S(1)}, u32[]{:S(2)}, u32[]{:S(2)}) collective-permute-start(bf16[112,128]{1,0:T(8,128)(2,1)S(1)} %get-tuple-element.59), channel_id=1, source_target_pairs={{0,16},{1,17},{2,18},{3,19},{4,20},{5,21},{6,22},{7,23},{8,24},{9,... | collective-permute-start | bytes 86024 | tf_op jit(solution)/shard_map/ppermute | solution.py:515
  35.7 6.3 %collective-permute-start.13 = (bf16[112,128]{1,0:T(8,128)(2,1)S(1)}, bf16[112,128]{1,0:T(8,128)(2,1)S(1)}, u32[]{:S(2)}, u32[]{:S(2)}) collective-permute-start(bf16[112,128]{1,0:T(8,128)(2,1)S(1)} %get-tuple-element.60), channel_id=1, source_target_pairs={{0,24},{1,25},{2,26},{3,27},{4,28},{5,29},{6,30},{7,31},{8,16},{9,... | collective-permute-start | bytes 86024 | tf_op jit(solution)/shard_map/ppermute | solution.py:515
  37.1 4.9 %collective-permute-start.14 = (bf16[112,128]{1,0:T(8,128)(2,1)S(1)}, bf16[112,128]{1,0:T(8,128)(2,1)S(1)}, u32[]{:S(2)}, u32[]{:S(2)}) collective-permute-start(bf16[112,128]{1,0:T(8,128)(2,1)S(1)} %get-tuple-element.61), channel_id=1, source_target_pairs={{0,8},{1,9},{2,10},{3,11},{4,12},{5,13},{6,14},{7,15},{8,0},{9,1},... | collective-permute-start | bytes 86024 | tf_op jit(solution)/shard_map/ppermute | solution.py:515
  37.5 4.9 %collective-permute-start.15 = (bf16[112,128]{1,0:T(8,128)(2,1)S(1)}, bf16[112,128]{1,0:T(8,128)(2,1)S(1)}, u32[]{:S(2)}, u32[]{:S(2)}) collective-permute-start(bf16[112,128]{1,0:T(8,128)(2,1)S(1)} %get-tuple-element.63), channel_id=1, source_target_pairs={{0,16},{1,17},{2,18},{3,19},{4,20},{5,21},{6,22},{7,23},{8,24},{9,... | collective-permute-start | bytes 86024 | tf_op jit(solution)/shard_map/ppermute | solution.py:515
  40.4 5.8 %collective-permute-start.16 = (bf16[112,128]{1,0:T(8,128)(2,1)S(1)}, bf16[112,128]{1,0:T(8,128)(2,1)S(1)}, u32[]{:S(2)}, u32[]{:S(2)}) collective-permute-start(bf16[112,128]{1,0:T(8,128)(2,1)S(1)} %get-tuple-element.64), channel_id=1, source_target_pairs={{0,24},{1,25},{2,26},{3,27},{4,28},{5,29},{6,30},{7,31},{8,16},{9,... | collective-permute-start | bytes 86024 | tf_op jit(solution)/shard_map/ppermute | solution.py:515
  41.8 4.4 %collective-permute-start.17 = (bf16[112,128]{1,0:T(8,128)(2,1)S(1)}, bf16[112,128]{1,0:T(8,128)(2,1)S(1)}, u32[]{:S(2)}, u32[]{:S(2)}) collective-permute-start(bf16[112,128]{1,0:T(8,128)(2,1)S(1)} %get-tuple-element.65), channel_id=1, source_target_pairs={{0,8},{1,9},{2,10},{3,11},{4,12},{5,13},{6,14},{7,15},{8,0},{9,1},... | collective-permute-start | bytes 86024 | tf_op jit(solution)/shard_map/ppermute | solution.py:515
  46.2 6.0 %collective-permute-start.20 = (bf16[224,128]{1,0:T(8,128)(2,1)S(1)}, bf16[224,128]{1,0:T(8,128)(2,1)S(1)}, u32[]{:S(2)}, u32[]{:S(2)}) collective-permute-start(bf16[224,128]{1,0:T(8,128)(2,1)S(1)} %shard_map.102.refs_0_), channel_id=1, source_target_pairs={{0,24},{1,25},{2,26},{3,27},{4,28},{5,29},{6,30},{7,31},{8,16},{9,... | collective-permute-start | bytes 172040 | tf_op jit(solution)/shard_map/ppermute | solution.py:515
  48.2 5.3 %collective-permute-start.19 = (bf16[224,128]{1,0:T(8,128)(2,1)S(1)}, bf16[224,128]{1,0:T(8,128)(2,1)S(1)}, u32[]{:S(2)}, u32[]{:S(2)}) collective-permute-start(bf16[224,128]{1,0:T(8,128)(2,1)S(1)} %shard_map.102.refs_0_), channel_id=1, source_target_pairs={{0,16},{1,17},{2,18},{3,19},{4,20},{5,21},{6,22},{7,23},{8,24},{9,... | collective-permute-start | bytes 172040 | tf_op jit(solution)/shard_map/ppermute | solution.py:515
  48.2 5.3 %collective-permute-start.18 = (bf16[224,128]{1,0:T(8,128)(2,1)S(1)}, bf16[224,128]{1,0:T(8,128)(2,1)S(1)}, u32[]{:S(2)}, u32[]{:S(2)}) collective-permute-start(bf16[224,128]{1,0:T(8,128)(2,1)S(1)} %shard_map.102.refs_0_), channel_id=1, source_target_pairs={{0,8},{1,9},{2,10},{3,11},{4,12},{5,13},{6,14},{7,15},{8,0},{9,1},... | collective-permute-start | bytes 172040 | tf_op jit(solution)/shard_map/ppermute | solution.py:515
  53.6 7.1 %collective-permute-start.23 = (bf16[848,128]{1,0:T(8,128)(2,1)S(1)}, bf16[848,128]{1,0:T(8,128)(2,1)S(1)}, u32[]{:S(2)}, u32[]{:S(2)}) collective-permute-start(bf16[848,128]{1,0:T(8,128)(2,1)S(1)} %shard_map.103.refs_0_), channel_id=1, source_target_pairs={{0,3},{1,2},{2,1},{3,0},{4,7},{5,6},{6,5},{7,4},{8,11},{9,10},{10,... | collective-permute-start | bytes 651272 | tf_op jit(solution)/shard_map/ppermute | solution.py:515
  54.8 8.1 %collective-permute-start.22 = (bf16[848,128]{1,0:T(8,128)(2,1)S(1)}, bf16[848,128]{1,0:T(8,128)(2,1)S(1)}, u32[]{:S(2)}, u32[]{:S(2)}) collective-permute-start(bf16[848,128]{1,0:T(8,128)(2,1)S(1)} %shard_map.103.refs_0_), channel_id=1, source_target_pairs={{0,2},{1,3},{2,0},{3,1},{4,6},{5,7},{6,4},{7,5},{8,10},{9,11},{10,... | collective-permute-start | bytes 651272 | tf_op jit(solution)/shard_map/ppermute | solution.py:515
  55.7 7.2 %collective-permute-start.21 = (bf16[848,128]{1,0:T(8,128)(2,1)S(1)}, bf16[848,128]{1,0:T(8,128)(2,1)S(1)}, u32[]{:S(2)}, u32[]{:S(2)}) collective-permute-start(bf16[848,128]{1,0:T(8,128)(2,1)S(1)} %shard_map.103.refs_0_), channel_id=1, source_target_pairs={{0,1},{1,0},{2,3},{3,2},{4,5},{5,4},{6,7},{7,6},{8,9},{9,8},{10,11... | collective-permute-start | bytes 651272 | tf_op jit(solution)/shard_map/ppermute | solution.py:515
  57.1 7.2 %collective-permute-start.24 = (bf16[848,128]{1,0:T(8,128)(2,1)S(1)}, bf16[848,128]{1,0:T(8,128)(2,1)S(1)}, u32[]{:S(2)}, u32[]{:S(2)}) collective-permute-start(bf16[848,128]{1,0:T(8,128)(2,1)S(1)} %shard_map.103.refs_0_), channel_id=1, source_target_pairs={{0,4},{1,5},{2,6},{3,7},{4,0},{5,1},{6,2},{7,3},{8,12},{9,13},{10,... | collective-permute-start | bytes 651272 | tf_op jit(solution)/shard_map/ppermute | solution.py:515
  60.7 3.6 %collective-permute-start.27 = (bf16[848,128]{1,0:T(8,128)(2,1)S(1)}, bf16[848,128]{1,0:T(8,128)(2,1)S(1)}, u32[]{:S(2)}, u32[]{:S(2)}) collective-permute-start(bf16[848,128]{1,0:T(8,128)(2,1)S(1)} %collective-permute-done.23.refs_3_), channel_id=1, source_target_pairs={{0,4},{1,5},{2,6},{3,7},{4,0},{5,1},{6,2},{7,3},{8,12},{9,13},{10,... | collective-permute-start | bytes 651272 | tf_op jit(solution)/shard_map/ppermute | solution.py:515
  62.9 1.5 %collective-permute-start.26 = (bf16[848,128]{1,0:T(8,128)(2,1)S(1)}, bf16[848,128]{1,0:T(8,128)(2,1)S(1)}, u32[]{:S(2)}, u32[]{:S(2)}) collective-permute-start(bf16[848,128]{1,0:T(8,128)(2,1)S(1)} %collective-permute-done.22.refs_2_), channel_id=1, source_target_pairs={{0,4},{1,5},{2,6},{3,7},{4,0},{5,1},{6,2},{7,3},{8,12},{9,13},{10,... | collective-permute-start | bytes 651272 | tf_op jit(solution)/shard_map/ppermute | solution.py:515
  62.9 1.8 %collective-permute-start.25 = (bf16[848,128]{1,0:T(8,128)(2,1)S(1)}, bf16[848,128]{1,0:T(8,128)(2,1)S(1)}, u32[]{:S(2)}, u32[]{:S(2)}) collective-permute-start(bf16[848,128]{1,0:T(8,128)(2,1)S(1)} %collective-permute-done.21.refs_1_), channel_id=1, source_target_pairs={{0,4},{1,5},{2,6},{3,7},{4,0},{5,1},{6,2},{7,3},{8,12},{9,13},{10,... | collective-permute-start | bytes 651272 | tf_op jit(solution)/shard_map/ppermute | solution.py:515
  (1 other events, 0.9 us)

commit v8 on v7

--- a/solution.py
+++ b/solution.py
@@ -199,9 +199,8 @@
         wnt_ref[total * k : total * k + total] = wn_ref[total * k : total * k + total].T
 
 
-def sigmoid_slope(value):
-    gate = jax.nn.sigmoid(value)
-    return gate, gate + value * gate * (1.0 - gate)
+def slope_at(value, gate):
+    return gate + value * gate * (1.0 - gate)
 
 
 def shifted(value):
@@ -283,10 +282,12 @@
             flat(ref[low + ky : low + ky + step]) for ky in range(3) for ref in (pair, side)
         ]
         pre = dot_rows(jnp.concatenate(taken, axis=1), wfwd[...], step * pitch // 3)
-        sig, slp = sigmoid_slope(pre)
+        sig = jax.nn.sigmoid(pre)
         own = flat(pair[low + 1 : low + 1 + step]).astype(F32)
         act[low : low + step] = (own + pre * sig).astype(BF).reshape(step, pitch, 256)
-        slope[low : low + step] = slp.reshape(step, pitch, 256)
+        first, last = max(low, 4), min(low + step, act_rows - 4)
+        here = slice((first - low) * pitch, (last - low) * pitch)
+        slope[first:last] = slope_at(pre[here], sig[here]).reshape(last - first, pitch, 256)
 
     def inside(value, first_row):
         r = lax.broadcasted_iota(jnp.int32, value.shape, 0) + (row * half_rows + first_row)
@@ -306,10 +307,12 @@
     gate_rows = neck_rows - 2
     taken = [flat(neck[kx, ky : ky + gate_rows]) for ky in range(3) for kx in range(3)]
     pre = dot_rows(jnp.concatenate(taken, axis=1), wn_ref[...], 4 * pitch)
-    sig, slp = sigmoid_slope(pre)
-    own = flat(neck[1, 1 : 1 + gate_rows]).astype(F32)
-    out = (own + pre * sig).astype(BF).reshape(gate_rows, pitch, total)
-    out = out[2 : 2 + half_rows, :half_cols].reshape(half_rows * half_cols, total)
+    sig = jax.nn.sigmoid(pre)
+    slp = slope_at(pre, sig)
+    own = flat(neck[1, 3 : 3 + half_rows]).astype(F32)
+    here = slice(2 * pitch, (2 + half_rows) * pitch)
+    out = (own + pre[here] * sig[here]).astype(BF).reshape(half_rows, pitch, total)
+    out = out[:, :half_cols].reshape(half_rows * half_cols, total)
     out_ref[...] = out
     value = (flat(cot_all[...]).astype(F32) * slp).astype(BF).reshape(gate_rows, pitch, total)
     before, behind = shifted(value.astype(F32))

time: 66.3 us -> 66.3 us (level)
  no operation moved by 1% of the time
where the time goes in v8:
time: 66.3 us; the launch traced here: 66.1 us
  starting transfers between devices  35.1 us (53%)
  waiting for transfers between devices  21.5 us (32%)
  Pallas kernels  7.97 us (12%)
  local copies, waits for them, and re-layouts  0.89 us (1%)
  between operations  0.74 us (1%)
    ppermute x28, starting transfers between devices, permute(): lax.ppermute(value, axes, [(a, b) for a, b in pairs if b is not None])  35.1 us
    ppermute x28, waiting for transfers between devices, permute(): lax.ppermute(value, axes, [(a, b) for a, b in pairs if b is not None])  21.5 us
    pallas_call x13, Pallas kernels, call(): pl.pallas_call(body, out_shape=out_shapes, in_specs=[VMEM] * len(args), o...  7.97 us
  transfers between devices with their start and end apart: 28, of which 13 were waited for; matrix products, arithmetic and copies ran while one was open for 0% of the time, Pallas kernels for 3%

profile of v8, /device:TPU:0, one launch (start us, length us, event | category | flops | bytes accessed | tf_op | source)
XLA Modules:
  0.0 66.1 jit_solution(16315388837535223696)
XLA Ops:
  0.7 0.9 %copy-done.3 = bf16[8,64,128]{2,1,0:T(8,128)(2,1)S(1)} copy-done((bf16[8,64,128]{2,1,0:T(8,128)(2,1)S(1)}, bf16[8,64,128]{2,1,0:T(8,128)(2,1)}, u32[]{:S(2)}) %copy-start.3) | copy-done | bytes 131096
  1.8 3.0 %collective-permute-start = (bf16[144,128]{1,0:T(8,128)(2,1)S(1)}, bf16[144,128]{1,0:T(8,128)(2,1)S(1)}, u32[]{:S(2)}, u32[]{:S(2)}) collective-permute-start(bf16[144,128]{1,0:T(8,128)(2,1)S(1)} %get-tuple-element.37), channel_id=1, source_target_pairs={{0,1},{1,0},{2,3},{3,2},{4,5},{5,4},{6,7},{7,6},{8,9},{9,8},{10,11... | collective-permute-start | bytes 110600 | tf_op jit(solution)/shard_map/ppermute | solution.py:518
  4.8 1.5 %collective-permute-start.2 = (bf16[144,128]{1,0:T(8,128)(2,1)S(1)}, bf16[144,128]{1,0:T(8,128)(2,1)S(1)}, u32[]{:S(2)}, u32[]{:S(2)}) collective-permute-start(bf16[144,128]{1,0:T(8,128)(2,1)S(1)} %get-tuple-element.39), channel_id=1, source_target_pairs={{0,3},{1,2},{2,1},{3,0},{4,7},{5,6},{6,5},{7,4},{8,11},{9,10},{10,... | collective-permute-start | bytes 110600 | tf_op jit(solution)/shard_map/ppermute | solution.py:518
  6.4 3.7 %collective-permute-done.1.refs_1_ = bf16[80,128]{1,0:T(8,128)(2,1)S(1)} collective-permute-done((bf16[80,128]{1,0:T(8,128)(2,1)S(1)}, bf16[80,128]{1,0:T(8,128)(2,1)S(1)}, u32[]{:S(2)}, u32[]{:S(2)}) %collective-permute-start.1) | collective-permute-done | bytes 20512 | tf_op jit(solution)/shard_map/ppermute | solution.py:518
  10.4 0.7 %collective-permute-start.3 = (bf16[720,128]{1,0:T(8,128)(2,1)S(1)}, bf16[720,128]{1,0:T(8,128)(2,1)S(1)}, u32[]{:S(2)}, u32[]{:S(2)}) collective-permute-start(bf16[720,128]{1,0:T(8,128)(2,1)S(1)} %get-tuple-element.41), channel_id=1, source_target_pairs={{4,8},{5,9},{6,10},{7,11},{8,4},{9,5},{10,6},{11,7},{12,16},{13,17... | collective-permute-start | bytes 552968 | tf_op jit(solution)/shard_map/ppermute | solution.py:518
  11.1 3.0 %collective-permute-start.4 = (bf16[720,128]{1,0:T(8,128)(2,1)S(1)}, bf16[720,128]{1,0:T(8,128)(2,1)S(1)}, u32[]{:S(2)}, u32[]{:S(2)}) collective-permute-start(bf16[720,128]{1,0:T(8,128)(2,1)S(1)} %get-tuple-element.42), channel_id=1, source_target_pairs={{0,4},{1,5},{2,6},{3,7},{4,0},{5,1},{6,2},{7,3},{8,12},{9,13},{10,... | collective-permute-start | bytes 552968 | tf_op jit(solution)/shard_map/ppermute | solution.py:518
  14.1 0.6 shard_map.95
  15.1 3.8 %shard_map.96 = (bf16[6784,128]{1,0:T(8,128)(2,1)S(1)}, bf16[3392,128]{1,0:T(8,128)(2,1)S(1)}, bf16[128,256]{1,0:T(8,128)(2,1)S(1)}, bf16[8,64,128]{2,1,0:T(8,128)(2,1)}) custom-call(bf16[1152,128]{1,0:T(8,128)(2,1)S(1)} %get-tuple-element.40.kept_ref, bf16[720,128]{1,0:T(8,128)(2,1)S(1)} %collective-permute-done.3.cross_ref, ...), custom_call_target="tpu_custom_call" | custom-call | flops 6000000000 | tf_op jit(solution)/shard_map/pallas_call | solution.py:18
  18.9 2.0 %collective-permute-start.5 = (bf16[3392,128]{1,0:T(8,128)(2,1)S(1)}, bf16[3392,128]{1,0:T(8,128)(2,1)S(1)}, u32[]{:S(2)}, u32[]{:S(2)}) collective-permute-start(bf16[3392,128]{1,0:T(8,128)(2,1)S(1)} %get-tuple-element.49), channel_id=1, source_target_pairs={{0,4},{1,5},{2,6},{3,7},{4,0},{5,1},{6,2},{7,3},{8,12},{9,13},{10,... | collective-permute-start | bytes 2605064 | tf_op jit(solution)/shard_map/ppermute | solution.py:518
  21.3 1.7 %collective-permute-done.5.got_ref = bf16[3392,128]{1,0:T(8,128)(2,1)S(1)} collective-permute-done((bf16[3392,128]{1,0:T(8,128)(2,1)S(1)}, bf16[3392,128]{1,0:T(8,128)(2,1)S(1)}, u32[]{:S(2)}, u32[]{:S(2)}) %collective-permute-start.5) | collective-permute-done | bytes 868384 | tf_op jit(solution)/shard_map/ppermute | solution.py:518
  23.2 1.6 %collective-permute-start.9 = (bf16[432,128]{1,0:T(8,128)(2,1)S(1)}, bf16[432,128]{1,0:T(8,128)(2,1)S(1)}, u32[]{:S(2)}, u32[]{:S(2)}) collective-permute-start(bf16[432,128]{1,0:T(8,128)(2,1)S(1)} %get-tuple-element.55), channel_id=1, source_target_pairs={{0,1},{1,0},{2,3},{3,2},{4,5},{5,4},{6,7},{7,6},{8,9},{9,8},{10,11... | collective-permute-start | bytes 331784 | tf_op jit(solution)/shard_map/ppermute | solution.py:518
  25.2 1.5 %collective-permute-start.11 = (bf16[432,128]{1,0:T(8,128)(2,1)S(1)}, bf16[432,128]{1,0:T(8,128)(2,1)S(1)}, u32[]{:S(2)}, u32[]{:S(2)}) collective-permute-start(bf16[432,128]{1,0:T(8,128)(2,1)S(1)} %get-tuple-element.57), channel_id=1, source_target_pairs={{0,3},{1,2},{2,1},{3,0},{4,7},{5,6},{6,5},{7,4},{8,11},{9,10},{10,... | collective-permute-start | bytes 331784 | tf_op jit(solution)/shard_map/ppermute | solution.py:518
  26.7 1.5 %collective-permute-start.6 = (bf16[480,128]{1,0:T(8,128)(2,1)S(1)}, bf16[480,128]{1,0:T(8,128)(2,1)S(1)}, u32[]{:S(2)}, u32[]{:S(2)}) collective-permute-start(bf16[480,128]{1,0:T(8,128)(2,1)S(1)} %get-tuple-element.50), channel_id=1, source_target_pairs={{0,1},{1,0},{2,3},{3,2},{4,5},{5,4},{6,7},{7,6},{8,9},{9,8},{10,11... | collective-permute-start | bytes 368648 | tf_op jit(solution)/shard_map/ppermute | solution.py:518
  28.7 1.6 %collective-permute-start.8 = (bf16[480,128]{1,0:T(8,128)(2,1)S(1)}, bf16[480,128]{1,0:T(8,128)(2,1)S(1)}, u32[]{:S(2)}, u32[]{:S(2)}) collective-permute-start(bf16[480,128]{1,0:T(8,128)(2,1)S(1)} %get-tuple-element.52), channel_id=1, source_target_pairs={{0,3},{1,2},{2,1},{3,0},{4,7},{5,6},{6,5},{7,4},{8,11},{9,10},{10,... | collective-permute-start | bytes 368648 | tf_op jit(solution)/shard_map/ppermute | solution.py:518
  30.3 2.4 %collective-permute-done.10.refs_1_ = bf16[432,128]{1,0:T(8,128)(2,1)S(1)} collective-permute-done((bf16[432,128]{1,0:T(8,128)(2,1)S(1)}, bf16[432,128]{1,0:T(8,128)(2,1)S(1)}, u32[]{:S(2)}, u32[]{:S(2)}) %collective-permute-start.10) | collective-permute-done | bytes 110624 | tf_op jit(solution)/shard_map/ppermute | solution.py:518
  32.7 3.0 %collective-permute-start.12 = (bf16[112,128]{1,0:T(8,128)(2,1)S(1)}, bf16[112,128]{1,0:T(8,128)(2,1)S(1)}, u32[]{:S(2)}, u32[]{:S(2)}) collective-permute-start(bf16[112,128]{1,0:T(8,128)(2,1)S(1)} %get-tuple-element.59), channel_id=1, source_target_pairs={{0,16},{1,17},{2,18},{3,19},{4,20},{5,21},{6,22},{7,23},{8,24},{9,... | collective-permute-start | bytes 86024 | tf_op jit(solution)/shard_map/ppermute | solution.py:518
  35.7 1.3 %collective-permute-start.13 = (bf16[112,128]{1,0:T(8,128)(2,1)S(1)}, bf16[112,128]{1,0:T(8,128)(2,1)S(1)}, u32[]{:S(2)}, u32[]{:S(2)}) collective-permute-start(bf16[112,128]{1,0:T(8,128)(2,1)S(1)} %get-tuple-element.60), channel_id=1, source_target_pairs={{0,24},{1,25},{2,26},{3,27},{4,28},{5,29},{6,30},{7,31},{8,16},{9,... | collective-permute-start | bytes 86024 | tf_op jit(solution)/shard_map/ppermute | solution.py:518
  37.5 2.9 %collective-permute-start.15 = (bf16[112,128]{1,0:T(8,128)(2,1)S(1)}, bf16[112,128]{1,0:T(8,128)(2,1)S(1)}, u32[]{:S(2)}, u32[]{:S(2)}) collective-permute-start(bf16[112,128]{1,0:T(8,128)(2,1)S(1)} %get-tuple-element.63), channel_id=1, source_target_pairs={{0,16},{1,17},{2,18},{3,19},{4,20},{5,21},{6,22},{7,23},{8,24},{9,... | collective-permute-start | bytes 86024 | tf_op jit(solution)/shard_map/ppermute | solution.py:518
  40.4 1.3 %collective-permute-start.16 = (bf16[112,128]{1,0:T(8,128)(2,1)S(1)}, bf16[112,128]{1,0:T(8,128)(2,1)S(1)}, u32[]{:S(2)}, u32[]{:S(2)}) collective-permute-start(bf16[112,128]{1,0:T(8,128)(2,1)S(1)} %get-tuple-element.64), channel_id=1, source_target_pairs={{0,24},{1,25},{2,26},{3,27},{4,28},{5,29},{6,30},{7,31},{8,16},{9,... | collective-permute-start | bytes 86024 | tf_op jit(solution)/shard_map/ppermute | solution.py:518
  42.3 3.9 %collective-permute-done.16.refs_6_ = bf16[112,128]{1,0:T(8,128)(2,1)S(1)} collective-permute-done((bf16[112,128]{1,0:T(8,128)(2,1)S(1)}, bf16[112,128]{1,0:T(8,128)(2,1)S(1)}, u32[]{:S(2)}, u32[]{:S(2)}) %collective-permute-start.16) | collective-permute-done | bytes 28704 | tf_op jit(solution)/shard_map/ppermute | solution.py:518
  46.2 2.0 %collective-permute-start.20 = (bf16[224,128]{1,0:T(8,128)(2,1)S(1)}, bf16[224,128]{1,0:T(8,128)(2,1)S(1)}, u32[]{:S(2)}, u32[]{:S(2)}) collective-permute-start(bf16[224,128]{1,0:T(8,128)(2,1)S(1)} %shard_map.102.refs_0_), channel_id=1, source_target_pairs={{0,24},{1,25},{2,26},{3,27},{4,28},{5,29},{6,30},{7,31},{8,16},{9,... | collective-permute-start | bytes 172040 | tf_op jit(solution)/shard_map/ppermute | solution.py:518
  48.2 2.5 %collective-permute-start.18 = (bf16[224,128]{1,0:T(8,128)(2,1)S(1)}, bf16[224,128]{1,0:T(8,128)(2,1)S(1)}, u32[]{:S(2)}, u32[]{:S(2)}) collective-permute-start(bf16[224,128]{1,0:T(8,128)(2,1)S(1)} %shard_map.102.refs_0_), channel_id=1, source_target_pairs={{0,8},{1,9},{2,10},{3,11},{4,12},{5,13},{6,14},{7,15},{8,0},{9,1},... | collective-permute-start | bytes 172040 | tf_op jit(solution)/shard_map/ppermute | solution.py:518
  50.7 1.6 %collective-permute-done.20.refs_3_ = bf16[224,128]{1,0:T(8,128)(2,1)S(1)} collective-permute-done((bf16[224,128]{1,0:T(8,128)(2,1)S(1)}, bf16[224,128]{1,0:T(8,128)(2,1)S(1)}, u32[]{:S(2)}, u32[]{:S(2)}) %collective-permute-start.20) | collective-permute-done | bytes 57376 | tf_op jit(solution)/shard_map/ppermute | solution.py:518
  52.3 1.2 %collective-permute-done.19.refs_2_ = bf16[224,128]{1,0:T(8,128)(2,1)S(1)} collective-permute-done((bf16[224,128]{1,0:T(8,128)(2,1)S(1)}, bf16[224,128]{1,0:T(8,128)(2,1)S(1)}, u32[]{:S(2)}, u32[]{:S(2)}) %collective-permute-start.19) | collective-permute-done | bytes 57376 | tf_op jit(solution)/shard_map/ppermute | solution.py:518
  53.6 1.2 %collective-permute-start.23 = (bf16[848,128]{1,0:T(8,128)(2,1)S(1)}, bf16[848,128]{1,0:T(8,128)(2,1)S(1)}, u32[]{:S(2)}, u32[]{:S(2)}) collective-permute-start(bf16[848,128]{1,0:T(8,128)(2,1)S(1)} %shard_map.103.refs_0_), channel_id=1, source_target_pairs={{0,3},{1,2},{2,1},{3,0},{4,7},{5,6},{6,5},{7,4},{8,11},{9,10},{10,... | collective-permute-start | bytes 651272 | tf_op jit(solution)/shard_map/ppermute | solution.py:518
  54.8 0.9 %collective-permute-start.22 = (bf16[848,128]{1,0:T(8,128)(2,1)S(1)}, bf16[848,128]{1,0:T(8,128)(2,1)S(1)}, u32[]{:S(2)}, u32[]{:S(2)}) collective-permute-start(bf16[848,128]{1,0:T(8,128)(2,1)S(1)} %shard_map.103.refs_0_), channel_id=1, source_target_pairs={{0,2},{1,3},{2,0},{3,1},{4,6},{5,7},{6,4},{7,5},{8,10},{9,11},{10,... | collective-permute-start | bytes 651272 | tf_op jit(solution)/shard_map/ppermute | solution.py:518
  55.7 1.4 %collective-permute-start.21 = (bf16[848,128]{1,0:T(8,128)(2,1)S(1)}, bf16[848,128]{1,0:T(8,128)(2,1)S(1)}, u32[]{:S(2)}, u32[]{:S(2)}) collective-permute-start(bf16[848,128]{1,0:T(8,128)(2,1)S(1)} %shard_map.103.refs_0_), channel_id=1, source_target_pairs={{0,1},{1,0},{2,3},{3,2},{4,5},{5,4},{6,7},{7,6},{8,9},{9,8},{10,11... | collective-permute-start | bytes 651272 | tf_op jit(solution)/shard_map/ppermute | solution.py:518
  57.1 3.5 %collective-permute-done.23.refs_3_ = bf16[848,128]{1,0:T(8,128)(2,1)S(1)} collective-permute-done((bf16[848,128]{1,0:T(8,128)(2,1)S(1)}, bf16[848,128]{1,0:T(8,128)(2,1)S(1)}, u32[]{:S(2)}, u32[]{:S(2)}) %collective-permute-start.23) | collective-permute-done | bytes 217120 | tf_op jit(solution)/shard_map/ppermute | solution.py:518
  60.7 2.2 %collective-permute-done.22.refs_2_ = bf16[848,128]{1,0:T(8,128)(2,1)S(1)} collective-permute-done((bf16[848,128]{1,0:T(8,128)(2,1)S(1)}, bf16[848,128]{1,0:T(8,128)(2,1)S(1)}, u32[]{:S(2)}, u32[]{:S(2)}) %collective-permute-start.22) | collective-permute-done | bytes 217120 | tf_op jit(solution)/shard_map/ppermute | solution.py:518
  62.9 0.5 collective-permute-start.25
  63.4 0.9 %shard_map.99 = bf16[4,64,128]{2,1,0:T(8,128)(2,1)} custom-call(bf16[4,64,128]{2,1,0:T(8,128)(2,1)S(1)} %shard_map.97.pieces_ref, bf16[480,128]{1,0:T(8,128)(2,1)S(1)} %collective-permute-done.6.refs_0_, bf16[480,128]{1,0:T(8,128)(2,1)S(1)} %collective-permute-done.7.refs_1_, bf16[480,128]{1,0:T(8,128)(2,1)S(1)} %collective-permute-done.8.refs_2_), custom_call_target="tpu_custom_call" | custom-call | flops 1000000000 | tf_op jit(solution)/shard_map/pallas_call | solution.py:18
  64.7 1.5 %shard_map.104 = (bf16[9,128,128]{2,1,0:T(8,128)(2,1)}, bf16[4,128,256]{2,1,0:T(8,128)(2,1)}, bf16[9,256,256]{2,1,0:T(8,128)(2,1)}) custom-call(bf16[848,128]{1,0:T(8,128)(2,1)S(1)} %shard_map.103.refs_0_, bf16[848,128]{1,0:T(8,128)(2,1)S(1)} %collective-permute-done.21.refs_1_, bf16[848,128]{1,0:T(8,128)(2,1)S(1)} %collective-permute-done.22.refs_2_, ...), custom_call_target="tpu_custom_call" | custom-call | flops 1000000000 | tf_op jit(solution)/shard_map/pallas_call | solution.py:18
  (47 shorter events, 4.2 us)
Async XLA Ops:
  0.6 0.9 %copy-start.3 = (bf16[8,64,128]{2,1,0:T(8,128)(2,1)S(1)}, bf16[8,64,128]{2,1,0:T(8,128)(2,1)}, u32[]{:S(2)}) copy-start(bf16[8,64,128]{2,1,0:T(8,128)(2,1)} %level_ref.3) | copy-start | bytes 393220
  1.8 8.3 %collective-permute-start = (bf16[144,128]{1,0:T(8,128)(2,1)S(1)}, bf16[144,128]{1,0:T(8,128)(2,1)S(1)}, u32[]{:S(2)}, u32[]{:S(2)}) collective-permute-start(bf16[144,128]{1,0:T(8,128)(2,1)S(1)} %get-tuple-element.37), channel_id=1, source_target_pairs={{0,1},{1,0},{2,3},{3,2},{4,5},{5,4},{6,7},{7,6},{8,9},{9,8},{10,11... | collective-permute-start | bytes 110600 | tf_op jit(solution)/shard_map/ppermute | solution.py:518
  4.8 5.3 %collective-permute-start.2 = (bf16[144,128]{1,0:T(8,128)(2,1)S(1)}, bf16[144,128]{1,0:T(8,128)(2,1)S(1)}, u32[]{:S(2)}, u32[]{:S(2)}) collective-permute-start(bf16[144,128]{1,0:T(8,128)(2,1)S(1)} %get-tuple-element.39), channel_id=1, source_target_pairs={{0,3},{1,2},{2,1},{3,0},{4,7},{5,6},{6,5},{7,4},{8,11},{9,10},{10,... | collective-permute-start | bytes 110600 | tf_op jit(solution)/shard_map/ppermute | solution.py:518
  6.3 7.8 %copy-start = (bf16[3,3,256,256]{3,2,1,0:T(8,128)(2,1)S(1)}, bf16[3,3,256,256]{3,2,1,0:T(8,128)(2,1)}, u32[]{:S(2)}) copy-start(bf16[3,3,256,256]{3,2,1,0:T(8,128)(2,1)} %param.8) | copy-start | bytes 3538948
  6.3 7.8 %copy-start.1 = (bf16[3,3,128,128]{3,2,1,0:T(8,128)(2,1)S(1)}, bf16[3,3,128,128]{3,2,1,0:T(8,128)(2,1)}, u32[]{:S(2)}) copy-start(bf16[3,3,128,128]{3,2,1,0:T(8,128)(2,1)} %param.6) | copy-start | bytes 884740
  6.3 7.8 %copy-start.2 = (bf16[2,2,128,256]{3,2,1,0:T(8,128)(2,1)S(1)}, bf16[2,2,128,256]{3,2,1,0:T(8,128)(2,1)}, u32[]{:S(2)}) copy-start(bf16[2,2,128,256]{3,2,1,0:T(8,128)(2,1)} %param.7) | copy-start | bytes 786436
  6.3 3.8 %collective-permute-start.1 = (bf16[80,128]{1,0:T(8,128)(2,1)S(1)}, bf16[80,128]{1,0:T(8,128)(2,1)S(1)}, u32[]{:S(2)}, u32[]{:S(2)}) collective-permute-start(bf16[80,128]{1,0:T(8,128)(2,1)S(1)} %get-tuple-element.38), channel_id=1, source_target_pairs={{0,2},{1,3},{2,0},{3,1},{4,6},{5,7},{6,4},{7,5},{8,10},{9,11},{10,... | collective-permute-start | bytes 61448 | tf_op jit(solution)/shard_map/ppermute | solution.py:518
  10.4 4.2 %collective-permute-start.3 = (bf16[720,128]{1,0:T(8,128)(2,1)S(1)}, bf16[720,128]{1,0:T(8,128)(2,1)S(1)}, u32[]{:S(2)}, u32[]{:S(2)}) collective-permute-start(bf16[720,128]{1,0:T(8,128)(2,1)S(1)} %get-tuple-element.41), channel_id=1, source_target_pairs={{4,8},{5,9},{6,10},{7,11},{8,4},{9,5},{10,6},{11,7},{12,16},{13,17... | collective-permute-start | bytes 552968 | tf_op jit(solution)/shard_map/ppermute | solution.py:518
  11.1 4.0 %collective-permute-start.4 = (bf16[720,128]{1,0:T(8,128)(2,1)S(1)}, bf16[720,128]{1,0:T(8,128)(2,1)S(1)}, u32[]{:S(2)}, u32[]{:S(2)}) collective-permute-start(bf16[720,128]{1,0:T(8,128)(2,1)S(1)} %get-tuple-element.42), channel_id=1, source_target_pairs={{0,4},{1,5},{2,6},{3,7},{4,0},{5,1},{6,2},{7,3},{8,12},{9,13},{10,... | collective-permute-start | bytes 552968 | tf_op jit(solution)/shard_map/ppermute | solution.py:518
  18.9 4.1 %collective-permute-start.5 = (bf16[3392,128]{1,0:T(8,128)(2,1)S(1)}, bf16[3392,128]{1,0:T(8,128)(2,1)S(1)}, u32[]{:S(2)}, u32[]{:S(2)}) collective-permute-start(bf16[3392,128]{1,0:T(8,128)(2,1)S(1)} %get-tuple-element.49), channel_id=1, source_target_pairs={{0,4},{1,5},{2,6},{3,7},{4,0},{5,1},{6,2},{7,3},{8,12},{9,13},{10,... | collective-permute-start | bytes 2605064 | tf_op jit(solution)/shard_map/ppermute | solution.py:518
  23.2 5.6 %collective-permute-start.9 = (bf16[432,128]{1,0:T(8,128)(2,1)S(1)}, bf16[432,128]{1,0:T(8,128)(2,1)S(1)}, u32[]{:S(2)}, u32[]{:S(2)}) collective-permute-start(bf16[432,128]{1,0:T(8,128)(2,1)S(1)} %get-tuple-element.55), channel_id=1, source_target_pairs={{0,1},{1,0},{2,3},{3,2},{4,5},{5,4},{6,7},{7,6},{8,9},{9,8},{10,11... | collective-permute-start | bytes 331784 | tf_op jit(solution)/shard_map/ppermute | solution.py:518
  24.7 7.9 %collective-permute-start.10 = (bf16[432,128]{1,0:T(8,128)(2,1)S(1)}, bf16[432,128]{1,0:T(8,128)(2,1)S(1)}, u32[]{:S(2)}, u32[]{:S(2)}) collective-permute-start(bf16[432,128]{1,0:T(8,128)(2,1)S(1)} %get-tuple-element.56), channel_id=1, source_target_pairs={{0,2},{1,3},{2,0},{3,1},{4,6},{5,7},{6,4},{7,5},{8,10},{9,11},{10,... | collective-permute-start | bytes 331784 | tf_op jit(solution)/shard_map/ppermute | solution.py:518
  25.2 7.4 %collective-permute-start.11 = (bf16[432,128]{1,0:T(8,128)(2,1)S(1)}, bf16[432,128]{1,0:T(8,128)(2,1)S(1)}, u32[]{:S(2)}, u32[]{:S(2)}) collective-permute-start(bf16[432,128]{1,0:T(8,128)(2,1)S(1)} %get-tuple-element.57), channel_id=1, source_target_pairs={{0,3},{1,2},{2,1},{3,0},{4,7},{5,6},{6,5},{7,4},{8,11},{9,10},{10,... | collective-permute-start | bytes 331784 | tf_op jit(solution)/shard_map/ppermute | solution.py:518
  26.7 10.4 %collective-permute-start.6 = (bf16[480,128]{1,0:T(8,128)(2,1)S(1)}, bf16[480,128]{1,0:T(8,128)(2,1)S(1)}, u32[]{:S(2)}, u32[]{:S(2)}) collective-permute-start(bf16[480,128]{1,0:T(8,128)(2,1)S(1)} %get-tuple-element.50), channel_id=1, source_target_pairs={{0,1},{1,0},{2,3},{3,2},{4,5},{5,4},{6,7},{7,6},{8,9},{9,8},{10,11... | collective-permute-start | bytes 368648 | tf_op jit(solution)/shard_map/ppermute | solution.py:518
  28.2 9.2 %collective-permute-start.7 = (bf16[480,128]{1,0:T(8,128)(2,1)S(1)}, bf16[480,128]{1,0:T(8,128)(2,1)S(1)}, u32[]{:S(2)}, u32[]{:S(2)}) collective-permute-start(bf16[480,128]{1,0:T(8,128)(2,1)S(1)} %get-tuple-element.51), channel_id=1, source_target_pairs={{0,2},{1,3},{2,0},{3,1},{4,6},{5,7},{6,4},{7,5},{8,10},{9,11},{10,... | collective-permute-start | bytes 368648 | tf_op jit(solution)/shard_map/ppermute | solution.py:518
  28.7 8.7 %collective-permute-start.8 = (bf16[480,128]{1,0:T(8,128)(2,1)S(1)}, bf16[480,128]{1,0:T(8,128)(2,1)S(1)}, u32[]{:S(2)}, u32[]{:S(2)}) collective-permute-start(bf16[480,128]{1,0:T(8,128)(2,1)S(1)} %get-tuple-element.52), channel_id=1, source_target_pairs={{0,3},{1,2},{2,1},{3,0},{4,7},{5,6},{6,5},{7,4},{8,11},{9,10},{10,... | collective-permute-start | bytes 368648 | tf_op jit(solution)/shard_map/ppermute | solution.py:518
  32.7 9.0 %collective-permute-start.12 = (bf16[112,128]{1,0:T(8,128)(2,1)S(1)}, bf16[112,128]{1,0:T(8,128)(2,1)S(1)}, u32[]{:S(2)}, u32[]{:S(2)}) collective-permute-start(bf16[112,128]{1,0:T(8,128)(2,1)S(1)} %get-tuple-element.59), channel_id=1, source_target_pairs={{0,16},{1,17},{2,18},{3,19},{4,20},{5,21},{6,22},{7,23},{8,24},{9,... | collective-permute-start | bytes 86024 | tf_op jit(solution)/shard_map/ppermute | solution.py:518
  35.7 6.3 %collective-permute-start.13 = (bf16[112,128]{1,0:T(8,128)(2,1)S(1)}, bf16[112,128]{1,0:T(8,128)(2,1)S(1)}, u32[]{:S(2)}, u32[]{:S(2)}) collective-permute-start(bf16[112,128]{1,0:T(8,128)(2,1)S(1)} %get-tuple-element.60), channel_id=1, source_target_pairs={{0,24},{1,25},{2,26},{3,27},{4,28},{5,29},{6,30},{7,31},{8,16},{9,... | collective-permute-start | bytes 86024 | tf_op jit(solution)/shard_map/ppermute | solution.py:518
  37.1 4.9 %collective-permute-start.14 = (bf16[112,128]{1,0:T(8,128)(2,1)S(1)}, bf16[112,128]{1,0:T(8,128)(2,1)S(1)}, u32[]{:S(2)}, u32[]{:S(2)}) collective-permute-start(bf16[112,128]{1,0:T(8,128)(2,1)S(1)} %get-tuple-element.61), channel_id=1, source_target_pairs={{0,8},{1,9},{2,10},{3,11},{4,12},{5,13},{6,14},{7,15},{8,0},{9,1},... | collective-permute-start | bytes 86024 | tf_op jit(solution)/shard_map/ppermute | solution.py:518
  37.5 4.9 %collective-permute-start.15 = (bf16[112,128]{1,0:T(8,128)(2,1)S(1)}, bf16[112,128]{1,0:T(8,128)(2,1)S(1)}, u32[]{:S(2)}, u32[]{:S(2)}) collective-permute-start(bf16[112,128]{1,0:T(8,128)(2,1)S(1)} %get-tuple-element.63), channel_id=1, source_target_pairs={{0,16},{1,17},{2,18},{3,19},{4,20},{5,21},{6,22},{7,23},{8,24},{9,... | collective-permute-start | bytes 86024 | tf_op jit(solution)/shard_map/ppermute | solution.py:518
  40.4 5.8 %collective-permute-start.16 = (bf16[112,128]{1,0:T(8,128)(2,1)S(1)}, bf16[112,128]{1,0:T(8,128)(2,1)S(1)}, u32[]{:S(2)}, u32[]{:S(2)}) collective-permute-start(bf16[112,128]{1,0:T(8,128)(2,1)S(1)} %get-tuple-element.64), channel_id=1, source_target_pairs={{0,24},{1,25},{2,26},{3,27},{4,28},{5,29},{6,30},{7,31},{8,16},{9,... | collective-permute-start | bytes 86024 | tf_op jit(solution)/shard_map/ppermute | solution.py:518
  41.8 4.4 %collective-permute-start.17 = (bf16[112,128]{1,0:T(8,128)(2,1)S(1)}, bf16[112,128]{1,0:T(8,128)(2,1)S(1)}, u32[]{:S(2)}, u32[]{:S(2)}) collective-permute-start(bf16[112,128]{1,0:T(8,128)(2,1)S(1)} %get-tuple-element.65), channel_id=1, source_target_pairs={{0,8},{1,9},{2,10},{3,11},{4,12},{5,13},{6,14},{7,15},{8,0},{9,1},... | collective-permute-start | bytes 86024 | tf_op jit(solution)/shard_map/ppermute | solution.py:518
  46.2 6.0 %collective-permute-start.20 = (bf16[224,128]{1,0:T(8,128)(2,1)S(1)}, bf16[224,128]{1,0:T(8,128)(2,1)S(1)}, u32[]{:S(2)}, u32[]{:S(2)}) collective-permute-start(bf16[224,128]{1,0:T(8,128)(2,1)S(1)} %shard_map.102.refs_0_), channel_id=1, source_target_pairs={{0,24},{1,25},{2,26},{3,27},{4,28},{5,29},{6,30},{7,31},{8,16},{9,... | collective-permute-start | bytes 172040 | tf_op jit(solution)/shard_map/ppermute | solution.py:518
  48.2 5.3 %collective-permute-start.19 = (bf16[224,128]{1,0:T(8,128)(2,1)S(1)}, bf16[224,128]{1,0:T(8,128)(2,1)S(1)}, u32[]{:S(2)}, u32[]{:S(2)}) collective-permute-start(bf16[224,128]{1,0:T(8,128)(2,1)S(1)} %shard_map.102.refs_0_), channel_id=1, source_target_pairs={{0,16},{1,17},{2,18},{3,19},{4,20},{5,21},{6,22},{7,23},{8,24},{9,... | collective-permute-start | bytes 172040 | tf_op jit(solution)/shard_map/ppermute | solution.py:518
  48.2 5.3 %collective-permute-start.18 = (bf16[224,128]{1,0:T(8,128)(2,1)S(1)}, bf16[224,128]{1,0:T(8,128)(2,1)S(1)}, u32[]{:S(2)}, u32[]{:S(2)}) collective-permute-start(bf16[224,128]{1,0:T(8,128)(2,1)S(1)} %shard_map.102.refs_0_), channel_id=1, source_target_pairs={{0,8},{1,9},{2,10},{3,11},{4,12},{5,13},{6,14},{7,15},{8,0},{9,1},... | collective-permute-start | bytes 172040 | tf_op jit(solution)/shard_map/ppermute | solution.py:518
  53.6 7.1 %collective-permute-start.23 = (bf16[848,128]{1,0:T(8,128)(2,1)S(1)}, bf16[848,128]{1,0:T(8,128)(2,1)S(1)}, u32[]{:S(2)}, u32[]{:S(2)}) collective-permute-start(bf16[848,128]{1,0:T(8,128)(2,1)S(1)} %shard_map.103.refs_0_), channel_id=1, source_target_pairs={{0,3},{1,2},{2,1},{3,0},{4,7},{5,6},{6,5},{7,4},{8,11},{9,10},{10,... | collective-permute-start | bytes 651272 | tf_op jit(solution)/shard_map/ppermute | solution.py:518
  54.8 8.1 %collective-permute-start.22 = (bf16[848,128]{1,0:T(8,128)(2,1)S(1)}, bf16[848,128]{1,0:T(8,128)(2,1)S(1)}, u32[]{:S(2)}, u32[]{:S(2)}) collective-permute-start(bf16[848,128]{1,0:T(8,128)(2,1)S(1)} %shard_map.103.refs_0_), channel_id=1, source_target_pairs={{0,2},{1,3},{2,0},{3,1},{4,6},{5,7},{6,4},{7,5},{8,10},{9,11},{10,... | collective-permute-start | bytes 651272 | tf_op jit(solution)/shard_map/ppermute | solution.py:518
  55.7 7.2 %collective-permute-start.21 = (bf16[848,128]{1,0:T(8,128)(2,1)S(1)}, bf16[848,128]{1,0:T(8,128)(2,1)S(1)}, u32[]{:S(2)}, u32[]{:S(2)}) collective-permute-start(bf16[848,128]{1,0:T(8,128)(2,1)S(1)} %shard_map.103.refs_0_), channel_id=1, source_target_pairs={{0,1},{1,0},{2,3},{3,2},{4,5},{5,4},{6,7},{7,6},{8,9},{9,8},{10,11... | collective-permute-start | bytes 651272 | tf_op jit(solution)/shard_map/ppermute | solution.py:518
  57.1 7.2 %collective-permute-start.24 = (bf16[848,128]{1,0:T(8,128)(2,1)S(1)}, bf16[848,128]{1,0:T(8,128)(2,1)S(1)}, u32[]{:S(2)}, u32[]{:S(2)}) collective-permute-start(bf16[848,128]{1,0:T(8,128)(2,1)S(1)} %shard_map.103.refs_0_), channel_id=1, source_target_pairs={{0,4},{1,5},{2,6},{3,7},{4,0},{5,1},{6,2},{7,3},{8,12},{9,13},{10,... | collective-permute-start | bytes 651272 | tf_op jit(solution)/shard_map/ppermute | solution.py:518
  60.7 3.6 %collective-permute-start.27 = (bf16[848,128]{1,0:T(8,128)(2,1)S(1)}, bf16[848,128]{1,0:T(8,128)(2,1)S(1)}, u32[]{:S(2)}, u32[]{:S(2)}) collective-permute-start(bf16[848,128]{1,0:T(8,128)(2,1)S(1)} %collective-permute-done.23.refs_3_), channel_id=1, source_target_pairs={{0,4},{1,5},{2,6},{3,7},{4,0},{5,1},{6,2},{7,3},{8,12},{9,13},{10,... | collective-permute-start | bytes 651272 | tf_op jit(solution)/shard_map/ppermute | solution.py:518
  62.9 1.5 %collective-permute-start.26 = (bf16[848,128]{1,0:T(8,128)(2,1)S(1)}, bf16[848,128]{1,0:T(8,128)(2,1)S(1)}, u32[]{:S(2)}, u32[]{:S(2)}) collective-permute-start(bf16[848,128]{1,0:T(8,128)(2,1)S(1)} %collective-permute-done.22.refs_2_), channel_id=1, source_target_pairs={{0,4},{1,5},{2,6},{3,7},{4,0},{5,1},{6,2},{7,3},{8,12},{9,13},{10,... | collective-permute-start | bytes 651272 | tf_op jit(solution)/shard_map/ppermute | solution.py:518
  62.9 1.8 %collective-permute-start.25 = (bf16[848,128]{1,0:T(8,128)(2,1)S(1)}, bf16[848,128]{1,0:T(8,128)(2,1)S(1)}, u32[]{:S(2)}, u32[]{:S(2)}) collective-permute-start(bf16[848,128]{1,0:T(8,128)(2,1)S(1)} %collective-permute-done.21.refs_1_), channel_id=1, source_target_pairs={{0,4},{1,5},{2,6},{3,7},{4,0},{5,1},{6,2},{7,3},{8,12},{9,13},{10,... | collective-permute-start | bytes 651272 | tf_op jit(solution)/shard_map/ppermute | solution.py:518
  (1 other events, 0.9 us)
